TPU v7x, 32 devices: a whole 2x2x4 slice. The times are simulated.
32 devices in a mesh: dp: 8 (over z, x), head: 4 (over y, core).
Axes of the slice: x: 2, y: 2, z: 4, core: 2. Of those that a mesh axis runs over, the one named last changes fastest.
Arguments:
- token_ids: int32 [2, 4096], P(None, ('dp', 'head')), may hold values from 0 to 31999
- lengths: int32 [2, 8, 3], P(None, 'dp'), may hold values from 1 to 409, 512 in all within a row
- valid: int32 [2, 4096], P(None, ('dp', 'head')), may hold values 0 or 1
- vocab_ids: int32 [4096], replicated, may hold values from 0 to 31999, as said below
- teacher: bfloat16 [2, 4096, 4096], P(None, ('dp', 'head')), may hold values from -12 to 12
- block: float32 [768, 12288], P(None, ('dp', 'head'))
- block_m: float32 [768, 12288], P(None, ('dp', 'head')), may hold values from -2.3841858e-07 to 2.3841858e-07
- block_v: float32 [768, 12288], P(None, ('dp', 'head')), may hold values from 1.1876942e-15 to 4.750777e-15
- bases: float32 [4, 768, 768], replicated
- table: float32 [32000, 768], P('dp'), may hold values from -0.4375 to 0.4375
- table_m: float32 [32000, 768], P('dp'), may hold values from -2.3841858e-07 to 2.3841858e-07
- table_v: float32 [32000, 768], P('dp'), may hold values from 1.1876942e-15 to 4.750777e-15
- gains: float32 [3, 768], replicated, may hold values from 0.5 to 1.5
- gains_m: float32 [3, 768], replicated, may hold values from -9.536743e-07 to 9.536743e-07
- gains_v: float32 [3, 768], replicated, may hold values from 1.899135e-14 to 7.6141784e-14
Outputs:
- loss: float32 [], replicated
- grad_norm: float32 [], replicated
- block_new: float32 [768, 12288], P(None, ('dp', 'head'))
- block_m_new: float32 [768, 12288], P(None, ('dp', 'head'))
- block_v_new: float32 [768, 12288], P(None, ('dp', 'head'))
- table_new: float32 [32000, 768], P('dp')
- table_m_new: float32 [32000, 768], P('dp')
- table_v_new: float32 [32000, 768], P('dp')
- gains_new: float32 [3, 768], replicated
- gains_m_new: float32 [3, 768], replicated
- gains_v_new: float32 [3, 768], replicated
- block_low: bfloat16 [768, 12288], P(None, ('dp', 'head'))
- table_low: bfloat16 [32000, 768], P('dp')
Inputs may be any that keep to these rules, and one draw needn't show every extreme that they name: `vocab_ids`: distinct ids. Each row holds the lengths of 3 sequences packed in order into one bucket; they sum to 512 and the largest is exactly 409.
All inputs are finite; a program needn't handle non-finite values. No bound on the sum of `valid` on one device may be relied on, other than what follows from the above.
Results may differ from a plain program's by a relative error of at most 0.02.
Values may be sent and summed in bfloat16 or wider, within the bound.
A program may use at most 248 MiB of HBM per device.

v0:
```python
import math

import jax
import jax.numpy as jnp
from jax import lax
from jax.sharding import PartitionSpec as P

D = 768
H = 12
HD = 64
FF = 3072
TOPV = 4096
STEP = 5


highest = lax.Precision.HIGHEST
eps_norm = 1e-05
clip_norm = 0.002
beta_one = 0.9
beta_two = 0.99
adam_eps = 1e-08
decay_rate = 0.1
rate_block = 0.03
rate_table = 0.05
rate_gain = 0.4


def product(left, right):
    return jnp.dot(left, right, preferred_element_type=jnp.float32)


def contract_rows(left, right):
    return lax.dot_general(
        left, right, (((0,), (0,)), ((), ())), preferred_element_type=jnp.float32
    )


def contract_cols(left, right):
    return lax.dot_general(
        left, right, (((1,), (1,)), ((), ())), preferred_element_type=jnp.float32
    )


def rms_norm(value, gain):
    return value * lax.rsqrt(jnp.mean(value * value, axis=-1, keepdims=True) + eps_norm) * gain


def rotary(value, cosine, sine):
    half = value.shape[-1] // 2
    turned = jnp.concatenate([-value[..., half:], value[..., :half]], axis=-1)
    return value * cosine[:, None, :] + turned * sine[:, None, :]


def tables(seq_lengths, size):
    ends = jnp.cumsum(seq_lengths)
    starts = ends - seq_lengths
    places = jnp.arange(size, dtype=jnp.int32)
    segment = jnp.sum((places[:, None] >= ends[None, :]).astype(jnp.int32), axis=1)
    member = segment[:, None] == jnp.arange(seq_lengths.shape[0], dtype=jnp.int32)[None, :]
    begin = jnp.sum(jnp.where(member, starts[None, :], 0), axis=1)
    position = (places - begin).astype(jnp.float32)
    freqs = jnp.exp(jnp.arange(0, HD, 2, dtype=jnp.float32) * (-math.log(10000.0) / HD))
    angle = position[:, None] * freqs[None, :]
    angle = jnp.concatenate([angle, angle], axis=1)
    allow = (segment[:, None] == segment[None, :]) & (places[:, None] >= places[None, :])
    return (allow, jnp.cos(angle), jnp.sin(angle))


def split_block(full, device_total):
    rows = full.shape[0]
    grouped = full.reshape(rows, device_total, -1)
    widths = [3 * D // device_total, D // device_total, 2 * FF // device_total, FF // device_total]
    pieces = []
    first = 0
    for width in widths:
        pieces.append(grouped[:, :, first : first + width].reshape(rows, device_total * width))
        first = first + width
    return pieces


def join_block(pieces, device_total):
    rows = pieces[0].shape[0]
    return jnp.concatenate(
        [piece.reshape(rows, device_total, -1) for piece in pieces], axis=2
    ).reshape(rows, -1)


def split_local(shard, device_total):
    widths = [3 * D // device_total, D // device_total, 2 * FF // device_total, FF // device_total]
    pieces = []
    first = 0
    for width in widths:
        pieces.append(shard[:, first : first + width])
        first = first + width
    return pieces


def scores_of(packed, allow, scale):
    score = (
        jnp.einsum("qhd,khd->hqk", packed[:, 0], packed[:, 1], preferred_element_type=jnp.float32)
        * scale
    )
    return jnp.where(allow[None], score, -1e30)


def attend_heads(packed, allow, scale):
    score = scores_of(packed, allow, scale)
    summit = jnp.max(score, axis=-1, keepdims=True)
    log_total = summit + jnp.log(jnp.sum(jnp.exp(score - summit), axis=-1, keepdims=True))
    weight = jnp.exp(score - log_total)
    mixed = jnp.einsum(
        "hqk,khd->qhd",
        weight.astype(jnp.bfloat16),
        packed[:, 2],
        preferred_element_type=jnp.float32,
    )
    return (mixed.astype(jnp.bfloat16), log_total)


def attend_back(packed, log_total, upstream, allow, scale):
    weight = jnp.exp(scores_of(packed, allow, scale) - log_total)
    d_value = jnp.einsum(
        "hqk,qhd->khd", weight.astype(jnp.bfloat16), upstream, preferred_element_type=jnp.float32
    )
    d_weight = jnp.einsum(
        "qhd,khd->hqk", upstream, packed[:, 2], preferred_element_type=jnp.float32
    )
    d_score = (weight * (d_weight - jnp.sum(d_weight * weight, axis=-1, keepdims=True))).astype(
        jnp.bfloat16
    )
    d_query = (
        jnp.einsum("hqk,khd->qhd", d_score, packed[:, 1], preferred_element_type=jnp.float32)
        * scale
    )
    d_key = (
        jnp.einsum("hqk,qhd->khd", d_score, packed[:, 0], preferred_element_type=jnp.float32)
        * scale
    )
    return jnp.stack([d_query, d_key, d_value], axis=1).astype(jnp.bfloat16)


def gated(gate_up):
    return jax.nn.silu(gate_up[:, :FF]) * gate_up[:, FF:]


def layer_forward(hidden, weights, gains, cosine, sine, allow, scale):
    w_qkv, w_out, w_gu, w_down = weights
    rows = hidden.shape[0]
    normed = rms_norm(hidden, gains[0]).astype(jnp.bfloat16)
    qkv = product(normed, w_qkv).reshape(rows, 3, H, HD)
    packed = jnp.stack(
        [rotary(qkv[:, 0], cosine, sine), rotary(qkv[:, 1], cosine, sine), qkv[:, 2]], axis=1
    ).astype(jnp.bfloat16)
    spread = lax.all_to_all(packed, "head", split_axis=2, concat_axis=0, tiled=True)
    mixed, log_total = attend_heads(spread, allow, scale)
    merged = lax.all_to_all(mixed, "head", split_axis=0, concat_axis=1, tiled=True).reshape(rows, D)
    middle = hidden + product(merged, w_out)
    normed_two = rms_norm(middle, gains[1]).astype(jnp.bfloat16)
    gate_up = product(normed_two, w_gu)
    action = gated(gate_up).astype(jnp.bfloat16)
    output = middle + contract_cols(action, w_down)
    return (
        output,
        (hidden, normed, spread, log_total, merged, middle, normed_two, gate_up, action),
    )


def layer_backward(gradient, weights, gains, saved, cosine, sine, allow, scale):
    w_qkv, w_out, w_gu, w_down = weights
    hidden, normed, spread, log_total, merged, middle, normed_two, gate_up, action = saved
    rows = hidden.shape[0]
    grad_low = gradient.astype(jnp.bfloat16)
    d_down = contract_rows(grad_low, action)
    unused, pull_gate = jax.vjp(gated, gate_up)
    d_gate_up = pull_gate(product(grad_low, w_down))[0].astype(jnp.bfloat16)
    d_gu = contract_rows(normed_two, d_gate_up)
    unused, pull_norm = jax.vjp(rms_norm, middle, gains[1])
    d_middle, d_gain_two = pull_norm(contract_cols(d_gate_up, w_gu))
    d_middle = gradient + d_middle
    middle_low = d_middle.astype(jnp.bfloat16)
    d_out = contract_rows(merged, middle_low)
    d_merged = contract_cols(middle_low, w_out).astype(jnp.bfloat16).reshape(rows, H, HD)
    upstream = lax.all_to_all(d_merged, "head", split_axis=1, concat_axis=0, tiled=True)
    d_packed = attend_back(spread, log_total, upstream, allow, scale)
    returned = lax.all_to_all(d_packed, "head", split_axis=0, concat_axis=2, tiled=True)
    unused, pull_rot = jax.vjp(
        lambda value: rotary(value, cosine, sine), returned[:, 0].astype(jnp.float32)
    )
    d_query = pull_rot(returned[:, 0].astype(jnp.float32))[0]
    d_key = pull_rot(returned[:, 1].astype(jnp.float32))[0]
    d_qkv = (
        jnp.stack([d_query, d_key, returned[:, 2].astype(jnp.float32)], axis=1)
        .reshape(rows, 3 * D)
        .astype(jnp.bfloat16)
    )
    d_qkv_w = contract_rows(normed, d_qkv)
    unused, pull_first = jax.vjp(rms_norm, hidden, gains[0])
    d_hidden, d_gain_one = pull_first(contract_cols(d_qkv, w_qkv))
    return (d_middle + d_hidden, [d_qkv_w, d_out, d_gu, d_down], d_gain_one, d_gain_two)


def adam_step(weight, gradient, first, second, rate, decay):
    first_new = beta_one * first + (1.0 - beta_one) * gradient
    second_new = beta_two * second + (1.0 - beta_two) * gradient * gradient
    direction = (
        first_new
        / (1.0 - beta_one**STEP)
        / (jnp.sqrt(second_new / (1.0 - beta_two**STEP)) + adam_eps)
    )
    return (weight - rate * (direction + decay * weight), first_new, second_new)


def on_device(
    token_ids,
    lengths,
    valid,
    vocab_ids,
    teacher,
    block,
    block_m,
    block_v,
    bases,
    table,
    table_m,
    table_v,
    gains,
    gains_m,
    gains_v,
):
    head_count = lax.axis_size("head")
    device_total = lax.axis_size("dp") * head_count
    batches, tokens = token_ids.shape
    bucket = tokens * head_count
    scale = HD ** (-0.5)
    shard_rows = table.shape[0]
    offset = lax.axis_index("dp") * shard_rows
    head_start = lax.axis_index("head") * tokens
    table_round = table.astype(jnp.bfloat16)
    zero_low = jnp.zeros((), jnp.bfloat16)
    all_ids = lax.all_gather(token_ids, "dp", axis=1, tiled=True)
    local_ids = all_ids - offset
    owned = (local_ids >= 0) & (local_ids < shard_rows)
    picked = jnp.where(
        owned[..., None], table_round[jnp.clip(local_ids, 0, shard_rows - 1)], zero_low
    )
    embedded = lax.psum_scatter(picked, "dp", scatter_dimension=1, tiled=True).astype(jnp.float32)
    vocab_local = vocab_ids - offset
    vocab_owned = (vocab_local >= 0) & (vocab_local < shard_rows)
    chosen_part = jnp.where(
        vocab_owned[:, None], table_round[jnp.clip(vocab_local, 0, shard_rows - 1)], zero_low
    )
    chosen = lax.psum(chosen_part, "dp").astype(jnp.float32).astype(jnp.bfloat16)
    gain_grads = jnp.zeros_like(gains)
    chosen_grads = jnp.zeros((TOPV, D), jnp.float32)
    block_grads = jnp.zeros_like(block)
    shapes = [(D, 3 * D), (D, D), (D, 2 * FF), (D, FF)]
    loss_sum = jnp.zeros((), jnp.float32)
    embed_grads = []
    for batch in range(batches):
        weights = split_block(
            lax.all_gather(block.astype(jnp.bfloat16), ("dp", "head"), axis=1, tiled=True),
            device_total,
        )
        allow, cos_all, sin_all = tables(lengths[batch, 0], bucket)
        cosine = lax.dynamic_slice_in_dim(cos_all, head_start, tokens, 0)
        sine = lax.dynamic_slice_in_dim(sin_all, head_start, tokens, 0)
        hidden = embedded[batch]
        saves = []
        for repeat in range(2):
            hidden, saved = layer_forward(hidden, weights, gains, cosine, sine, allow, scale)
            saves.append(saved)
        normed = rms_norm(hidden, gains[2]).astype(jnp.bfloat16)
        log_prob = jax.nn.log_softmax(contract_cols(normed, chosen), axis=-1)
        teach = jax.nn.log_softmax(teacher[batch].astype(jnp.float32), axis=-1)
        weighting = valid[batch].astype(jnp.float32)
        loss_sum = loss_sum + jnp.sum(
            weighting * jnp.sum(jnp.exp(teach) * (teach - log_prob), axis=-1)
        )
        logit_grads = ((jnp.exp(log_prob) - jnp.exp(teach)) * weighting[:, None]).astype(
            jnp.bfloat16
        )
        chosen_grads = chosen_grads + contract_rows(logit_grads, normed)
        unused, pull_final = jax.vjp(rms_norm, hidden, gains[2])
        gradient, d_gain_final = pull_final(product(logit_grads, chosen))
        gain_grads = gain_grads.at[2].add(d_gain_final)
        batch_grads = [jnp.zeros(shape, jnp.float32) for shape in shapes]
        for repeat in range(2):
            gradient, layer_grads, d_gain_one, d_gain_two = layer_backward(
                gradient, weights, gains, saves[1 - repeat], cosine, sine, allow, scale
            )
            batch_grads = [total + extra for total, extra in zip(batch_grads, layer_grads)]
            gain_grads = gain_grads.at[0].add(d_gain_one).at[1].add(d_gain_two)
        embed_grads.append(gradient.astype(jnp.bfloat16))
        block_grads = block_grads + lax.psum_scatter(
            join_block(batch_grads, device_total), ("dp", "head"), scatter_dimension=1, tiled=True
        )
    token_grads = lax.all_gather(jnp.stack(embed_grads), "dp", axis=1, tiled=True)
    dump_index = jnp.where(owned, local_ids, shard_rows).reshape(-1)
    table_grads = jax.ops.segment_sum(
        token_grads.reshape(-1, D).astype(jnp.float32), dump_index, num_segments=shard_rows + 1
    )[:shard_rows]
    totals = jnp.stack([loss_sum, jnp.sum(valid.astype(jnp.float32))])
    chosen_grads, gain_grads, totals = (
        lax.psum(chosen_grads.astype(jnp.bfloat16), "dp").astype(jnp.float32),
        lax.psum(gain_grads.astype(jnp.bfloat16), "dp").astype(jnp.float32),
        lax.psum(totals.astype(jnp.bfloat16), "dp").astype(jnp.float32),
    )
    vocab_index = jnp.where(vocab_owned, vocab_local, shard_rows)
    table_grads = (
        table_grads
        + jax.ops.segment_sum(chosen_grads, vocab_index, num_segments=shard_rows + 1)[:shard_rows]
    )
    table_grads, gain_grads, totals = (
        lax.psum(table_grads.astype(jnp.bfloat16), "head").astype(jnp.float32),
        lax.psum(gain_grads.astype(jnp.bfloat16), "head").astype(jnp.float32),
        lax.psum(totals.astype(jnp.bfloat16), "head").astype(jnp.float32),
    )
    count = totals[1]
    block_grads = block_grads / count
    table_grads = table_grads / count
    gain_grads = gain_grads / count
    head_first = (lax.axis_index("head") == 0).astype(jnp.float32)
    squares = lax.psum(
        jnp.sum(block_grads * block_grads) + head_first * jnp.sum(table_grads * table_grads),
        ("dp", "head"),
    )
    grad_norm = jnp.sqrt(squares + jnp.sum(gain_grads * gain_grads))
    clip = jnp.minimum(1.0, clip_norm / grad_norm)
    block_grads = block_grads * clip
    table_grads = table_grads * clip
    gain_grads = gain_grads * clip
    rotated = jnp.concatenate(
        [
            jnp.dot(bases[index].T, piece, precision=highest)
            for index, piece in enumerate(split_local(block_grads, device_total))
        ],
        axis=1,
    )
    block_m_new = beta_one * block_m + (1.0 - beta_one) * rotated
    block_v_new = beta_two * block_v + (1.0 - beta_two) * rotated * rotated
    direction = (
        block_m_new
        / (1.0 - beta_one**STEP)
        / (jnp.sqrt(block_v_new / (1.0 - beta_two**STEP)) + adam_eps)
    )
    update = jnp.concatenate(
        [
            jnp.dot(bases[index], piece, precision=highest)
            for index, piece in enumerate(split_local(direction, device_total))
        ],
        axis=1,
    )
    block_new = block - rate_block * (update + decay_rate * block)
    table_new, table_m_new, table_v_new = adam_step(
        table, table_grads, table_m, table_v, rate_table, decay_rate
    )
    gains_new, gains_m_new, gains_v_new = adam_step(
        gains, gain_grads, gains_m, gains_v, rate_gain, 0.0
    )
    return (
        totals[0] / count,
        grad_norm,
        block_new,
        block_m_new,
        block_v_new,
        table_new,
        table_m_new,
        table_v_new,
        gains_new,
        gains_m_new,
        gains_v_new,
        block_new.astype(jnp.bfloat16),
        table_new.astype(jnp.bfloat16),
    )


def solution(mesh):
    return jax.shard_map(
        on_device,
        mesh=mesh,
        in_specs=(
            P(None, ("dp", "head")),
            P(None, "dp", None),
            P(None, ("dp", "head")),
            P(),
            P(None, ("dp", "head"), None),
            P(None, ("dp", "head")),
            P(None, ("dp", "head")),
            P(None, ("dp", "head")),
            P(),
            P("dp", None),
            P("dp", None),
            P("dp", None),
            P(),
            P(),
            P(),
        ),
        out_specs=(
            P(),
            P(),
            P(None, ("dp", "head")),
            P(None, ("dp", "head")),
            P(None, ("dp", "head")),
            P("dp", None),
            P("dp", None),
            P("dp", None),
            P(),
            P(),
            P(),
            P(None, ("dp", "head")),
            P("dp", None),
        ),
        check_vma=False,
    )
```

profile of v0, /device:TPU:0, one launch (start us, length us, event | category | flops | bytes accessed | tf_op | source)
XLA Modules:
  0.0 1421.1 jit_solution(14949590530537953438)
XLA Ops:
  8.1 22.5 %all_gather.10 = s32[2,1024]{1,0:T(2,128)S(1)} all-gather(s32[2,128]{1,0:T(2,128)} %param.36), channel_id=1, replica_groups=mesh['dp'=8,'head'=4] {'dp'}, dimensions={1}, use_global_device_ids=true | all-gather | bytes 9216 | tf_op jit(solution)/shard_map/all_gather | solution.py:240
  30.6 7.7 convert_element_type.394
  38.3 12.0 gather_fusion
  55.1 22.9 %gather_fusion.1 = bf16[4096,768]{1,0:T(8,128)(2,1)} fusion(bf16[4000,768]{1,0:T(8,128)(2,1)} %convert_element_type.394, s32[4096]{0:T(1024)S(1)} %get-tuple-element.329), kind=kCustom, calls=%fused_computation.1 | custom fusion | bytes 12599296 | tf_op jit(solution)/shard_map/gather | solution.py:250
  78.0 7.5 broadcast_select_fusion
  94.0 102.6 %reduce-scatter.3.cloned.1.call-done = bf16[2,128,768]{2,1,0:T(8,128)(2,1)} async-done(((bf16[2,1024,768]{2,1,0:T(8,128)(2,1)}), bf16[2,128,768]{2,1,0:T(8,128)(2,1)}) %reduce-scatter.3.cloned.1.call-update) | async-done | bytes 393232 | tf_op jit(solution)/shard_map/reduce_scatter | solution.py:246
  198.4 23.0 %copy.250 = bf16[768,12288]{0,1:T(8,128)(2,1)} copy(bf16[768,12288]{1,0:T(8,128)(2,1)} %all-gather.3.cloned.1.call-done) | data formatting | bytes 37748736 | tf_op jit(solution)/shard_map/all_gather | solution.py:261
  226.2 4.4 all-to-all-start.4
  237.8 8.6 slice.611
  246.5 5.0 slice.614
  252.7 4.4 all-to-all-start
  272.5 4.1 all-to-all-start.5
  292.4 4.4 all-to-all-start.1
  303.6 6.9 fusion.305
  315.6 4.2 all-to-all-start.6
  327.0 6.9 fusion.300
  338.9 4.4 all-to-all-start.2
  378.2 4.2 all-to-all-start.3
  389.1 6.9 fusion.307
  399.2 12.1 all-reduce.31.cloned.1.call-done
  411.3 5.2 fusion.332
  425.0 6.9 fusion.302
  447.9 5.2 fusion.267
  455.4 7.9 fusion.187
  467.3 8.1 fusion.190
  475.4 6.4 fusion.303
  485.5 4.0 all-to-all-start.12
  489.6 9.6 add_convert_fusion
  518.4 4.4 all-to-all-start.13
  522.8 6.4 fusion.255
  544.6 4.9 fusion.233
  560.4 16.8 %convolution_add_fusion = f32[768,6144]{1,0:T(8,128)} fusion(f32[768,6144]{1,0:T(8,128)} %fusion.190, f32[128,3072]{1,0:T(8,128)} %copy-done.100, f32[128,3072]{1,0:T(8,128)} %copy-done.99, f32[128,768]{1,0:T(8,128)} %copy-done.31, f32[128]{0:T(128)} %copy-done.143, f32[768]{0:T(1024)S(1)} %get-tuple-element.228), kind=kOutput, calls=%fused_computation.16 | convolution fusion | flops 1214545920 | bytes 41291264 | tf_op jit(solution)/shard_map/dot_general | solution.py:33
  580.0 4.4 all-to-all-start.14
  608.7 4.2 all-to-all-start.9
  624.4 4.3 all-to-all-start.15
  652.2 5.2 fusion.231
  657.5 7.0 multiply_reduce_fusion.10
  668.3 4.0 all-to-all-start.10
  693.3 4.2 all-to-all-start.11
  701.0 6.1 all-to-all-done.11
  719.5 8.8 convolution_add_fusion.4
  728.3 10.0 copy.312
  738.3 18.8 %copy.311 = f32[768,6144]{0,1:T(8,128)} copy(f32[768,6144]{1,0:T(8,128)} %convolution_add_fusion) | data formatting | bytes 37748736 | tf_op jit(solution)/shard_map/add | solution.py:291
  760.7 4.2 fusion.306
  764.9 9.0 convolution_add_fusion.5
  773.8 9.6 copy.293
  783.5 12.8 convolution_add_fusion.1
  796.3 18.7 %copy.292 = f32[768,6144]{0,1:T(8,128)} copy(f32[768,6144]{1,0:T(8,128)} %convolution_add_fusion.1) | data formatting | bytes 37748736 | tf_op jit(solution)/shard_map/add | solution.py:291
  815.0 7.4 convolution_add_fusion.2
  822.4 8.0 copy.310
  835.5 4.2 convolution_add_fusion.3
  839.7 8.0 copy.291
  847.7 33.6 %scatter_custom_fusion.1 = f32[4001,768]{1,0:T(8,128)} fusion(s32[4096]{0:T(1024)} %get-tuple-element.328, bf16[4096,768]{1,0:T(8,128)(2,1)} %all-reduce.33.cloned.1.call-done, f32[]{:T(128)} %constant.327.clone.1), kind=kCustom, calls=%fused_computation.6 | custom fusion | flops 6291456 | bytes 18583040 | tf_op jit(solution)/shard_map/scatter-add | solution.py:311
  881.3 19.9 %scatter_custom_fusion = f32[4001,768]{1,0:T(8,128)} fusion(s32[2048]{0:T(1024)} %bitcast.729, bf16[2048,768]{1,0:T(8,128)(2,1)} %bitcast.708, f32[]{:T(128)} %constant.327.clone.1), kind=kCustom, calls=%fused_computation.18 | custom fusion | flops 3145728 | bytes 15437312 | tf_op jit(solution)/shard_map/scatter-add | solution.py:299
  901.1 11.5 fusion.3
  912.7 37.8 %maximum_add_fusion = f32[768,32,384]{0,2,1:T(8,128)} fusion(f32[768,32,96]{0,2,1:T(8,128)} %bitcast.676, f32[768,32,192]{0,2,1:T(8,128)} %bitcast.670, f32[768,32,24]{0,2,1:T(8,128)} %bitcast.683, f32[768,32,72]{0,2,1:T(8,128)} %bitcast.680, f32[768,32,96]{0,2,1:T(8,128)} %bitcast.675, f32[768,32,192]{0,2,1:T(8,128)} %bitcast.669, ...), kind=kLoop, calls=%fused_computation.4 | loop fusion | flops 66060288 | bytes 113246208 | tf_op jit(solution)/shard_map/add | solution.py:294
  964.9 20.1 %all-reduce.25 = (bf16[2]{0:T(256)(128)(2,1)S(1)}, bf16[3,768]{1,0:T(4,128)(2,1)S(1)}) all-reduce(bf16[2]{0:T(256)(128)(2,1)S(1)} %pad_maximum_fusion.12, bf16[3,768]{1,0:T(4,128)(2,1)S(1)} %convert_element_type.489), channel_id=1, replica_groups=mesh['dp'=8,'head'=4] {'dp'}, use_global_device_ids=true, to_apply=%region_33.35 | all-reduce | flops 2306 | bytes 9224 | tf_op jit(solution)/shard_map/psum | solution.py:306
  985.0 6.5 all-reduce.26
  993.4 35.9 %all-reduce.35.cloned.1.call-done = bf16[4000,768]{1,0:T(8,128)(2,1)} async-done(((bf16[4000,768]{1,0:T(8,128)(2,1)}), bf16[4000,768]{1,0:T(8,128)(2,1)}) %all-reduce.35.cloned.1.call-update) | async-done | bytes 6144016 | tf_op jit(solution)/shard_map/psum | solution.py:314
  1029.3 7.1 multiply_reduce_fusion
  1037.1 261.2 %reduce-scatter.5.cloned.1.call-done = f32[768,384]{0,1:T(8,128)} async-done(((f32[768,12288]{0,1:T(8,128)}), f32[768,384]{0,1:T(8,128)}) %reduce-scatter.5.cloned.1.call-update) | async-done | bytes 1179664 | tf_op jit(solution)/shard_map/reduce_scatter | solution.py:294
  1303.1 39.8 %psum.61 = f32[]{:T(128)} all-reduce(f32[]{:T(128)S(6)} %add.538), channel_id=1, replica_groups=mesh['dp'=8,'head'=4] {'dp','head'}, use_global_device_ids=true, to_apply=%region_57.59 | all-reduce | flops 1 | bytes 8 | tf_op jit(solution)/shard_map/psum | solution.py:323
  1361.3 4.0 fusion.92
  1381.9 29.4 %fusion.317 = (bf16[4000,768]{1,0:T(8,128)(2,1)}, f32[4000,768]{1,0:T(8,128)}, f32[4000,768]{1,0:T(8,128)}, f32[4000,768]{1,0:T(8,128)}) fusion(f32[4000,768]{1,0:T(8,128)} %param.45, f32[]{:T(128)S(6)} %min_shard_map.3, f32[]{:T(128)} %bitcast.101, bf16[4000,768]{1,0:T(8,128)(2,1)} %all-reduce.35.cloned.1.call-done, f32[4000,768]{1,0:T(8,128)} %param.46, ...), kind=kLoop, calls=%fused_computation.620 | loop fusion | flops 58368000 | bytes 86016008 | tf_op jit(solution)/shard_map/convert_element_type | solution.py:373
  (743 shorter events, 368.7 us)
Async XLA Ops:
  8.0 188.6 %reduce-scatter.3.cloned.1.call-start = ((), (), s32[]{:S(2)}) async-start(), calls=%async_computation.18 | async-start | bytes 3538944 | tf_op jit(solution)/shard_map/reduce_scatter | solution.py:246
  52.3 146.2 %all-gather.3.cloned.1.call-start = ((), (), s32[]{:S(2)}) async-start(), calls=%async_computation.19 | async-start | bytes 19464192 | tf_op jit(solution)/shard_map/all_gather | solution.py:261
  54.4 356.9 %all-reduce.31.cloned.1.call-start = ((), (), s32[]{:S(2)}) async-start(), calls=%async_computation.20 | async-start | bytes 12582912 | tf_op jit(solution)/shard_map/psum | solution.py:252
  89.0 132.4 %copy-start.160 = (f32[128]{0:T(128)}, f32[128]{0:T(128)S(1)}, u32[]{:S(2)}) copy-start(f32[128]{0:T(128)S(1)} %convert_reduce_fusion) | copy-start | bytes 1540
  89.6 131.8 %copy-start.158 = (f32[128]{0:T(128)}, f32[128]{0:T(128)S(1)}, u32[]{:S(2)}) copy-start(f32[128]{0:T(128)S(1)} %get-tuple-element.202) | copy-start | bytes 1540
  197.6 23.8 %copy-start.4 = (f32[2,128,768]{2,1,0:T(8,128)}, f32[2,128,768]{2,1,0:T(8,128)S(1)}, u32[]{:S(2)}) copy-start(f32[2,128,768]{2,1,0:T(8,128)S(1)} %convert_element_type.395) | copy-start | bytes 2359300
  197.8 23.6 %copy-start.166 = (f32[128]{0:T(128)}, f32[128]{0:T(128)S(1)}, u32[]{:S(2)}) copy-start(f32[128]{0:T(128)S(1)} %get-tuple-element.225) | copy-start | bytes 1540
  197.8 23.6 %copy-start.168 = (f32[128]{0:T(128)}, f32[128]{0:T(128)S(1)}, u32[]{:S(2)}) copy-start(f32[128]{0:T(128)S(1)} %get-tuple-element.226) | copy-start | bytes 1540
  198.4 32.2 %copy-start.153 = (f32[128]{0:T(128)}, f32[128]{0:T(128)S(1)}, u32[]{:S(2)}) copy-start(f32[128]{0:T(128)S(1)} %fusion.278) | copy-start | bytes 1540
  226.2 26.4 %all-to-all-start.4 = ((bf16[128,3,12,64]{0,3,1,2:T(8,128)(2,1)}), bf16[128,3,12,64]{0,3,1,2:T(8,128)(2,1)}, u32[]{:S(2)}, u32[]{:S(2)}) async-start(bf16[128,3,12,64]{0,3,1,2:T(8,128)(2,1)} %copy.263), calls=%async_computation.5 | async-start | bytes 1179648 | tf_op jit(solution)/shard_map/all_to_all | solution.py:154
  252.7 19.9 %all-to-all-start = ((bf16[128,3,12,64]{0,3,1,2:T(8,128)(2,1)}), bf16[128,3,12,64]{0,3,1,2:T(8,128)(2,1)}, u32[]{:S(2)}, u32[]{:S(2)}) async-start(bf16[128,3,12,64]{0,3,1,2:T(8,128)(2,1)} %copy.251), calls=%async_computation.1 | async-start | bytes 1179648 | tf_op jit(solution)/shard_map/all_to_all | solution.py:154
  272.5 19.9 %all-to-all-start.5 = ((bf16[4,2,12288]{2,1,0:T(2,128)(2,1)}), bf16[4,2,12288]{2,1,0:T(2,128)(2,1)}, u32[]{:S(2)}, u32[]{:S(2)}) async-start(bf16[4,2,12288]{2,1,0:T(2,128)(2,1)} %reshape.1208), calls=%async_computation.6 | async-start | bytes 393216 | tf_op jit(solution)/shard_map/all_to_all | solution.py:156
  292.4 23.2 %all-to-all-start.1 = ((bf16[4,2,12288]{2,1,0:T(2,128)(2,1)}), bf16[4,2,12288]{2,1,0:T(2,128)(2,1)}, u32[]{:S(2)}, u32[]{:S(2)}) async-start(bf16[4,2,12288]{2,1,0:T(2,128)(2,1)} %reshape.1212), calls=%async_computation.2 | async-start | bytes 393216 | tf_op jit(solution)/shard_map/all_to_all | solution.py:156
  300.7 10.2 slice-start.8
  302.9 8.0 copy-start.31
  303.6 7.4 slice-start.9
  315.6 23.3 %all-to-all-start.6 = ((bf16[128,3,12,64]{0,3,1,2:T(8,128)(2,1)}), bf16[128,3,12,64]{0,3,1,2:T(8,128)(2,1)}, u32[]{:S(2)}, u32[]{:S(2)}) async-start(bf16[128,3,12,64]{0,3,1,2:T(8,128)(2,1)} %copy.269), calls=%async_computation.7 | async-start | bytes 1179648 | tf_op jit(solution)/shard_map/all_to_all | solution.py:154
  323.7 10.7 slice-start.10
  325.9 8.5 copy-start.16
  327.0 7.4 slice-start.11
  338.9 19.9 %all-to-all-start.2 = ((bf16[128,3,12,64]{0,3,1,2:T(8,128)(2,1)}), bf16[128,3,12,64]{0,3,1,2:T(8,128)(2,1)}, u32[]{:S(2)}, u32[]{:S(2)}) async-start(bf16[128,3,12,64]{0,3,1,2:T(8,128)(2,1)} %copy.257), calls=%async_computation.3 | async-start | bytes 1179648 | tf_op jit(solution)/shard_map/all_to_all | solution.py:154
  358.8 19.5 %all-to-all-start.7 = ((bf16[4,2,12288]{2,1,0:T(2,128)(2,1)}), bf16[4,2,12288]{2,1,0:T(2,128)(2,1)}, u32[]{:S(2)}, u32[]{:S(2)}) async-start(bf16[4,2,12288]{2,1,0:T(2,128)(2,1)} %reshape.1210), calls=%async_computation.8 | async-start | bytes 393216 | tf_op jit(solution)/shard_map/all_to_all | solution.py:156
  378.2 40.6 %all-to-all-start.3 = ((bf16[4,2,12288]{2,1,0:T(2,128)(2,1)}), bf16[4,2,12288]{2,1,0:T(2,128)(2,1)}, u32[]{:S(2)}, u32[]{:S(2)}) async-start(bf16[4,2,12288]{2,1,0:T(2,128)(2,1)} %reshape.1214), calls=%async_computation.4 | async-start | bytes 393216 | tf_op jit(solution)/shard_map/all_to_all | solution.py:156
  386.4 10.1 slice-start.12
  388.6 7.9 copy-start.23
  422.8 12.9 slice-start.6
  425.0 30.4 %copy-start.42 = (f32[128,768]{1,0:T(8,128)}, f32[128,768]{1,0:T(8,128)S(1)}, u32[]{:S(2)}) copy-start(f32[128,768]{1,0:T(8,128)S(1)} %get-tuple-element.373) | copy-start | bytes 1179652
  425.0 30.4 %copy-start.137 = (f32[128]{0:T(128)}, f32[128]{0:T(128)S(1)}, u32[]{:S(2)}) copy-start(f32[128]{0:T(128)S(1)} %fusion.281) | copy-start | bytes 1540
  425.0 10.7 slice-start.7
  445.9 35.9 %copy-start.89 = (f32[128,768]{1,0:T(8,128)}, f32[128,768]{1,0:T(8,128)S(1)}, u32[]{:S(2)}) copy-start(f32[128,768]{1,0:T(8,128)S(1)} %get-tuple-element.336) | copy-start | bytes 1179652
  455.4 7.9 copy-start.48
  475.4 7.4 copy-start
  485.5 16.7 %all-to-all-start.12 = ((bf16[128,12,64]{0,2,1:T(8,128)(2,1)}), bf16[128,12,64]{0,2,1:T(8,128)(2,1)}, u32[]{:S(2)}, u32[]{:S(2)}) async-start(bf16[128,12,64]{0,2,1:T(8,128)(2,1)} %bitcast.727), calls=%async_computation.13 | async-start | bytes 393216 | tf_op jit(solution)/shard_map/all_to_all | solution.py:183
  489.5 358.1 %all-reduce.33.cloned.1.call-start = ((), (), s32[]{:S(2)}) async-start(), calls=%async_computation.22 | async-start | bytes 12582912 | tf_op jit(solution)/shard_map/psum | solution.py:304
  518.4 14.0 all-to-all-start.13
  540.6 8.9 slice-start.3
  556.4 23.6 %all-to-all-start.8 = ((bf16[128,12,64]{0,2,1:T(8,128)(2,1)}), bf16[128,12,64]{0,2,1:T(8,128)(2,1)}, u32[]{:S(2)}, u32[]{:S(2)}) async-start(bf16[128,12,64]{0,2,1:T(8,128)(2,1)} %bitcast.728), calls=%async_computation.9 | async-start | bytes 393216 | tf_op jit(solution)/shard_map/all_to_all | solution.py:183
  560.4 16.9 %copy-start.2 = (bf16[768,32,24]{0,2,1:T(8,128)(2,1)S(1)}, bf16[768,32,24]{0,2,1:T(8,128)(2,1)}, u32[]{:S(2)}) copy-start(bf16[768,32,24]{0,2,1:T(8,128)(2,1)} %slice.610) | copy-start | bytes 3538948
  560.4 16.9 %copy-start.64 = (f32[128,768]{1,0:T(8,128)S(1)}, f32[128,768]{1,0:T(8,128)}, u32[]{:S(2)}) copy-start(f32[128,768]{1,0:T(8,128)} %get-tuple-element.332) | copy-start | bytes 1179652
  560.4 24.1 %copy-start.128 = (f32[3,512]{1,0:T(4,128)S(1)}, f32[3,512]{1,0:T(4,128)}, u32[]{:S(2)}) copy-start(f32[3,512]{1,0:T(4,128)} %copy-done.127) | copy-start | bytes 18436
  580.0 13.6 all-to-all-start.14
  608.7 15.7 %all-to-all-start.9 = ((bf16[4,2,36864]{2,1,0:T(2,128)(2,1)}), bf16[4,2,36864]{2,1,0:T(2,128)(2,1)}, u32[]{:S(2)}, u32[]{:S(2)}) async-start(bf16[4,2,36864]{2,1,0:T(2,128)(2,1)} %reshape.1216), calls=%async_computation.10 | async-start | bytes 1179648 | tf_op jit(solution)/shard_map/all_to_all | solution.py:185
  624.4 16.9 %all-to-all-start.15 = ((bf16[4,2,36864]{2,1,0:T(2,128)(2,1)}), bf16[4,2,36864]{2,1,0:T(2,128)(2,1)}, u32[]{:S(2)}, u32[]{:S(2)}) async-start(bf16[4,2,36864]{2,1,0:T(2,128)(2,1)} %reshape.1222), calls=%async_computation.16 | async-start | bytes 1179648 | tf_op jit(solution)/shard_map/all_to_all | solution.py:185
  641.3 8.9 copy-start.175
  652.2 12.4 copy-start.85
  657.5 8.0 copy-start.3
  665.5 12.2 copy-start.124
  668.3 9.4 all-to-all-start.10
  693.3 13.8 all-to-all-start.11
  697.5 183.8 %all-gather.5.cloned.1.call-start = ((), (), s32[]{:S(2)}) async-start(), calls=%async_computation.21 | async-start | bytes 3538944 | tf_op jit(solution)/shard_map/all_gather | solution.py:297
  719.3 310.0 %all-reduce.35.cloned.1.call-start = ((), (), s32[]{:S(2)}) async-start(), calls=%async_computation.23 | async-start | bytes 12288000 | tf_op jit(solution)/shard_map/psum | solution.py:314
  738.3 18.8 %copy-start.61 = (f32[128,768]{1,0:T(8,128)S(1)}, f32[128,768]{1,0:T(8,128)}, u32[]{:S(2)}) copy-start(f32[128,768]{1,0:T(8,128)} %copy-done.60) | copy-start | bytes 1179652
  738.3 18.8 %copy-start.97 = (bf16[128,4,3,64]{0,3,2,1:T(8,128)(2,1)S(1)}, bf16[128,4,3,64]{0,3,2,1:T(8,128)(2,1)}, u32[]{:S(2)}) copy-start(bf16[128,4,3,64]{0,3,2,1:T(8,128)(2,1)} %copy.262) | copy-start | bytes 589828
  738.3 20.7 %copy-start.98 = (bf16[128,4,3,64]{0,3,2,1:T(8,128)(2,1)S(1)}, bf16[128,4,3,64]{0,3,2,1:T(8,128)(2,1)}, u32[]{:S(2)}) copy-start(bf16[128,4,3,64]{0,3,2,1:T(8,128)(2,1)} %copy.268) | copy-start | bytes 589828
  773.8 9.6 copy-start.18
  773.8 9.6 copy-start.136
  796.3 18.7 %copy-start.7 = (f32[2,128,768]{2,1,0:T(8,128)S(1)}, f32[2,128,768]{2,1,0:T(8,128)}, u32[]{:S(2)}) copy-start(f32[2,128,768]{2,1,0:T(8,128)} %copy-done.4) | copy-start | bytes 2359300
  912.7 385.6 %reduce-scatter.5.cloned.1.call-start = ((), (), s32[]{:S(2)}) async-start(), calls=%async_computation.24 | async-start | bytes 38928384 | tf_op jit(solution)/shard_map/reduce_scatter | solution.py:294
  950.6 8.4 copy-start.141
  950.6 9.9 copy-start.140
  950.6 10.7 copy-start.142
  950.6 10.8 copy-start.139
  1346.2 19.1 %slice-start.16 = ((s8[9437184]{0:T(1024)(128)(4,1)}), s8[4194304]{0:T(1024)(128)(4,1)S(1)}, s32[]{:S(2)}) async-start(s8[9437184]{0:T(1024)(128)(4,1)} %bitcast.677), calls=%async_computation.41 | async-start | bytes 8388608
  1352.9 12.4 slice-start.17
  (167 other events, 459.0 us)
Sparse Core Ops, SparseCore 0:
  52.4 144.1 reduce-scatter.2
  200.9 210.3 all-reduce.30
  502.3 210.8 all-reduce.32
  719.5 59.0 all-gather.4
  912.8 116.4 all-reduce.34
Sparse Core Ops, SparseCore 1:
  56.6 141.3 all-gather.2
  950.7 347.6 reduce-scatter.4
where the time goes:
time: 1440 us; the launch traced here: 1420 us
  waiting for transfers between devices  424 us (29%)
  local copies, waits for them, and re-layouts  313 us (22%)
  matrix products  286 us (20%)
  other arithmetic  216 us (15%)
  blocking collectives  88.8 us (6%)
  starting transfers between devices  67.7 us (5%)
  between operations  26.3 us (2%)
    reduce_scatter x1, waiting for transfers between devices, on_device(): lax.psum_scatter(join_block(batch_grads, device_total), ('dp', 'head'), s...  261 us
    dot_general x18, matrix products, contract_rows(): lax.dot_general(left, right, (((0,), (0,)), ((), ())), preferred_element_...  117 us
    reduce_scatter x1, waiting for transfers between devices, on_device(): lax.psum_scatter(picked, 'dp', scatter_dimension=1, tiled=True)  103 us
    unnamed x440, local copies, waits for them, and re-layouts  83.8 us
    add x6, local copies, waits for them, and re-layouts, on_device(): total + extra  73.1 us
    dot_general x18, matrix products, product(): return jnp.dot(left, right, preferred_element_type=jnp.float32)  58.6 us
    psum x1, blocking collectives, on_device(): lax.psum(jnp.sum(block_grads * block_grads) + head_first * jnp.sum(table_...  39.8 us
    dot_general x18, matrix products, contract_cols(): lax.dot_general(left, right, (((1,), (1,)), ((), ())), preferred_element_...  38 us
  transfers between devices with their start and end apart: 23, of which 7 were waited for; matrix products, arithmetic and copies ran while one was open for 42% of the time, Pallas kernels for 0%

commit v1 on v0

v1 whole, which is shorter than its diff:
```python
import math

import jax
import jax.numpy as jnp
from jax import lax
from jax.sharding import PartitionSpec as P

D = 768
H = 12
HD = 64
FF = 3072
TOPV = 4096
STEP = 5

low = jnp.bfloat16
scale = HD**-0.5
eps_norm = 1e-05
clip_norm = 0.002
beta_one = 0.9
beta_two = 0.99
adam_eps = 1e-08
decay_rate = 0.1
rate_block = 0.03
rate_table = 0.05
rate_gain = 0.4


def product(left, right):
    return jnp.dot(left, right, preferred_element_type=jnp.float32)


def contract_rows(left, right):
    return lax.dot_general(
        left, right, (((0,), (0,)), ((), ())), preferred_element_type=jnp.float32
    )


def contract_cols(left, right):
    return lax.dot_general(
        left, right, (((1,), (1,)), ((), ())), preferred_element_type=jnp.float32
    )


def rms_norm(value, gain):
    return value * lax.rsqrt(jnp.mean(value * value, axis=-1, keepdims=True) + eps_norm) * gain


def rms_back(value, gain, grad):
    r = lax.rsqrt(jnp.mean(value * value, axis=-1, keepdims=True) + eps_norm)
    scaled = grad * gain
    d_value = r * scaled - value * (r * r * r) * jnp.mean(value * scaled, axis=-1, keepdims=True)
    return d_value, jnp.sum(grad * value * r, axis=0)


def rotary(value, cosine, sine):
    half = HD // 2
    turned = jnp.concatenate([-value[..., half:], value[..., :half]], axis=-1)
    return value * cosine[:, None, :] + turned * sine[:, None, :]


def rotary_back(grad, cosine, sine):
    half = HD // 2
    part = grad * sine[:, None, :]
    turned = jnp.concatenate([part[..., half:], -part[..., :half]], axis=-1)
    return grad * cosine[:, None, :] + turned


def segments(lengths, places):
    segment = jnp.zeros_like(places)
    begin = jnp.zeros_like(places)
    end = jnp.zeros((), jnp.int32)
    for index in range(lengths.shape[0] - 1):
        end = end + lengths[index]
        past = places >= end
        segment = segment + past.astype(jnp.int32)
        begin = jnp.where(past, end, begin)
    return segment, places - begin


def scores_of(query, keys, allow):
    score = jnp.einsum("qhd,khd->hqk", query, keys, preferred_element_type=jnp.float32) * scale
    return jnp.where(allow[None], score, -1e30)


def attend(query, keys, values, allow):
    score = scores_of(query, keys, allow)
    summit = jnp.max(score, axis=-1, keepdims=True)
    log_total = summit + jnp.log(jnp.sum(jnp.exp(score - summit), axis=-1, keepdims=True))
    weight = jnp.exp(score - log_total)
    mixed = jnp.einsum(
        "hqk,khd->qhd", weight.astype(low), values, preferred_element_type=jnp.float32
    )
    return mixed.astype(low), log_total


def attend_back(query, keys, values, log_total, upstream, allow):
    weight = jnp.exp(scores_of(query, keys, allow) - log_total)
    d_value = jnp.einsum(
        "hqk,qhd->khd", weight.astype(low), upstream, preferred_element_type=jnp.float32
    )
    d_weight = jnp.einsum("qhd,khd->hqk", upstream, values, preferred_element_type=jnp.float32)
    d_score = (weight * (d_weight - jnp.sum(d_weight * weight, axis=-1, keepdims=True))).astype(low)
    d_query = jnp.einsum("hqk,khd->qhd", d_score, keys, preferred_element_type=jnp.float32) * scale
    d_key = jnp.einsum("hqk,qhd->khd", d_score, query, preferred_element_type=jnp.float32) * scale
    return d_query, d_key, d_value


def swap(value, head_count, offset):
    return lax.ppermute(value, "head", [(h, h ^ offset) for h in range(head_count)])


def layer_forward(hidden, weights, gains, cosine, sine, allow, head_count):
    w_qkv, w_out, w_gu, w_down = weights
    rows = hidden.shape[0]
    normed = rms_norm(hidden, gains[0]).astype(low)
    qkv = contract_cols(normed, w_qkv).reshape(rows, 3, H, HD)
    query = rotary(qkv[:, 0], cosine, sine).astype(low)
    key = rotary(qkv[:, 1], cosine, sine).astype(low)
    own = jnp.concatenate([key, qkv[:, 2].astype(low)], axis=1)
    both = jnp.concatenate([own, swap(own, head_count, 1)], axis=0)
    keys, values = both[:, :H], both[:, H:]
    mixed, log_total = attend(query, keys, values, allow)
    merged = mixed.reshape(rows, D)
    middle = hidden + contract_cols(merged, w_out)
    normed_two = rms_norm(middle, gains[1]).astype(low)
    gate_up = contract_cols(normed_two, w_gu)
    action = (jax.nn.silu(gate_up[:, :FF]) * gate_up[:, FF:]).astype(low)
    output = middle + product(action, w_down)
    saved = (hidden, normed, query, keys, values, log_total, merged, middle, normed_two, gate_up, action)
    return output, saved


def layer_backward(gradient, weights, gains, saved, cosine, sine, allow, head_count):
    w_qkv, w_out, w_gu, w_down = weights
    hidden, normed, query, keys, values, log_total, merged, middle, normed_two, gate_up, action = saved
    rows = hidden.shape[0]
    grad_low = gradient.astype(low)
    d_down = contract_rows(action, grad_low)
    d_action = contract_cols(grad_low, w_down)
    gate, up = gate_up[:, :FF], gate_up[:, FF:]
    chance = jax.nn.sigmoid(gate)
    d_gate = d_action * up * (chance + gate * chance * (1.0 - chance))
    d_up = d_action * gate * chance
    d_gate_up = jnp.concatenate([d_gate, d_up], axis=1).astype(low)
    d_gu = contract_rows(d_gate_up, normed_two)
    d_middle, d_gain_two = rms_back(middle, gains[1], product(d_gate_up, w_gu))
    d_middle = gradient + d_middle
    middle_low = d_middle.astype(low)
    d_out = contract_rows(middle_low, merged)
    upstream = product(middle_low, w_out).astype(low).reshape(rows, H, HD)
    d_query, d_key, d_value = attend_back(query, keys, values, log_total, upstream, allow)
    d_own = jnp.concatenate([d_key[:rows], d_value[:rows]], axis=1)
    d_far = jnp.concatenate([d_key[rows:], d_value[rows:]], axis=1).astype(low)
    d_own = (d_own + swap(d_far, head_count, 1).astype(jnp.float32)).astype(low).astype(jnp.float32)
    d_query = rotary_back(d_query.astype(low).astype(jnp.float32), cosine, sine)
    d_key = rotary_back(d_own[:, :H], cosine, sine)
    d_qkv = jnp.concatenate([d_query, d_key, d_own[:, H:]], axis=1).reshape(rows, 3 * D).astype(low)
    d_qkv_w = contract_rows(d_qkv, normed)
    d_hidden, d_gain_one = rms_back(hidden, gains[0], product(d_qkv, w_qkv))
    return d_middle + d_hidden, [d_qkv_w, d_out, d_gu, d_down], d_gain_one, d_gain_two


def adam_step(weight, gradient, first, second, rate, decay):
    first_new = beta_one * first + (1.0 - beta_one) * gradient
    second_new = beta_two * second + (1.0 - beta_two) * gradient * gradient
    direction = (
        first_new
        / (1.0 - beta_one**STEP)
        / (jnp.sqrt(second_new / (1.0 - beta_two**STEP)) + adam_eps)
    )
    return (weight - rate * (direction + decay * weight), first_new, second_new)


def on_device(
    token_ids,
    lengths,
    valid,
    vocab_ids,
    teacher,
    block,
    block_m,
    block_v,
    bases,
    table,
    table_m,
    table_v,
    gains,
    gains_m,
    gains_v,
):
    dp_count, head_count = lax.axis_size("dp"), lax.axis_size("head")
    device_total = dp_count * head_count
    head, dp = lax.axis_index("head"), lax.axis_index("dp")
    batch = head // 2
    tokens = token_ids.shape[1]
    shard_rows = table.shape[0]
    offset = dp * shard_rows
    part = TOPV // device_total

    codes = lax.all_gather(token_ids * 2 + valid, ("dp", "head"), axis=1, tiled=True)
    count = jnp.sum(codes & 1).astype(jnp.float32)
    codes = lax.dynamic_index_in_dim(codes, batch, 0, keepdims=False).reshape(
        dp_count, head_count, tokens
    )
    first = lax.dynamic_index_in_dim(codes, head, 1, keepdims=False)
    second = lax.dynamic_index_in_dim(codes, head ^ 2, 1, keepdims=False)
    codes = jnp.concatenate([first, second], axis=1)
    weighting = (lax.dynamic_index_in_dim(codes, dp, 0, keepdims=False) & 1).astype(jnp.float32)
    vocab = lax.dynamic_index_in_dim(
        vocab_ids.reshape(dp_count, head_count, part), head, 1, keepdims=False
    )
    local = jnp.concatenate([vocab, codes >> 1], axis=1) - offset
    owned = (local >= 0) & (local < shard_rows)
    rows_out = jnp.where(
        owned[..., None], table[jnp.clip(local, 0, shard_rows - 1)], 0.0
    ).astype(low)
    rows_in = lax.psum_scatter(rows_out, "dp", scatter_dimension=0, tiled=True)
    rows_in = rows_in.reshape(part + 2 * tokens, D)
    chosen = lax.all_gather(rows_in[:part], ("dp", "head"), axis=0, tiled=True)
    hidden = rows_in[part:].astype(jnp.float32)

    widths = [3 * D // device_total, D // device_total, 2 * FF // device_total, FF // device_total]
    cuts = [sum(widths[:index]) for index in range(5)]
    gathered = lax.all_gather(block.T.astype(low), ("dp", "head"), axis=0)
    weights = [
        gathered[:, cuts[index] : cuts[index + 1]].reshape(-1, D) for index in range(4)
    ]

    teacher_own = lax.dynamic_index_in_dim(teacher, batch, 0, keepdims=False)
    teacher_far = swap(
        lax.dynamic_index_in_dim(teacher, 1 - batch, 0, keepdims=False), head_count, 2
    )
    teacher_rows = jnp.concatenate([teacher_own, teacher_far], axis=0)

    run = jnp.arange(tokens, dtype=jnp.int32)
    places = jnp.concatenate([head * tokens + run, (head ^ 2) * tokens + run])
    places_far = jnp.concatenate([(head ^ 1) * tokens + run, (head ^ 3) * tokens + run])
    own_lengths = lax.dynamic_index_in_dim(lengths, batch, 0, keepdims=False)[0]
    segment, position = segments(own_lengths, places)
    segment_far, unused = segments(own_lengths, places_far)
    places_all = jnp.concatenate([places, places_far])
    segment_all = jnp.concatenate([segment, segment_far])
    allow = (segment[:, None] == segment_all[None, :]) & (places[:, None] >= places_all[None, :])
    freqs = jnp.exp(jnp.arange(0, HD, 2, dtype=jnp.float32) * (-math.log(10000.0) / HD))
    angle = position.astype(jnp.float32)[:, None] * freqs[None, :]
    angle = jnp.concatenate([angle, angle], axis=1)
    cosine, sine = jnp.cos(angle), jnp.sin(angle)

    saves = []
    for repeat in range(2):
        hidden, saved = layer_forward(hidden, weights, gains, cosine, sine, allow, head_count)
        saves.append(saved)

    normed = rms_norm(hidden, gains[2]).astype(low)
    log_prob = jax.nn.log_softmax(contract_cols(normed, chosen), axis=-1)
    teach = jax.nn.log_softmax(teacher_rows.astype(jnp.float32), axis=-1)
    loss_sum = jnp.sum(weighting * jnp.sum(jnp.exp(teach) * (teach - log_prob), axis=-1))
    logit_grads = ((jnp.exp(log_prob) - jnp.exp(teach)) * weighting[:, None]).astype(low)
    chosen_grads = contract_rows(logit_grads, normed).astype(low)
    gradient, d_gain_final = rms_back(hidden, gains[2], product(logit_grads, chosen))
    chosen_grads = lax.psum_scatter(chosen_grads, ("dp", "head"), scatter_dimension=0, tiled=True)

    block_grads = None
    d_gains = [0.0, 0.0]
    for repeat in range(2):
        gradient, layer_grads, d_gain_one, d_gain_two = layer_backward(
            gradient, weights, gains, saves[1 - repeat], cosine, sine, allow, head_count
        )
        d_gains = [d_gains[0] + d_gain_one, d_gains[1] + d_gain_two]
        if block_grads is None:
            block_grads = layer_grads
        else:
            block_grads = [total + extra for total, extra in zip(block_grads, layer_grads)]

    joined = jnp.concatenate(
        [piece.astype(low).reshape(device_total, -1, D) for piece in block_grads], axis=1
    )
    block_grads = lax.psum_scatter(joined, ("dp", "head"), scatter_dimension=0, tiled=True)
    block_grads = block_grads.reshape(-1, D).astype(jnp.float32).T

    rows_back = jnp.concatenate([chosen_grads, gradient.astype(low)], axis=0)
    rows_back = lax.all_gather(rows_back, "dp", axis=0, tiled=True)
    dump_index = jnp.where(owned, local, shard_rows).reshape(-1)
    table_grads = jax.ops.segment_sum(
        rows_back.astype(jnp.float32), dump_index, num_segments=shard_rows + 1
    )[:shard_rows]
    table_grads = lax.psum(table_grads.astype(low), "head").astype(jnp.float32)

    small = jnp.concatenate([d_gains[0], d_gains[1], d_gain_final, loss_sum[None]])
    small = lax.psum(small, ("dp", "head"))
    gain_grads = small[: 3 * D].reshape(3, D) / count
    loss = small[3 * D] / count

    squares = lax.psum(
        jnp.sum(block_grads * block_grads)
        + jnp.where(head == 0, jnp.sum(table_grads * table_grads), 0.0),
        ("dp", "head"),
    )
    grad_norm = jnp.sqrt(squares / (count * count) + jnp.sum(gain_grads * gain_grads))
    clip = jnp.minimum(1.0, clip_norm / grad_norm)
    factor = clip / count
    block_grads = block_grads * factor
    table_grads = table_grads * factor
    gain_grads = gain_grads * clip

    rotated = jnp.concatenate(
        [
            contract_rows(bases[index], block_grads[:, cuts[index] : cuts[index + 1]])
            for index in range(4)
        ],
        axis=1,
    )
    block_m_new = beta_one * block_m + (1.0 - beta_one) * rotated
    block_v_new = beta_two * block_v + (1.0 - beta_two) * rotated * rotated
    direction = (
        block_m_new
        / (1.0 - beta_one**STEP)
        / (jnp.sqrt(block_v_new / (1.0 - beta_two**STEP)) + adam_eps)
    )
    update = jnp.concatenate(
        [product(bases[index], direction[:, cuts[index] : cuts[index + 1]]) for index in range(4)],
        axis=1,
    )
    block_new = block - rate_block * (update + decay_rate * block)
    table_new, table_m_new, table_v_new = adam_step(
        table, table_grads, table_m, table_v, rate_table, decay_rate
    )
    gains_new, gains_m_new, gains_v_new = adam_step(
        gains, gain_grads, gains_m, gains_v, rate_gain, 0.0
    )
    return (
        loss,
        grad_norm,
        block_new,
        block_m_new,
        block_v_new,
        table_new,
        table_m_new,
        table_v_new,
        gains_new,
        gains_m_new,
        gains_v_new,
        block_new.astype(low),
        table_new.astype(low),
    )


def solution(mesh):
    tokens = P(None, ("dp", "head"))
    columns = P(None, ("dp", "head"))
    table = P("dp", None)
    return jax.shard_map(
        on_device,
        mesh=mesh,
        in_specs=(
            tokens,
            P(None, "dp", None),
            tokens,
            P(),
            P(None, ("dp", "head"), None),
            columns,
            columns,
            columns,
            P(),
            table,
            table,
            table,
            P(),
            P(),
            P(),
        ),
        out_specs=(
            P(),
            P(),
            columns,
            columns,
            columns,
            table,
            table,
            table,
            P(),
            P(),
            P(),
            columns,
            table,
        ),
        check_vma=False,
    )
```

time: 1440 us -> 978 us (0.68)
  local copies, waits for them, and re-layouts: 313 us -> 113 us
  matrix products: 286 us -> 121 us
  other arithmetic: 216 us -> 139 us
  starting transfers between devices: 67.7 us -> 2.83 us
  waiting for transfers between devices: 424 us -> 485 us
    dot_general x18 -> x13, matrix products: 117 us -> 42.8 us  [contract_rows(): lax.dot_general(left, right, (((0,), (0,)), ((), ())), preferred_element_...]
    add x6 -> x0, local copies, waits for them, and re-layouts: 73.1 us -> none  [on_device(): total + extra]
    all_to_all x16 -> x0, starting transfers between devices: 67.4 us -> none  [the longest x4 17.3 us: layer_forward(): lax.all_to_all(packed, 'head', split_axis=2, concat_axis=0, tiled=True)]
    unnamed x440 -> x338, local copies, waits for them, and re-layouts: 83.8 us -> 31.6 us
    all_gather x2 -> x3, waiting for transfers between devices: 0.01 us -> 51.3 us  [the longest x1 49.3 us: on_device(): rows_back = lax.all_gather(rows_back, 'dp', axis=0, tiled=True)]
    psum x3 -> x1, waiting for transfers between devices: 48.1 us -> 97.6 us  [on_device(): table_grads = lax.psum(table_grads.astype(low), 'head').astype(jnp.float32)]
    dot_general x32 -> x12, matrix products: 72.3 us -> 29.3 us  [the longest x2 8.98 us: attend_back(): jnp.einsum('hqk,qhd->khd', weight.astype(low), upstream, preferred_elemen...]
    add x13 -> x11, other arithmetic: 41.3 us -> 1.8 us  [the longest x1 0.7 us: on_device(): token_ids * 2 + valid]
  transfers between devices with their start and end apart: 23 -> 12, of which waited for: 7 -> 7; matrix products, arithmetic and copies ran while one was open for 42% -> 17% of each run, Pallas kernels for 0% -> 0%
where the time goes in v1:
time: 978 us; the launch traced here: 970 us
  waiting for transfers between devices  485 us (50%)
  other arithmetic  139 us (14%)
  matrix products  121 us (12%)
  local copies, waits for them, and re-layouts  113 us (12%)
  blocking collectives  83.2 us (9%)
  between operations  25.5 us (3%)
    reduce_scatter x1, waiting for transfers between devices, on_device(): rows_in = lax.psum_scatter(rows_out, 'dp', scatter_dimension=0, tiled=True)  156 us
    reduce_scatter x1, waiting for transfers between devices, on_device(): lax.psum_scatter(joined, ('dp', 'head'), scatter_dimension=0, tiled=True)  107 us
    psum x1, waiting for transfers between devices, on_device(): table_grads = lax.psum(table_grads.astype(low), 'head').astype(jnp.float32)  97.6 us
    reduce_scatter x1, waiting for transfers between devices, on_device(): lax.psum_scatter(chosen_grads, ('dp', 'head'), scatter_dimension=0, tiled...  71.6 us
    all_gather x1, waiting for transfers between devices, on_device(): rows_back = lax.all_gather(rows_back, 'dp', axis=0, tiled=True)  49.3 us
    all_gather x1, blocking collectives, on_device(): lax.all_gather(token_ids * 2 + valid, ('dp', 'head'), axis=1, tiled=True)  43.2 us
    dot_general x13, matrix products, contract_rows(): lax.dot_general(left, right, (((0,), (0,)), ((), ())), preferred_element_...  42.8 us
    psum x1, blocking collectives, on_device(): small = lax.psum(small, ('dp', 'head'))  39.9 us
  transfers between devices with their start and end apart: 12, of which 7 were waited for; matrix products, arithmetic and copies ran while one was open for 17% of the time, Pallas kernels for 0%

profile of v1, /device:TPU:0, one launch (start us, length us, event | category | flops | bytes accessed | tf_op | source)
XLA Modules:
  0.0 969.5 jit_solution(10707794897695880077)
XLA Ops:
  8.8 43.2 %all_gather.15 = s32[2,4096]{1,0:T(2,128)S(1)} all-gather(s32[2,128]{1,0:T(2,128)S(1)} %multiply_add_fusion.2), channel_id=1, replica_groups=mesh['dp'=8,'head'=4] {'dp','head'}, dimensions={1}, use_global_device_ids=true | all-gather | bytes 33792 | tf_op jit(solution)/shard_map/all_gather | solution.py:200
  53.4 19.0 %gather_fusion = bf16[3072,768]{1,0:T(8,128)(2,1)} fusion(f32[4000,768]{1,0:T(8,128)} %param.25, s32[3072]{0:T(1024)S(1)} %broadcast_clamp_fusion), kind=kCustom, calls=%fused_computation | custom fusion | bytes 9449472 | tf_op jit(solution)/shard_map/gather | solution.py:215
  72.5 5.8 select_convert_fusion
  85.2 155.6 %reduce-scatter.4.cloned.1.call-done = bf16[1,384,768]{2,1,0:T(8,128)(2,1)} async-done(((bf16[8,384,768]{2,1,0:T(8,128)(2,1)}), bf16[1,384,768]{2,1,0:T(8,128)(2,1)}) %reduce-scatter.4.cloned.1.call-update) | async-done | bytes 589840 | tf_op jit(solution)/shard_map/reduce_scatter | solution.py:217
  242.5 24.5 %copy.41 = bf16[12288,768]{1,0:T(8,128)(2,1)} copy(bf16[12288,768]{0,1:T(8,128)(2,1)} %all-gather.8.cloned.1.call-done) | data formatting | bytes 37748736 | tf_op jit(solution)/shard_map/all_gather | solution.py:224
  267.1 2.3 slice.311
  281.2 2.4 slice.320
  283.6 8.4 slice.321
  292.0 4.9 slice.324
  299.7 2.0 exponential_reduce_fusion.1
  302.3 3.5 convolution_convert_fusion.2
  307.1 2.7 fusion.177
  312.5 4.4 multiply_reduce_fusion.12
  324.2 2.1 fusion.22
  329.8 2.2 exponential_reduce_fusion
  333.0 3.7 convolution_convert_fusion.1
  337.4 2.7 fusion.179
  342.8 5.2 multiply_reduce_fusion.10
  348.0 2.0 all-gather.10.cloned.1.call-done
  350.0 5.0 fusion.192
  355.8 4.2 fusion.20
  360.0 2.6 multiply_reduce_fusion.9
  362.9 2.4 multiply_convert_fusion.5
  365.6 3.4 multiply_reduce_fusion.8
  371.4 1.9 copy.42
  373.4 4.6 convolution_bitcast_fusion.1
  378.0 2.4 multiply_reduce_fusion.1
  380.5 1.8 multiply_convert_fusion.1
  386.3 4.7 convolution_convert_fusion
  391.1 2.2 slice-done.23
  395.1 2.2 broadcast_multiply_fusion.1
  398.1 2.0 copy-done.5
  400.3 1.9 multiply_reduce_fusion.7
  402.6 2.8 multiply_convert_fusion.3
  405.7 3.4 multiply_reduce_fusion.5
  412.7 4.4 convolution_bitcast_fusion
  417.6 2.4 multiply_reduce_fusion
  420.0 1.8 multiply_convert_fusion
  423.2 1.9 collective-permute-done.4
  425.3 2.1 broadcast_multiply_fusion
  428.0 2.1 copy-done.6
  430.3 1.9 fusion.102
  432.5 71.6 %reduce-scatter.8.cloned.1.call-done = bf16[128,768]{1,0:T(8,128)(2,1)} async-done(((bf16[4096,768]{1,0:T(8,128)(2,1)}), bf16[128,768]{1,0:T(8,128)(2,1)}) %reduce-scatter.8.cloned.1.call-update) | async-done | bytes 196624 | tf_op jit(solution)/shard_map/reduce_scatter | solution.py:261
  504.1 1.8 pad_maximum_fusion.16
  510.6 8.2 fusion.50
  520.8 3.7 add_convert_fusion.1
  524.5 11.0 %add_convert_fusion = bf16[6144,768]{1,0:T(8,128)(2,1)} fusion(f32[6144,768]{1,0:T(8,128)} %fusion.50, bf16[256,3072]{1,0:T(8,128)(2,1)} %copy-done.91, bf16[256,3072]{1,0:T(8,128)(2,1)S(1)} %copy-done.90, f32[256,768]{1,0:T(8,128)S(1)} %copy-done.14, f32[768]{0:T(1024)S(1)} %get-tuple-element.51, f32[256]{0:T(256)S(1)} %copy-done.112), kind=kOutput, calls=%fused_computation.3 | convolution fusion | flops 2432237568 | bytes 32247808 | tf_op jit(solution)/shard_map/dot_general | solution.py:33
  535.5 49.3 %all-gather.6.cloned.1.call-done = bf16[3072,768]{1,0:T(8,128)(2,1)} async-done(((bf16[384,768]{1,0:T(8,128)(2,1)}), bf16[3072,768]{1,0:T(8,128)(2,1)}) %all-gather.6.cloned.1.call-update) | async-done | bytes 4718608 | tf_op jit(solution)/shard_map/all_gather | solution.py:282
  584.9 27.0 %scatter_custom_fusion = f32[4001,768]{1,0:T(8,128)} fusion(s32[3072]{0:T(1024)S(1)} %bitcast.297, bf16[3072,768]{1,0:T(8,128)(2,1)} %all-gather.6.cloned.1.call-done, f32[]{:T(128)} %constant.61.clone.1), kind=kCustom, calls=%fused_computation.13 | custom fusion | flops 4718592 | bytes 17009668 | tf_op jit(solution)/shard_map/scatter-add | solution.py:284
  611.9 7.7 slice.532
  624.0 15.2 %pad_maximum_fusion = bf16[32,384,768]{2,1,0:T(8,128)(2,1)} fusion(bf16[32,96,768]{2,1,0:T(8,128)(2,1)} %bitcast.265, bf16[32,192,768]{2,1,0:T(8,128)(2,1)} %bitcast.245, bf16[32,24,768]{2,1,0:T(8,128)(2,1)S(1)} %bitcast.271, bf16[32,72,768]{2,1,0:T(8,128)(2,1)S(1)} %bitcast.266), kind=kLoop, calls=%fused_computation.2 | loop fusion | flops 75497472 | bytes 37748736 | tf_op jit(solution)/shard_map/concatenate | solution.py:275
  646.6 97.6 %all-reduce.3.cloned.1.call-done = bf16[4000,768]{1,0:T(8,128)(2,1)} async-done(((bf16[4000,768]{1,0:T(8,128)(2,1)}), bf16[4000,768]{1,0:T(8,128)(2,1)}) %all-reduce.3.cloned.1.call-update) | async-done | bytes 6144016 | tf_op jit(solution)/shard_map/psum | solution.py:287
  744.3 6.6 fusion.2
  751.5 106.8 %reduce-scatter.6.cloned.1.call-done = bf16[1,384,768]{2,1,0:T(8,128)(2,1)} async-done(((bf16[32,384,768]{2,1,0:T(8,128)(2,1)}), bf16[1,384,768]{2,1,0:T(8,128)(2,1)}) %reduce-scatter.6.cloned.1.call-update) | async-done | bytes 589840 | tf_op jit(solution)/shard_map/reduce_scatter | solution.py:278
  858.3 2.0 fusion.66
  860.9 39.9 %all-reduce = (f32[2305]{0:T(1024)S(1)}, f32[]{:T(128)}) all-reduce(f32[2305]{0:T(1024)S(1)} %pad_maximum_fusion.18, f32[]{:T(128)S(6)} %add.365), channel_id=1, replica_groups=mesh['dp'=8,'head'=4] {'dp','head'}, use_global_device_ids=true, to_apply=%region_25.27 | all-reduce | flops 2306 | bytes 18448 | tf_op jit(solution)/shard_map/psum | solution.py:290
  904.6 2.2 fusion.71
  906.7 2.1 fusion.60
  908.8 2.0 fusion.83
  910.8 2.2 fusion.77
  913.0 2.2 add_divide_fusion.2
  920.7 2.8 fusion.183
  923.5 2.8 copy.48
  930.8 28.9 %fusion.180 = (bf16[4000,768]{1,0:T(8,128)(2,1)}, f32[4000,768]{1,0:T(8,128)}, f32[4000,768]{1,0:T(8,128)}, f32[4000,768]{1,0:T(8,128)}) fusion(f32[4000,768]{1,0:T(8,128)} %param.25, f32[]{:T(128)S(6)} %div.137, bf16[4000,768]{1,0:T(8,128)(2,1)} %all-reduce.3.cloned.1.call-done, f32[4000,768]{1,0:T(8,128)} %param.26, f32[4000,768]{1,0:T(8,128)} %param.27), kind=kLoop, calls=%fused_computation.347 | loop fusion | flops 55296000 | bytes 86016000 | tf_op jit(solution)/shard_map/convert_element_type | solution.py:344
  (488 shorter events, 90.3 us)
Async XLA Ops:
  8.0 72.6 %copy-start = (s32[2,1,3]{2,1,0:T(1,128)S(1)}, s32[2,1,3]{2,1,0:T(1,128)}, u32[]{:S(2)}) copy-start(s32[2,1,3]{2,1,0:T(1,128)} %param.17) | copy-start | bytes 76
  8.0 232.8 %reduce-scatter.4.cloned.1.call-start = ((), (), s32[]{:S(2)}) async-start(), calls=%async_computation.3 | async-start | bytes 5308416 | tf_op jit(solution)/shard_map/reduce_scatter | solution.py:217
  52.0 20.4 %copy-start.95 = (s32[2,4096]{1,0:T(2,128)}, s32[2,4096]{1,0:T(2,128)S(1)}, u32[]{:S(2)}) copy-start(s32[2,4096]{1,0:T(2,128)S(1)} %all_gather.15) | copy-start | bytes 98308
  52.8 19.7 %copy-start.103 = (s32[8,1,128]{2,1,0:T(1,128)}, s32[8,1,128]{2,1,0:T(1,128)S(1)}, u32[]{:S(2)}) copy-start(s32[8,1,128]{2,1,0:T(1,128)S(1)} %get-tuple-element.156) | copy-start | bytes 12292
  52.8 19.6 %copy-start.101 = (s32[8,256]{1,0:T(8,128)}, s32[8,256]{1,0:T(8,128)S(1)}, u32[]{:S(2)}) copy-start(s32[8,256]{1,0:T(8,128)S(1)} %get-tuple-element.112) | copy-start | bytes 24580
  78.3 5.9 copy-start.105
  78.4 164.2 %all-gather.8.cloned.1.call-start = ((), (), s32[]{:S(2)}) async-start(), calls=%async_computation.8 | async-start | bytes 19464192 | tf_op jit(solution)/shard_map/all_gather | solution.py:224
  80.5 269.5 %all-gather.10.cloned.1.call-start = ((), (), s32[]{:S(2)}) async-start(), calls=%async_computation.9 | async-start | bytes 6488064 | tf_op jit(solution)/shard_map/all_gather | solution.py:219
  83.1 184.0 %copy-start.136 = (s32[128]{0:T(128)}, s32[128]{0:T(128)S(1)}, u32[]{:S(2)}) copy-start(s32[128]{0:T(128)S(1)} %iota_add_fusion.3) | copy-start | bytes 1540
  269.4 48.3 %copy-start.4 = (bf16[32,72,768]{2,1,0:T(8,128)(2,1)}, bf16[32,72,768]{2,1,0:T(8,128)(2,1)S(1)}, u32[]{:S(2)}) copy-start(bf16[32,72,768]{2,1,0:T(8,128)(2,1)S(1)} %slice.311) | copy-start | bytes 10616836
  273.6 23.3 %collective-permute-start = (bf16[256,24,64]{0,2,1:T(8,128)(2,1)}, bf16[256,24,64]{0,2,1:T(8,128)(2,1)}, u32[]{:S(2)}, u32[]{:S(2)}) collective-permute-start(bf16[256,24,64]{0,2,1:T(8,128)(2,1)} %pad_maximum_fusion.12), channel_id=1, source_target_pairs={{0,1},{1,0},{2,3},{3,2},{4,5},{5,4},{6,7},{7,6},{8,9},{9,8},{10,11... | collective-permute-start | bytes 2359304 | tf_op jit(solution)/shard_map/ppermute | solution.py:109
  275.2 47.4 %collective-permute-start.2 = (bf16[128,4096]{1,0:T(8,128)(2,1)}, bf16[128,4096]{1,0:T(8,128)(2,1)}, u32[]{:S(2)}, u32[]{:S(2)}) collective-permute-start(bf16[128,4096]{1,0:T(8,128)(2,1)} %get-tuple-element.82), channel_id=1, source_target_pairs={{0,2},{1,3},{2,0},{3,1},{4,6},{5,7},{6,4},{7,5},{8,10},{9,11},{10,... | collective-permute-start | bytes 3145736 | tf_op jit(solution)/shard_map/ppermute | solution.py:109
  281.2 222.9 %reduce-scatter.8.cloned.1.call-start = ((), (), s32[]{:S(2)}) async-start(), calls=%async_computation.5 | async-start | bytes 6488064 | tf_op jit(solution)/shard_map/reduce_scatter | solution.py:261
  292.0 4.9 copy-start.60
  292.0 4.9 copy-start.66
  301.7 5.4 slice-start
  306.4 6.1 copy-start.12
  318.9 8.0 copy-start.62
  321.1 5.8 copy-start.68
  321.2 5.8 collective-permute-start.1
  329.7 7.7 slice-start.3
  337.3 31.7 %copy-start.15 = (f32[256,768]{1,0:T(8,128)}, f32[256,768]{1,0:T(8,128)S(1)}, u32[]{:S(2)}) copy-start(f32[256,768]{1,0:T(8,128)S(1)} %get-tuple-element.138) | copy-start | bytes 2359300
  337.4 31.6 %copy-start.108 = (f32[256]{0:T(256)}, f32[256]{0:T(256)S(1)}, u32[]{:S(2)}) copy-start(f32[256]{0:T(256)S(1)} %get-tuple-element.121) | copy-start | bytes 3076
  342.8 5.2 copy-start.32
  348.0 14.6 %copy-start.121 = (f32[256]{0:T(256)}, f32[256]{0:T(256)S(1)}, u32[]{:S(2)}) copy-start(f32[256]{0:T(256)S(1)} %get-tuple-element.123) | copy-start | bytes 3076
  355.0 5.0 copy-start.75
  355.0 5.0 copy-start.137
  355.7 7.1 slice-start.21
  355.7 7.1 slice-start.24
  360.0 5.3 slice-start.6
  360.0 5.4 slice-start.7
  362.8 6.2 copy-start.40
  370.2 7.8 slice-start.14
  383.0 8.0 copy-start.50
  384.3 6.8 collective-permute-start.3
  391.0 11.5 %slice-start.26 = ((s8[4718592]{0:T(1024)(128)(4,1)}), s8[524288]{0:T(1024)(128)(4,1)S(1)}, s32[]{:S(2)}) async-start(s8[4718592]{0:T(1024)(128)(4,1)} %bitcast.277), calls=%async_computation.36 | async-start | bytes 1048576
  391.0 193.8 %all-gather.6.cloned.1.call-start = ((), (), s32[]{:S(2)}) async-start(), calls=%async_computation.6 | async-start | bytes 5308416 | tf_op jit(solution)/shard_map/all_gather | solution.py:282
  393.3 9.2 slice-start.19
  395.1 7.4 slice-start.20
  395.1 7.4 slice-start.27
  400.3 5.1 slice-start.9
  402.5 6.6 copy-start.42
  409.1 8.0 slice-start.12
  412.7 4.9 copy-start.45
  412.7 4.9 copy-start.98
  422.7 2.4 collective-permute-start.4
  432.2 73.9 %copy-start.102 = (s32[8,256]{1,0:T(8,128)S(1)}, s32[8,256]{1,0:T(8,128)}, u32[]{:S(2)}) copy-start(s32[8,256]{1,0:T(8,128)} %copy-done.101) | copy-start | bytes 24580
  432.2 74.7 %copy-start.25 = (f32[256,768]{1,0:T(8,128)S(1)}, f32[256,768]{1,0:T(8,128)}, u32[]{:S(2)}) copy-start(f32[256,768]{1,0:T(8,128)} %copy-done.23) | copy-start | bytes 2359300
  432.5 76.0 %copy-start.33 = (bf16[256,3072]{1,0:T(8,128)(2,1)S(1)}, bf16[256,3072]{1,0:T(8,128)(2,1)}, u32[]{:S(2)}) copy-start(bf16[256,3072]{1,0:T(8,128)(2,1)} %copy-done.32) | copy-start | bytes 4718596
  505.9 238.4 %all-reduce.3.cloned.1.call-start = ((), (), s32[]{:S(2)}) async-start(), calls=%async_computation.7 | async-start | bytes 12288000 | tf_op jit(solution)/shard_map/psum | solution.py:287
  510.6 8.2 copy-start.86
  619.7 238.6 %reduce-scatter.6.cloned.1.call-start = ((), (), s32[]{:S(2)}) async-start(), calls=%async_computation.4 | async-start | bytes 19464192 | tf_op jit(solution)/shard_map/reduce_scatter | solution.py:278
  640.5 4.8 copy-start.128
  640.5 5.4 copy-start.131
  640.5 5.4 copy-start.133
  640.5 5.4 copy-start.132
  640.5 5.4 copy-start.134
  640.5 5.4 copy-start.130
  744.3 170.9 %slice-start.16 = ((s8[9437184]{0:T(1024)(128)(4,1)}), s8[1048576]{0:T(1024)(128)(4,1)S(1)}, s32[]{:S(2)}) async-start(s8[9437184]{0:T(1024)(128)(4,1)} %bitcast.254), calls=%async_computation.26 | async-start | bytes 2097152
  904.6 10.6 %slice-start.17 = ((s8[9437184]{0:T(1024)(128)(4,1)}), s8[4194304]{0:T(1024)(128)(4,1)S(1)}, s32[]{:S(2)}) async-start(s8[9437184]{0:T(1024)(128)(4,1)} %bitcast.254), calls=%async_computation.27 | async-start | bytes 8388608
  920.7 5.6 copy-start.55
  923.5 5.6 copy-start.104
  923.5 5.6 copy-start.77
  930.8 28.9 %copy-start.1 = (s32[2,1,3]{2,1,0:T(1,128)S(1)}, s32[2,1,3]{2,1,0:T(1,128)}, u32[]{:S(2)}) copy-start(s32[2,1,3]{2,1,0:T(1,128)} %param.17) | copy-start | bytes 76
  (114 other events, 310.9 us)
Sparse Core Ops, SparseCore 0:
  78.5 162.2 reduce-scatter.3
  506.0 78.8 all-gather.5
  619.8 124.4 all-reduce.2
Sparse Core Ops, SparseCore 1:
  82.3 157.9 all-gather.7
  281.3 68.7 all-gather.9
  391.1 112.9 reduce-scatter.7
  639.3 218.9 reduce-scatter.5

commit v2 on v1

--- a/solution.py
+++ b/solution.py
@@ -1,8 +1,11 @@
+import functools
 import math
 
 import jax
 import jax.numpy as jnp
 from jax import lax
+from jax.experimental import pallas as pl
+from jax.experimental.pallas import tpu as pltpu
 from jax.sharding import PartitionSpec as P
 
 D = 768
@@ -160,6 +163,303 @@
     return d_middle + d_hidden, [d_qkv_w, d_out, d_gu, d_down], d_gain_one, d_gain_two
 
 
+MESH = pl.DeviceIdType.MESH
+ANY = pl.BlockSpec(memory_space=pl.ANY)
+
+
+def coordinates(depth):
+    dp, head = lax.axis_index("dp"), lax.axis_index("head")
+    return dp // 2, dp % 2, head // 2, head % 2
+
+
+def device(z, x, y, c):
+    return (z * 2 + x, y * 2 + c)
+
+
+def slot(z, x, y, c):
+    return ((z * 2 + x) * 2 + y) * 2 + c
+
+
+def greet(depth, z, x, y, c):
+    barrier = pltpu.get_barrier_semaphore()
+    for target in (device(z, 1 - x, y, c), device(z, x, 1 - y, c), device(z, x, y, 1 - c)):
+        pl.semaphore_signal(barrier, 1, device_id=target, device_id_type=MESH)
+
+    @pl.when(z > 0)
+    def below():
+        pl.semaphore_signal(barrier, 1, device_id=device(z - 1, x, y, c), device_id_type=MESH)
+
+    @pl.when(z < depth - 1)
+    def above():
+        pl.semaphore_signal(barrier, 1, device_id=device(z + 1, x, y, c), device_id_type=MESH)
+
+    pl.semaphore_wait(barrier, 3 + jnp.where(z > 0, 1, 0) + jnp.where(z < depth - 1, 1, 0))
+
+
+def start_kernel(depth, *refs):
+    pieces = refs[0:3]
+    rows_ref = refs[3]
+    wholes = refs[4:7]
+    sum_ref = refs[7]
+    far_x, from_low, from_high, total = refs[8:12]
+    local_sem, up_sem, down_sem, x_sem, y_sem, c_sem, block_sem = refs[12:19]
+    rx_send, rx_recv, ru_send, ru_recv, rd_send, rd_recv = refs[19:25]
+    z, x, y, c = coordinates(depth)
+    mine = slot(z, x, y, c)
+    greet(depth, z, x, y, c)
+
+    def own(block, piece, target, sem):
+        return pltpu.make_async_remote_copy(
+            pieces[piece],
+            wholes[piece].at[block],
+            sem.at[piece],
+            block_sem.at[block, piece],
+            device_id=target,
+            device_id_type=MESH,
+        )
+
+    def onward(block, piece, target, sem):
+        return pltpu.make_async_remote_copy(
+            wholes[piece].at[block],
+            wholes[piece].at[block],
+            sem.at[piece],
+            block_sem.at[block, piece],
+            device_id=target,
+            device_id_type=MESH,
+        )
+
+    def send(make, block, target, sem):
+        for piece in range(3):
+            make(block, piece, target, sem).start()
+
+    def arrive(block):
+        for piece in range(3):
+            onward(block, piece, device(z, x, y, 1 - c), c_sem.at[0]).wait_recv()
+
+    across_x, across_y, across_c = (
+        device(z, 1 - x, y, c),
+        device(z, x, 1 - y, c),
+        device(z, x, y, 1 - c),
+    )
+    rows_x = [
+        pltpu.make_async_remote_copy(
+            rows_ref.at[goal * 2 + 1 - x],
+            far_x.at[goal],
+            rx_send.at[goal],
+            rx_recv.at[goal],
+            device_id=across_x,
+            device_id_type=MESH,
+        )
+        for goal in range(depth)
+    ]
+
+    def rows_up(goal):
+        return pltpu.make_async_remote_copy(
+            total.at[goal],
+            from_low.at[goal],
+            ru_send.at[goal],
+            ru_recv.at[goal],
+            device_id=device(z + 1, x, y, c),
+            device_id_type=MESH,
+        )
+
+    def rows_down(goal):
+        return pltpu.make_async_remote_copy(
+            total.at[goal],
+            from_high.at[goal],
+            rd_send.at[goal],
+            rd_recv.at[goal],
+            device_id=device(z - 1, x, y, c),
+            device_id_type=MESH,
+        )
+
+    goals = [
+        goal for pair in zip(range(depth // 2), range(depth - 1, 0, -1)) for goal in pair
+    ]
+    local = [
+        pltpu.make_async_copy(pieces[piece], wholes[piece].at[mine], local_sem.at[piece])
+        for piece in range(3)
+    ]
+    send(own, mine, across_y, y_sem.at[mine // 4])
+    for goal in goals:
+        rows_x[goal].start()
+
+    @pl.when(z < depth - 1)
+    def first_up():
+        send(own, mine, device(z + 1, x, y, c), up_sem.at[0])
+
+    @pl.when(z > 0)
+    def first_down():
+        send(own, mine, device(z - 1, x, y, c), down_sem.at[0])
+
+    send(own, mine, across_x, x_sem.at[z])
+    send(own, mine, across_c, c_sem.at[mine // 2])
+    for copy in local:
+        copy.start()
+
+    def spread(block, over_x):
+        send(onward, block, across_y, y_sem.at[block // 4])
+        if over_x:
+            send(onward, block, across_x, x_sem.at[block // 8])
+        send(onward, block, across_c, c_sem.at[block // 2])
+
+    for step in range(1, depth):
+
+        @pl.when(z - step >= 0)
+        def risen():
+            block = slot(z - step, x, y, c)
+            arrive(block)
+
+            @pl.when(z < depth - 1)
+            def further():
+                send(onward, block, device(z + 1, x, y, c), up_sem.at[step])
+
+            spread(block, True)
+
+        @pl.when(z + step < depth)
+        def fallen():
+            block = slot(z + step, x, y, c)
+            arrive(block)
+
+            @pl.when(z > 0)
+            def further():
+                send(onward, block, device(z - 1, x, y, c), down_sem.at[step])
+
+            spread(block, True)
+
+    for goal in goals:
+        rows_x[goal].wait_recv()
+        part = rows_ref[goal * 2 + x] + far_x[goal]
+
+        @pl.when(goal > z)
+        def rising():
+            @pl.when(z > 0)
+            def more():
+                rows_up(goal).wait_recv()
+                total[goal] = part + from_low[goal]
+
+            @pl.when(z == 0)
+            def alone():
+                total[goal] = part
+
+            rows_up(goal).start()
+
+        @pl.when(goal < z)
+        def falling():
+            @pl.when(z < depth - 1)
+            def more():
+                rows_down(goal).wait_recv()
+                total[goal] = part + from_high[goal]
+
+            @pl.when(z == depth - 1)
+            def alone():
+                total[goal] = part
+
+            rows_down(goal).start()
+
+        @pl.when(goal == z)
+        def here():
+            total[goal] = part
+
+    for step in range(depth):
+        for sign in (1, -1) if step else (1,):
+
+            @pl.when((z + sign * step >= 0) & (z + sign * step < depth))
+            def crossed():
+                block = slot(z + sign * step, 1 - x, y, c)
+                arrive(block)
+                spread(block, False)
+
+    for goal in range(depth):
+
+        @pl.when(goal == z)
+        def landed():
+            @pl.when(z > 0)
+            def low_part():
+                rows_up(goal).wait_recv()
+                total[goal] = total[goal] + from_low[goal]
+
+            @pl.when(z < depth - 1)
+            def high_part():
+                rows_down(goal).wait_recv()
+                total[goal] = total[goal] + from_high[goal]
+
+            sum_ref[...] = total[goal]
+
+    for step in range(depth):
+        for sign in (1, -1) if step else (1,):
+
+            @pl.when((z + sign * step >= 0) & (z + sign * step < depth))
+            def crossed():
+                for side in (x, 1 - x):
+                    block = slot(z + sign * step, side, 1 - y, c)
+                    arrive(block)
+                    send(onward, block, across_c, c_sem.at[block // 2])
+
+    for block in range(depth * 8):
+
+        @pl.when(block % 2 != c)
+        def from_core():
+            arrive(block)
+
+    for copy in local:
+        copy.wait()
+    for goal in range(depth):
+        rows_x[goal].wait_send()
+
+        @pl.when(goal > z)
+        def rose():
+            rows_up(goal).wait_send()
+
+        @pl.when(goal < z)
+        def fell():
+            rows_down(goal).wait_send()
+
+    def sent(block, target, sem):
+        for piece in range(3):
+            onward(block, piece, target, sem).wait_send()
+
+    for step in range(depth):
+
+        @pl.when((z - step >= 0) & (z < depth - 1))
+        def rose():
+            sent(mine, device(z + 1, x, y, c), up_sem.at[step])
+
+        @pl.when((z + step < depth) & (z > 0))
+        def fell():
+            sent(mine, device(z - 1, x, y, c), down_sem.at[step])
+
+        sent(mine, across_x, x_sem.at[step])
+    for index in range(depth * 2):
+        sent(mine, across_y, y_sem.at[index])
+    for index in range(depth * 4):
+        sent(mine, across_c, c_sem.at[index])
+
+
+def start(pieces, rows):
+    groups, height, width = rows.shape
+    depth = groups // 2
+    blocks = depth * 8
+    dma = pltpu.SemaphoreType.DMA
+    buffer = pltpu.VMEM((depth, height, width), low)
+    return pl.pallas_call(
+        functools.partial(start_kernel, depth),
+        out_shape=[jax.ShapeDtypeStruct((blocks,) + piece.shape, low) for piece in pieces]
+        + [jax.ShapeDtypeStruct((height, width), low)],
+        in_specs=[ANY] * 3 + [pl.BlockSpec(memory_space=pltpu.VMEM)],
+        out_specs=[ANY] * 3 + [pl.BlockSpec(memory_space=pltpu.VMEM)],
+        scratch_shapes=[buffer] * 4
+        + [dma((3,))]
+        + [dma((depth, 3))] * 3
+        + [dma((depth * 2, 3)), dma((depth * 4, 3)), dma((blocks, 3))]
+        + [dma((depth,))] * 6,
+        compiler_params=pltpu.CompilerParams(
+            collective_id=0, has_side_effects=True, vmem_limit_bytes=58 * 2**20
+        ),
+        name="start",
+    )(*pieces, rows)
+
+
 def adam_step(weight, gradient, first, second, rate, decay):
     first_new = beta_one * first + (1.0 - beta_one) * gradient
     second_new = beta_two * second + (1.0 - beta_two) * gradient * gradient
@@ -214,17 +514,20 @@
     rows_out = jnp.where(
         owned[..., None], table[jnp.clip(local, 0, shard_rows - 1)], 0.0
     ).astype(low)
-    rows_in = lax.psum_scatter(rows_out, "dp", scatter_dimension=0, tiled=True)
-    rows_in = rows_in.reshape(part + 2 * tokens, D)
+    widths = [3 * D // device_total, D // device_total, 2 * FF // device_total, FF // device_total]
+    cuts = [sum(widths[:index]) for index in range(5)]
+    block_low = block.T.astype(low)
+    attention, gate_up, down, rows_in = start(
+        [block_low[: cuts[2]], block_low[cuts[2] : cuts[3]], block_low[cuts[3] :]], rows_out
+    )
+    weights = [
+        attention[:, : cuts[1]].reshape(-1, D),
+        attention[:, cuts[1] :].reshape(-1, D),
+        gate_up.reshape(-1, D),
+        down.reshape(-1, D),
+    ]
     chosen = lax.all_gather(rows_in[:part], ("dp", "head"), axis=0, tiled=True)
     hidden = rows_in[part:].astype(jnp.float32)
-
-    widths = [3 * D // device_total, D // device_total, 2 * FF // device_total, FF // device_total]
-    cuts = [sum(widths[:index]) for index in range(5)]
-    gathered = lax.all_gather(block.T.astype(low), ("dp", "head"), axis=0)
-    weights = [
-        gathered[:, cuts[index] : cuts[index + 1]].reshape(-1, D) for index in range(4)
-    ]
 
     teacher_own = lax.dynamic_index_in_dim(teacher, batch, 0, keepdims=False)
     teacher_far = swap(

time: 978 us -> 1020 us (1.043)
  Pallas kernels: 0 us -> 123 us
  waiting for transfers between devices: 485 us -> 437 us
  local copies, waits for them, and re-layouts: 113 us -> 76.3 us
    reduce_scatter x1 -> x0, waiting for transfers between devices: 156 us -> none  [on_device(): rows_in = lax.psum_scatter(rows_out, 'dp', scatter_dimension=0, tiled=True)]
    pallas_call x0 -> x1, Pallas kernels: none -> 123 us  [start(): pl.pallas_call(functools.partial(start_kernel, depth), out_shape=[jax.Sha...]
    reduce_scatter x1, waiting for transfers between devices: 107 us -> 207 us  [on_device(): lax.psum_scatter(joined, ('dp', 'head'), scatter_dimension=0, tiled=True)]
    all_gather x1 -> x0, local copies, waits for them, and re-layouts: 24.5 us -> none  [on_device(): gathered = lax.all_gather(block.T.astype(low), ('dp', 'head'), axis=0)]
    slice x5 -> x4, local copies, waits for them, and re-layouts: 18 us -> 6.23 us  [the longest x1 2.37 us: on_device(): attention[:, cuts[1]:].reshape(-1, D)]
    reduce_scatter x1, waiting for transfers between devices: 71.6 us -> 81.8 us  [on_device(): lax.psum_scatter(chosen_grads, ('dp', 'head'), scatter_dimension=0, tiled...]
    unnamed x338 -> x336, local copies, waits for them, and re-layouts: 31.6 us -> 28.6 us
  transfers between devices with their start and end apart: 12 -> 10, of which waited for: 7 -> 6; matrix products, arithmetic and copies ran while one was open for 17% -> 16% of each run, Pallas kernels for 0% -> 0%
where the time goes in v2:
time: 1020 us; the launch traced here: 1010 us
  waiting for transfers between devices  437 us (43%)
  other arithmetic  143 us (14%)
  matrix products  124 us (12%)
  Pallas kernels  123 us (12%)
  blocking collectives  82.6 us (8%)
  local copies, waits for them, and re-layouts  76.3 us (7%)
  between operations  23.8 us (2%)
    reduce_scatter x1, waiting for transfers between devices, on_device(): lax.psum_scatter(joined, ('dp', 'head'), scatter_dimension=0, tiled=True)  207 us
    pallas_call x1, Pallas kernels, start(): pl.pallas_call(functools.partial(start_kernel, depth), out_shape=[jax.Sha...  123 us
    psum x1, waiting for transfers between devices, on_device(): table_grads = lax.psum(table_grads.astype(low), 'head').astype(jnp.float32)  91.1 us
    reduce_scatter x1, waiting for transfers between devices, on_device(): lax.psum_scatter(chosen_grads, ('dp', 'head'), scatter_dimension=0, tiled...  81.8 us
    all_gather x1, waiting for transfers between devices, on_device(): rows_back = lax.all_gather(rows_back, 'dp', axis=0, tiled=True)  50.3 us
    dot_general x13, matrix products, contract_rows(): lax.dot_general(left, right, (((0,), (0,)), ((), ())), preferred_element_...  43.4 us
    all_gather x1, blocking collectives, on_device(): lax.all_gather(token_ids * 2 + valid, ('dp', 'head'), axis=1, tiled=True)  43.3 us
    psum x1, blocking collectives, on_device(): small = lax.psum(small, ('dp', 'head'))  39.4 us
  transfers between devices with their start and end apart: 10, of which 6 were waited for; matrix products, arithmetic and copies ran while one was open for 16% of the time, Pallas kernels for 0%

profile of v2, /device:TPU:0, one launch (start us, length us, event | category | flops | bytes accessed | tf_op | source)
XLA Modules:
  0.0 1014.6 jit_solution(16259815589020672832)
XLA Ops:
  10.6 43.3 %all_gather.9 = s32[2,4096]{1,0:T(2,128)S(1)} all-gather(s32[2,128]{1,0:T(2,128)S(1)} %multiply_add_fusion.2), channel_id=1, replica_groups=mesh['dp'=8,'head'=4] {'dp','head'}, dimensions={1}, use_global_device_ids=true | all-gather | bytes 33792 | tf_op jit(solution)/shard_map/all_gather | solution.py:500
  55.3 19.0 %gather_fusion = bf16[3072,768]{1,0:T(8,128)(2,1)} fusion(f32[4000,768]{1,0:T(8,128)} %param.25, s32[3072]{0:T(1024)S(1)} %broadcast_clamp_fusion), kind=kCustom, calls=%fused_computation | custom fusion | bytes 9449472 | tf_op jit(solution)/shard_map/gather | solution.py:515
  74.4 5.8 select_convert_fusion.refs_3_
  80.2 122.5 %start.1 = (bf16[32,96,768]{2,1,0:T(8,128)(2,1)}, bf16[32,192,768]{2,1,0:T(8,128)(2,1)}, bf16[32,96,768]{2,1,0:T(8,128)(2,1)}, bf16[384,768]{1,0:T(8,128)(2,1)}) custom-call(bf16[96,768]{1,0:T(8,128)(2,1)} %get-tuple-element.112.refs_0_, bf16[192,768]{1,0:T(8,128)(2,1)} %slice.305.refs_1_, bf16[96,768]{1,0:T(8,128)(2,1)} %get-tuple-element.111.refs_2_, ...), custom_call_target="tpu_custom_call" | custom-call | tf_op jit(solution)/shard_map/start/pallas_call | solution.py:445
  206.1 2.3 slice.238
  216.7 1.9 pad_add_fusion.3
  220.7 2.7 fusion.106
  225.0 3.1 dynamic-slice_bitcast_fusion.1
  228.1 4.2 collective-permute-start.2
  232.3 2.4 slice.250
  239.9 2.0 exponential_reduce_fusion.1
  242.6 4.0 convolution_convert_fusion.2
  247.8 2.7 fusion.166
  253.2 4.4 multiply_reduce_fusion.12
  264.8 2.1 fusion.18
  270.5 2.0 exponential_reduce_fusion
  273.7 3.7 convolution_convert_fusion.1
  278.2 2.7 fusion.168
  283.6 5.2 multiply_reduce_fusion.10
  288.8 4.5 all-gather.3.cloned.1.call-done
  293.3 5.0 fusion.183
  299.1 4.5 fusion.16
  303.6 2.6 multiply_reduce_fusion.9
  306.5 2.4 multiply_convert_fusion.5
  309.2 3.4 multiply_reduce_fusion.8
  315.0 1.9 copy.42
  316.9 4.6 convolution_bitcast_fusion.1
  321.6 2.4 multiply_reduce_fusion.1
  324.1 2.0 multiply_convert_fusion.1
  330.1 4.7 convolution_convert_fusion
  335.9 1.9 fusion.86
  337.8 2.2 broadcast_multiply_fusion.1
  340.8 1.8 copy-done.5
  342.8 1.9 multiply_reduce_fusion.7
  345.1 4.8 multiply_convert_fusion.3
  349.9 3.4 multiply_reduce_fusion.5
  356.9 4.8 convolution_bitcast_fusion
  361.8 2.4 multiply_reduce_fusion
  364.3 1.8 multiply_convert_fusion
  367.4 2.0 collective-permute-done.4
  369.6 2.1 broadcast_multiply_fusion
  372.5 1.9 copy-done.6
  374.6 1.9 fusion.96
  376.8 81.8 %reduce-scatter.5.cloned.1.call-done = bf16[128,768]{1,0:T(8,128)(2,1)} async-done(((bf16[4096,768]{1,0:T(8,128)(2,1)}), bf16[128,768]{1,0:T(8,128)(2,1)}) %reduce-scatter.5.cloned.1.call-update) | async-done | bytes 196624 | tf_op jit(solution)/shard_map/reduce_scatter | solution.py:564
  465.0 8.7 fusion.46
  475.7 3.7 add_convert_fusion.1
  479.4 11.0 %add_convert_fusion = bf16[6144,768]{1,0:T(8,128)(2,1)} fusion(f32[6144,768]{1,0:T(8,128)} %fusion.46, bf16[256,3072]{1,0:T(8,128)(2,1)} %copy-done.90, bf16[256,3072]{1,0:T(8,128)(2,1)S(1)} %copy-done.89, f32[256,768]{1,0:T(8,128)S(1)} %copy-done.15, f32[768]{0:T(1024)S(1)} %get-tuple-element.59, f32[256]{0:T(256)S(1)} %copy-done.111), kind=kOutput, calls=%fused_computation.3 | convolution fusion | flops 2432237568 | bytes 32247808 | tf_op jit(solution)/shard_map/dot_general | solution.py:36
  490.5 50.3 %all-gather.5.cloned.1.call-done = bf16[3072,768]{1,0:T(8,128)(2,1)} async-done(((bf16[384,768]{1,0:T(8,128)(2,1)}), bf16[3072,768]{1,0:T(8,128)(2,1)}) %all-gather.5.cloned.1.call-update) | async-done | bytes 4718608 | tf_op jit(solution)/shard_map/all_gather | solution.py:585
  540.7 26.6 %scatter_custom_fusion = f32[4001,768]{1,0:T(8,128)} fusion(s32[3072]{0:T(1024)S(1)} %bitcast.245, bf16[3072,768]{1,0:T(8,128)(2,1)} %all-gather.5.cloned.1.call-done, f32[]{:T(128)} %constant.61.clone.1), kind=kCustom, calls=%fused_computation.13 | custom fusion | flops 4718592 | bytes 17009668 | tf_op jit(solution)/shard_map/scatter-add | solution.py:587
  567.4 7.7 slice.515
  579.3 15.3 %pad_maximum_fusion = bf16[32,384,768]{2,1,0:T(8,128)(2,1)} fusion(bf16[32,96,768]{2,1,0:T(8,128)(2,1)} %bitcast.221, bf16[32,192,768]{2,1,0:T(8,128)(2,1)} %bitcast.193, bf16[32,24,768]{2,1,0:T(8,128)(2,1)S(1)} %bitcast.227, bf16[32,72,768]{2,1,0:T(8,128)(2,1)S(1)} %bitcast.222), kind=kLoop, calls=%fused_computation.2 | loop fusion | flops 75497472 | bytes 37748736 | tf_op jit(solution)/shard_map/concatenate | solution.py:578
  600.1 91.1 %all-reduce.3.cloned.1.call-done = bf16[4000,768]{1,0:T(8,128)(2,1)} async-done(((bf16[4000,768]{1,0:T(8,128)(2,1)}), bf16[4000,768]{1,0:T(8,128)(2,1)}) %all-reduce.3.cloned.1.call-update) | async-done | bytes 6144016 | tf_op jit(solution)/shard_map/psum | solution.py:590
  691.2 6.6 fusion.2
  698.4 207.0 %reduce-scatter.3.cloned.1.call-done = bf16[1,384,768]{2,1,0:T(8,128)(2,1)} async-done(((bf16[32,384,768]{2,1,0:T(8,128)(2,1)}), bf16[1,384,768]{2,1,0:T(8,128)(2,1)}) %reduce-scatter.3.cloned.1.call-update) | async-done | bytes 589840 | tf_op jit(solution)/shard_map/reduce_scatter | solution.py:581
  905.4 2.0 fusion.62
  908.0 39.4 %all-reduce = (f32[2305]{0:T(1024)S(1)}, f32[]{:T(128)}) all-reduce(f32[2305]{0:T(1024)S(1)} %pad_maximum_fusion.17, f32[]{:T(128)S(6)} %add.363), channel_id=1, replica_groups=mesh['dp'=8,'head'=4] {'dp','head'}, use_global_device_ids=true, to_apply=%region_24.26 | all-reduce | flops 2306 | bytes 18448 | tf_op jit(solution)/shard_map/psum | solution.py:593
  951.1 2.2 fusion.67
  953.3 2.1 fusion.56
  955.4 2.0 fusion.79
  957.3 2.2 fusion.73
  959.5 2.2 add_divide_fusion.2
  966.7 2.8 fusion.173
  969.5 2.8 copy.48
  976.7 28.9 %fusion.170 = (bf16[4000,768]{1,0:T(8,128)(2,1)}, f32[4000,768]{1,0:T(8,128)}, f32[4000,768]{1,0:T(8,128)}, f32[4000,768]{1,0:T(8,128)}) fusion(f32[4000,768]{1,0:T(8,128)} %param.25, f32[]{:T(128)S(6)} %div.137, bf16[4000,768]{1,0:T(8,128)(2,1)} %all-reduce.3.cloned.1.call-done, f32[4000,768]{1,0:T(8,128)} %param.26, f32[4000,768]{1,0:T(8,128)} %param.27), kind=kLoop, calls=%fused_computation.340 | loop fusion | flops 55296000 | bytes 86016000 | tf_op jit(solution)/shard_map/convert_element_type | solution.py:647
  (478 shorter events, 88.0 us)
Async XLA Ops:
  7.2 205.7 %copy-start = (s32[2,1,3]{2,1,0:T(1,128)S(1)}, s32[2,1,3]{2,1,0:T(1,128)}, u32[]{:S(2)}) copy-start(s32[2,1,3]{2,1,0:T(1,128)} %param.17) | copy-start | bytes 76
  7.2 286.1 %all-gather.3.cloned.1.call-start = ((), (), s32[]{:S(2)}) async-start(), calls=%async_computation.2 | async-start | bytes 6488064 | tf_op jit(solution)/shard_map/all_gather | solution.py:529
  8.9 65.4 %copy-start.33 = (f32[768,384]{0,1:T(8,128)}, f32[768,384]{0,1:T(8,128)S(1)}, u32[]{:S(2)}) copy-start(f32[768,384]{0,1:T(8,128)S(1)} %copy.41) | copy-start | bytes 3538948
  53.9 20.5 %copy-start.94 = (s32[2,4096]{1,0:T(2,128)}, s32[2,4096]{1,0:T(2,128)S(1)}, u32[]{:S(2)}) copy-start(s32[2,4096]{1,0:T(2,128)S(1)} %all_gather.9) | copy-start | bytes 98308
  54.6 19.7 %copy-start.101 = (s32[8,1,128]{2,1,0:T(1,128)}, s32[8,1,128]{2,1,0:T(1,128)S(1)}, u32[]{:S(2)}) copy-start(s32[8,1,128]{2,1,0:T(1,128)S(1)} %get-tuple-element.167) | copy-start | bytes 12292
  55.2 19.1 %copy-start.100 = (s32[8,256]{1,0:T(8,128)}, s32[8,256]{1,0:T(8,128)S(1)}, u32[]{:S(2)}) copy-start(s32[8,256]{1,0:T(8,128)S(1)} %get-tuple-element.123) | copy-start | bytes 24580
  204.4 254.2 %reduce-scatter.5.cloned.1.call-start = ((), (), s32[]{:S(2)}) async-start(), calls=%async_computation.4 | async-start | bytes 6488064 | tf_op jit(solution)/shard_map/reduce_scatter | solution.py:564
  208.4 49.8 %copy-start.4 = (bf16[32,72,768]{2,1,0:T(8,128)(2,1)}, bf16[32,72,768]{2,1,0:T(8,128)(2,1)S(1)}, u32[]{:S(2)}) copy-start(bf16[32,72,768]{2,1,0:T(8,128)(2,1)S(1)} %slice.238) | copy-start | bytes 10616836
  216.7 6.7 copy-start.59
  219.5 4.9 copy-start.78
  219.5 4.9 copy-start.92
  224.4 12.5 %collective-permute-start = (bf16[256,24,64]{0,2,1:T(8,128)(2,1)}, bf16[256,24,64]{0,2,1:T(8,128)(2,1)}, u32[]{:S(2)}, u32[]{:S(2)}) collective-permute-start(bf16[256,24,64]{0,2,1:T(8,128)(2,1)} %pad_maximum_fusion.11), channel_id=1, source_target_pairs={{0,1},{1,0},{2,3},{3,2},{4,5},{5,4},{6,7},{7,6},{8,9},{9,8},{10,11... | collective-permute-start | bytes 2359304 | tf_op jit(solution)/shard_map/ppermute | solution.py:112
  228.1 35.0 %collective-permute-start.2 = (bf16[128,4096]{1,0:T(8,128)(2,1)}, bf16[128,4096]{1,0:T(8,128)(2,1)}, u32[]{:S(2)}, u32[]{:S(2)}) collective-permute-start(bf16[128,4096]{1,0:T(8,128)(2,1)} %get-tuple-element.90), channel_id=1, source_target_pairs={{0,2},{1,3},{2,0},{3,1},{4,6},{5,7},{6,4},{7,5},{8,10},{9,11},{10,... | collective-permute-start | bytes 3145736 | tf_op jit(solution)/shard_map/ppermute | solution.py:112
  237.0 5.0 copy-start.31
  241.9 5.9 slice-start.4
  242.6 5.3 slice-start.5
  242.6 5.2 slice-start.6
  247.2 6.0 copy-start.13
  259.6 7.9 copy-start.62
  261.7 5.7 copy-start.68
  261.8 5.7 collective-permute-start.1
  264.7 5.7 copy-start.120
  270.5 7.7 slice-start.7
  278.1 34.5 %copy-start.16 = (f32[256,768]{1,0:T(8,128)}, f32[256,768]{1,0:T(8,128)S(1)}, u32[]{:S(2)}) copy-start(f32[256,768]{1,0:T(8,128)S(1)} %get-tuple-element.149) | copy-start | bytes 2359300
  278.1 34.5 %copy-start.108 = (f32[256]{0:T(256)}, f32[256]{0:T(256)S(1)}, u32[]{:S(2)}) copy-start(f32[256]{0:T(256)S(1)} %get-tuple-element.132) | copy-start | bytes 3076
  283.6 5.2 copy-start.35
  288.8 17.4 %copy-start.122 = (f32[256]{0:T(256)}, f32[256]{0:T(256)S(1)}, u32[]{:S(2)}) copy-start(f32[256]{0:T(256)S(1)} %get-tuple-element.134) | copy-start | bytes 3076
  298.3 5.2 copy-start.138
  299.1 7.3 slice-start.21
  299.1 7.3 slice-start.24
  303.6 5.3 slice-start.10
  303.6 5.3 slice-start.11
  306.4 6.2 copy-start.43
  313.8 7.8 slice-start.2
  326.8 8.0 copy-start.53
  328.0 6.8 collective-permute-start.3
  334.8 205.9 %all-gather.5.cloned.1.call-start = ((), (), s32[]{:S(2)}) async-start(), calls=%async_computation.5 | async-start | bytes 5308416 | tf_op jit(solution)/shard_map/all_gather | solution.py:585
  335.8 9.1 slice-start.19
  337.8 7.2 slice-start.20
  342.8 7.0 slice-start.13
  345.0 8.3 copy-start.45
  345.0 4.9 slice-start.14
  345.0 4.9 slice-start.15
  345.0 4.9 copy-start.14
  345.0 4.9 copy-start.111
  353.3 8.4 slice-start
  356.9 4.9 slice-start.1
  356.9 4.9 copy-start.48
  356.9 4.9 copy-start.97
  366.9 2.4 collective-permute-start.4
  376.5 83.9 %copy-start.102 = (s32[8,1,128]{2,1,0:T(1,128)S(1)}, s32[8,1,128]{2,1,0:T(1,128)}, u32[]{:S(2)}) copy-start(s32[8,1,128]{2,1,0:T(1,128)} %copy-done.101) | copy-start | bytes 12292
  376.5 84.8 %copy-start.26 = (f32[256,768]{1,0:T(8,128)S(1)}, f32[256,768]{1,0:T(8,128)}, u32[]{:S(2)}) copy-start(f32[256,768]{1,0:T(8,128)} %copy-done.24) | copy-start | bytes 2359300
  376.8 86.0 %copy-start.36 = (bf16[256,3072]{1,0:T(8,128)(2,1)S(1)}, bf16[256,3072]{1,0:T(8,128)(2,1)}, u32[]{:S(2)}) copy-start(bf16[256,3072]{1,0:T(8,128)(2,1)} %copy-done.35) | copy-start | bytes 4718596
  460.4 230.8 %all-reduce.3.cloned.1.call-start = ((), (), s32[]{:S(2)}) async-start(), calls=%async_computation.6 | async-start | bytes 12288000 | tf_op jit(solution)/shard_map/psum | solution.py:590
  464.9 8.7 copy-start.85
  575.2 330.2 %reduce-scatter.3.cloned.1.call-start = ((), (), s32[]{:S(2)}) async-start(), calls=%async_computation.3 | async-start | bytes 19464192 | tf_op jit(solution)/shard_map/reduce_scatter | solution.py:581
  594.7 4.7 copy-start.132
  594.7 4.7 copy-start.134
  594.7 4.7 copy-start.131
  691.1 270.5 %slice-start.16 = ((s8[9437184]{0:T(1024)(128)(4,1)}), s8[1048576]{0:T(1024)(128)(4,1)S(1)}, s32[]{:S(2)}) async-start(s8[9437184]{0:T(1024)(128)(4,1)} %bitcast.210), calls=%async_computation.23 | async-start | bytes 2097152
  951.1 10.6 %slice-start.17 = ((s8[9437184]{0:T(1024)(128)(4,1)}), s8[4194304]{0:T(1024)(128)(4,1)S(1)}, s32[]{:S(2)}) async-start(s8[9437184]{0:T(1024)(128)(4,1)} %bitcast.210), calls=%async_computation.24 | async-start | bytes 8388608
  966.7 5.6 copy-start.58
  969.4 5.6 copy-start.77
  976.7 28.9 %copy-start.1 = (s32[2,1,3]{2,1,0:T(1,128)S(1)}, s32[2,1,3]{2,1,0:T(1,128)}, u32[]{:S(2)}) copy-start(s32[2,1,3]{2,1,0:T(1,128)} %param.17) | copy-start | bytes 76
  (111 other events, 300.9 us)
Sparse Core Ops, SparseCore 0:
  204.5 88.7 all-gather.2
  334.9 123.6 reduce-scatter.4
  461.6 79.0 all-gather.4
  575.3 115.8 all-reduce.2
  698.5 206.8 reduce-scatter.2

commit v3 on v2

--- a/solution.py
+++ b/solution.py
@@ -460,6 +460,437 @@
     )(*pieces, rows)
 
 
+def by_distance(depth, z, act):
+    for step in range(depth - 1, -1, -1):
+        for sign in (1, -1) if step else (1,):
+
+            @pl.when((z + sign * step >= 0) & (z + sign * step < depth))
+            def reached():
+                act(z + sign * step)
+
+
+def add_into(total, block, *terms):
+    height = total.shape[1]
+    chunk = 96 if height % 96 == 0 else height
+
+    @pl.loop(0, height // chunk)
+    def chunks(index):
+        part = pl.ds(pl.multiple_of(index * chunk, chunk), chunk)
+        value = total[block, part].astype(jnp.float32)
+        for buffer, place in terms:
+            value = value + buffer[place, part].astype(jnp.float32)
+        total[block, part] = value.astype(low)
+
+
+def end_kernel(depth, heights, *refs):
+    pieces, rows_ref, grad_ref, rows_out = refs[0:3], refs[3], refs[4], refs[5]
+    total, far_c, far_y, far_x, from_low, from_high = refs[6:12]
+    local_sem, c_send, c_recv, y_send, y_recv, x_send, x_recv = refs[12:19]
+    u_send, u_recv, d_send, d_recv = refs[19:23]
+    own_sem, ru_send, rd_send, rx_send, r_recv = refs[23:28]
+    z, x, y, c = coordinates(depth)
+    greet(depth, z, x, y, c)
+    firsts = [sum(heights[:index]) for index in range(3)]
+    up, down = device(z + 1, x, y, c), device(z - 1, x, y, c)
+    across_x, across_y, across_c = (
+        device(z, 1 - x, y, c),
+        device(z, x, 1 - y, c),
+        device(z, x, y, 1 - c),
+    )
+
+    def remote(source, goal, send_sem, recv_sem, target):
+        return pltpu.make_async_remote_copy(
+            source, goal, send_sem, recv_sem, device_id=target, device_id_type=MESH
+        )
+
+    def local(block, piece):
+        return pltpu.make_async_copy(
+            pieces[piece].at[block * 2 + c],
+            total.at[block, pl.ds(firsts[piece], heights[piece])],
+            local_sem.at[block, piece],
+        )
+
+    def over_c(block, piece):
+        return remote(
+            pieces[piece].at[block * 2 + 1 - c],
+            far_c.at[block, pl.ds(firsts[piece], heights[piece])],
+            c_send.at[block, piece],
+            c_recv.at[block, piece],
+            across_c,
+        )
+
+    def over_y(place, side):
+        pair = place * 2 + side
+        return remote(
+            total.at[pair * 2 + 1 - y], far_y.at[pair], y_send.at[pair], y_recv.at[pair], across_y
+        )
+
+    def over_x(place):
+        return remote(
+            total.at[(place * 2 + 1 - x) * 2 + y],
+            far_x.at[place],
+            x_send.at[place],
+            x_recv.at[place],
+            across_x,
+        )
+
+    def rise(place):
+        block = (place * 2 + x) * 2 + y
+        return remote(
+            total.at[block], from_low.at[place], u_send.at[place], u_recv.at[place], up
+        )
+
+    def fall(place):
+        block = (place * 2 + x) * 2 + y
+        return remote(
+            total.at[block], from_high.at[place], d_send.at[place], d_recv.at[place], down
+        )
+
+    def own_rows(send_sem, target):
+        mine = z * 2 + x
+        return remote(rows_ref, rows_out.at[mine], send_sem, r_recv.at[mine], target)
+
+    def rows_on(place, send_sem, target):
+        there = place * 2 + x
+        return remote(rows_out.at[there], rows_out.at[there], send_sem, r_recv.at[there], target)
+
+    own = pltpu.make_async_copy(rows_ref, rows_out.at[z * 2 + x], own_sem)
+    own.start()
+
+    @pl.when(z < depth - 1)
+    def first_up():
+        own_rows(ru_send.at[0], up).start()
+
+    @pl.when(z > 0)
+    def first_down():
+        own_rows(rd_send.at[0], down).start()
+
+    own_rows(rx_send.at[z], across_x).start()
+    for turn in range(2):
+        for side in (1 - x, x):
+
+            def launch(place):
+                block = (place * 2 + side) * 2 + (1 - y if turn == 0 else y)
+                for piece in range(3):
+                    over_c(block, piece).start()
+                    local(block, piece).start()
+
+            by_distance(depth, z, launch)
+
+    def ready(block):
+        for piece in range(3):
+            local(block, piece).wait()
+            over_c(block, piece).wait_recv()
+
+    for side in (1 - x, x):
+
+        def give_y(place):
+            block = (place * 2 + side) * 2 + 1 - y
+            ready(block)
+            add_into(total, block, (far_c, block))
+            over_y(place, side).start()
+
+        by_distance(depth, z, give_y)
+
+    def rows_step(step):
+        @pl.when(z - step >= 0)
+        def risen():
+            rows_on(z - step, ru_send.at[step], up).wait_recv()
+
+            @pl.when(z < depth - 1)
+            def further():
+                rows_on(z - step, ru_send.at[step], up).start()
+
+            rows_on(z - step, rx_send.at[z - step], across_x).start()
+
+        @pl.when(z + step < depth)
+        def fallen():
+            rows_on(z + step, rd_send.at[step], down).wait_recv()
+
+            @pl.when(z > 0)
+            def further():
+                rows_on(z + step, rd_send.at[step], down).start()
+
+            rows_on(z + step, rx_send.at[z + step], across_x).start()
+
+    def give_x(place):
+        block = (place * 2 + 1 - x) * 2 + y
+        ready(block)
+        over_y(place, 1 - x).wait_recv()
+        add_into(total, block, (far_c, block), (far_y, place * 2 + 1 - x))
+        over_x(place).start()
+
+    for step in range(depth - 1, -1, -1):
+        if step:
+            rows_step(depth - step)
+        for sign in (1, -1) if step else (1,):
+
+            @pl.when((z + sign * step >= 0) & (z + sign * step < depth))
+            def reached():
+                give_x(z + sign * step)
+
+    def give_z(place):
+        block = (place * 2 + x) * 2 + y
+        pair = place * 2 + x
+        ready(block)
+        over_y(place, x).wait_recv()
+        over_x(place).wait_recv()
+        add_into(total, block, (far_c, block), (far_y, pair), (far_x, place))
+
+        @pl.when(place > z)
+        def rising():
+            @pl.when(z > 0)
+            def more():
+                rise(place).wait_recv()
+                add_into(total, block, (from_low, place))
+
+            rise(place).start()
+
+        @pl.when(place < z)
+        def falling():
+            @pl.when(z < depth - 1)
+            def more():
+                fall(place).wait_recv()
+                add_into(total, block, (from_high, place))
+
+            fall(place).start()
+
+    by_distance(depth, z, give_z)
+    mine = (z * 2 + x) * 2 + y
+    grad_ref[...] = total[mine].astype(jnp.float32)
+
+    @pl.when(z > 0)
+    def low_part():
+        rise(z).wait_recv()
+        grad_ref[...] = grad_ref[...] + from_low[z].astype(jnp.float32)
+
+    @pl.when(z < depth - 1)
+    def high_part():
+        fall(z).wait_recv()
+        grad_ref[...] = grad_ref[...] + from_high[z].astype(jnp.float32)
+
+    own.wait()
+    for place in range(depth):
+        there = place * 2 + 1 - x
+        remote(
+            rows_out.at[there], rows_out.at[there], rx_send.at[place], r_recv.at[there], across_x
+        ).wait_recv()
+        rows_on(place, rx_send.at[place], across_x).wait_send()
+        over_x(place).wait_send()
+        for side in range(2):
+            over_y(place, side).wait_send()
+            for rank in range(2):
+                for piece in range(3):
+                    over_c((place * 2 + side) * 2 + rank, piece).wait_send()
+
+        @pl.when(place > z)
+        def rose():
+            rise(place).wait_send()
+
+        @pl.when(place < z)
+        def fell():
+            fall(place).wait_send()
+
+        @pl.when((z - place >= 0) & (z < depth - 1))
+        def rows_rose():
+            rows_on(z, ru_send.at[place], up).wait_send()
+
+        @pl.when((z + place < depth) & (z > 0))
+        def rows_fell():
+            rows_on(z, rd_send.at[place], down).wait_send()
+
+
+def end(pieces, rows):
+    blocks = pieces[0].shape[0]
+    heights = [piece.shape[1] for piece in pieces]
+    height, width = sum(heights), pieces[0].shape[2]
+    depth = blocks // 8
+    dma = pltpu.SemaphoreType.DMA
+
+    def buffer(count):
+        return pltpu.VMEM((count, height, width), low)
+
+    return pl.pallas_call(
+        functools.partial(end_kernel, depth, heights),
+        out_shape=[
+            jax.ShapeDtypeStruct((height, width), jnp.float32),
+            jax.ShapeDtypeStruct((depth * 2,) + rows.shape, low),
+        ],
+        in_specs=[ANY] * 4,
+        out_specs=[pl.BlockSpec(memory_space=pltpu.VMEM), ANY],
+        scratch_shapes=[buffer(depth * 4), buffer(depth * 4), buffer(depth * 2)]
+        + [buffer(depth)] * 3
+        + [dma((depth * 4, 3))] * 3
+        + [dma((depth * 2,))] * 2
+        + [dma((depth,))] * 6
+        + [dma(())]
+        + [dma((depth,))] * 3
+        + [dma((depth * 2,))],
+        compiler_params=pltpu.CompilerParams(
+            collective_id=1, has_side_effects=True, vmem_limit_bytes=58 * 2**20
+        ),
+        name="end",
+    )(*pieces, rows)
+
+
+def collect_kernel(step, places_ref, rows_ref, table_ref):
+    base = pl.program_id(0) * step
+    at = base + lax.broadcasted_iota(jnp.int32, (step, places_ref.shape[1]), 0)
+    picked = jnp.where(at == places_ref[...], 1.0, 0.0).astype(low)
+    table_ref[...] = product(picked, rows_ref[...]).astype(low)
+
+
+def collect(places, rows, height, step):
+    count, width = rows.shape
+    return pl.pallas_call(
+        functools.partial(collect_kernel, step),
+        grid=(height // step,),
+        out_shape=jax.ShapeDtypeStruct((height, width), low),
+        in_specs=[
+            pl.BlockSpec((1, count), lambda i: (0, 0)),
+            pl.BlockSpec((count, width), lambda i: (0, 0)),
+        ],
+        out_specs=pl.BlockSpec((step, width), lambda i: (i, 0)),
+        compiler_params=pltpu.CompilerParams(vmem_limit_bytes=58 * 2**20),
+        cost_estimate=pl.CostEstimate(
+            flops=2 * count * width * height,
+            bytes_accessed=2 * width * (count + height),
+            transcendentals=0,
+        ),
+        name="collect",
+    )(places, rows)
+
+
+def share_kernel(depth, table_ref, small_ref, table_out, small_out, *refs):
+    far_c, part, far_y, small, far_small = refs[0:5]
+    c_send, c_recv, y_send, y_recv, o_send, o_recv, s_send, s_recv = refs[5:13]
+    z, x, y, c = coordinates(depth)
+    partners = [device(z, x, y, 1 - c), device(z, x, 1 - y, c), device(z, 1 - x, y, c)]
+    reach = 1
+    while reach < depth:
+        partners.append(device(z ^ reach, x, y, c))
+        reach = reach * 2
+    barrier = pltpu.get_barrier_semaphore()
+    for target in partners:
+        pl.semaphore_signal(barrier, 1, device_id=target, device_id_type=MESH)
+    pl.semaphore_wait(barrier, len(partners))
+    across_c, across_y = partners[:2]
+
+    def remote(source, goal, send_sem, recv_sem, target):
+        return pltpu.make_async_remote_copy(
+            source, goal, send_sem, recv_sem, device_id=target, device_id_type=MESH
+        )
+
+    def over_c(rank):
+        return remote(
+            table_ref.at[rank * 2 + 1 - c],
+            far_c.at[rank],
+            c_send.at[rank],
+            c_recv.at[rank],
+            across_c,
+        )
+
+    def out(rank, core, index, target):
+        where = table_out.at[rank * 2 + core]
+        return remote(where, where, o_send.at[index], o_recv.at[rank * 2 + core], target)
+
+    height = part.shape[0]
+    chunk = 80 if height % 80 == 0 else height
+    over_c(1 - y).start()
+    over_c(y).start()
+    over_c(1 - y).wait_recv()
+
+    @pl.loop(0, height // chunk)
+    def first_sum(index):
+        rows = pl.ds(pl.multiple_of(index * chunk, chunk), chunk)
+        part[rows] = (
+            table_ref[(1 - y) * 2 + c, rows].astype(jnp.float32)
+            + far_c[1 - y, rows].astype(jnp.float32)
+        ).astype(low)
+
+    over_y = remote(part, far_y, y_send, y_recv, across_y)
+    over_y.start()
+    over_c(y).wait_recv()
+    over_y.wait_recv()
+    mine = y * 2 + c
+
+    def second_sum(index, squares):
+        rows = pl.ds(pl.multiple_of(index * chunk, chunk), chunk)
+        value = (
+            table_ref[mine, rows].astype(jnp.float32)
+            + far_c[y, rows].astype(jnp.float32)
+            + far_y[rows].astype(jnp.float32)
+        ).astype(low)
+        table_out[mine, rows] = value
+        value = value.astype(jnp.float32)
+        return squares + jnp.sum((value * value).reshape(-1, 8, 768), axis=0)
+
+    squares = lax.fori_loop(0, height // chunk, second_sum, jnp.zeros((8, 768), jnp.float32))
+    out(y, c, 0, across_y).start()
+    out(y, c, 1, across_c).start()
+    lines = lax.broadcasted_iota(jnp.int32, small.shape[1:], 0)
+    lanes = lax.broadcasted_iota(jnp.int32, small.shape[1:], 1)
+    last = (lines == small.shape[1] - 1) & (lanes == 0)
+    small[0] = small_ref[...] + jnp.where(last, jnp.sum(squares), 0.0)
+    for turn, target in enumerate(partners):
+        copy = remote(
+            small.at[turn], far_small.at[turn], s_send.at[turn], s_recv.at[turn], target
+        )
+        copy.start()
+        copy.wait_recv()
+        small[turn + 1] = small[turn] + far_small[turn]
+    small_out[...] = small[len(partners)]
+    out(1 - y, c, 0, across_y).wait_recv()
+    out(1 - y, c, 2, across_c).start()
+    out(y, 1 - c, 1, across_c).wait_recv()
+    out(1 - y, 1 - c, 2, across_c).wait_recv()
+    for turn, target in enumerate(partners):
+        remote(
+            small.at[turn], far_small.at[turn], s_send.at[turn], s_recv.at[turn], target
+        ).wait_send()
+    over_y.wait_send()
+    for rank in range(2):
+        over_c(rank).wait_send()
+    out(y, c, 0, across_y).wait_send()
+    out(y, c, 1, across_c).wait_send()
+    out(1 - y, c, 2, across_c).wait_send()
+
+
+def share(depth, table, small):
+    quarters, height, width = table.shape
+    turns = 3 + (depth - 1).bit_length()
+    dma = pltpu.SemaphoreType.DMA
+    vmem = pl.BlockSpec(memory_space=pltpu.VMEM)
+    return pl.pallas_call(
+        functools.partial(share_kernel, depth),
+        out_shape=[
+            jax.ShapeDtypeStruct(table.shape, low),
+            jax.ShapeDtypeStruct(small.shape, jnp.float32),
+        ],
+        in_specs=[vmem, vmem],
+        out_specs=[vmem, vmem],
+        scratch_shapes=[
+            pltpu.VMEM((2, height, width), low),
+            pltpu.VMEM((height, width), low),
+            pltpu.VMEM((height, width), low),
+            pltpu.VMEM((turns + 1,) + small.shape, jnp.float32),
+            pltpu.VMEM((turns,) + small.shape, jnp.float32),
+            dma((2,)),
+            dma((2,)),
+            dma(()),
+            dma(()),
+            dma((3,)),
+            dma((4,)),
+            dma((turns,)),
+            dma((turns,)),
+        ],
+        compiler_params=pltpu.CompilerParams(
+            collective_id=2, has_side_effects=True, vmem_limit_bytes=58 * 2**20
+        ),
+        name="share",
+    )(table, small)
+
+
 def adam_step(weight, gradient, first, second, rate, decay):
     first_new = beta_one * first + (1.0 - beta_one) * gradient
     second_new = beta_two * second + (1.0 - beta_two) * gradient * gradient
@@ -575,30 +1006,36 @@
         else:
             block_grads = [total + extra for total, extra in zip(block_grads, layer_grads)]
 
-    joined = jnp.concatenate(
-        [piece.astype(low).reshape(device_total, -1, D) for piece in block_grads], axis=1
-    )
-    block_grads = lax.psum_scatter(joined, ("dp", "head"), scatter_dimension=0, tiled=True)
-    block_grads = block_grads.reshape(-1, D).astype(jnp.float32).T
-
+    d_qkv, d_out, d_gu, d_down = [
+        piece.astype(low).reshape(device_total, -1, D) for piece in block_grads
+    ]
     rows_back = jnp.concatenate([chosen_grads, gradient.astype(low)], axis=0)
-    rows_back = lax.all_gather(rows_back, "dp", axis=0, tiled=True)
-    dump_index = jnp.where(owned, local, shard_rows).reshape(-1)
-    table_grads = jax.ops.segment_sum(
-        rows_back.astype(jnp.float32), dump_index, num_segments=shard_rows + 1
-    )[:shard_rows]
-    table_grads = lax.psum(table_grads.astype(low), "head").astype(jnp.float32)
-
+    block_grads, rows_back = end(
+        [jnp.concatenate([d_qkv, d_out], axis=1), d_gu, d_down], rows_back
+    )
+    block_grads = block_grads.T
+
+    step = 80 if shard_rows % 80 == 0 else 40
+    quarter = -(-shard_rows // (step * head_count)) * step
+    tile = quarter // 5 if quarter % 80 == 0 and quarter // 5 % 16 == 0 else step
+    table_grads = collect(
+        jnp.where(owned, local, -1).reshape(1, -1),
+        rows_back.reshape(-1, D),
+        quarter * head_count,
+        tile,
+    )
+    squares = jnp.sum(block_grads * block_grads)
     small = jnp.concatenate([d_gains[0], d_gains[1], d_gain_final, loss_sum[None]])
-    small = lax.psum(small, ("dp", "head"))
+    small = jnp.pad(small, (0, 6 * 128 - 1)).reshape(-1, 128)
+    small = small.at[-1, 0].set(squares)
+    table_grads, small = share(
+        dp_count // 2, table_grads.reshape(head_count, quarter, D), small
+    )
+    table_grads = table_grads.reshape(-1, D)[:shard_rows].astype(jnp.float32)
+    squares = small[-1, 0]
+    small = small.reshape(-1)
     gain_grads = small[: 3 * D].reshape(3, D) / count
     loss = small[3 * D] / count
-
-    squares = lax.psum(
-        jnp.sum(block_grads * block_grads)
-        + jnp.where(head == 0, jnp.sum(table_grads * table_grads), 0.0),
-        ("dp", "head"),
-    )
     grad_norm = jnp.sqrt(squares / (count * count) + jnp.sum(gain_grads * gain_grads))
     clip = jnp.minimum(1.0, clip_norm / grad_norm)
     factor = clip / count

time: 1020 us -> 798 us (0.78)
  waiting for transfers between devices: 437 us -> 46.6 us
  Pallas kernels: 123 us -> 362 us
  other arithmetic: 143 us -> 97.6 us
  blocking collectives: 82.6 us -> 43.3 us
    pallas_call x0 -> x3, Pallas kernels: none -> 240 us  [the longest x1 115 us: end(): pl.pallas_call(functools.partial(end_kernel, depth, heights), out_shape=[...]
    reduce_scatter x1 -> x0, waiting for transfers between devices: 207 us -> none  [on_device(): lax.psum_scatter(joined, ('dp', 'head'), scatter_dimension=0, tiled=True)]
    psum x1 -> x0, waiting for transfers between devices: 91.1 us -> none  [on_device(): table_grads = lax.psum(table_grads.astype(low), 'head').astype(jnp.float32)]
    reduce_scatter x1, waiting for transfers between devices: 81.8 us -> 31.4 us  [on_device(): lax.psum_scatter(chosen_grads, ('dp', 'head'), scatter_dimension=0, tiled...]
    all_gather x1 -> x0, waiting for transfers between devices: 50.3 us -> none  [on_device(): rows_back = lax.all_gather(rows_back, 'dp', axis=0, tiled=True)]
    psum x1 -> x0, blocking collectives: 39.4 us -> none  [on_device(): small = lax.psum(small, ('dp', 'head'))]
    scatter-add x1 -> x0, other arithmetic: 26.6 us -> none  [on_device(): jax.ops.segment_sum(rows_back.astype(jnp.float32), dump_index, num_segmen...]
    dot_general x13, matrix products: 43.4 us -> 56.9 us  [contract_rows(): lax.dot_general(left, right, (((0,), (0,)), ((), ())), preferred_element_...]
  transfers between devices with their start and end apart: 10 -> 7, of which waited for: 6 -> 2; matrix products, arithmetic and copies ran while one was open for 16% -> 17% of each run, Pallas kernels for 0% -> 0%
where the time goes in v3:
time: 798 us; the launch traced here: 788 us
  Pallas kernels  362 us (45%)
  matrix products  134 us (17%)
  other arithmetic  97.6 us (12%)
  local copies, waits for them, and re-layouts  75.8 us (9%)
  waiting for transfers between devices  46.6 us (6%)
  blocking collectives  43.3 us (5%)
  between operations  23 us (3%)
    pallas_call x1, Pallas kernels, start(): pl.pallas_call(functools.partial(start_kernel, depth), out_shape=[jax.Sha...  123 us
    pallas_call x1, Pallas kernels, end(): pl.pallas_call(functools.partial(end_kernel, depth, heights), out_shape=[...  115 us
    pallas_call x1, Pallas kernels, share(): pl.pallas_call(functools.partial(share_kernel, depth), out_shape=[jax.Sha...  97.5 us
    dot_general x13, matrix products, contract_rows(): lax.dot_general(left, right, (((0,), (0,)), ((), ())), preferred_element_...  56.9 us
    all_gather x1, blocking collectives, on_device(): lax.all_gather(token_ids * 2 + valid, ('dp', 'head'), axis=1, tiled=True)  43.3 us
    unnamed x328, local copies, waits for them, and re-layouts  34.2 us
    reduce_scatter x1, waiting for transfers between devices, on_device(): lax.psum_scatter(chosen_grads, ('dp', 'head'), scatter_dimension=0, tiled...  31.4 us
    convert_element_type x1, other arithmetic, on_device(): table_new.astype(low)  28.9 us
  transfers between devices with their start and end apart: 7, of which 2 were waited for; matrix products, arithmetic and copies ran while one was open for 17% of the time, Pallas kernels for 0%

profile of v3, /device:TPU:0, one launch (start us, length us, event | category | flops | bytes accessed | tf_op | source)
XLA Modules:
  0.0 788.2 jit_solution(6101793284625646795)
XLA Ops:
  11.1 43.3 %all_gather.6 = s32[2,4096]{1,0:T(2,128)S(1)} all-gather(s32[2,128]{1,0:T(2,128)S(1)} %multiply_add_fusion.3), channel_id=1, replica_groups=mesh['dp'=8,'head'=4] {'dp','head'}, dimensions={1}, use_global_device_ids=true | all-gather | bytes 33792 | tf_op jit(solution)/shard_map/all_gather | solution.py:931
  55.8 19.0 %gather_fusion = bf16[3072,768]{1,0:T(8,128)(2,1)} fusion(f32[4000,768]{1,0:T(8,128)} %param.27, s32[3072]{0:T(1024)S(1)} %broadcast_clamp_fusion), kind=kCustom, calls=%fused_computation | custom fusion | bytes 9449472 | tf_op jit(solution)/shard_map/gather | solution.py:946
  74.9 5.8 select_convert_fusion.refs_3_
  80.7 122.5 %start.1 = (bf16[32,96,768]{2,1,0:T(8,128)(2,1)}, bf16[32,192,768]{2,1,0:T(8,128)(2,1)}, bf16[32,96,768]{2,1,0:T(8,128)(2,1)}, bf16[384,768]{1,0:T(8,128)(2,1)}) custom-call(bf16[96,768]{1,0:T(8,128)(2,1)} %get-tuple-element.130.refs_0_, bf16[192,768]{1,0:T(8,128)(2,1)} %slice.328.refs_1_, bf16[96,768]{1,0:T(8,128)(2,1)} %get-tuple-element.129.refs_2_, ...), custom_call_target="tpu_custom_call" | custom-call | tf_op jit(solution)/shard_map/start/pallas_call | solution.py:445
  203.3 2.3 slice.260
  215.0 2.0 pad_add_fusion.3
  219.1 2.7 fusion.98
  225.1 3.1 dynamic-slice_bitcast_fusion.1
  228.1 4.2 collective-permute-start.2
  233.6 2.4 slice.272
  239.4 2.7 copy.44
  242.0 2.7 copy.45
  250.5 2.2 exponential_reduce_fusion.1
  253.2 3.1 convolution_convert_fusion.2
  258.3 3.8 fusion.159
  263.1 1.7 copy-done.9
  264.8 4.5 multiply_reduce_fusion.13
  275.1 2.1 fusion.12
  278.7 2.0 exponential_reduce_fusion
  281.4 1.7 convolution_convert_fusion.1
  284.5 2.7 fusion.161
  288.1 1.7 copy-done.10
  289.8 4.4 multiply_reduce_fusion.11
  294.9 15.2 %all-gather.2.cloned.1.call-done = bf16[4096,768]{1,0:T(8,128)(2,1)} async-done(((bf16[128,768]{1,0:T(8,128)(2,1)}), bf16[4096,768]{1,0:T(8,128)(2,1)}) %all-gather.2.cloned.1.call-update) | async-done | bytes 6291472 | tf_op jit(solution)/shard_map/all_gather | solution.py:960
  310.2 4.7 fusion.175
  315.7 4.2 fusion.11
  319.9 2.6 multiply_reduce_fusion.3
  322.8 2.4 multiply_convert_fusion.5
  326.4 3.4 multiply_reduce_fusion.5
  332.4 1.9 copy.42
  334.4 4.6 convolution_bitcast_fusion.1
  339.0 2.4 multiply_reduce_fusion.1
  342.3 1.8 multiply_convert_fusion.1
  347.6 8.5 %fusion.40 = f32[6144,768]{1,0:T(8,128)} fusion(bf16[256,3072]{1,0:T(8,128)(2,1)S(1)} %copy-done.82, bf16[256,3072]{1,0:T(8,128)(2,1)S(1)} %copy-done.80, f32[256,768]{1,0:T(8,128)S(1)} %copy-done.17, f32[256]{0:T(256)S(1)} %get-tuple-element.150, f32[768]{0:T(1024)S(1)} %get-tuple-element.79), kind=kOutput, calls=%fused_computation.80 | convolution fusion | flops 2422800384 | bytes 22810624 | tf_op jit(solution)/shard_map/dot_general | solution.py:36
  356.2 4.6 convolution_convert_fusion
  363.1 1.9 fusion.122
  365.0 5.5 fusion.125
  374.8 2.0 copy-done.5
  376.9 1.9 multiply_reduce_fusion.6
  379.2 4.9 multiply_convert_fusion.3
  384.2 3.4 multiply_reduce_fusion.4
  391.2 4.5 convolution_bitcast_fusion
  396.1 2.4 multiply_reduce_fusion
  398.6 1.8 multiply_convert_fusion
  403.4 4.1 fusion.160
  407.6 12.5 %add_convert_fusion = bf16[6144,768]{1,0:T(8,128)(2,1)} fusion(f32[6144,768]{1,0:T(8,128)} %fusion.40, bf16[256,3072]{1,0:T(8,128)(2,1)} %copy-done.89, bf16[256,3072]{1,0:T(8,128)(2,1)} %copy-done.88, f32[256,768]{1,0:T(8,128)S(1)} %copy-done.15, f32[768]{0:T(1024)S(1)} %get-tuple-element.79, f32[256]{0:T(256)S(1)} %copy-done.111), kind=kOutput, calls=%fused_computation.1 | convolution fusion | flops 2432237568 | bytes 32247808 | tf_op jit(solution)/shard_map/dot_general | solution.py:36
  420.1 2.5 add_convert_fusion.3
  422.7 7.6 add_convert_fusion.1
  432.6 2.4 broadcast_multiply_fusion
  440.6 2.8 pad_maximum_fusion.refs_0_
  443.7 31.4 %reduce-scatter.2.cloned.1.call-done = bf16[128,768]{1,0:T(8,128)(2,1)} async-done(((bf16[4096,768]{1,0:T(8,128)(2,1)}), bf16[128,768]{1,0:T(8,128)(2,1)}) %reduce-scatter.2.cloned.1.call-update) | async-done | bytes 196624 | tf_op jit(solution)/shard_map/reduce_scatter | solution.py:995
  475.1 1.8 pad_maximum_fusion.15.refs_3_
  476.8 115.2 %end.1 = (f32[384,768]{1,0:T(8,128)}, bf16[8,384,768]{2,1,0:T(8,128)(2,1)}) custom-call(bf16[32,96,768]{2,1,0:T(8,128)(2,1)} %pad_maximum_fusion.refs_0_, bf16[32,192,768]{2,1,0:T(8,128)(2,1)} %bitcast.197, bf16[32,96,768]{2,1,0:T(8,128)(2,1)} %bitcast.225, bf16[384,768]{1,0:T(8,128)(2,1)} %pad_maximum_fusion.15.refs_3_), custom_call_target="tpu_custom_call" | custom-call | tf_op jit(solution)/shard_map/end/pallas_call | solution.py:713
  592.0 2.2 multiply_reduce_fusion.2
  594.2 26.9 %collect.1 = bf16[4160,768]{1,0:T(8,128)(2,1)} custom-call(s32[1,3072]{1,0:T(1,128)} %and_select_fusion.places_ref, bf16[3072,768]{1,0:T(8,128)(2,1)} %bitcast.261), custom_call_target="tpu_custom_call" | custom-call | flops 19629342720 | bytes 11108352 | tf_op jit(solution)/shard_map/collect/pallas_call | solution.py:745
  622.4 97.5 %share.1 = (bf16[4,1040,768]{2,1,0:T(8,128)(2,1)}, f32[24,128]{1,0:T(8,128)}) custom-call(bf16[4,1040,768]{2,1,0:T(8,128)(2,1)} %bitcast.229, f32[24,128]{1,0:T(8,128)} %copy-done.102), custom_call_target="tpu_custom_call" | custom-call | tf_op jit(solution)/shard_map/share/pallas_call | solution.py:864
  723.9 2.2 fusion.59
  726.1 2.1 fusion.50
  728.2 2.1 fusion.71
  730.3 2.2 fusion.65
  732.5 1.8 add_divide_fusion.2
  739.8 2.7 fusion.165
  742.5 2.8 copy.48
  749.1 28.9 %fusion.163 = (bf16[4000,768]{1,0:T(8,128)(2,1)}, f32[4000,768]{1,0:T(8,128)}, f32[4000,768]{1,0:T(8,128)}, f32[4000,768]{1,0:T(8,128)}) fusion(f32[4000,768]{1,0:T(8,128)} %param.27, f32[]{:T(128)S(6)} %div.137, bf16[4160,768]{1,0:T(8,128)(2,1)} %bitcast.230, f32[4000,768]{1,0:T(8,128)} %param.28, f32[4000,768]{1,0:T(8,128)} %param.29), kind=kLoop, calls=%fused_computation.334 | loop fusion | flops 55296000 | bytes 86016000 | tf_op jit(solution)/shard_map/convert_element_type | solution.py:1084
  (464 shorter events, 86.7 us)
Async XLA Ops:
  7.2 203.9 %copy-start = (s32[2,1,3]{2,1,0:T(1,128)S(1)}, s32[2,1,3]{2,1,0:T(1,128)}, u32[]{:S(2)}) copy-start(s32[2,1,3]{2,1,0:T(1,128)} %param.19) | copy-start | bytes 76
  7.2 302.9 %all-gather.2.cloned.1.call-start = ((), (), s32[]{:S(2)}) async-start(), calls=%async_computation.1 | async-start | bytes 6488064 | tf_op jit(solution)/shard_map/all_gather | solution.py:960
  8.9 65.9 %copy-start.33 = (f32[768,384]{0,1:T(8,128)}, f32[768,384]{0,1:T(8,128)S(1)}, u32[]{:S(2)}) copy-start(f32[768,384]{0,1:T(8,128)S(1)} %copy.41) | copy-start | bytes 3538948
  54.4 20.5 %copy-start.94 = (s32[2,4096]{1,0:T(2,128)}, s32[2,4096]{1,0:T(2,128)S(1)}, u32[]{:S(2)}) copy-start(s32[2,4096]{1,0:T(2,128)S(1)} %all_gather.6) | copy-start | bytes 98308
  55.2 19.7 %copy-start.99 = (s32[8,256]{1,0:T(8,128)}, s32[8,256]{1,0:T(8,128)S(1)}, u32[]{:S(2)}) copy-start(s32[8,256]{1,0:T(8,128)S(1)} %get-tuple-element.142) | copy-start | bytes 24580
  205.6 64.4 %copy-start.4 = (bf16[32,72,768]{2,1,0:T(8,128)(2,1)}, bf16[32,72,768]{2,1,0:T(8,128)(2,1)S(1)}, u32[]{:S(2)}) copy-start(bf16[32,72,768]{2,1,0:T(8,128)(2,1)S(1)} %slice.260) | copy-start | bytes 10616836
  215.0 6.8 copy-start.57
  217.8 4.9 copy-start.77
  222.7 24.8 %collective-permute-start = (bf16[256,24,64]{0,2,1:T(8,128)(2,1)}, bf16[256,24,64]{0,2,1:T(8,128)(2,1)}, u32[]{:S(2)}, u32[]{:S(2)}) collective-permute-start(bf16[256,24,64]{0,2,1:T(8,128)(2,1)} %pad_maximum_fusion.11), channel_id=1, source_target_pairs={{0,1},{1,0},{2,3},{3,2},{4,5},{5,4},{6,7},{7,6},{8,9},{9,8},{10,11... | collective-permute-start | bytes 2359304 | tf_op jit(solution)/shard_map/ppermute | solution.py:112
  225.0 250.1 %reduce-scatter.2.cloned.1.call-start = ((), (), s32[]{:S(2)}) async-start(), calls=%async_computation.2 | async-start | bytes 6488064 | tf_op jit(solution)/shard_map/reduce_scatter | solution.py:995
  228.1 45.4 %collective-permute-start.2 = (bf16[128,4096]{1,0:T(8,128)(2,1)}, bf16[128,4096]{1,0:T(8,128)(2,1)}, u32[]{:S(2)}, u32[]{:S(2)}) collective-permute-start(bf16[128,4096]{1,0:T(8,128)(2,1)} %get-tuple-element.108), channel_id=1, source_target_pairs={{0,2},{1,3},{2,0},{3,1},{4,6},{5,7},{6,4},{7,5},{8,10},{9,11},{10,... | collective-permute-start | bytes 3145736 | tf_op jit(solution)/shard_map/ppermute | solution.py:112
  233.6 11.1 %copy-start.107 = (s32[8,1,128]{2,1,0:T(1,128)S(1)}, s32[8,1,128]{2,1,0:T(1,128)}, u32[]{:S(2)}) copy-start(s32[8,1,128]{2,1,0:T(1,128)} %copy-done.106) | copy-start | bytes 12292
  233.6 11.1 %copy-start.109 = (s32[8,1,128]{2,1,0:T(1,128)S(1)}, s32[8,1,128]{2,1,0:T(1,128)}, u32[]{:S(2)}) copy-start(s32[8,1,128]{2,1,0:T(1,128)} %copy-done.108) | copy-start | bytes 12292
  247.5 33.2 %copy-start.31 = (pred[256,512]{1,0:T(8,128)(4,1)}, pred[256,512]{1,0:T(8,128)(4,1)S(1)}, u32[]{:S(2)}) copy-start(pred[256,512]{1,0:T(8,128)(4,1)S(1)} %compare_and_fusion) | copy-start | bytes 393220
  252.8 5.5 slice-start.4
  253.1 5.2 slice-start.5
  253.1 5.2 slice-start.6
  269.4 13.8 %copy-start.18 = (f32[256,768]{1,0:T(8,128)}, f32[256,768]{1,0:T(8,128)S(1)}, u32[]{:S(2)}) copy-start(f32[256,768]{1,0:T(8,128)S(1)} %get-tuple-element.163) | copy-start | bytes 2359300
  272.5 8.2 %copy-start.65 = (bf16[256,12,64]{0,2,1:T(8,128)(2,1)}, bf16[256,12,64]{0,2,1:T(8,128)(2,1)S(1)}, u32[]{:S(2)}) copy-start(bf16[256,12,64]{0,2,1:T(8,128)(2,1)S(1)} %get-tuple-element.99) | copy-start | bytes 1179652
  272.6 8.1 %copy-start.60 = (bf16[256,12,64]{0,2,1:T(8,128)(2,1)}, bf16[256,12,64]{0,2,1:T(8,128)(2,1)S(1)}, u32[]{:S(2)}) copy-start(bf16[256,12,64]{0,2,1:T(8,128)(2,1)S(1)} %fusion.108) | copy-start | bytes 1179652
  272.7 4.5 collective-permute-start.1
  283.8 46.0 %copy-start.16 = (f32[256,768]{1,0:T(8,128)}, f32[256,768]{1,0:T(8,128)S(1)}, u32[]{:S(2)}) copy-start(f32[256,768]{1,0:T(8,128)S(1)} %get-tuple-element.167) | copy-start | bytes 2359300
  289.8 20.3 %copy-start.105 = (f32[768]{0:T(1024)S(1)}, f32[768]{0:T(1024)}, u32[]{:S(2)}) copy-start(f32[768]{0:T(1024)} %get-tuple-element.78) | copy-start | bytes 9220
  294.3 28.2 %copy-start.71 = (f32[256,768]{1,0:T(8,128)}, f32[256,768]{1,0:T(8,128)S(1)}, u32[]{:S(2)}) copy-start(f32[256,768]{1,0:T(8,128)S(1)} %get-tuple-element.169) | copy-start | bytes 2359300
  294.9 20.0 %copy-start.118 = (f32[256]{0:T(256)}, f32[256]{0:T(256)S(1)}, u32[]{:S(2)}) copy-start(f32[256]{0:T(256)S(1)} %get-tuple-element.152) | copy-start | bytes 3076
  314.9 5.0 copy-start.135
  315.6 7.1 slice-start.20
  315.6 7.1 slice-start.25
  319.9 6.5 slice-start.7
  319.9 6.5 slice-start.8
  322.8 7.1 copy-start.42
  331.2 7.8 slice-start.2
  347.6 8.6 %copy-start.30 = (bf16[256,4096]{1,0:T(8,128)(2,1)S(1)}, bf16[256,4096]{1,0:T(8,128)(2,1)}, u32[]{:S(2)}) copy-start(bf16[256,4096]{1,0:T(8,128)(2,1)} %copy-done.29) | copy-start | bytes 6291460
  347.6 8.6 %copy-start.72 = (f32[256,768]{1,0:T(8,128)S(1)}, f32[256,768]{1,0:T(8,128)}, u32[]{:S(2)}) copy-start(f32[256,768]{1,0:T(8,128)} %copy-done.71) | copy-start | bytes 2359300
  347.6 8.6 %copy-start.120 = (f32[256]{0:T(256)S(1)}, f32[256]{0:T(256)}, u32[]{:S(2)}) copy-start(f32[256]{0:T(256)} %copy-done.118) | copy-start | bytes 3076
  361.8 8.7 %collective-permute-start.3 = (bf16[256,24,64]{0,2,1:T(8,128)(2,1)}, bf16[256,24,64]{0,2,1:T(8,128)(2,1)}, u32[]{:S(2)}, u32[]{:S(2)}) collective-permute-start(bf16[256,24,64]{0,2,1:T(8,128)(2,1)} %pad_maximum_fusion.13), channel_id=1, source_target_pairs={{0,1},{1,0},{2,3},{3,2},{4,5},{5,4},{6,7},{7,6},{8,9},{9,8},{10,11... | collective-permute-start | bytes 2359304 | tf_op jit(solution)/shard_map/ppermute | solution.py:112
  365.0 5.5 slice-start.23
  365.0 5.6 copy-start.74
  365.0 7.2 copy-start.91
  365.0 14.1 %slice-start.18 = ((s8[6291456]{0:T(1024)(128)(4,1)}), s8[4194304]{0:T(1024)(128)(4,1)S(1)}, s32[]{:S(2)}) async-start(s8[6291456]{0:T(1024)(128)(4,1)} %bitcast.220), calls=%async_computation.21 | async-start | bytes 8388608
  372.9 6.1 slice-start.19
  376.9 7.2 slice-start.10
  379.1 8.5 %copy-start.44 = (f32[256,768]{1,0:T(8,128)}, f32[256,768]{1,0:T(8,128)S(1)}, u32[]{:S(2)}) copy-start(f32[256,768]{1,0:T(8,128)S(1)} %subtract_add_fusion.1) | copy-start | bytes 2359300
  379.1 5.0 slice-start.11
  379.1 5.0 slice-start.12
  379.1 5.0 copy-start.14
  379.1 5.0 copy-start.111
  387.6 8.1 %slice-start = ((s8[6291456]{0:T(1024)(128)(4,1)}), s8[2097152]{0:T(1024)(128)(4,1)S(1)}, s32[]{:S(2)}) async-start(s8[6291456]{0:T(1024)(128)(4,1)} %bitcast.193), calls=%async_computation.3 | async-start | bytes 4194304
  401.1 21.5 %copy-start.52 = (f32[512,12,64]{0,2,1:T(8,128)}, f32[512,12,64]{0,2,1:T(8,128)S(1)}, u32[]{:S(2)}) copy-start(f32[512,12,64]{0,2,1:T(8,128)S(1)} %multiply_bitcast_fusion) | copy-start | bytes 4718596
  402.4 5.1 copy-start.15
  402.4 27.8 %collective-permute-start.4 = (bf16[256,24,64]{0,2,1:T(8,128)(2,1)}, bf16[256,24,64]{0,2,1:T(8,128)(2,1)}, u32[]{:S(2)}, u32[]{:S(2)}) collective-permute-start(bf16[256,24,64]{0,2,1:T(8,128)(2,1)} %pad_maximum_fusion.14), channel_id=1, source_target_pairs={{0,1},{1,0},{2,3},{3,2},{4,5},{5,4},{6,7},{7,6},{8,9},{9,8},{10,11... | collective-permute-start | bytes 2359304 | tf_op jit(solution)/shard_map/ppermute | solution.py:112
  407.6 12.5 %copy-start.22 = (f32[256,768]{1,0:T(8,128)S(1)}, f32[256,768]{1,0:T(8,128)}, u32[]{:S(2)}) copy-start(f32[256,768]{1,0:T(8,128)} %copy-done.21) | copy-start | bytes 2359300
  422.7 7.6 slice-start.22
  422.7 7.6 slice-start.24
  430.3 9.1 %slice-start.13 = ((s8[7077888]{0:T(1024)(128)(4,1)}), s8[4194304]{0:T(1024)(128)(4,1)S(1)}, s32[]{:S(2)}) async-start(s8[7077888]{0:T(1024)(128)(4,1)} %bitcast.212), calls=%async_computation.16 | async-start | bytes 8388608
  432.6 6.8 slice-start.14
  622.4 101.5 %copy-start.56 = (f32[384,768]{1,0:T(8,128)S(1)}, f32[384,768]{1,0:T(8,128)}, u32[]{:S(2)}) copy-start(f32[384,768]{1,0:T(8,128)} %get-tuple-element.39) | copy-start | bytes 3538948
  622.4 111.9 %slice-start.15 = ((s8[9437184]{0:T(1024)(128)(4,1)}), s8[1048576]{0:T(1024)(128)(4,1)S(1)}, s32[]{:S(2)}) async-start(s8[9437184]{0:T(1024)(128)(4,1)} %bitcast.214), calls=%async_computation.18 | async-start | bytes 2097152
  723.9 10.4 %slice-start.16 = ((s8[9437184]{0:T(1024)(128)(4,1)}), s8[4194304]{0:T(1024)(128)(4,1)S(1)}, s32[]{:S(2)}) async-start(s8[9437184]{0:T(1024)(128)(4,1)} %bitcast.214), calls=%async_computation.19 | async-start | bytes 8388608
  742.5 5.6 copy-start.76
  749.1 28.9 %copy-start.104 = (f32[3,768]{1,0:T(4,128)S(1)}, f32[3,768]{1,0:T(4,128)}, u32[]{:S(2)}) copy-start(f32[3,768]{1,0:T(4,128)} %param.30) | copy-start | bytes 27652
  749.1 28.9 %copy-start.116 = (f32[3,768]{1,0:T(4,128)S(1)}, f32[3,768]{1,0:T(4,128)}, u32[]{:S(2)}) copy-start(f32[3,768]{1,0:T(4,128)} %param.31) | copy-start | bytes 27652
  749.1 28.9 %copy-start.117 = (f32[3,768]{1,0:T(4,128)S(1)}, f32[3,768]{1,0:T(4,128)}, u32[]{:S(2)}) copy-start(f32[3,768]{1,0:T(4,128)} %param.32) | copy-start | bytes 27652
  749.1 29.6 %copy-start.1 = (s32[2,1,3]{2,1,0:T(1,128)S(1)}, s32[2,1,3]{2,1,0:T(1,128)}, u32[]{:S(2)}) copy-start(s32[2,1,3]{2,1,0:T(1,128)} %param.19) | copy-start | bytes 76
  (106 other events, 283.7 us)
Sparse Core Ops, SparseCore 0:
  225.1 84.9 all-gather.1
  362.2 112.7 reduce-scatter.1

commit v4 on v3

--- a/solution.py
+++ b/solution.py
@@ -198,15 +198,82 @@
 
 def start_kernel(depth, *refs):
     pieces = refs[0:3]
-    rows_ref = refs[3]
-    wholes = refs[4:7]
-    sum_ref = refs[7]
-    far_x, from_low, from_high, total = refs[8:12]
-    local_sem, up_sem, down_sem, x_sem, y_sem, c_sem, block_sem = refs[12:19]
-    rx_send, rx_recv, ru_send, ru_recv, rd_send, rd_recv = refs[19:25]
+    table_ref, codes_ref, vocab_ref = refs[3:6]
+    wholes = refs[6:9]
+    sum_ref, ids_ref = refs[9:11]
+    far_x, from_low, from_high, total, rows_ref, shard, ids = refs[11:18]
+    local_sem, up_sem, down_sem, x_sem, y_sem, c_sem, block_sem = refs[18:25]
+    rx_send, rx_recv, ru_send, ru_recv, rd_send, rd_recv = refs[25:31]
+    id_send, id_recv, table_sem, copy_sem = refs[31:35]
     z, x, y, c = coordinates(depth)
     mine = slot(z, x, y, c)
-    greet(depth, z, x, y, c)
+    dp, head = z * 2 + x, y * 2 + c
+    groups, height = rows_ref.shape[:2]
+    shard_rows, tokens = table_ref.shape[0], codes_ref.shape[2]
+    part = height - 2 * tokens
+    offset = dp * shard_rows
+    barrier = pltpu.get_barrier_semaphore()
+    pl.semaphore_signal(barrier, 1, device_id=device(z, x, y, 1 - c), device_id_type=MESH)
+    for group in range(groups):
+        for rank in range(2):
+
+            @pl.when((group != dp) | (rank != y))
+            def hello():
+                pl.semaphore_signal(
+                    barrier, 1, device_id=(group, rank * 2 + c), device_id_type=MESH
+                )
+
+    pl.semaphore_wait(barrier, groups * 2)
+
+    def tell(group, rank):
+        second = jnp.where(rank == y, 0, 1)
+        return pltpu.make_async_remote_copy(
+            codes_ref.at[rank],
+            ids_ref.at[dp, second],
+            id_send.at[group, rank],
+            id_recv.at[dp, second],
+            device_id=(group, rank * 2 + c),
+            device_id_type=MESH,
+        )
+
+    def told(group, second):
+        return pltpu.make_async_remote_copy(
+            codes_ref.at[0],
+            ids_ref.at[group, second],
+            id_send.at[group, second],
+            id_recv.at[group, second],
+            device_id=device(z, x, y, 1 - c),
+            device_id_type=MESH,
+        )
+
+    keep = pltpu.make_async_copy(codes_ref.at[y], ids_ref.at[dp, 0], copy_sem)
+    fetch = pltpu.make_async_copy(table_ref, shard.at[pl.ds(0, shard_rows)], table_sem)
+    fetch.start()
+    keep.start()
+    for group in range(groups):
+        for rank in range(2):
+
+            @pl.when((group != dp) | (rank != y))
+            def telling():
+                tell(group, rank).start()
+
+    def gather(group):
+        def load(first, read):
+            @pl.loop(0, (tokens if first else part) // 16)
+            def some(index):
+                base = index * 16
+                lines = []
+                for line in range(16):
+                    place = read(base + line) - offset
+                    held = (place >= 0) & (place < shard_rows)
+                    lines.append(shard[pl.ds(jnp.where(held, place, shard_rows), 1)])
+                rows_ref[group, pl.ds(pl.multiple_of(first + base, 16), 16)] = jnp.concatenate(
+                    lines, axis=0
+                ).astype(low)
+
+        load(0, lambda index: vocab_ref[(group * 4 + head) * part + index])
+        for second in range(2):
+            load(part + second * tokens, lambda index: ids[group, second, 0, index] >> 1)
 
     def own(block, piece, target, sem):
         return pltpu.make_async_remote_copy(
@@ -281,8 +348,6 @@
         for piece in range(3)
     ]
     send(own, mine, across_y, y_sem.at[mine // 4])
-    for goal in goals:
-        rows_x[goal].start()
 
     @pl.when(z < depth - 1)
     def first_up():
@@ -296,6 +361,23 @@
     send(own, mine, across_c, c_sem.at[mine // 2])
     for copy in local:
         copy.start()
+    shard[pl.ds(shard_rows, 8)] = jnp.zeros((8, shard.shape[1]), jnp.float32)
+    keep.wait()
+    for group in range(groups):
+        for second in range(2):
+
+            @pl.when((group != dp) | (second != 0))
+            def heard():
+                told(group, second).wait_recv()
+
+    to_scalars = pltpu.make_async_copy(ids_ref, ids, copy_sem)
+    to_scalars.start()
+    fetch.wait()
+    to_scalars.wait()
+    for goal in goals:
+        gather(goal * 2 + 1 - x)
+        rows_x[goal].start()
+    nearer = list(goals)
 
     def spread(block, over_x):
         send(onward, block, across_y, y_sem.at[block // 4])
@@ -326,6 +408,10 @@
                 send(onward, block, device(z - 1, x, y, c), down_sem.at[step])
 
             spread(block, True)
+
+        for goal in nearer[:2]:
+            gather(goal * 2 + x)
+        nearer = nearer[2:]
 
     for goal in goals:
         rows_x[goal].wait_recv()
@@ -404,6 +490,13 @@
 
     for copy in local:
         copy.wait()
+    for group in range(groups):
+        for rank in range(2):
+
+            @pl.when((group != dp) | (rank != y))
+            def spoken():
+                tell(group, rank).wait_send()
+
     for goal in range(depth):
         rows_x[goal].wait_send()
 
@@ -436,28 +529,38 @@
         sent(mine, across_c, c_sem.at[index])
 
 
-def start(pieces, rows):
-    groups, height, width = rows.shape
+def start(pieces, table, codes, vocab_ids, groups):
+    width = table.shape[1]
+    height = vocab_ids.shape[0] // (groups * 4) + 2 * codes.shape[2]
     depth = groups // 2
     blocks = depth * 8
+    told = (groups, 2, 1, codes.shape[2])
     dma = pltpu.SemaphoreType.DMA
     buffer = pltpu.VMEM((depth, height, width), low)
     return pl.pallas_call(
         functools.partial(start_kernel, depth),
         out_shape=[jax.ShapeDtypeStruct((blocks,) + piece.shape, low) for piece in pieces]
-        + [jax.ShapeDtypeStruct((height, width), low)],
-        in_specs=[ANY] * 3 + [pl.BlockSpec(memory_space=pltpu.VMEM)],
-        out_specs=[ANY] * 3 + [pl.BlockSpec(memory_space=pltpu.VMEM)],
+        + [jax.ShapeDtypeStruct((height, width), low), jax.ShapeDtypeStruct(told, jnp.int32)],
+        in_specs=[ANY] * 4
+        + [pl.BlockSpec(memory_space=pltpu.VMEM), pl.BlockSpec(memory_space=pltpu.SMEM)],
+        out_specs=[ANY] * 3 + [pl.BlockSpec(memory_space=pltpu.VMEM)] * 2,
         scratch_shapes=[buffer] * 4
+        + [
+            pltpu.VMEM((groups, height, width), low),
+            pltpu.VMEM((table.shape[0] + 8, width), jnp.float32),
+            pltpu.SMEM(told, jnp.int32),
+        ]
         + [dma((3,))]
         + [dma((depth, 3))] * 3
         + [dma((depth * 2, 3)), dma((depth * 4, 3)), dma((blocks, 3))]
-        + [dma((depth,))] * 6,
+        + [dma((depth,))] * 6
+        + [dma((groups, 2))] * 2
+        + [dma(())] * 2,
         compiler_params=pltpu.CompilerParams(
             collective_id=0, has_side_effects=True, vmem_limit_bytes=58 * 2**20
         ),
         name="start",
-    )(*pieces, rows)
+    )(*pieces, table, codes, vocab_ids)
 
 
 def by_distance(depth, z, act):
@@ -928,29 +1031,23 @@
     offset = dp * shard_rows
     part = TOPV // device_total
 
-    codes = lax.all_gather(token_ids * 2 + valid, ("dp", "head"), axis=1, tiled=True)
-    count = jnp.sum(codes & 1).astype(jnp.float32)
-    codes = lax.dynamic_index_in_dim(codes, batch, 0, keepdims=False).reshape(
-        dp_count, head_count, tokens
-    )
-    first = lax.dynamic_index_in_dim(codes, head, 1, keepdims=False)
-    second = lax.dynamic_index_in_dim(codes, head ^ 2, 1, keepdims=False)
-    codes = jnp.concatenate([first, second], axis=1)
+    widths = [3 * D // device_total, D // device_total, 2 * FF // device_total, FF // device_total]
+    cuts = [sum(widths[:index]) for index in range(5)]
+    block_low = block.T.astype(low)
+    attention, gate_up, down, rows_in, codes = start(
+        [block_low[: cuts[2]], block_low[cuts[2] : cuts[3]], block_low[cuts[3] :]],
+        table,
+        (token_ids * 2 + valid).reshape(-1, 1, tokens),
+        vocab_ids,
+        dp_count,
+    )
+    codes = codes.reshape(dp_count, 2 * tokens)
     weighting = (lax.dynamic_index_in_dim(codes, dp, 0, keepdims=False) & 1).astype(jnp.float32)
     vocab = lax.dynamic_index_in_dim(
         vocab_ids.reshape(dp_count, head_count, part), head, 1, keepdims=False
     )
     local = jnp.concatenate([vocab, codes >> 1], axis=1) - offset
     owned = (local >= 0) & (local < shard_rows)
-    rows_out = jnp.where(
-        owned[..., None], table[jnp.clip(local, 0, shard_rows - 1)], 0.0
-    ).astype(low)
-    widths = [3 * D // device_total, D // device_total, 2 * FF // device_total, FF // device_total]
-    cuts = [sum(widths[:index]) for index in range(5)]
-    block_low = block.T.astype(low)
-    attention, gate_up, down, rows_in = start(
-        [block_low[: cuts[2]], block_low[cuts[2] : cuts[3]], block_low[cuts[3] :]], rows_out
-    )
     weights = [
         attention[:, : cuts[1]].reshape(-1, D),
         attention[:, cuts[1] :].reshape(-1, D),
@@ -1025,8 +1122,8 @@
         tile,
     )
     squares = jnp.sum(block_grads * block_grads)
-    small = jnp.concatenate([d_gains[0], d_gains[1], d_gain_final, loss_sum[None]])
-    small = jnp.pad(small, (0, 6 * 128 - 1)).reshape(-1, 128)
+    small = jnp.concatenate([d_gains[0], d_gains[1], d_gain_final, loss_sum[None], jnp.sum(weighting)[None]])
+    small = jnp.pad(small, (0, 6 * 128 - 2)).reshape(-1, 128)
     small = small.at[-1, 0].set(squares)
     table_grads, small = share(
         dp_count // 2, table_grads.reshape(head_count, quarter, D), small
@@ -1034,6 +1131,7 @@
     table_grads = table_grads.reshape(-1, D)[:shard_rows].astype(jnp.float32)
     squares = small[-1, 0]
     small = small.reshape(-1)
+    count = small[3 * D + 1]
     gain_grads = small[: 3 * D].reshape(3, D) / count
     loss = small[3 * D] / count
     grad_norm = jnp.sqrt(squares / (count * count) + jnp.sum(gain_grads * gain_grads))

time: 798 us -> 739 us (0.926)
  blocking collectives: 43.3 us -> 0 us
  local copies, waits for them, and re-layouts: 75.8 us -> 61.3 us
  matrix products: 134 us -> 147 us
  waiting for transfers between devices: 46.6 us -> 34.9 us
    all_gather x1 -> x0, blocking collectives: 43.3 us -> none  [on_device(): lax.all_gather(token_ids * 2 + valid, ('dp', 'head'), axis=1, tiled=True)]
    gather x1 -> x0, local copies, waits for them, and re-layouts: 19 us -> none  [on_device(): table[jnp.clip(local, 0, shard_rows - 1)]]
    reduce_scatter x1, waiting for transfers between devices: 31.4 us -> 19.7 us  [on_device(): lax.psum_scatter(chosen_grads, ('dp', 'head'), scatter_dimension=0, tiled...]
    dot_general x13, matrix products: 56.9 us -> 66.4 us  [contract_rows(): lax.dot_general(left, right, (((0,), (0,)), ((), ())), preferred_element_...]
    unnamed x328 -> x297, local copies, waits for them, and re-layouts: 34.2 us -> 37.3 us
  transfers between devices with their start and end apart: 7 -> 7, of which waited for: 2 -> 2; matrix products, arithmetic and copies ran while one was open for 17% -> 20% of each run, Pallas kernels for 0% -> 0%
where the time goes in v4:
time: 739 us; the launch traced here: 729 us
  Pallas kernels  369 us (50%)
  matrix products  147 us (20%)
  other arithmetic  89.9 us (12%)
  local copies, waits for them, and re-layouts  61.3 us (8%)
  waiting for transfers between devices  34.9 us (5%)
  between operations  24.6 us (3%)
    pallas_call x1, Pallas kernels, start(): pl.pallas_call(functools.partial(start_kernel, depth), out_shape=[jax.Sha...  129 us
    pallas_call x1, Pallas kernels, end(): pl.pallas_call(functools.partial(end_kernel, depth, heights), out_shape=[...  115 us
    pallas_call x1, Pallas kernels, share(): pl.pallas_call(functools.partial(share_kernel, depth), out_shape=[jax.Sha...  97.9 us
    dot_general x13, matrix products, contract_rows(): lax.dot_general(left, right, (((0,), (0,)), ((), ())), preferred_element_...  66.4 us
    unnamed x297, local copies, waits for them, and re-layouts  37.3 us
    dot_general x13, matrix products, product(): return jnp.dot(left, right, preferred_element_type=jnp.float32)  29.4 us
    convert_element_type x1, other arithmetic, on_device(): table_new.astype(low)  28.9 us
    pallas_call x1, Pallas kernels, collect(): pl.pallas_call(functools.partial(collect_kernel, step), grid=(height // s...  26.6 us
  transfers between devices with their start and end apart: 7, of which 2 were waited for; matrix products, arithmetic and copies ran while one was open for 20% of the time, Pallas kernels for 0%

profile of v4, /device:TPU:0, one launch (start us, length us, event | category | flops | bytes accessed | tf_op | source)
XLA Modules:
  0.0 729.1 jit_solution(3972345162743067137)
XLA Ops:
  11.7 129.2 %start.1 = (bf16[32,96,768]{2,1,0:T(8,128)(2,1)}, bf16[32,192,768]{2,1,0:T(8,128)(2,1)}, bf16[32,96,768]{2,1,0:T(8,128)(2,1)}, bf16[384,768]{1,0:T(8,128)(2,1)}, s32[8,2,1,128]{3,2,1,0:T(1,128)}) custom-call(bf16[96,768]{1,0:T(8,128)(2,1)} %get-tuple-element.134.refs_0_, bf16[192,768]{1,0:T(8,128)(2,1)} %slice.330.refs_1_, ...), custom_call_target="tpu_custom_call" | custom-call | tf_op jit(solution)/shard_map/start/pallas_call | solution.py:540
  142.7 2.3 slice.263
  152.9 2.1 pad_add_fusion.2
  162.2 3.1 dynamic-slice_bitcast_fusion.1
  166.7 2.4 slice.275
  172.3 2.7 copy.44
  174.9 2.7 copy.45
  177.6 2.0 fusion.166
  184.9 1.8 exponential_reduce_fusion.1
  187.6 4.0 convolution_convert_fusion.2
  193.7 3.8 fusion.156
  198.5 1.7 copy-done.9
  200.2 4.4 multiply_reduce_fusion.13
  210.3 2.1 fusion.12
  213.9 2.2 exponential_reduce_fusion
  216.6 1.7 convolution_convert_fusion.1
  219.0 2.7 fusion.158
  222.6 1.7 copy-done.10
  224.4 4.4 multiply_reduce_fusion.11
  228.8 15.2 %all-gather.2.cloned.1.call-done = bf16[4096,768]{1,0:T(8,128)(2,1)} async-done(((bf16[128,768]{1,0:T(8,128)(2,1)}), bf16[4096,768]{1,0:T(8,128)(2,1)}) %all-gather.2.cloned.1.call-update) | async-done | bytes 6291472 | tf_op jit(solution)/shard_map/all_gather | solution.py:1057
  244.1 4.7 fusion.175
  249.5 3.6 fusion.11
  253.2 2.6 multiply_reduce_fusion.3
  256.0 2.4 multiply_convert_fusion.5
  258.9 3.4 multiply_reduce_fusion.5
  265.0 1.9 copy.42
  266.9 5.6 multiply_reduce_fusion.1
  272.5 1.7 convolution_bitcast_fusion.1
  274.2 2.2 multiply_convert_fusion.1
  280.0 4.6 convolution_convert_fusion
  284.6 10.6 %fusion.40 = f32[6144,768]{1,0:T(8,128)} fusion(bf16[256,3072]{1,0:T(8,128)(2,1)} %copy-done.81, bf16[256,3072]{1,0:T(8,128)(2,1)S(1)} %copy-done.80, f32[256,768]{1,0:T(8,128)S(1)} %get-tuple-element.169, f32[256]{0:T(256)S(1)} %get-tuple-element.152, f32[768]{0:T(1024)S(1)} %get-tuple-element.81), kind=kOutput, calls=%fused_computation.78 | convolution fusion | flops 2422800384 | bytes 22810624 | tf_op jit(solution)/shard_map/dot_general | solution.py:36
  297.5 1.9 fusion.122
  299.5 5.5 fusion.125
  309.6 2.0 copy-done.5
  311.8 1.9 multiply_reduce_fusion.6
  314.0 5.1 multiply_convert_fusion.3
  319.2 3.4 multiply_reduce_fusion.4
  325.5 1.9 copy.43
  327.4 5.8 multiply_reduce_fusion
  333.3 1.7 multiply_convert_fusion
  340.4 4.1 fusion.157
  344.5 14.6 %add_convert_fusion = bf16[6144,768]{1,0:T(8,128)(2,1)} fusion(f32[6144,768]{1,0:T(8,128)} %fusion.40, bf16[256,3072]{1,0:T(8,128)(2,1)} %copy-done.89, bf16[256,3072]{1,0:T(8,128)(2,1)} %copy-done.88, f32[256,768]{1,0:T(8,128)} %get-tuple-element.163, f32[768]{0:T(1024)S(1)} %get-tuple-element.81, f32[256]{0:T(256)S(1)} %copy-done.104), kind=kOutput, calls=%fused_computation | convolution fusion | flops 2432237568 | bytes 32247808 | tf_op jit(solution)/shard_map/dot_general | solution.py:36
  359.1 3.9 add_convert_fusion.3
  363.0 7.6 %add_convert_fusion.1 = bf16[3072,768]{1,0:T(8,128)(2,1)} fusion(f32[3072,768]{1,0:T(8,128)} %fusion.125, bf16[256,3072]{1,0:T(8,128)(2,1)S(1)} %copy-done.50, f32[256,768]{1,0:T(8,128)S(1)} %copy-done.46), kind=kOutput, calls=%fused_computation.6 | convolution fusion | flops 1212874752 | bytes 16515072 | tf_op jit(solution)/shard_map/dot_general | solution.py:36
  372.9 2.1 broadcast_multiply_fusion
  376.8 2.6 fusion.88
  381.6 5.0 add_convert_fusion.2
  386.7 2.8 pad_maximum_fusion.refs_0_
  389.8 19.7 %reduce-scatter.2.cloned.1.call-done = bf16[128,768]{1,0:T(8,128)(2,1)} async-done(((bf16[4096,768]{1,0:T(8,128)(2,1)}), bf16[128,768]{1,0:T(8,128)(2,1)}) %reduce-scatter.2.cloned.1.call-update) | async-done | bytes 196624 | tf_op jit(solution)/shard_map/reduce_scatter | solution.py:1092
  409.4 1.8 pad_maximum_fusion.15.refs_3_
  411.2 115.1 %end.1 = (f32[384,768]{1,0:T(8,128)}, bf16[8,384,768]{2,1,0:T(8,128)(2,1)}) custom-call(bf16[32,96,768]{2,1,0:T(8,128)(2,1)} %pad_maximum_fusion.refs_0_, bf16[32,192,768]{2,1,0:T(8,128)(2,1)} %bitcast.198, bf16[32,96,768]{2,1,0:T(8,128)(2,1)} %bitcast.223, bf16[384,768]{1,0:T(8,128)(2,1)} %pad_maximum_fusion.15.refs_3_), custom_call_target="tpu_custom_call" | custom-call | tf_op jit(solution)/shard_map/end/pallas_call | solution.py:816
  526.3 2.2 multiply_reduce_fusion.2
  528.5 26.6 %collect.1 = bf16[4160,768]{1,0:T(8,128)(2,1)} custom-call(s32[1,3072]{1,0:T(1,128)} %and_select_fusion.places_ref, bf16[3072,768]{1,0:T(8,128)(2,1)} %bitcast.256), custom_call_target="tpu_custom_call" | custom-call | flops 19629342720 | bytes 11108352 | tf_op jit(solution)/shard_map/collect/pallas_call | solution.py:848
  556.4 97.9 %share.1 = (bf16[4,1040,768]{2,1,0:T(8,128)(2,1)}, f32[24,128]{1,0:T(8,128)}) custom-call(bf16[4,1040,768]{2,1,0:T(8,128)(2,1)} %bitcast.227, f32[24,128]{1,0:T(8,128)} %copy-done.99), custom_call_target="tpu_custom_call" | custom-call | tf_op jit(solution)/shard_map/share/pallas_call | solution.py:967
  655.6 2.0 multiply_reduce_fusion.15
  663.6 2.2 fusion.50
  665.9 2.0 fusion.59
  667.9 2.2 fusion.65
  670.1 2.1 fusion.71
  672.2 1.8 add_divide_fusion.2
  678.3 2.7 fusion.162
  681.0 2.7 copy.48
  683.8 2.2 copy.51
  690.7 28.9 %fusion.160 = (bf16[4000,768]{1,0:T(8,128)(2,1)}, f32[4000,768]{1,0:T(8,128)}, f32[4000,768]{1,0:T(8,128)}, f32[4000,768]{1,0:T(8,128)}) fusion(f32[4000,768]{1,0:T(8,128)} %refs_3_.1, f32[]{:T(128)S(6)} %div.137, bf16[4160,768]{1,0:T(8,128)(2,1)} %bitcast.228, f32[4000,768]{1,0:T(8,128)} %param.28, f32[4000,768]{1,0:T(8,128)} %param.29), kind=kLoop, calls=%fused_computation.317 | loop fusion | flops 55296000 | bytes 86016000 | tf_op jit(solution)/shard_map/convert_element_type | solution.py:1182
  (424 shorter events, 85.2 us)
Async XLA Ops:
  7.2 141.8 %copy-start = (s32[2,1,3]{2,1,0:T(1,128)S(1)}, s32[2,1,3]{2,1,0:T(1,128)}, u32[]{:S(2)}) copy-start(s32[2,1,3]{2,1,0:T(1,128)} %param.19) | copy-start | bytes 76
  7.2 236.8 %all-gather.2.cloned.1.call-start = ((), (), s32[]{:S(2)}) async-start(), calls=%async_computation.1 | async-start | bytes 6488064 | tf_op jit(solution)/shard_map/all_gather | solution.py:1057
  9.4 131.5 %copy-start.33 = (f32[768,384]{0,1:T(8,128)}, f32[768,384]{0,1:T(8,128)S(1)}, u32[]{:S(2)}) copy-start(f32[768,384]{0,1:T(8,128)S(1)} %copy.41) | copy-start | bytes 3538948
  145.0 60.2 %copy-start.4 = (bf16[32,72,768]{2,1,0:T(8,128)(2,1)}, bf16[32,72,768]{2,1,0:T(8,128)(2,1)S(1)}, u32[]{:S(2)}) copy-start(bf16[32,72,768]{2,1,0:T(8,128)(2,1)S(1)} %slice.263) | copy-start | bytes 10616836
  152.9 4.6 copy-start.12
  159.6 22.3 %collective-permute-start = (bf16[256,24,64]{0,2,1:T(8,128)(2,1)}, bf16[256,24,64]{0,2,1:T(8,128)(2,1)}, u32[]{:S(2)}, u32[]{:S(2)}) collective-permute-start(bf16[256,24,64]{0,2,1:T(8,128)(2,1)} %pad_maximum_fusion.11), channel_id=1, source_target_pairs={{0,1},{1,0},{2,3},{3,2},{4,5},{5,4},{6,7},{7,6},{8,9},{9,8},{10,11... | collective-permute-start | bytes 2359304 | tf_op jit(solution)/shard_map/ppermute | solution.py:112
  161.9 247.6 %reduce-scatter.2.cloned.1.call-start = ((), (), s32[]{:S(2)}) async-start(), calls=%async_computation.2 | async-start | bytes 6488064 | tf_op jit(solution)/shard_map/reduce_scatter | solution.py:1092
  162.2 6.9 copy-start.102
  165.2 43.4 %collective-permute-start.2 = (bf16[128,4096]{1,0:T(8,128)(2,1)}, bf16[128,4096]{1,0:T(8,128)(2,1)}, u32[]{:S(2)}, u32[]{:S(2)}) collective-permute-start(bf16[128,4096]{1,0:T(8,128)(2,1)} %get-tuple-element.112), channel_id=1, source_target_pairs={{0,2},{1,3},{2,0},{3,1},{4,6},{5,7},{6,4},{7,5},{8,10},{9,11},{10,... | collective-permute-start | bytes 3145736 | tf_op jit(solution)/shard_map/ppermute | solution.py:112
  177.6 5.9 copy-start.67
  181.9 34.2 %copy-start.30 = (pred[256,512]{1,0:T(8,128)(4,1)}, pred[256,512]{1,0:T(8,128)(4,1)S(1)}, u32[]{:S(2)}) copy-start(pred[256,512]{1,0:T(8,128)(4,1)S(1)} %compare_and_fusion) | copy-start | bytes 393220
  186.7 7.0 slice-start.4
  187.6 6.1 slice-start.5
  187.6 6.1 slice-start.6
  200.2 4.4 copy-start.49
  204.6 13.7 %copy-start.16 = (f32[256,768]{1,0:T(8,128)}, f32[256,768]{1,0:T(8,128)S(1)}, u32[]{:S(2)}) copy-start(f32[256,768]{1,0:T(8,128)S(1)} %get-tuple-element.165) | copy-start | bytes 2359300
  207.7 4.8 copy-start.69
  207.7 8.4 %copy-start.65 = (bf16[256,12,64]{0,2,1:T(8,128)(2,1)}, bf16[256,12,64]{0,2,1:T(8,128)(2,1)S(1)}, u32[]{:S(2)}) copy-start(bf16[256,12,64]{0,2,1:T(8,128)(2,1)S(1)} %get-tuple-element.103) | copy-start | bytes 1179652
  207.9 4.5 collective-permute-start.1
  224.4 4.4 copy-start.35
  228.8 26.9 %copy-start.71 = (f32[256,768]{1,0:T(8,128)}, f32[256,768]{1,0:T(8,128)S(1)}, u32[]{:S(2)}) copy-start(f32[256,768]{1,0:T(8,128)S(1)} %get-tuple-element.171) | copy-start | bytes 2359300
  248.8 4.4 copy-start.121
  249.5 6.5 slice-start.18
  249.5 6.5 slice-start.24
  253.2 5.3 slice-start.7
  253.2 5.4 slice-start.8
  256.0 6.3 copy-start.43
  262.3 4.5 copy-start.31
  263.7 8.7 %slice-start.2 = ((s8[6291456]{0:T(1024)(128)(4,1)}), s8[2097152]{0:T(1024)(128)(4,1)S(1)}, s32[]{:S(2)}) async-start(s8[6291456]{0:T(1024)(128)(4,1)} %bitcast.196), calls=%async_computation.5 | async-start | bytes 4194304
  266.9 5.6 slice-start.3
  266.9 5.6 copy-start.87
  274.2 4.7 copy-start.73
  280.0 4.6 copy-start.80
  284.6 10.6 %copy-start.83 = (bf16[256,12,64]{0,2,1:T(8,128)(2,1)S(1)}, bf16[256,12,64]{0,2,1:T(8,128)(2,1)}, u32[]{:S(2)}) copy-start(bf16[256,12,64]{0,2,1:T(8,128)(2,1)} %slice.543) | copy-start | bytes 1179652
  295.3 9.7 %collective-permute-start.3 = (bf16[256,24,64]{0,2,1:T(8,128)(2,1)S(1)}, bf16[256,24,64]{0,2,1:T(8,128)(2,1)S(1)}, u32[]{:S(2)}, u32[]{:S(2)}) collective-permute-start(bf16[256,24,64]{0,2,1:T(8,128)(2,1)S(1)} %pad_maximum_fusion.13), channel_id=1, source_target_pairs={{0,1},{1,0},{2,3},{3,2},{4,5},{5,4},{6,7},{7,6},{8,9},{9,8},{10,11... | collective-permute-start | bytes 2359304 | tf_op jit(solution)/shard_map/ppermute | solution.py:112
  299.5 5.5 slice-start.21
  299.5 5.6 slice-start.22
  299.5 5.8 copy-start.92
  299.5 14.4 %slice-start.16 = ((s8[6291456]{0:T(1024)(128)(4,1)}), s8[4194304]{0:T(1024)(128)(4,1)S(1)}, s32[]{:S(2)}) async-start(s8[6291456]{0:T(1024)(128)(4,1)} %bitcast.219), calls=%async_computation.19 | async-start | bytes 8388608
  307.1 6.8 slice-start.17
  311.8 7.4 %slice-start.10 = ((s8[9437184]{0:T(1024)(128)(4,1)}), s8[4194304]{0:T(1024)(128)(4,1)S(1)}, s32[]{:S(2)}) async-start(s8[9437184]{0:T(1024)(128)(4,1)} %bitcast.206), calls=%async_computation.13 | async-start | bytes 8388608
  314.0 8.6 %copy-start.45 = (f32[256,768]{1,0:T(8,128)}, f32[256,768]{1,0:T(8,128)S(1)}, u32[]{:S(2)}) copy-start(f32[256,768]{1,0:T(8,128)S(1)} %subtract_add_fusion.1) | copy-start | bytes 2359300
  314.0 5.2 slice-start.11
  314.0 5.2 slice-start.12
  314.0 5.2 copy-start.15
  314.0 5.2 copy-start.104
  327.4 5.8 slice-start
  327.4 5.9 slice-start.1
  327.4 5.9 copy-start.32
  327.4 5.9 copy-start.97
  340.1 30.4 %collective-permute-start.4 = (bf16[256,24,64]{0,2,1:T(8,128)(2,1)}, bf16[256,24,64]{0,2,1:T(8,128)(2,1)}, u32[]{:S(2)}, u32[]{:S(2)}) collective-permute-start(bf16[256,24,64]{0,2,1:T(8,128)(2,1)} %pad_maximum_fusion.14), channel_id=1, source_target_pairs={{0,1},{1,0},{2,3},{3,2},{4,5},{5,4},{6,7},{7,6},{8,9},{9,8},{10,11... | collective-permute-start | bytes 2359304 | tf_op jit(solution)/shard_map/ppermute | solution.py:112
  363.0 7.6 %slice-start.20 = ((f32[512,12,64]{0,2,1:T(8,128)}), f32[256,12,64]{0,2,1:T(8,128)S(1)}, s32[]{:S(2)}) async-start(f32[512,12,64]{0,2,1:T(8,128)} %copy-done.51), calls=%async_computation.23 | async-start | bytes 1572864 | tf_op jit(solution)/shard_map/slice | solution.py:155
  363.0 7.6 %slice-start.23 = ((f32[512,12,64]{0,2,1:T(8,128)}), f32[256,12,64]{0,2,1:T(8,128)S(1)}, s32[]{:S(2)}) async-start(f32[512,12,64]{0,2,1:T(8,128)} %copy-done.74), calls=%async_computation.26 | async-start | bytes 1572864 | tf_op jit(solution)/shard_map/slice | solution.py:155
  363.0 9.2 %copy-start.95 = (f32[256,64]{0,1:T(8,128)S(1)}, f32[256,64]{0,1:T(8,128)}, u32[]{:S(2)}) copy-start(f32[256,64]{0,1:T(8,128)} %copy-done.93) | copy-start | bytes 196612
  381.6 5.0 copy-start.54
  556.4 107.1 %copy-start.58 = (f32[384,768]{1,0:T(8,128)S(1)}, f32[384,768]{1,0:T(8,128)}, u32[]{:S(2)}) copy-start(f32[384,768]{1,0:T(8,128)} %get-tuple-element.41) | copy-start | bytes 3538948
  556.4 117.6 %slice-start.13 = ((s8[9437184]{0:T(1024)(128)(4,1)}), s8[1048576]{0:T(1024)(128)(4,1)S(1)}, s32[]{:S(2)}) async-start(s8[9437184]{0:T(1024)(128)(4,1)} %bitcast.213), calls=%async_computation.16 | async-start | bytes 2097152
  663.6 10.4 %slice-start.14 = ((s8[9437184]{0:T(1024)(128)(4,1)}), s8[4194304]{0:T(1024)(128)(4,1)S(1)}, s32[]{:S(2)}) async-start(s8[9437184]{0:T(1024)(128)(4,1)} %bitcast.213), calls=%async_computation.17 | async-start | bytes 8388608
  667.9 4.3 copy-start.55
  681.0 4.9 copy-start.57
  683.8 6.3 copy-start.101
  683.8 6.3 copy-start.109
  683.8 6.3 copy-start.110
  690.7 28.9 %copy-start.1 = (s32[2,1,3]{2,1,0:T(1,128)S(1)}, s32[2,1,3]{2,1,0:T(1,128)}, u32[]{:S(2)}) copy-start(s32[2,1,3]{2,1,0:T(1,128)} %param.19) | copy-start | bytes 76
  (91 other events, 222.1 us)
Sparse Core Ops, SparseCore 0:
  162.0 82.0 all-gather.1
  296.4 112.9 reduce-scatter.1

commit v5 on v4

--- a/solution.py
+++ b/solution.py
@@ -585,14 +585,18 @@
         total[block, part] = value.astype(low)
 
 
-def end_kernel(depth, heights, *refs):
-    pieces, rows_ref, grad_ref, rows_out = refs[0:3], refs[3], refs[4], refs[5]
-    total, far_c, far_y, far_x, from_low, from_high = refs[6:12]
-    local_sem, c_send, c_recv, y_send, y_recv, x_send, x_recv = refs[12:19]
-    u_send, u_recv, d_send, d_recv = refs[19:23]
-    own_sem, ru_send, rd_send, rx_send, r_recv = refs[23:28]
+def finish_kernel(depth, heights, tile, *refs):
+    pieces = refs[0:3]
+    rows_ref, places_ref, small_ref = refs[3:6]
+    grad_ref, table_out, small_out = refs[6:9]
+    total, far_c, far_p, far_s, from_low, from_high = refs[9:15]
+    rows, given, far_t, part, mine, far_part, small, far_small = refs[15:23]
+    local_sem, c_send, c_recv, p_send, p_recv, s_send, s_recv = refs[23:30]
+    u_send, u_recv, d_send, d_recv = refs[30:34]
+    own_sem, ru_send, rd_send, rx_send, r_recv = refs[34:39]
+    t_send, t_recv, ty_send, ty_recv, o_send, o_recv, e_send, e_recv = refs[39:47]
     z, x, y, c = coordinates(depth)
-    greet(depth, z, x, y, c)
+    dp = z * 2 + x
     firsts = [sum(heights[:index]) for index in range(3)]
     up, down = device(z + 1, x, y, c), device(z - 1, x, y, c)
     across_x, across_y, across_c = (
@@ -600,11 +604,39 @@
         device(z, x, 1 - y, c),
         device(z, x, y, 1 - c),
     )
+    even = c == 0
+    across_p = tuple(jnp.where(even, a, b) for a, b in zip(across_y, across_x))
+    across_s = tuple(jnp.where(even, b, a) for a, b in zip(across_y, across_x))
+    own_p, own_s = jnp.where(even, y, x), jnp.where(even, x, y)
+    partners = [across_c, across_y, across_x]
+    reach = 1
+    while reach < depth:
+        partners.append(device(z ^ reach, x, y, c))
+        reach = reach * 2
+
+    barrier = pltpu.get_barrier_semaphore()
+    for target in partners[:3] + partners[4:]:
+        pl.semaphore_signal(barrier, 1, device_id=target, device_id_type=MESH)
+
+    @pl.when(z > 0)
+    def below():
+        pl.semaphore_signal(barrier, 1, device_id=down, device_id_type=MESH)
+
+    @pl.when(z < depth - 1)
+    def above():
+        pl.semaphore_signal(barrier, 1, device_id=up, device_id_type=MESH)
+
+    pl.semaphore_wait(
+        barrier, len(partners) - 1 + jnp.where(z > 0, 1, 0) + jnp.where(z < depth - 1, 1, 0)
+    )
 
     def remote(source, goal, send_sem, recv_sem, target):
         return pltpu.make_async_remote_copy(
             source, goal, send_sem, recv_sem, device_id=target, device_id_type=MESH
         )
+
+    def block_of(place, s, p):
+        return place * 4 + jnp.where(even, s * 2 + p, p * 2 + s)
 
     def local(block, piece):
         return pltpu.make_async_copy(
@@ -622,42 +654,45 @@
             across_c,
         )
 
-    def over_y(place, side):
-        pair = place * 2 + side
+    def over_p(place, s):
+        pair = place * 2 + s
         return remote(
-            total.at[pair * 2 + 1 - y], far_y.at[pair], y_send.at[pair], y_recv.at[pair], across_y
-        )
-
-    def over_x(place):
+            total.at[block_of(place, s, 1 - own_p)],
+            far_p.at[pair],
+            p_send.at[pair],
+            p_recv.at[pair],
+            across_p,
+        )
+
+    def over_s(place):
         return remote(
-            total.at[(place * 2 + 1 - x) * 2 + y],
-            far_x.at[place],
-            x_send.at[place],
-            x_recv.at[place],
-            across_x,
+            total.at[block_of(place, 1 - own_s, own_p)],
+            far_s.at[place],
+            s_send.at[place],
+            s_recv.at[place],
+            across_s,
         )
 
     def rise(place):
-        block = (place * 2 + x) * 2 + y
+        block = block_of(place, own_s, own_p)
         return remote(
             total.at[block], from_low.at[place], u_send.at[place], u_recv.at[place], up
         )
 
     def fall(place):
-        block = (place * 2 + x) * 2 + y
+        block = block_of(place, own_s, own_p)
         return remote(
             total.at[block], from_high.at[place], d_send.at[place], d_recv.at[place], down
         )
 
     def own_rows(send_sem, target):
-        mine = z * 2 + x
-        return remote(rows_ref, rows_out.at[mine], send_sem, r_recv.at[mine], target)
+        return remote(rows_ref, rows.at[dp], send_sem, r_recv.at[dp], target)
 
     def rows_on(place, send_sem, target):
         there = place * 2 + x
-        return remote(rows_out.at[there], rows_out.at[there], send_sem, r_recv.at[there], target)
-
-    own = pltpu.make_async_copy(rows_ref, rows_out.at[z * 2 + x], own_sem)
+        return remote(rows.at[there], rows.at[there], send_sem, r_recv.at[there], target)
+
+    own = pltpu.make_async_copy(rows_ref, rows.at[dp], own_sem)
     own.start()
 
     @pl.when(z < depth - 1)
@@ -669,14 +704,18 @@
         own_rows(rd_send.at[0], down).start()
 
     own_rows(rx_send.at[z], across_x).start()
+
     for turn in range(2):
-        for side in (1 - x, x):
+        for s, s_there in ((1 - own_s, 1 - own_p), (own_s, own_p)):
+            p, p_there = (1 - own_p, 1 - own_s) if turn == 0 else (own_p, own_s)
 
             def launch(place):
-                block = (place * 2 + side) * 2 + (1 - y if turn == 0 else y)
                 for piece in range(3):
-                    over_c(block, piece).start()
-                    local(block, piece).start()
+                    over_c(
+                        place * 4 + jnp.where(even, p_there * 2 + s_there, s_there * 2 + p_there),
+                        piece,
+                    ).start()
+                    local(block_of(place, s, p), piece).start()
 
             by_distance(depth, z, launch)
 
@@ -685,17 +724,23 @@
             local(block, piece).wait()
             over_c(block, piece).wait_recv()
 
-    for side in (1 - x, x):
-
-        def give_y(place):
-            block = (place * 2 + side) * 2 + 1 - y
-            ready(block)
-            add_into(total, block, (far_c, block))
-            over_y(place, side).start()
-
-        by_distance(depth, z, give_y)
-
-    def rows_step(step):
+    def give_p():
+        for s in (1 - own_s, own_s):
+
+            def give(place):
+                block = block_of(place, s, 1 - own_p)
+                ready(block)
+                add_into(total, block, (far_c, block))
+                over_p(place, s).start()
+
+            by_distance(depth, z, give)
+
+    @pl.when(even)
+    def early():
+        give_p()
+
+    for step in range(1, depth):
+
         @pl.when(z - step >= 0)
         def risen():
             rows_on(z - step, ru_send.at[step], up).wait_recv()
@@ -716,29 +761,110 @@
 
             rows_on(z + step, rx_send.at[z + step], across_x).start()
 
-    def give_x(place):
-        block = (place * 2 + 1 - x) * 2 + y
+    @pl.when(c == 1)
+    def late():
+        give_p()
+
+    own.wait()
+    for place in range(depth):
+        there = place * 2 + 1 - x
+        remote(
+            rows.at[there], rows.at[there], rx_send.at[place], r_recv.at[there], across_x
+        ).wait_recv()
+
+    height = part.shape[0]
+    count = places_ref.shape[1]
+
+    def collect(rank, core, goal):
+        @pl.loop(0, height // tile)
+        def tiles(index):
+            first = index * tile
+            at = (
+                (rank * 2 + core) * height
+                + first
+                + lax.broadcasted_iota(jnp.int32, (tile, count), 0)
+            )
+            picked = jnp.where(at == places_ref[...], 1.0, 0.0).astype(low)
+            goal[pl.ds(pl.multiple_of(first, tile), tile)] = product(
+                picked, rows[...].reshape(count, rows.shape[2])
+            ).astype(low)
+
+    def over_t(rank):
+        index = jnp.where(rank == y, 1, 0)
+        return remote(
+            given.at[index], far_t.at[index], t_send.at[index], t_recv.at[index], across_c
+        )
+
+    chunk = 80 if height % 80 == 0 else height
+
+    def pieces_of(act):
+        @pl.loop(0, height // chunk)
+        def step(index):
+            act(pl.ds(pl.multiple_of(index * chunk, chunk), chunk))
+
+    collect(1 - y, 1 - c, given.at[0])
+    over_t(1 - y).start()
+    collect(y, 1 - c, given.at[1])
+    over_t(y).start()
+    collect(1 - y, c, part)
+    over_t(1 - y).wait_recv()
+
+    def first_sum(lines):
+        part[lines] = (part[lines].astype(jnp.float32) + far_t[0, lines].astype(jnp.float32)).astype(
+            low
+        )
+
+    pieces_of(first_sum)
+    over_part = remote(part, far_part, ty_send, ty_recv, across_y)
+    over_part.start()
+    collect(y, c, mine)
+
+    def give_s(place):
+        block = block_of(place, 1 - own_s, own_p)
         ready(block)
-        over_y(place, 1 - x).wait_recv()
-        add_into(total, block, (far_c, block), (far_y, place * 2 + 1 - x))
-        over_x(place).start()
-
-    for step in range(depth - 1, -1, -1):
-        if step:
-            rows_step(depth - step)
-        for sign in (1, -1) if step else (1,):
-
-            @pl.when((z + sign * step >= 0) & (z + sign * step < depth))
-            def reached():
-                give_x(z + sign * step)
+        over_p(place, 1 - own_s).wait_recv()
+        add_into(total, block, (far_c, block), (far_p, place * 2 + 1 - own_s))
+        over_s(place).start()
+
+    by_distance(depth, z, give_s)
+
+    over_t(y).wait_recv()
+    over_part.wait_recv()
+
+    def second_sum(index, squares):
+        lines = pl.ds(pl.multiple_of(index * chunk, chunk), chunk)
+        value = (
+            mine[lines].astype(jnp.float32)
+            + far_t[1, lines].astype(jnp.float32)
+            + far_part[lines].astype(jnp.float32)
+        ).astype(low)
+        mine[lines] = value
+        value = value.astype(jnp.float32)
+        return squares + jnp.sum((value * value).reshape(-1, 8, value.shape[1]), axis=0)
+
+    squares = lax.fori_loop(
+        0, height // chunk, second_sum, jnp.zeros((8, part.shape[1]), jnp.float32)
+    )
+
+    def out_mine(index, target):
+        where = table_out.at[y * 2 + c]
+        return remote(mine, where, o_send.at[index], o_recv.at[y * 2 + c], target)
+
+    def out(rank, core):
+        where = table_out.at[rank * 2 + core]
+        return remote(where, where, o_send.at[2], o_recv.at[rank * 2 + core], across_c)
+
+    keep = pltpu.make_async_copy(mine, table_out.at[y * 2 + c], own_sem)
+    out_mine(0, across_y).start()
+    out_mine(1, across_c).start()
+    keep.start()
 
     def give_z(place):
-        block = (place * 2 + x) * 2 + y
-        pair = place * 2 + x
+        block = block_of(place, own_s, own_p)
         ready(block)
-        over_y(place, x).wait_recv()
-        over_x(place).wait_recv()
-        add_into(total, block, (far_c, block), (far_y, pair), (far_x, place))
+        over_p(place, own_s).wait_recv()
+        over_s(place).wait_recv()
+        add_into(total, block, (far_c, block), (far_p, place * 2 + own_s), (far_s, place))
 
         @pl.when(place > z)
         def rising():
@@ -759,8 +885,7 @@
             fall(place).start()
 
     by_distance(depth, z, give_z)
-    mine = (z * 2 + x) * 2 + y
-    grad_ref[...] = total[mine].astype(jnp.float32)
+    grad_ref[...] = total[block_of(z, own_s, own_p)].astype(jnp.float32)
 
     @pl.when(z > 0)
     def low_part():
@@ -772,16 +897,41 @@
         fall(z).wait_recv()
         grad_ref[...] = grad_ref[...] + from_high[z].astype(jnp.float32)
 
-    own.wait()
+    lines = lax.broadcasted_iota(jnp.int32, small.shape[1:], 0)
+    lanes = lax.broadcasted_iota(jnp.int32, small.shape[1:], 1)
+    last = (lines == small.shape[1] - 1) & (lanes == 0)
+    grad_squares = jnp.sum(grad_ref[...] * grad_ref[...])
+    small[0] = small_ref[...] + jnp.where(last, jnp.sum(squares) + grad_squares, 0.0)
+
+    def exchange(turn):
+        return remote(
+            small.at[turn], far_small.at[turn], e_send.at[turn], e_recv.at[turn], partners[turn]
+        )
+
+    for turn in range(len(partners)):
+        exchange(turn).start()
+        exchange(turn).wait_recv()
+        small[turn + 1] = small[turn] + far_small[turn]
+    small_out[...] = small[len(partners)]
+    out(1 - y, c).wait_recv()
+    out(1 - y, c).start()
+    out(y, 1 - c).wait_recv()
+    out(1 - y, 1 - c).wait_recv()
+
+    keep.wait()
+    out_mine(0, across_y).wait_send()
+    out_mine(1, across_c).wait_send()
+    out(1 - y, c).wait_send()
+    over_part.wait_send()
+    for turn in range(len(partners)):
+        exchange(turn).wait_send()
+    for rank in range(2):
+        over_t(rank).wait_send()
     for place in range(depth):
-        there = place * 2 + 1 - x
-        remote(
-            rows_out.at[there], rows_out.at[there], rx_send.at[place], r_recv.at[there], across_x
-        ).wait_recv()
         rows_on(place, rx_send.at[place], across_x).wait_send()
-        over_x(place).wait_send()
+        over_s(place).wait_send()
         for side in range(2):
-            over_y(place, side).wait_send()
+            over_p(place, side).wait_send()
             for rank in range(2):
                 for piece in range(3):
                     over_c((place * 2 + side) * 2 + rank, piece).wait_send()
@@ -803,195 +953,54 @@
             rows_on(z, rd_send.at[place], down).wait_send()
 
 
-def end(pieces, rows):
+def finish(pieces, rows, places, small, quarter, tile):
     blocks = pieces[0].shape[0]
     heights = [piece.shape[1] for piece in pieces]
     height, width = sum(heights), pieces[0].shape[2]
     depth = blocks // 8
+    turns = 3 + (depth - 1).bit_length()
     dma = pltpu.SemaphoreType.DMA
+    vmem = pl.BlockSpec(memory_space=pltpu.VMEM)
 
     def buffer(count):
         return pltpu.VMEM((count, height, width), low)
 
     return pl.pallas_call(
-        functools.partial(end_kernel, depth, heights),
+        functools.partial(finish_kernel, depth, heights, tile),
         out_shape=[
             jax.ShapeDtypeStruct((height, width), jnp.float32),
-            jax.ShapeDtypeStruct((depth * 2,) + rows.shape, low),
+            jax.ShapeDtypeStruct((4, quarter, width), low),
+            jax.ShapeDtypeStruct(small.shape, jnp.float32),
         ],
-        in_specs=[ANY] * 4,
-        out_specs=[pl.BlockSpec(memory_space=pltpu.VMEM), ANY],
+        in_specs=[ANY] * 4 + [vmem] * 2,
+        out_specs=[vmem, ANY, vmem],
         scratch_shapes=[buffer(depth * 4), buffer(depth * 4), buffer(depth * 2)]
         + [buffer(depth)] * 3
+        + [
+            pltpu.VMEM((depth * 2,) + rows.shape, low),
+            pltpu.VMEM((2, quarter, width), low),
+            pltpu.VMEM((2, quarter, width), low),
+            pltpu.VMEM((quarter, width), low),
+            pltpu.VMEM((quarter, width), low),
+            pltpu.VMEM((quarter, width), low),
+            pltpu.VMEM((turns + 1,) + small.shape, jnp.float32),
+            pltpu.VMEM((turns,) + small.shape, jnp.float32),
+        ]
         + [dma((depth * 4, 3))] * 3
         + [dma((depth * 2,))] * 2
         + [dma((depth,))] * 6
         + [dma(())]
         + [dma((depth,))] * 3
-        + [dma((depth * 2,))],
+        + [dma((depth * 2,))]
+        + [dma((2,))] * 2
+        + [dma(())] * 2
+        + [dma((3,)), dma((4,))]
+        + [dma((turns,))] * 2,
         compiler_params=pltpu.CompilerParams(
-            collective_id=1, has_side_effects=True, vmem_limit_bytes=58 * 2**20
+            collective_id=1, has_side_effects=True, vmem_limit_bytes=62 * 2**20
         ),
-        name="end",
-    )(*pieces, rows)
-
-
-def collect_kernel(step, places_ref, rows_ref, table_ref):
-    base = pl.program_id(0) * step
-    at = base + lax.broadcasted_iota(jnp.int32, (step, places_ref.shape[1]), 0)
-    picked = jnp.where(at == places_ref[...], 1.0, 0.0).astype(low)
-    table_ref[...] = product(picked, rows_ref[...]).astype(low)
-
-
-def collect(places, rows, height, step):
-    count, width = rows.shape
-    return pl.pallas_call(
-        functools.partial(collect_kernel, step),
-        grid=(height // step,),
-        out_shape=jax.ShapeDtypeStruct((height, width), low),
-        in_specs=[
-            pl.BlockSpec((1, count), lambda i: (0, 0)),
-            pl.BlockSpec((count, width), lambda i: (0, 0)),
-        ],
-        out_specs=pl.BlockSpec((step, width), lambda i: (i, 0)),
-        compiler_params=pltpu.CompilerParams(vmem_limit_bytes=58 * 2**20),
-        cost_estimate=pl.CostEstimate(
-            flops=2 * count * width * height,
-            bytes_accessed=2 * width * (count + height),
-            transcendentals=0,
-        ),
-        name="collect",
-    )(places, rows)
-
-
-def share_kernel(depth, table_ref, small_ref, table_out, small_out, *refs):
-    far_c, part, far_y, small, far_small = refs[0:5]
-    c_send, c_recv, y_send, y_recv, o_send, o_recv, s_send, s_recv = refs[5:13]
-    z, x, y, c = coordinates(depth)
-    partners = [device(z, x, y, 1 - c), device(z, x, 1 - y, c), device(z, 1 - x, y, c)]
-    reach = 1
-    while reach < depth:
-        partners.append(device(z ^ reach, x, y, c))
-        reach = reach * 2
-    barrier = pltpu.get_barrier_semaphore()
-    for target in partners:
-        pl.semaphore_signal(barrier, 1, device_id=target, device_id_type=MESH)
-    pl.semaphore_wait(barrier, len(partners))
-    across_c, across_y = partners[:2]
-
-    def remote(source, goal, send_sem, recv_sem, target):
-        return pltpu.make_async_remote_copy(
-            source, goal, send_sem, recv_sem, device_id=target, device_id_type=MESH
-        )
-
-    def over_c(rank):
-        return remote(
-            table_ref.at[rank * 2 + 1 - c],
-            far_c.at[rank],
-            c_send.at[rank],
-            c_recv.at[rank],
-            across_c,
-        )
-
-    def out(rank, core, index, target):
-        where = table_out.at[rank * 2 + core]
-        return remote(where, where, o_send.at[index], o_recv.at[rank * 2 + core], target)
-
-    height = part.shape[0]
-    chunk = 80 if height % 80 == 0 else height
-    over_c(1 - y).start()
-    over_c(y).start()
-    over_c(1 - y).wait_recv()
-
-    @pl.loop(0, height // chunk)
-    def first_sum(index):
-        rows = pl.ds(pl.multiple_of(index * chunk, chunk), chunk)
-        part[rows] = (
-            table_ref[(1 - y) * 2 + c, rows].astype(jnp.float32)
-            + far_c[1 - y, rows].astype(jnp.float32)
-        ).astype(low)
-
-    over_y = remote(part, far_y, y_send, y_recv, across_y)
-    over_y.start()
-    over_c(y).wait_recv()
-    over_y.wait_recv()
-    mine = y * 2 + c
-
-    def second_sum(index, squares):
-        rows = pl.ds(pl.multiple_of(index * chunk, chunk), chunk)
-        value = (
-            table_ref[mine, rows].astype(jnp.float32)
-            + far_c[y, rows].astype(jnp.float32)
-            + far_y[rows].astype(jnp.float32)
-        ).astype(low)
-        table_out[mine, rows] = value
-        value = value.astype(jnp.float32)
-        return squares + jnp.sum((value * value).reshape(-1, 8, 768), axis=0)
-
-    squares = lax.fori_loop(0, height // chunk, second_sum, jnp.zeros((8, 768), jnp.float32))
-    out(y, c, 0, across_y).start()
-    out(y, c, 1, across_c).start()
-    lines = lax.broadcasted_iota(jnp.int32, small.shape[1:], 0)
-    lanes = lax.broadcasted_iota(jnp.int32, small.shape[1:], 1)
-    last = (lines == small.shape[1] - 1) & (lanes == 0)
-    small[0] = small_ref[...] + jnp.where(last, jnp.sum(squares), 0.0)
-    for turn, target in enumerate(partners):
-        copy = remote(
-            small.at[turn], far_small.at[turn], s_send.at[turn], s_recv.at[turn], target
-        )
-        copy.start()
-        copy.wait_recv()
-        small[turn + 1] = small[turn] + far_small[turn]
-    small_out[...] = small[len(partners)]
-    out(1 - y, c, 0, across_y).wait_recv()
-    out(1 - y, c, 2, across_c).start()
-    out(y, 1 - c, 1, across_c).wait_recv()
-    out(1 - y, 1 - c, 2, across_c).wait_recv()
-    for turn, target in enumerate(partners):
-        remote(
-            small.at[turn], far_small.at[turn], s_send.at[turn], s_recv.at[turn], target
-        ).wait_send()
-    over_y.wait_send()
-    for rank in range(2):
-        over_c(rank).wait_send()
-    out(y, c, 0, across_y).wait_send()
-    out(y, c, 1, across_c).wait_send()
-    out(1 - y, c, 2, across_c).wait_send()
-
-
-def share(depth, table, small):
-    quarters, height, width = table.shape
-    turns = 3 + (depth - 1).bit_length()
-    dma = pltpu.SemaphoreType.DMA
-    vmem = pl.BlockSpec(memory_space=pltpu.VMEM)
-    return pl.pallas_call(
-        functools.partial(share_kernel, depth),
-        out_shape=[
-            jax.ShapeDtypeStruct(table.shape, low),
-            jax.ShapeDtypeStruct(small.shape, jnp.float32),
-        ],
-        in_specs=[vmem, vmem],
-        out_specs=[vmem, vmem],
-        scratch_shapes=[
-            pltpu.VMEM((2, height, width), low),
-            pltpu.VMEM((height, width), low),
-            pltpu.VMEM((height, width), low),
-            pltpu.VMEM((turns + 1,) + small.shape, jnp.float32),
-            pltpu.VMEM((turns,) + small.shape, jnp.float32),
-            dma((2,)),
-            dma((2,)),
-            dma(()),
-            dma(()),
-            dma((3,)),
-            dma((4,)),
-            dma((turns,)),
-            dma((turns,)),
-        ],
-        compiler_params=pltpu.CompilerParams(
-            collective_id=2, has_side_effects=True, vmem_limit_bytes=58 * 2**20
-        ),
-        name="share",
-    )(table, small)
+        name="finish",
+    )(*pieces, rows, places, small)
 
 
 def adam_step(weight, gradient, first, second, rate, decay):
@@ -1107,27 +1116,20 @@
         piece.astype(low).reshape(device_total, -1, D) for piece in block_grads
     ]
     rows_back = jnp.concatenate([chosen_grads, gradient.astype(low)], axis=0)
-    block_grads, rows_back = end(
-        [jnp.concatenate([d_qkv, d_out], axis=1), d_gu, d_down], rows_back
-    )
-    block_grads = block_grads.T
-
     step = 80 if shard_rows % 80 == 0 else 40
     quarter = -(-shard_rows // (step * head_count)) * step
     tile = quarter // 5 if quarter % 80 == 0 and quarter // 5 % 16 == 0 else step
-    table_grads = collect(
+    small = [d_gains[0], d_gains[1], d_gain_final, loss_sum[None], jnp.sum(weighting)[None]]
+    small = jnp.pad(jnp.concatenate(small), (0, 6 * 128 - 2)).reshape(-1, 128)
+    block_grads, table_grads, small = finish(
+        [jnp.concatenate([d_qkv, d_out], axis=1), d_gu, d_down],
+        rows_back,
         jnp.where(owned, local, -1).reshape(1, -1),
-        rows_back.reshape(-1, D),
-        quarter * head_count,
+        small,
+        quarter,
         tile,
     )
-    squares = jnp.sum(block_grads * block_grads)
-    small = jnp.concatenate([d_gains[0], d_gains[1], d_gain_final, loss_sum[None], jnp.sum(weighting)[None]])
-    small = jnp.pad(small, (0, 6 * 128 - 2)).reshape(-1, 128)
-    small = small.at[-1, 0].set(squares)
-    table_grads, small = share(
-        dp_count // 2, table_grads.reshape(head_count, quarter, D), small
-    )
+    block_grads = block_grads.T
     table_grads = table_grads.reshape(-1, D)[:shard_rows].astype(jnp.float32)
     squares = small[-1, 0]
     small = small.reshape(-1)

time: 739 us -> 682 us (0.923)
  Pallas kernels: 369 us -> 308 us
    pallas_call x3 -> x1, Pallas kernels: 240 us -> 179 us  [finish(): pl.pallas_call(functools.partial(finish_kernel, depth, heights, tile), ou...]
    dot_general x13, matrix products: 29.4 us -> 36.8 us  [product(): return jnp.dot(left, right, preferred_element_type=jnp.float32)]
    unnamed x297 -> x287, local copies, waits for them, and re-layouts: 37.3 us -> 36.7 us
  transfers between devices with their start and end apart: 7 -> 7, of which waited for: 2 -> 2; matrix products, arithmetic and copies ran while one was open for 20% -> 21% of each run, Pallas kernels for 0% -> 0%
where the time goes in v5:
time: 682 us; the launch traced here: 672 us
  Pallas kernels  308 us (45%)
  matrix products  154 us (23%)
  other arithmetic  87.9 us (13%)
  local copies, waits for them, and re-layouts  61.3 us (9%)
  waiting for transfers between devices  33.7 us (5%)
  between operations  24.3 us (4%)
    pallas_call x1, Pallas kernels, finish(): pl.pallas_call(functools.partial(finish_kernel, depth, heights, tile), ou...  179 us
    pallas_call x1, Pallas kernels, start(): pl.pallas_call(functools.partial(start_kernel, depth), out_shape=[jax.Sha...  129 us
    dot_general x13, matrix products, contract_rows(): lax.dot_general(left, right, (((0,), (0,)), ((), ())), preferred_element_...  66.3 us
    dot_general x13, matrix products, product(): return jnp.dot(left, right, preferred_element_type=jnp.float32)  36.8 us
    unnamed x287, local copies, waits for them, and re-layouts  36.7 us
    convert_element_type x1, other arithmetic, on_device(): table_new.astype(low)  28.9 us
    dot_general x9, matrix products, contract_cols(): lax.dot_general(left, right, (((1,), (1,)), ((), ())), preferred_element_...  23.2 us
    reduce_scatter x1, waiting for transfers between devices, on_device(): lax.psum_scatter(chosen_grads, ('dp', 'head'), scatter_dimension=0, tiled...  18.6 us
  transfers between devices with their start and end apart: 7, of which 2 were waited for; matrix products, arithmetic and copies ran while one was open for 21% of the time, Pallas kernels for 0%

profile of v5, /device:TPU:0, one launch (start us, length us, event | category | flops | bytes accessed | tf_op | source)
XLA Modules:
  0.0 672.4 jit_solution(14666347947747819278)
XLA Ops:
  11.7 129.2 %start.1 = (bf16[32,96,768]{2,1,0:T(8,128)(2,1)}, bf16[32,192,768]{2,1,0:T(8,128)(2,1)}, bf16[32,96,768]{2,1,0:T(8,128)(2,1)}, bf16[384,768]{1,0:T(8,128)(2,1)}, s32[8,2,1,128]{3,2,1,0:T(1,128)}) custom-call(bf16[96,768]{1,0:T(8,128)(2,1)} %get-tuple-element.120.refs_0_, bf16[192,768]{1,0:T(8,128)(2,1)} %slice.311.refs_1_, ...), custom_call_target="tpu_custom_call" | custom-call | tf_op jit(solution)/shard_map/start/pallas_call | solution.py:540
  142.7 2.3 slice.244
  153.0 2.0 pad_add_fusion.2
  162.5 3.1 dynamic-slice_bitcast_fusion.1
  167.0 2.4 slice.256
  172.6 2.7 copy.44
  175.3 2.7 copy.45
  177.9 2.0 fusion.166
  185.2 1.8 exponential_reduce_fusion.1
  187.9 4.0 convolution_convert_fusion.2
  193.9 3.8 fusion.156
  198.8 1.7 copy-done.9
  200.5 4.4 multiply_reduce_fusion.12
  210.6 2.1 fusion.12
  214.2 2.0 exponential_reduce_fusion
  216.9 1.7 convolution_convert_fusion.1
  219.3 2.7 fusion.158
  223.0 1.7 copy-done.10
  224.7 4.4 multiply_reduce_fusion.10
  229.1 15.0 %all-gather.2.cloned.1.call-done = bf16[4096,768]{1,0:T(8,128)(2,1)} async-done(((bf16[128,768]{1,0:T(8,128)(2,1)}), bf16[4096,768]{1,0:T(8,128)(2,1)}) %all-gather.2.cloned.1.call-update) | async-done | bytes 6291472 | tf_op jit(solution)/shard_map/all_gather | solution.py:1066
  244.1 4.7 fusion.175
  249.6 3.6 fusion.11
  253.3 2.6 multiply_reduce_fusion.2
  256.2 2.4 multiply_convert_fusion.5
  259.0 3.4 multiply_reduce_fusion.4
  265.0 1.9 copy.42
  267.0 5.6 multiply_reduce_fusion.1
  272.6 1.7 convolution_bitcast_fusion.1
  274.3 2.3 multiply_convert_fusion.1
  280.2 4.6 convolution_convert_fusion
  284.8 10.6 %fusion.40 = f32[6144,768]{1,0:T(8,128)} fusion(bf16[256,3072]{1,0:T(8,128)(2,1)} %copy-done.79, bf16[256,3072]{1,0:T(8,128)(2,1)S(1)} %copy-done.78, f32[256,768]{1,0:T(8,128)S(1)} %get-tuple-element.155, f32[256]{0:T(256)S(1)} %get-tuple-element.138, f32[768]{0:T(1024)S(1)} %get-tuple-element.67), kind=kOutput, calls=%fused_computation.78 | convolution fusion | flops 2422800384 | bytes 22810624 | tf_op jit(solution)/shard_map/dot_general | solution.py:36
  297.6 2.0 fusion.122
  299.7 5.5 fusion.125
  309.7 2.0 copy-done.5
  311.9 1.9 multiply_reduce_fusion.5
  314.2 5.1 multiply_convert_fusion.3
  319.4 3.4 multiply_reduce_fusion.3
  325.6 1.9 copy.43
  327.5 5.8 multiply_reduce_fusion
  333.4 1.7 multiply_convert_fusion
  340.5 4.1 fusion.157
  344.6 14.6 %add_convert_fusion = bf16[6144,768]{1,0:T(8,128)(2,1)} fusion(f32[6144,768]{1,0:T(8,128)} %fusion.40, bf16[256,3072]{1,0:T(8,128)(2,1)} %copy-done.87, bf16[256,3072]{1,0:T(8,128)(2,1)} %copy-done.86, f32[256,768]{1,0:T(8,128)} %get-tuple-element.149, f32[768]{0:T(1024)S(1)} %get-tuple-element.67, f32[256]{0:T(256)S(1)} %copy-done.102), kind=kOutput, calls=%fused_computation | convolution fusion | flops 2432237568 | bytes 32247808 | tf_op jit(solution)/shard_map/dot_general | solution.py:36
  359.2 3.9 add_convert_fusion.3
  363.1 7.6 %add_convert_fusion.1 = bf16[3072,768]{1,0:T(8,128)(2,1)} fusion(f32[3072,768]{1,0:T(8,128)} %fusion.125, bf16[256,3072]{1,0:T(8,128)(2,1)S(1)} %copy-done.50, f32[256,768]{1,0:T(8,128)S(1)} %copy-done.46), kind=kOutput, calls=%fused_computation.6 | convolution fusion | flops 1212874752 | bytes 16515072 | tf_op jit(solution)/shard_map/dot_general | solution.py:36
  373.0 2.1 broadcast_multiply_fusion
  377.0 2.7 fusion.88
  382.3 5.3 add_convert_fusion.2
  387.7 2.8 pad_maximum_fusion.refs_0_
  390.7 18.6 %reduce-scatter.2.cloned.1.call-done = bf16[128,768]{1,0:T(8,128)(2,1)} async-done(((bf16[4096,768]{1,0:T(8,128)(2,1)}), bf16[128,768]{1,0:T(8,128)(2,1)}) %reduce-scatter.2.cloned.1.call-update) | async-done | bytes 196624 | tf_op jit(solution)/shard_map/reduce_scatter | solution.py:1101
  409.4 1.8 pad_maximum_fusion.15.refs_3_
  411.1 178.9 %finish.1 = (f32[384,768]{1,0:T(8,128)}, bf16[4,1040,768]{2,1,0:T(8,128)(2,1)}, f32[24,128]{1,0:T(8,128)}) custom-call(bf16[32,96,768]{2,1,0:T(8,128)(2,1)} %pad_maximum_fusion.refs_0_, bf16[32,192,768]{2,1,0:T(8,128)(2,1)} %bitcast.195, bf16[32,96,768]{2,1,0:T(8,128)(2,1)} %bitcast.218, bf16[384,768]{1,0:T(8,128)(2,1)} %pad_maximum_fusion.15.refs_3_, ...), custom_call_target="tpu_custom_call" | custom-call | tf_op jit(solution)/shard_map/finish/pallas_call | solution.py:968
  591.4 2.0 multiply_reduce_fusion.14
  600.6 2.1 fusion.50
  602.7 2.0 fusion.59
  604.8 2.2 fusion.65
  606.9 2.0 fusion.71
  609.7 3.1 fusion.53
  612.8 2.9 fusion.62
  615.7 3.0 fusion.68
  618.6 2.8 fusion.74
  622.0 2.7 fusion.162
  624.7 2.7 copy.48
  627.3 2.2 copy.51
  634.3 28.9 %fusion.160 = (bf16[4000,768]{1,0:T(8,128)(2,1)}, f32[4000,768]{1,0:T(8,128)}, f32[4000,768]{1,0:T(8,128)}, f32[4000,768]{1,0:T(8,128)}) fusion(f32[4000,768]{1,0:T(8,128)} %refs_3_.1, f32[]{:T(128)S(6)} %div.137, bf16[4160,768]{1,0:T(8,128)(2,1)} %bitcast.222, f32[4000,768]{1,0:T(8,128)} %param.26, f32[4000,768]{1,0:T(8,128)} %param.27), kind=kLoop, calls=%fused_computation.316 | loop fusion | flops 55296000 | bytes 86016000 | tf_op jit(solution)/shard_map/convert_element_type | solution.py:1184
  (409 shorter events, 83.4 us)
Async XLA Ops:
  7.2 141.8 %copy-start = (s32[2,1,3]{2,1,0:T(1,128)S(1)}, s32[2,1,3]{2,1,0:T(1,128)}, u32[]{:S(2)}) copy-start(s32[2,1,3]{2,1,0:T(1,128)} %param.17) | copy-start | bytes 76
  7.2 236.9 %all-gather.2.cloned.1.call-start = ((), (), s32[]{:S(2)}) async-start(), calls=%async_computation.1 | async-start | bytes 6488064 | tf_op jit(solution)/shard_map/all_gather | solution.py:1066
  9.4 131.5 %copy-start.33 = (f32[768,384]{0,1:T(8,128)}, f32[768,384]{0,1:T(8,128)S(1)}, u32[]{:S(2)}) copy-start(f32[768,384]{0,1:T(8,128)S(1)} %copy.41) | copy-start | bytes 3538948
  145.0 60.5 %copy-start.4 = (bf16[32,72,768]{2,1,0:T(8,128)(2,1)}, bf16[32,72,768]{2,1,0:T(8,128)(2,1)S(1)}, u32[]{:S(2)}) copy-start(bf16[32,72,768]{2,1,0:T(8,128)(2,1)S(1)} %slice.244) | copy-start | bytes 10616836
  153.0 4.5 copy-start.12
  159.7 22.6 %collective-permute-start = (bf16[256,24,64]{0,2,1:T(8,128)(2,1)}, bf16[256,24,64]{0,2,1:T(8,128)(2,1)}, u32[]{:S(2)}, u32[]{:S(2)}) collective-permute-start(bf16[256,24,64]{0,2,1:T(8,128)(2,1)} %pad_maximum_fusion.11), channel_id=1, source_target_pairs={{0,1},{1,0},{2,3},{3,2},{4,5},{5,4},{6,7},{7,6},{8,9},{9,8},{10,11... | collective-permute-start | bytes 2359304 | tf_op jit(solution)/shard_map/ppermute | solution.py:112
  161.9 247.4 %reduce-scatter.2.cloned.1.call-start = ((), (), s32[]{:S(2)}) async-start(), calls=%async_computation.2 | async-start | bytes 6488064 | tf_op jit(solution)/shard_map/reduce_scatter | solution.py:1101
  162.5 6.9 %copy-start.100 = (s32[8,2,1,128]{3,2,1,0:T(1,128)S(1)}, s32[8,2,1,128]{3,2,1,0:T(1,128)}, u32[]{:S(2)}) copy-start(s32[8,2,1,128]{3,2,1,0:T(1,128)} %get-tuple-element.26) | copy-start | bytes 24580
  165.5 43.4 %collective-permute-start.2 = (bf16[128,4096]{1,0:T(8,128)(2,1)}, bf16[128,4096]{1,0:T(8,128)(2,1)}, u32[]{:S(2)}, u32[]{:S(2)}) collective-permute-start(bf16[128,4096]{1,0:T(8,128)(2,1)} %get-tuple-element.98), channel_id=1, source_target_pairs={{0,2},{1,3},{2,0},{3,1},{4,6},{5,7},{6,4},{7,5},{8,10},{9,11},{10,... | collective-permute-start | bytes 3145736 | tf_op jit(solution)/shard_map/ppermute | solution.py:112
  177.9 5.9 copy-start.65
  182.2 34.0 %copy-start.30 = (pred[256,512]{1,0:T(8,128)(4,1)}, pred[256,512]{1,0:T(8,128)(4,1)S(1)}, u32[]{:S(2)}) copy-start(pred[256,512]{1,0:T(8,128)(4,1)S(1)} %compare_and_fusion) | copy-start | bytes 393220
  187.0 6.9 %slice-start.4 = ((s8[9437184]{0:T(1024)(128)(4,1)}), s8[4194304]{0:T(1024)(128)(4,1)S(1)}, s32[]{:S(2)}) async-start(s8[9437184]{0:T(1024)(128)(4,1)} %bitcast.196), calls=%async_computation.7 | async-start | bytes 8388608
  187.9 6.1 slice-start.5
  187.9 6.1 slice-start.6
  200.5 4.4 copy-start.49
  204.9 13.8 %copy-start.16 = (f32[256,768]{1,0:T(8,128)}, f32[256,768]{1,0:T(8,128)S(1)}, u32[]{:S(2)}) copy-start(f32[256,768]{1,0:T(8,128)S(1)} %get-tuple-element.151) | copy-start | bytes 2359300
  208.0 4.8 copy-start.67
  208.0 8.2 %copy-start.63 = (bf16[256,12,64]{0,2,1:T(8,128)(2,1)}, bf16[256,12,64]{0,2,1:T(8,128)(2,1)S(1)}, u32[]{:S(2)}) copy-start(bf16[256,12,64]{0,2,1:T(8,128)(2,1)S(1)} %get-tuple-element.89) | copy-start | bytes 1179652
  208.2 4.5 collective-permute-start.1
  224.7 4.4 copy-start.35
  229.1 26.7 %copy-start.69 = (f32[256,768]{1,0:T(8,128)}, f32[256,768]{1,0:T(8,128)S(1)}, u32[]{:S(2)}) copy-start(f32[256,768]{1,0:T(8,128)S(1)} %get-tuple-element.157) | copy-start | bytes 2359300
  248.8 4.4 copy-start.119
  249.6 6.5 slice-start.15
  249.6 6.5 slice-start.21
  253.3 5.3 slice-start.7
  253.3 5.4 slice-start.8
  256.1 6.3 copy-start.43
  262.4 4.6 copy-start.31
  263.8 8.8 %slice-start.2 = ((s8[6291456]{0:T(1024)(128)(4,1)}), s8[2097152]{0:T(1024)(128)(4,1)S(1)}, s32[]{:S(2)}) async-start(s8[6291456]{0:T(1024)(128)(4,1)} %bitcast.193), calls=%async_computation.5 | async-start | bytes 4194304
  267.0 5.6 slice-start.3
  267.0 5.6 copy-start.85
  274.3 4.8 copy-start.71
  280.2 4.6 copy-start.78
  284.7 10.6 %copy-start.81 = (bf16[256,12,64]{0,2,1:T(8,128)(2,1)S(1)}, bf16[256,12,64]{0,2,1:T(8,128)(2,1)}, u32[]{:S(2)}) copy-start(bf16[256,12,64]{0,2,1:T(8,128)(2,1)} %slice.524) | copy-start | bytes 1179652
  295.5 9.7 %collective-permute-start.3 = (bf16[256,24,64]{0,2,1:T(8,128)(2,1)S(1)}, bf16[256,24,64]{0,2,1:T(8,128)(2,1)S(1)}, u32[]{:S(2)}, u32[]{:S(2)}) collective-permute-start(bf16[256,24,64]{0,2,1:T(8,128)(2,1)S(1)} %pad_maximum_fusion.13), channel_id=1, source_target_pairs={{0,1},{1,0},{2,3},{3,2},{4,5},{5,4},{6,7},{7,6},{8,9},{9,8},{10,11... | collective-permute-start | bytes 2359304 | tf_op jit(solution)/shard_map/ppermute | solution.py:112
  299.7 5.5 slice-start.18
  299.7 5.5 slice-start.19
  299.7 5.8 copy-start.90
  299.7 14.4 %slice-start.13 = ((s8[6291456]{0:T(1024)(128)(4,1)}), s8[4194304]{0:T(1024)(128)(4,1)S(1)}, s32[]{:S(2)}) async-start(s8[6291456]{0:T(1024)(128)(4,1)} %bitcast.214), calls=%async_computation.16 | async-start | bytes 8388608
  307.2 6.8 %slice-start.14 = ((s8[6291456]{0:T(1024)(128)(4,1)}), s8[2097152]{0:T(1024)(128)(4,1)S(1)}, s32[]{:S(2)}) async-start(s8[6291456]{0:T(1024)(128)(4,1)} %bitcast.214), calls=%async_computation.17 | async-start | bytes 4194304
  309.7 4.1 copy-start.41
  311.9 7.4 %slice-start.10 = ((s8[9437184]{0:T(1024)(128)(4,1)}), s8[4194304]{0:T(1024)(128)(4,1)S(1)}, s32[]{:S(2)}) async-start(s8[9437184]{0:T(1024)(128)(4,1)} %bitcast.203), calls=%async_computation.13 | async-start | bytes 8388608
  314.1 8.7 %copy-start.45 = (f32[256,768]{1,0:T(8,128)}, f32[256,768]{1,0:T(8,128)S(1)}, u32[]{:S(2)}) copy-start(f32[256,768]{1,0:T(8,128)S(1)} %subtract_add_fusion.1) | copy-start | bytes 2359300
  314.1 5.2 slice-start.11
  314.1 5.2 slice-start.12
  314.1 5.2 copy-start.15
  314.1 5.2 copy-start.102
  327.5 5.8 slice-start
  327.5 5.9 slice-start.1
  327.5 5.9 copy-start.32
  327.5 5.9 copy-start.95
  340.2 30.5 %collective-permute-start.4 = (bf16[256,24,64]{0,2,1:T(8,128)(2,1)}, bf16[256,24,64]{0,2,1:T(8,128)(2,1)}, u32[]{:S(2)}, u32[]{:S(2)}) collective-permute-start(bf16[256,24,64]{0,2,1:T(8,128)(2,1)} %pad_maximum_fusion.14), channel_id=1, source_target_pairs={{0,1},{1,0},{2,3},{3,2},{4,5},{5,4},{6,7},{7,6},{8,9},{9,8},{10,11... | collective-permute-start | bytes 2359304 | tf_op jit(solution)/shard_map/ppermute | solution.py:112
  363.1 7.6 %slice-start.17 = ((f32[512,12,64]{0,2,1:T(8,128)}), f32[256,12,64]{0,2,1:T(8,128)S(1)}, s32[]{:S(2)}) async-start(f32[512,12,64]{0,2,1:T(8,128)} %copy-done.51), calls=%async_computation.20 | async-start | bytes 1572864 | tf_op jit(solution)/shard_map/slice | solution.py:155
  363.1 7.6 %slice-start.20 = ((f32[512,12,64]{0,2,1:T(8,128)}), f32[256,12,64]{0,2,1:T(8,128)S(1)}, s32[]{:S(2)}) async-start(f32[512,12,64]{0,2,1:T(8,128)} %copy-done.72), calls=%async_computation.23 | async-start | bytes 1572864 | tf_op jit(solution)/shard_map/slice | solution.py:155
  363.1 9.2 %copy-start.93 = (f32[256,64]{0,1:T(8,128)S(1)}, f32[256,64]{0,1:T(8,128)}, u32[]{:S(2)}) copy-start(f32[256,64]{0,1:T(8,128)} %copy-done.91) | copy-start | bytes 196612
  382.3 5.3 copy-start.54
  604.8 4.1 copy-start.55
  604.8 4.1 copy-start.56
  615.7 6.3 copy-start.34
  627.3 6.3 copy-start.97
  627.3 6.3 copy-start.99
  627.3 6.3 copy-start.107
  627.3 6.3 copy-start.108
  634.3 28.9 %copy-start.1 = (s32[2,1,3]{2,1,0:T(1,128)S(1)}, s32[2,1,3]{2,1,0:T(1,128)}, u32[]{:S(2)}) copy-start(s32[2,1,3]{2,1,0:T(1,128)} %param.17) | copy-start | bytes 76
  (86 other events, 207.2 us)
Sparse Core Ops, SparseCore 0:
  162.1 82.0 all-gather.1
  296.5 112.7 reduce-scatter.1

commit v6 on v5

--- a/solution.py
+++ b/solution.py
@@ -271,7 +271,7 @@
                     lines, axis=0
                 ).astype(low)
 
-        load(0, lambda index: vocab_ref[(group * 4 + head) * part + index])
+        load(0, lambda index: vocab_ref[(head * groups + group) * part + index])
         for second in range(2):
             load(part + second * tokens, lambda index: ids[group, second, 0, index] >> 1)
 
@@ -1003,7 +1003,7 @@
     )(*pieces, rows, places, small)
 
 
-def adam_step(weight, gradient, first, second, rate, decay):
+def moments(gradient, first, second):
     first_new = beta_one * first + (1.0 - beta_one) * gradient
     second_new = beta_two * second + (1.0 - beta_two) * gradient * gradient
     direction = (
@@ -1011,7 +1011,200 @@
         / (1.0 - beta_one**STEP)
         / (jnp.sqrt(second_new / (1.0 - beta_two**STEP)) + adam_eps)
     )
-    return (weight - rate * (direction + decay * weight), first_new, second_new)
+    return direction, first_new, second_new
+
+
+def update_kernel(steps, cuts, *refs):
+    table_ref, table_m_ref, table_v_ref, table_g_ref = refs[0:4]
+    small_ref, sums_ref, gains_ref, gains_m_ref, gains_v_ref = refs[4:9]
+    grad_ref, block_ref, block_m_ref, block_v_ref, bases_ref = refs[9:14]
+    table_new, table_m_new, table_v_new, table_low = refs[14:18]
+    values_ref, gains_new, gains_m_new, gains_v_new = refs[18:22]
+    block_new, block_m_new, block_v_new, block_low = refs[22:26]
+    bases, turned, factor_ref, bases_sem = refs[26:30]
+    now = pl.program_id(0)
+
+    def base(index):
+        return pltpu.make_async_copy(bases_ref.at[index], bases.at[index], bases_sem.at[index])
+
+    @pl.when(now == 0)
+    def begin():
+        for index in range(4):
+            base(index).start()
+        lines = lax.broadcasted_iota(jnp.int32, small_ref.shape, 0)
+        lanes = lax.broadcasted_iota(jnp.int32, small_ref.shape, 1)
+
+        def value_at(place):
+            chosen = (lines == place // 128) & (lanes == place % 128)
+            return jnp.sum(jnp.where(chosen, small_ref[...], 0.0), axis=(0, 1), keepdims=True)
+
+        count = value_at(3 * D + 1)
+        gain_grads = sums_ref[...] / count
+        squares = value_at((small_ref.shape[0] - 1) * 128) / (count * count)
+        norm = jnp.sqrt(squares + jnp.sum(gain_grads * gain_grads, axis=(0, 1), keepdims=True))
+        clip = jnp.minimum(1.0, clip_norm / norm)
+        factor_ref[...] = jnp.broadcast_to(clip / count, factor_ref.shape)
+        spots = lax.broadcasted_iota(jnp.int32, values_ref.shape, 1)
+        values_ref[...] = jnp.where(spots == 0, value_at(3 * D) / count, norm)
+        direction, gains_m_new[...], gains_v_new[...] = moments(
+            gain_grads * clip, gains_m_ref[...], gains_v_ref[...]
+        )
+        gains_new[...] = gains_ref[...] - rate_gain * direction
+
+    factor = factor_ref[0:1, 0:1]
+    direction, table_m_new[...], table_v_new[...] = moments(
+        table_g_ref[...].astype(jnp.float32) * factor, table_m_ref[...], table_v_ref[...]
+    )
+    table_tile = table_ref[...]
+    table_tile = table_tile - rate_table * (direction + decay_rate * table_tile)
+    table_new[...] = table_tile
+    table_low[...] = table_tile.astype(low)
+
+    spots = lax.broadcasted_iota(jnp.int32, turned.shape, 1)
+
+    def columns(index, value):
+        mine = (spots >= cuts[index]) & (spots < cuts[index + 1])
+        return jnp.where(mine, value, 0.0).astype(low)
+
+    for index in range(4):
+
+        @pl.when(now == min(2 + index, steps - 1))
+        def rotate():
+            base(index).wait()
+            term = contract_rows(
+                bases[index].astype(low), columns(index, grad_ref[...] * factor_ref[0:1, 0:1])
+            )
+            turned[...] = term if index == 0 else turned[...] + term
+
+    @pl.when(now == min(6, steps - 1))
+    def move():
+        direction, block_m_new[...], block_v_new[...] = moments(
+            turned[...], block_m_ref[...], block_v_ref[...]
+        )
+        turned[...] = direction
+        block_new[...] = jnp.zeros_like(block_new)
+
+    for index in range(4):
+
+        @pl.when(now == min(7 + index, steps - 1))
+        def rotate_back():
+            block_new[...] += product(bases[index].astype(low), columns(index, turned[...]))
+
+    @pl.when(now == min(11, steps - 1))
+    def store():
+        block = block_ref[...]
+        block = block - rate_block * (block_new[...] + decay_rate * block)
+        block_new[...] = block
+        block_low[...] = block.astype(low)
+
+
+def update(cuts, tables, table_grads, small, gain_sums, gains, block_grads, blocks, bases):
+    rows, width = tables[0].shape
+    tile = max(
+        size
+        for size in range(8, 201, 8)
+        if rows % size == 0 and (size % 16 == 0 or rows % 16)
+    )
+    steps = rows // tile
+    f32 = jnp.float32
+
+    def whole(array):
+        return pl.BlockSpec(array.shape, lambda i: (0,) * array.ndim)
+
+    tiles = pl.BlockSpec((tile, width), lambda i: (i, 0))
+    table = jax.ShapeDtypeStruct(tables[0].shape, f32)
+    gain = jax.ShapeDtypeStruct(gains[0].shape, f32)
+    matrix = jax.ShapeDtypeStruct(blocks[0].shape, f32)
+    values = jax.ShapeDtypeStruct((8, 128), f32)
+    outs = [table] * 3 + [jax.ShapeDtypeStruct(table.shape, low)]
+    outs += [values] + [gain] * 3
+    outs += [matrix] * 3 + [jax.ShapeDtypeStruct(matrix.shape, low)]
+    return pl.pallas_call(
+        functools.partial(update_kernel, steps, cuts),
+        grid=(steps,),
+        out_shape=outs,
+        in_specs=[tiles] * 4
+        + [whole(small), whole(gain_sums)]
+        + [whole(gain)] * 3
+        + [whole(matrix)] * 4
+        + [ANY],
+        out_specs=[tiles] * 4 + [whole(values)] + [whole(gain)] * 3 + [whole(matrix)] * 4,
+        scratch_shapes=[
+            pltpu.VMEM(bases.shape, f32),
+            pltpu.VMEM(matrix.shape, f32),
+            pltpu.VMEM((8, 128), f32),
+            pltpu.SemaphoreType.DMA((4,)),
+        ],
+        compiler_params=pltpu.CompilerParams(vmem_limit_bytes=58 * 2**20),
+        name="update",
+    )(*tables, table_grads, small, gain_sums, *gains, block_grads, *blocks, bases)
+
+
+def loss_kernel(hidden_ref, gain_ref, near_ref, far_ref, own_ref, other_ref, weight_ref, *refs):
+    gradient_ref, gain_out, loss_ref, near_out, far_out, logits, teach = refs
+    head = lax.axis_index("head")
+    rows = hidden_ref.shape[0]
+    half = rows // 2
+    size = near_ref.shape[1]
+    hidden = hidden_ref[...]
+    r = lax.rsqrt(jnp.mean(hidden * hidden, axis=-1, keepdims=True) + eps_norm)
+    normed = (hidden * r * gain_ref[...]).astype(low)
+    parts = [(near_ref, near_out, 0, 0), (near_ref, near_out, 1, 2)]
+    parts += [(far_ref, far_out, 0, 1), (far_ref, far_out, 1, 3)]
+    for index, (source, unused, place, offset) in enumerate(parts):
+        columns = pl.ds(pl.multiple_of((head ^ offset) * size, size), size)
+        logits[index] = contract_cols(normed, source[place])
+        teach[index, :half] = own_ref[:, columns].astype(jnp.float32)
+        teach[index, half:] = other_ref[:, columns].astype(jnp.float32)
+
+    def log_total(values):
+        summit = jnp.max(jnp.max(values[...], axis=0), axis=-1, keepdims=True)
+        return summit + jnp.log(
+            jnp.sum(jnp.sum(jnp.exp(values[...] - summit[None]), axis=0), axis=-1, keepdims=True)
+        )
+
+    log_logits, log_teach = log_total(logits), log_total(teach)
+    weighting = weight_ref[...]
+    gradient = jnp.zeros((rows, hidden.shape[1]), jnp.float32)
+    loss = jnp.zeros((rows, 1), jnp.float32)
+    for index, (source, goal, place, offset) in enumerate(parts):
+        log_prob = logits[index] - log_logits
+        log_true = teach[index] - log_teach
+        true = jnp.exp(log_true)
+        loss = loss + jnp.sum(true * (log_true - log_prob), axis=-1, keepdims=True)
+        d_logits = ((jnp.exp(log_prob) - true) * weighting).astype(low)
+        goal[place] = contract_rows(d_logits, normed).astype(low)
+        gradient = gradient + product(d_logits, source[place])
+    loss_ref[...] = jnp.broadcast_to(
+        jnp.sum(loss * weighting, axis=0, keepdims=True), loss_ref.shape
+    )
+    scaled = gradient * gain_ref[...]
+    gradient_ref[...] = r * scaled - hidden * (r * r * r) * jnp.mean(
+        hidden * scaled, axis=-1, keepdims=True
+    )
+    gain_out[...] = jnp.sum(gradient * hidden * r, axis=0, keepdims=True)
+
+
+def distill(hidden, gain, near, far, own, other, weighting):
+    rows, width = hidden.shape
+    size = near.shape[1]
+    vmem = pl.BlockSpec(memory_space=pltpu.VMEM)
+    f32 = jnp.float32
+    return pl.pallas_call(
+        loss_kernel,
+        out_shape=[
+            jax.ShapeDtypeStruct(hidden.shape, f32),
+            jax.ShapeDtypeStruct(gain.shape, f32),
+            jax.ShapeDtypeStruct((8, 128), f32),
+            jax.ShapeDtypeStruct(near.shape, low),
+            jax.ShapeDtypeStruct(far.shape, low),
+        ],
+        in_specs=[vmem] * 7,
+        out_specs=[vmem] * 5,
+        scratch_shapes=[pltpu.VMEM((4, rows, size), f32)] * 2,
+        compiler_params=pltpu.CompilerParams(vmem_limit_bytes=58 * 2**20),
+        name="distill",
+    )(hidden, gain, near, far, own, other, weighting)
 
 
 def on_device(
@@ -1053,7 +1246,7 @@
     codes = codes.reshape(dp_count, 2 * tokens)
     weighting = (lax.dynamic_index_in_dim(codes, dp, 0, keepdims=False) & 1).astype(jnp.float32)
     vocab = lax.dynamic_index_in_dim(
-        vocab_ids.reshape(dp_count, head_count, part), head, 1, keepdims=False
+        vocab_ids.reshape(head_count, dp_count, part), head, 0, keepdims=False
     )
     local = jnp.concatenate([vocab, codes >> 1], axis=1) - offset
     owned = (local >= 0) & (local < shard_rows)
@@ -1063,14 +1256,15 @@
         gate_up.reshape(-1, D),
         down.reshape(-1, D),
     ]
-    chosen = lax.all_gather(rows_in[:part], ("dp", "head"), axis=0, tiled=True)
+    quarter = lax.all_gather(rows_in[:part], "dp", axis=0, tiled=True)
+    near = jnp.stack([quarter, swap(quarter, head_count, 2)])
+    far = swap(near, head_count, 1)
     hidden = rows_in[part:].astype(jnp.float32)
 
     teacher_own = lax.dynamic_index_in_dim(teacher, batch, 0, keepdims=False)
     teacher_far = swap(
         lax.dynamic_index_in_dim(teacher, 1 - batch, 0, keepdims=False), head_count, 2
     )
-    teacher_rows = jnp.concatenate([teacher_own, teacher_far], axis=0)
 
     run = jnp.arange(tokens, dtype=jnp.int32)
     places = jnp.concatenate([head * tokens + run, (head ^ 2) * tokens + run])
@@ -1091,14 +1285,17 @@
         hidden, saved = layer_forward(hidden, weights, gains, cosine, sine, allow, head_count)
         saves.append(saved)
 
-    normed = rms_norm(hidden, gains[2]).astype(low)
-    log_prob = jax.nn.log_softmax(contract_cols(normed, chosen), axis=-1)
-    teach = jax.nn.log_softmax(teacher_rows.astype(jnp.float32), axis=-1)
-    loss_sum = jnp.sum(weighting * jnp.sum(jnp.exp(teach) * (teach - log_prob), axis=-1))
-    logit_grads = ((jnp.exp(log_prob) - jnp.exp(teach)) * weighting[:, None]).astype(low)
-    chosen_grads = contract_rows(logit_grads, normed).astype(low)
-    gradient, d_gain_final = rms_back(hidden, gains[2], product(logit_grads, chosen))
-    chosen_grads = lax.psum_scatter(chosen_grads, ("dp", "head"), scatter_dimension=0, tiled=True)
+    gradient, d_gain_final, loss_sum, d_near, d_far = distill(
+        hidden, gains[2:3], near, far, teacher_own, teacher_far, weighting[:, None]
+    )
+    d_gain_final, loss_sum = d_gain_final[0], loss_sum[0, 0]
+    f32 = jnp.float32
+    d_near = d_near.astype(f32) + swap(d_far, head_count, 1).astype(f32)
+    d_near = d_near.astype(low)
+    d_quarter = d_near[0].astype(f32) + swap(d_near[1], head_count, 2).astype(f32)
+    chosen_grads = lax.psum_scatter(
+        d_quarter.astype(low), "dp", scatter_dimension=0, tiled=True
+    )
 
     block_grads = None
     d_gains = [0.0, 0.0]
@@ -1129,48 +1326,23 @@
         quarter,
         tile,
     )
-    block_grads = block_grads.T
-    table_grads = table_grads.reshape(-1, D)[:shard_rows].astype(jnp.float32)
-    squares = small[-1, 0]
-    small = small.reshape(-1)
-    count = small[3 * D + 1]
-    gain_grads = small[: 3 * D].reshape(3, D) / count
-    loss = small[3 * D] / count
-    grad_norm = jnp.sqrt(squares / (count * count) + jnp.sum(gain_grads * gain_grads))
-    clip = jnp.minimum(1.0, clip_norm / grad_norm)
-    factor = clip / count
-    block_grads = block_grads * factor
-    table_grads = table_grads * factor
-    gain_grads = gain_grads * clip
-
-    rotated = jnp.concatenate(
-        [
-            contract_rows(bases[index], block_grads[:, cuts[index] : cuts[index + 1]])
-            for index in range(4)
-        ],
-        axis=1,
-    )
-    block_m_new = beta_one * block_m + (1.0 - beta_one) * rotated
-    block_v_new = beta_two * block_v + (1.0 - beta_two) * rotated * rotated
-    direction = (
-        block_m_new
-        / (1.0 - beta_one**STEP)
-        / (jnp.sqrt(block_v_new / (1.0 - beta_two**STEP)) + adam_eps)
-    )
-    update = jnp.concatenate(
-        [product(bases[index], direction[:, cuts[index] : cuts[index + 1]]) for index in range(4)],
-        axis=1,
-    )
-    block_new = block - rate_block * (update + decay_rate * block)
-    table_new, table_m_new, table_v_new = adam_step(
-        table, table_grads, table_m, table_v, rate_table, decay_rate
-    )
-    gains_new, gains_m_new, gains_v_new = adam_step(
-        gains, gain_grads, gains_m, gains_v, rate_gain, 0.0
-    )
+    outs = update(
+        cuts,
+        [table, table_m, table_v],
+        table_grads.reshape(-1, D),
+        small,
+        small[: 3 * D // 128].reshape(3, D),
+        [gains, gains_m, gains_v],
+        block_grads.T,
+        [block, block_m, block_v],
+        bases,
+    )
+    table_new, table_m_new, table_v_new, table_low = outs[0:4]
+    values, gains_new, gains_m_new, gains_v_new = outs[4:8]
+    block_new, block_m_new, block_v_new, block_low = outs[8:12]
     return (
-        loss,
-        grad_norm,
+        values[0, 0],
+        values[0, 1],
         block_new,
         block_m_new,
         block_v_new,
@@ -1180,8 +1352,8 @@
         gains_new,
         gains_m_new,
         gains_v_new,
-        block_new.astype(low),
-        table_new.astype(low),
+        block_low,
+        table_low,
     )
 
 

time: 682 us -> 736 us (1.079)
  waiting for transfers between devices: 33.7 us -> 121 us
  Pallas kernels: 308 us -> 373 us
  matrix products: 154 us -> 114 us
  other arithmetic: 87.9 us -> 48.6 us
  local copies, waits for them, and re-layouts: 61.3 us -> 45.8 us
    pallas_call x0 -> x2, Pallas kernels: none -> 62.9 us  [the longest x1 49 us: update(): pl.pallas_call(functools.partial(update_kernel, steps, cuts), grid=(steps...]
    ppermute x5 -> x9, waiting for transfers between devices: 0.01 us -> 55.9 us  [swap(): lax.ppermute(value, 'head', [(h, h ^ offset) for h in range(head_count)])]
    reduce_scatter x1, waiting for transfers between devices: 18.6 us -> 57.6 us  [on_device(): lax.psum_scatter(d_quarter.astype(low), 'dp', scatter_dimension=0, tiled=...]
    convert_element_type x3, other arithmetic: 31.6 us -> 5.37 us  [the longest x1 3.74 us: on_device(): d_near = d_near.astype(low)]
    dot_general x13 -> x8, matrix products: 66.3 us -> 41.9 us  [contract_rows(): lax.dot_general(left, right, (((0,), (0,)), ((), ())), preferred_element_...]
    unnamed x287 -> x259, local copies, waits for them, and re-layouts: 36.7 us -> 16.4 us
    dot_general x13 -> x8, matrix products: 36.8 us -> 22 us  [product(): return jnp.dot(left, right, preferred_element_type=jnp.float32)]
    reduce_sum x5 -> x0, other arithmetic: 8.95 us -> none  [the longest x1 3.62 us: on_device(): jnp.sum(jnp.exp(teach) * (teach - log_prob), axis=-1)]
  transfers between devices with their start and end apart: 7 -> 11, of which waited for: 2 -> 4; matrix products, arithmetic and copies ran while one was open for 21% -> 21% of each run, Pallas kernels for 0% -> 18%
where the time goes in v6:
time: 736 us; the launch traced here: 728 us
  Pallas kernels  373 us (51%)
  waiting for transfers between devices  121 us (16%)
  matrix products  114 us (15%)
  other arithmetic  48.6 us (7%)
  local copies, waits for them, and re-layouts  45.8 us (6%)
  between operations  17.4 us (2%)
  starting transfers between devices  7.49 us (1%)
    pallas_call x1, Pallas kernels, finish(): pl.pallas_call(functools.partial(finish_kernel, depth, heights, tile), ou...  178 us
    pallas_call x1, Pallas kernels, start(): pl.pallas_call(functools.partial(start_kernel, depth), out_shape=[jax.Sha...  132 us
    reduce_scatter x1, waiting for transfers between devices, on_device(): lax.psum_scatter(d_quarter.astype(low), 'dp', scatter_dimension=0, tiled=...  57.6 us
    ppermute x9, waiting for transfers between devices, swap(): lax.ppermute(value, 'head', [(h, h ^ offset) for h in range(head_count)])  55.9 us
    pallas_call x1, Pallas kernels, update(): pl.pallas_call(functools.partial(update_kernel, steps, cuts), grid=(steps...  49 us
    dot_general x8, matrix products, contract_rows(): lax.dot_general(left, right, (((0,), (0,)), ((), ())), preferred_element_...  41.9 us
    dot_general x8, matrix products, contract_cols(): lax.dot_general(left, right, (((1,), (1,)), ((), ())), preferred_element_...  22.3 us
    dot_general x8, matrix products, product(): return jnp.dot(left, right, preferred_element_type=jnp.float32)  22 us
  transfers between devices with their start and end apart: 11, of which 4 were waited for; matrix products, arithmetic and copies ran while one was open for 21% of the time, Pallas kernels for 18%

profile of v6, /device:TPU:0, one launch (start us, length us, event | category | flops | bytes accessed | tf_op | source)
XLA Modules:
  0.0 727.7 jit_solution(10877980280308968101)
XLA Ops:
  7.3 3.2 dynamic-slice_bitcast_fusion
  10.5 3.0 collective-permute-start.4
  15.7 132.0 %start.1 = (bf16[32,96,768]{2,1,0:T(8,128)(2,1)}, bf16[32,192,768]{2,1,0:T(8,128)(2,1)}, bf16[32,96,768]{2,1,0:T(8,128)(2,1)}, bf16[384,768]{1,0:T(8,128)(2,1)}, s32[8,2,1,128]{3,2,1,0:T(1,128)}) custom-call(bf16[96,768]{1,0:T(8,128)(2,1)} %get-tuple-element.108.refs_0_, bf16[192,768]{1,0:T(8,128)(2,1)} %slice.261.refs_1_, ...), custom_call_target="tpu_custom_call" | custom-call | tf_op jit(solution)/shard_map/start/pallas_call | solution.py:540
  147.7 1.6 slice.233
  152.4 2.3 slice.205
  161.1 2.0 pad_add_fusion.2
  164.1 1.6 slice_negate_fusion.6
  168.4 2.4 slice.217
  175.0 1.5 pad_maximum_fusion.8
  176.6 1.3 fusion
  177.9 1.8 exponential_reduce_fusion.1
  180.6 4.0 convolution_convert_fusion.1
  184.7 1.5 multiply_reduce_fusion.10
  186.8 3.8 fusion.88
  191.6 1.7 copy-done.9
  193.3 4.4 multiply_reduce_fusion.9
  201.3 7.2 all-gather.2.cloned.1.call-done
  208.5 1.5 collective-permute-start.2
  212.2 1.3 fusion.1
  213.6 2.2 exponential_reduce_fusion
  215.8 28.6 %collective-permute-done.2 = bf16[1024,768]{1,0:T(8,128)(2,1)} collective-permute-done((bf16[1024,768]{1,0:T(8,128)(2,1)}, bf16[1024,768]{1,0:T(8,128)(2,1)}, u32[]{:S(2)}, u32[]{:S(2)}) %collective-permute-start.2) | collective-permute-done | bytes 1572896 | tf_op jit(solution)/shard_map/ppermute | solution.py:112
  244.3 3.5 pad_maximum_fusion.1.near_ref
  248.0 1.7 convolution_convert_fusion
  251.1 2.7 fusion.90
  254.7 1.7 copy-done.10
  256.5 5.2 convolution_add_fusion.1.hidden_ref
  261.7 13.9 %distill.1 = (f32[256,768]{1,0:T(8,128)}, f32[1,768]{1,0:T(1,128)}, f32[8,128]{1,0:T(8,128)}, bf16[2,1024,768]{2,1,0:T(8,128)(2,1)}, bf16[2,1024,768]{2,1,0:T(8,128)(2,1)}) custom-call(f32[256,768]{1,0:T(8,128)} %convolution_add_fusion.1.hidden_ref, f32[1,768]{1,0:T(1,128)} %get-tuple-element.117.gain_ref, bf16[2,1024,768]{2,1,0:T(8,128)(2,1)} %pad_maximum_fusion.1.near_ref, ...), custom_call_target="tpu_custom_call" | custom-call | tf_op jit(solution)/shard_map/distill/pallas_call | solution.py:1193
  275.6 6.5 multiply_convert_fusion.5
  282.5 3.4 multiply_reduce_fusion.3
  288.3 1.9 copy.36
  290.2 4.6 convolution_bitcast_fusion.1
  295.9 2.4 multiply_reduce_fusion.1
  298.3 2.0 multiply_convert_fusion.1
  305.8 11.1 %fusion.6 = f32[6144,768]{1,0:T(8,128)} fusion(bf16[256,3072]{1,0:T(8,128)(2,1)} %copy-done.72, bf16[256,3072]{1,0:T(8,128)(2,1)} %copy-done.71, f32[256,768]{1,0:T(8,128)S(1)} %copy-done.17, f32[256]{0:T(256)S(1)} %get-tuple-element.127, f32[768]{0:T(1024)S(1)} %get-tuple-element.71), kind=kOutput, calls=%fused_computation.38 | convolution fusion | flops 2422800384 | bytes 22810624 | tf_op jit(solution)/shard_map/dot_general | solution.py:36
  317.0 1.6 fusion.17
  321.1 1.8 copy-done.5
  323.1 1.9 multiply_reduce_fusion.4
  325.3 4.8 multiply_convert_fusion.3
  330.2 3.4 multiply_reduce_fusion.2
  337.2 4.7 convolution_bitcast_fusion
  342.0 2.4 multiply_reduce_fusion
  344.4 1.8 multiply_convert_fusion
  349.2 4.1 fusion.89
  353.4 5.2 fusion.53
  358.6 11.5 %add_convert_fusion = bf16[6144,768]{1,0:T(8,128)(2,1)} fusion(f32[6144,768]{1,0:T(8,128)} %fusion.6, bf16[256,3072]{1,0:T(8,128)(2,1)} %copy-done.80, bf16[256,3072]{1,0:T(8,128)(2,1)} %copy-done.79, f32[256,768]{1,0:T(8,128)S(1)} %copy-done.15, f32[768]{0:T(1024)S(1)} %get-tuple-element.71, f32[256]{0:T(256)S(1)} %get-tuple-element.123), kind=kOutput, calls=%fused_computation | convolution fusion | flops 2432237568 | bytes 32247808 | tf_op jit(solution)/shard_map/dot_general | solution.py:36
  370.1 3.7 add_convert_fusion.3
  374.0 1.5 collective-permute-start.8
  376.2 1.5 add_convert_fusion.4
  378.2 3.7 add_convert_fusion.1
  381.9 1.4 fusion.16
  383.3 27.3 %collective-permute-done.8 = bf16[1024,768]{1,0:T(8,128)(2,1)S(1)} collective-permute-done((bf16[1024,768]{1,0:T(8,128)(2,1)S(1)}, bf16[1024,768]{1,0:T(8,128)(2,1)S(1)}, u32[]{:S(2)}, u32[]{:S(2)}) %collective-permute-start.8) | collective-permute-done | bytes 1572896 | tf_op jit(solution)/shard_map/ppermute | solution.py:112
  410.6 1.6 fusion.4
  412.2 3.1 broadcast_multiply_fusion
  416.1 1.4 copy-done.6
  417.6 1.3 fusion.27
  419.0 1.4 concatenate.143
  421.0 4.3 add_convert_fusion.2
  425.3 2.8 pad_maximum_fusion.refs_0_
  428.3 57.6 %reduce-scatter.2.cloned.1.call-done = bf16[128,768]{1,0:T(8,128)(2,1)} async-done(((bf16[1024,768]{1,0:T(8,128)(2,1)}), bf16[128,768]{1,0:T(8,128)(2,1)}) %reduce-scatter.2.cloned.1.call-update) | async-done | bytes 196624 | tf_op jit(solution)/shard_map/reduce_scatter | solution.py:1296
  486.0 1.8 pad_maximum_fusion.14.refs_3_
  487.7 178.5 %finish.1 = (f32[384,768]{1,0:T(8,128)}, bf16[4,1040,768]{2,1,0:T(8,128)(2,1)}, f32[24,128]{1,0:T(8,128)}) custom-call(bf16[32,96,768]{2,1,0:T(8,128)(2,1)} %pad_maximum_fusion.refs_0_, bf16[32,192,768]{2,1,0:T(8,128)(2,1)} %bitcast.149, bf16[32,96,768]{2,1,0:T(8,128)(2,1)} %bitcast.174, bf16[384,768]{1,0:T(8,128)(2,1)} %pad_maximum_fusion.14.refs_3_, ...), custom_call_target="tpu_custom_call" | custom-call | tf_op jit(solution)/shard_map/finish/pallas_call | solution.py:968
  667.5 2.7 copy.38
  670.3 49.0 %update.1 = (f32[4000,768]{1,0:T(8,128)}, f32[4000,768]{1,0:T(8,128)}, f32[4000,768]{1,0:T(8,128)}, bf16[4000,768]{1,0:T(8,128)(2,1)}, f32[8,128]{1,0:T(8,128)},...) custom-call(f32[4000,768]{1,0:T(8,128)} %refs_0_.1, ...), custom_call_target="tpu_custom_call" | custom-call | tf_op jit(solution)/shard_map/update/pallas_call | solution.py:1122
  719.3 1.3 fusion.96
  (368 shorter events, 51.6 us)
Async XLA Ops:
  7.2 151.6 %copy-start = (s32[2,1,3]{2,1,0:T(1,128)S(1)}, s32[2,1,3]{2,1,0:T(1,128)}, u32[]{:S(2)}) copy-start(s32[2,1,3]{2,1,0:T(1,128)} %param.16) | copy-start | bytes 76
  7.2 6.2 copy-start.50
  7.2 201.3 %all-gather.2.cloned.1.call-start = ((), (), s32[]{:S(2)}) async-start(), calls=%async_computation.1 | async-start | bytes 1769472 | tf_op jit(solution)/shard_map/all_gather | solution.py:1259
  7.3 7.9 %copy-start.105 = (s32[2,128]{1,0:T(2,128)S(1)}, s32[2,128]{1,0:T(2,128)}, u32[]{:S(2)}) copy-start(s32[2,128]{1,0:T(2,128)} %param.17) | copy-start | bytes 3076
  7.3 7.8 %copy-start.106 = (s32[2,128]{1,0:T(2,128)S(1)}, s32[2,128]{1,0:T(2,128)}, u32[]{:S(2)}) copy-start(s32[2,128]{1,0:T(2,128)} %param.15) | copy-start | bytes 3076
  10.5 251.2 %collective-permute-start.4 = (bf16[128,4096]{1,0:T(8,128)(2,1)}, bf16[128,4096]{1,0:T(8,128)(2,1)}, u32[]{:S(2)}, u32[]{:S(2)}) collective-permute-start(bf16[128,4096]{1,0:T(8,128)(2,1)} %get-tuple-element.85), channel_id=1, source_target_pairs={{0,2},{1,3},{2,0},{3,1},{4,6},{5,7},{6,4},{7,5},{8,10},{9,11},{10,... | collective-permute-start | bytes 3145736 | tf_op jit(solution)/shard_map/ppermute | solution.py:112
  15.7 135.5 %copy-start.90 = (f32[3,768]{1,0:T(4,128)S(1)}, f32[3,768]{1,0:T(4,128)}, u32[]{:S(2)}) copy-start(f32[3,768]{1,0:T(4,128)} %refs_6_.1) | copy-start | bytes 27652
  149.3 336.6 %reduce-scatter.2.cloned.1.call-start = ((), (), s32[]{:S(2)}) async-start(), calls=%async_computation.2 | async-start | bytes 1769472 | tf_op jit(solution)/shard_map/reduce_scatter | solution.py:1296
  154.7 43.7 %copy-start.4 = (bf16[32,72,768]{2,1,0:T(8,128)(2,1)}, bf16[32,72,768]{2,1,0:T(8,128)(2,1)S(1)}, u32[]{:S(2)}) copy-start(bf16[32,72,768]{2,1,0:T(8,128)(2,1)S(1)} %slice.205) | copy-start | bytes 10616836
  167.8 7.2 collective-permute-start
  170.7 5.8 copy-start.61
  175.0 4.8 copy-start.30
  179.7 7.0 slice-start.4
  180.6 6.2 slice-start.5
  180.6 6.1 slice-start.6
  199.7 48.3 %copy-start.54 = (bf16[256,12,64]{0,2,1:T(8,128)(2,1)}, bf16[256,12,64]{0,2,1:T(8,128)(2,1)S(1)}, u32[]{:S(2)}) copy-start(bf16[256,12,64]{0,2,1:T(8,128)(2,1)S(1)} %fusion.45) | copy-start | bytes 1179652
  200.0 10.5 %copy-start.91 = (s32[8,2,1,128]{3,2,1,0:T(1,128)S(1)}, s32[8,2,1,128]{3,2,1,0:T(1,128)}, u32[]{:S(2)}) copy-start(s32[8,2,1,128]{3,2,1,0:T(1,128)} %get-tuple-element.42) | copy-start | bytes 24580
  201.1 12.4 %copy-start.63 = (bf16[256,12,64]{0,2,1:T(8,128)(2,1)}, bf16[256,12,64]{0,2,1:T(8,128)(2,1)S(1)}, u32[]{:S(2)}) copy-start(bf16[256,12,64]{0,2,1:T(8,128)(2,1)S(1)} %get-tuple-element.78) | copy-start | bytes 1179652
  201.1 46.9 %copy-start.59 = (bf16[256,12,64]{0,2,1:T(8,128)(2,1)}, bf16[256,12,64]{0,2,1:T(8,128)(2,1)S(1)}, u32[]{:S(2)}) copy-start(bf16[256,12,64]{0,2,1:T(8,128)(2,1)S(1)} %get-tuple-element.77) | copy-start | bytes 1179652
  201.1 11.1 %copy-start.31 = (pred[256,512]{1,0:T(8,128)(4,1)S(1)}, pred[256,512]{1,0:T(8,128)(4,1)}, u32[]{:S(2)}) copy-start(pred[256,512]{1,0:T(8,128)(4,1)} %copy-done.30) | copy-start | bytes 393220
  201.2 10.8 %collective-permute-start.1 = (bf16[256,24,64]{0,2,1:T(8,128)(2,1)S(1)}, bf16[256,24,64]{0,2,1:T(8,128)(2,1)S(1)}, u32[]{:S(2)}, u32[]{:S(2)}) collective-permute-start(bf16[256,24,64]{0,2,1:T(8,128)(2,1)S(1)} %pad_maximum_fusion.11), channel_id=1, source_target_pairs={{0,1},{1,0},{2,3},{3,2},{4,5},{5,4},{6,7},{7,6},{8,9},{9,8},{10,11... | collective-permute-start | bytes 2359304 | tf_op jit(solution)/shard_map/ppermute | solution.py:112
  208.5 35.8 %collective-permute-start.2 = (bf16[1024,768]{1,0:T(8,128)(2,1)}, bf16[1024,768]{1,0:T(8,128)(2,1)}, u32[]{:S(2)}, u32[]{:S(2)}) collective-permute-start(bf16[1024,768]{1,0:T(8,128)(2,1)} %all-gather.2.cloned.1.call-done), channel_id=1, source_target_pairs={{0,2},{1,3},{2,0},{3,1},{4,6},{5,7},{6,4},{7,5},{8,10},{9,11},{10,... | collective-permute-start | bytes 4718600 | tf_op jit(solution)/shard_map/ppermute | solution.py:112
  213.5 34.4 %copy-start.3 = (f32[12,256,512]{2,1,0:T(8,128)}, f32[12,256,512]{2,1,0:T(8,128)S(1)}, u32[]{:S(2)}) copy-start(f32[12,256,512]{2,1,0:T(8,128)S(1)} %get-tuple-element.140) | copy-start | bytes 18874372
  213.5 30.8 %copy-start.75 = (bf16[1024,768]{1,0:T(8,128)(2,1)S(1)}, bf16[1024,768]{1,0:T(8,128)(2,1)}, u32[]{:S(2)}) copy-start(bf16[1024,768]{1,0:T(8,128)(2,1)} %all-gather.2.cloned.1.call-done) | copy-start | bytes 4718596
  215.8 32.2 %copy-start.88 = (f32[12,256]{1,0:T(8,128)}, f32[12,256]{1,0:T(8,128)S(1)}, u32[]{:S(2)}) copy-start(f32[12,256]{1,0:T(8,128)S(1)} %log_add_fusion) | copy-start | bytes 36868
  244.3 6.1 slice-start.7
  247.9 13.8 %collective-permute-start.3 = (bf16[2,1024,768]{2,1,0:T(8,128)(2,1)}, bf16[2,1024,768]{2,1,0:T(8,128)(2,1)}, u32[]{:S(2)}, u32[]{:S(2)}) collective-permute-start(bf16[2,1024,768]{2,1,0:T(8,128)(2,1)} %pad_maximum_fusion.1.near_ref), channel_id=1, source_target_pairs={{0,1},{1,0},{2,3},{3,2},{4,5},{5,4},{6,7},{7,6},{8,9},{9,8},{10,11... | collective-permute-start | bytes 9437192 | tf_op jit(solution)/shard_map/ppermute | solution.py:112
  250.4 35.6 %copy-start.16 = (f32[256,768]{1,0:T(8,128)}, f32[256,768]{1,0:T(8,128)S(1)}, u32[]{:S(2)}) copy-start(f32[256,768]{1,0:T(8,128)S(1)} %get-tuple-element.142) | copy-start | bytes 2359300
  256.5 5.2 copy-start.45
  261.7 20.5 %slice-start.10 = ((s8[9437184]{0:T(1024)(128)(4,1)}), s8[1048576]{0:T(1024)(128)(4,1)S(1)}, s32[]{:S(2)}) async-start(s8[9437184]{0:T(1024)(128)(4,1)} %bitcast.156), calls=%async_computation.13 | async-start | bytes 2097152
  275.6 6.5 slice-start.11
  275.6 6.9 slice-start.12
  287.1 8.8 %slice-start.2 = ((s8[6291456]{0:T(1024)(128)(4,1)}), s8[2097152]{0:T(1024)(128)(4,1)S(1)}, s32[]{:S(2)}) async-start(s8[6291456]{0:T(1024)(128)(4,1)} %bitcast.147), calls=%async_computation.5 | async-start | bytes 4194304
  290.2 5.6 slice-start.3
  290.2 5.6 copy-start.44
  290.2 5.6 copy-start.78
  290.2 5.6 copy-start.89
  301.1 4.7 copy-start.17
  303.7 66.3 %collective-permute-start.7 = (bf16[2,1024,768]{2,1,0:T(8,128)(2,1)}, bf16[2,1024,768]{2,1,0:T(8,128)(2,1)}, u32[]{:S(2)}, u32[]{:S(2)}) collective-permute-start(bf16[2,1024,768]{2,1,0:T(8,128)(2,1)} %get-tuple-element.45), channel_id=1, source_target_pairs={{0,1},{1,0},{2,3},{3,2},{4,5},{5,4},{6,7},{7,6},{8,9},{9,8},{10,11... | collective-permute-start | bytes 9437192 | tf_op jit(solution)/shard_map/ppermute | solution.py:112
  304.7 12.2 %collective-permute-start.5 = (bf16[256,24,64]{0,2,1:T(8,128)(2,1)}, bf16[256,24,64]{0,2,1:T(8,128)(2,1)}, u32[]{:S(2)}, u32[]{:S(2)}) collective-permute-start(bf16[256,24,64]{0,2,1:T(8,128)(2,1)} %pad_maximum_fusion.12), channel_id=1, source_target_pairs={{0,1},{1,0},{2,3},{3,2},{4,5},{5,4},{6,7},{7,6},{8,9},{9,8},{10,11... | collective-permute-start | bytes 2359304 | tf_op jit(solution)/shard_map/ppermute | solution.py:112
  305.8 11.1 %slice-start.22 = ((f32[512,12,64]{0,2,1:T(8,128)}), f32[256,12,64]{0,2,1:T(8,128)S(1)}, s32[]{:S(2)}) async-start(f32[512,12,64]{0,2,1:T(8,128)} %copy-done.48), calls=%async_computation.25 | async-start | bytes 1572864 | tf_op jit(solution)/shard_map/slice | solution.py:155
  305.8 11.1 %copy-start.67 = (f32[256,12,64]{0,2,1:T(8,128)S(1)}, f32[256,12,64]{0,2,1:T(8,128)}, u32[]{:S(2)}) copy-start(f32[256,12,64]{0,2,1:T(8,128)} %slice.287) | copy-start | bytes 2359300
  305.8 12.7 %copy-start.83 = (bf16[256,24,64]{0,2,1:T(8,128)(2,1)S(1)}, bf16[256,24,64]{0,2,1:T(8,128)(2,1)}, u32[]{:S(2)}) copy-start(bf16[256,24,64]{0,2,1:T(8,128)(2,1)} %copy-done.81) | copy-start | bytes 2359300
  317.0 8.3 %slice-start.19 = ((s8[6291456]{0:T(1024)(128)(4,1)}), s8[4194304]{0:T(1024)(128)(4,1)S(1)}, s32[]{:S(2)}) async-start(s8[6291456]{0:T(1024)(128)(4,1)} %bitcast.172), calls=%async_computation.22 | async-start | bytes 8388608
  319.2 6.0 slice-start.20
  323.1 7.0 slice-start.13
  325.3 8.3 %copy-start.39 = (f32[256,768]{1,0:T(8,128)}, f32[256,768]{1,0:T(8,128)S(1)}, u32[]{:S(2)}) copy-start(f32[256,768]{1,0:T(8,128)S(1)} %subtract_add_fusion.1) | copy-start | bytes 2359300
  325.3 4.9 slice-start.14
  325.3 4.9 slice-start.15
  325.3 4.9 copy-start.14
  333.6 8.3 %slice-start = ((s8[6291456]{0:T(1024)(128)(4,1)}), s8[2097152]{0:T(1024)(128)(4,1)S(1)}, s32[]{:S(2)}) async-start(s8[6291456]{0:T(1024)(128)(4,1)} %bitcast.145), calls=%async_computation.3 | async-start | bytes 4194304
  337.1 4.8 slice-start.1
  337.2 4.8 copy-start.42
  337.2 4.8 copy-start.87
  342.0 5.0 copy-start.68
  347.0 30.8 %copy-start.47 = (f32[512,12,64]{0,2,1:T(8,128)}, f32[512,12,64]{0,2,1:T(8,128)S(1)}, u32[]{:S(2)}) copy-start(f32[512,12,64]{0,2,1:T(8,128)S(1)} %multiply_bitcast_fusion) | copy-start | bytes 4718596
  348.9 32.9 %collective-permute-start.6 = (bf16[256,24,64]{0,2,1:T(8,128)(2,1)}, bf16[256,24,64]{0,2,1:T(8,128)(2,1)}, u32[]{:S(2)}, u32[]{:S(2)}) collective-permute-start(bf16[256,24,64]{0,2,1:T(8,128)(2,1)} %pad_maximum_fusion.13), channel_id=1, source_target_pairs={{0,1},{1,0},{2,3},{3,2},{4,5},{5,4},{6,7},{7,6},{8,9},{9,8},{10,11... | collective-permute-start | bytes 2359304 | tf_op jit(solution)/shard_map/ppermute | solution.py:112
  353.4 5.2 copy-start.15
  370.1 7.7 %slice-start.16 = ((s8[9437184]{0:T(1024)(128)(4,1)}), s8[4194304]{0:T(1024)(128)(4,1)S(1)}, s32[]{:S(2)}) async-start(s8[9437184]{0:T(1024)(128)(4,1)} %bitcast.162), calls=%async_computation.19 | async-start | bytes 8388608
  370.1 7.7 %slice-start.17 = ((s8[9437184]{0:T(1024)(128)(4,1)}), s8[4194304]{0:T(1024)(128)(4,1)S(1)}, s32[]{:S(2)}) async-start(s8[9437184]{0:T(1024)(128)(4,1)} %bitcast.162), calls=%async_computation.20 | async-start | bytes 8388608
  374.0 36.6 %collective-permute-start.8 = (bf16[1024,768]{1,0:T(8,128)(2,1)S(1)}, bf16[1024,768]{1,0:T(8,128)(2,1)S(1)}, u32[]{:S(2)}, u32[]{:S(2)}) collective-permute-start(bf16[1024,768]{1,0:T(8,128)(2,1)S(1)} %slice_bitcast_fusion), channel_id=1, source_target_pairs={{0,2},{1,3},{2,0},{3,1},{4,6},{5,7},{6,4},{7,5},{8,10},{9,11},{10,... | collective-permute-start | bytes 4718600 | tf_op jit(solution)/shard_map/ppermute | solution.py:112
  383.3 28.9 %copy-start.53 = (bf16[256,12,64]{0,2,1:T(8,128)(2,1)S(1)}, bf16[256,12,64]{0,2,1:T(8,128)(2,1)}, u32[]{:S(2)}) copy-start(bf16[256,12,64]{0,2,1:T(8,128)(2,1)} %fusion.44) | copy-start | bytes 1179652
  383.3 28.9 %copy-start.58 = (bf16[256,12,64]{0,2,1:T(8,128)(2,1)S(1)}, bf16[256,12,64]{0,2,1:T(8,128)(2,1)}, u32[]{:S(2)}) copy-start(bf16[256,12,64]{0,2,1:T(8,128)(2,1)} %copy-done.56) | copy-start | bytes 1179652
  670.3 50.4 %copy-start.1 = (s32[2,1,3]{2,1,0:T(1,128)S(1)}, s32[2,1,3]{2,1,0:T(1,128)}, u32[]{:S(2)}) copy-start(s32[2,1,3]{2,1,0:T(1,128)} %param.16) | copy-start | bytes 76
  (78 other events, 197.3 us)
Sparse Core Ops, SparseCore 0:
  149.4 59.0 all-gather.1
  412.3 73.6 reduce-scatter.1

commit v7 on v6

--- a/solution.py
+++ b/solution.py
@@ -44,30 +44,6 @@
     )
 
 
-def rms_norm(value, gain):
-    return value * lax.rsqrt(jnp.mean(value * value, axis=-1, keepdims=True) + eps_norm) * gain
-
-
-def rms_back(value, gain, grad):
-    r = lax.rsqrt(jnp.mean(value * value, axis=-1, keepdims=True) + eps_norm)
-    scaled = grad * gain
-    d_value = r * scaled - value * (r * r * r) * jnp.mean(value * scaled, axis=-1, keepdims=True)
-    return d_value, jnp.sum(grad * value * r, axis=0)
-
-
-def rotary(value, cosine, sine):
-    half = HD // 2
-    turned = jnp.concatenate([-value[..., half:], value[..., :half]], axis=-1)
-    return value * cosine[:, None, :] + turned * sine[:, None, :]
-
-
-def rotary_back(grad, cosine, sine):
-    half = HD // 2
-    part = grad * sine[:, None, :]
-    turned = jnp.concatenate([part[..., half:], -part[..., :half]], axis=-1)
-    return grad * cosine[:, None, :] + turned
-
-
 def segments(lengths, places):
     segment = jnp.zeros_like(places)
     begin = jnp.zeros_like(places)
@@ -80,87 +56,8 @@
     return segment, places - begin
 
 
-def scores_of(query, keys, allow):
-    score = jnp.einsum("qhd,khd->hqk", query, keys, preferred_element_type=jnp.float32) * scale
-    return jnp.where(allow[None], score, -1e30)
-
-
-def attend(query, keys, values, allow):
-    score = scores_of(query, keys, allow)
-    summit = jnp.max(score, axis=-1, keepdims=True)
-    log_total = summit + jnp.log(jnp.sum(jnp.exp(score - summit), axis=-1, keepdims=True))
-    weight = jnp.exp(score - log_total)
-    mixed = jnp.einsum(
-        "hqk,khd->qhd", weight.astype(low), values, preferred_element_type=jnp.float32
-    )
-    return mixed.astype(low), log_total
-
-
-def attend_back(query, keys, values, log_total, upstream, allow):
-    weight = jnp.exp(scores_of(query, keys, allow) - log_total)
-    d_value = jnp.einsum(
-        "hqk,qhd->khd", weight.astype(low), upstream, preferred_element_type=jnp.float32
-    )
-    d_weight = jnp.einsum("qhd,khd->hqk", upstream, values, preferred_element_type=jnp.float32)
-    d_score = (weight * (d_weight - jnp.sum(d_weight * weight, axis=-1, keepdims=True))).astype(low)
-    d_query = jnp.einsum("hqk,khd->qhd", d_score, keys, preferred_element_type=jnp.float32) * scale
-    d_key = jnp.einsum("hqk,qhd->khd", d_score, query, preferred_element_type=jnp.float32) * scale
-    return d_query, d_key, d_value
-
-
 def swap(value, head_count, offset):
     return lax.ppermute(value, "head", [(h, h ^ offset) for h in range(head_count)])
-
-
-def layer_forward(hidden, weights, gains, cosine, sine, allow, head_count):
-    w_qkv, w_out, w_gu, w_down = weights
-    rows = hidden.shape[0]
-    normed = rms_norm(hidden, gains[0]).astype(low)
-    qkv = contract_cols(normed, w_qkv).reshape(rows, 3, H, HD)
-    query = rotary(qkv[:, 0], cosine, sine).astype(low)
-    key = rotary(qkv[:, 1], cosine, sine).astype(low)
-    own = jnp.concatenate([key, qkv[:, 2].astype(low)], axis=1)
-    both = jnp.concatenate([own, swap(own, head_count, 1)], axis=0)
-    keys, values = both[:, :H], both[:, H:]
-    mixed, log_total = attend(query, keys, values, allow)
-    merged = mixed.reshape(rows, D)
-    middle = hidden + contract_cols(merged, w_out)
-    normed_two = rms_norm(middle, gains[1]).astype(low)
-    gate_up = contract_cols(normed_two, w_gu)
-    action = (jax.nn.silu(gate_up[:, :FF]) * gate_up[:, FF:]).astype(low)
-    output = middle + product(action, w_down)
-    saved = (hidden, normed, query, keys, values, log_total, merged, middle, normed_two, gate_up, action)
-    return output, saved
-
-
-def layer_backward(gradient, weights, gains, saved, cosine, sine, allow, head_count):
-    w_qkv, w_out, w_gu, w_down = weights
-    hidden, normed, query, keys, values, log_total, merged, middle, normed_two, gate_up, action = saved
-    rows = hidden.shape[0]
-    grad_low = gradient.astype(low)
-    d_down = contract_rows(action, grad_low)
-    d_action = contract_cols(grad_low, w_down)
-    gate, up = gate_up[:, :FF], gate_up[:, FF:]
-    chance = jax.nn.sigmoid(gate)
-    d_gate = d_action * up * (chance + gate * chance * (1.0 - chance))
-    d_up = d_action * gate * chance
-    d_gate_up = jnp.concatenate([d_gate, d_up], axis=1).astype(low)
-    d_gu = contract_rows(d_gate_up, normed_two)
-    d_middle, d_gain_two = rms_back(middle, gains[1], product(d_gate_up, w_gu))
-    d_middle = gradient + d_middle
-    middle_low = d_middle.astype(low)
-    d_out = contract_rows(middle_low, merged)
-    upstream = product(middle_low, w_out).astype(low).reshape(rows, H, HD)
-    d_query, d_key, d_value = attend_back(query, keys, values, log_total, upstream, allow)
-    d_own = jnp.concatenate([d_key[:rows], d_value[:rows]], axis=1)
-    d_far = jnp.concatenate([d_key[rows:], d_value[rows:]], axis=1).astype(low)
-    d_own = (d_own + swap(d_far, head_count, 1).astype(jnp.float32)).astype(low).astype(jnp.float32)
-    d_query = rotary_back(d_query.astype(low).astype(jnp.float32), cosine, sine)
-    d_key = rotary_back(d_own[:, :H], cosine, sine)
-    d_qkv = jnp.concatenate([d_query, d_key, d_own[:, H:]], axis=1).reshape(rows, 3 * D).astype(low)
-    d_qkv_w = contract_rows(d_qkv, normed)
-    d_hidden, d_gain_one = rms_back(hidden, gains[0], product(d_qkv, w_qkv))
-    return d_middle + d_hidden, [d_qkv_w, d_out, d_gu, d_down], d_gain_one, d_gain_two
 
 
 MESH = pl.DeviceIdType.MESH
@@ -200,11 +97,12 @@
     pieces = refs[0:3]
     table_ref, codes_ref, vocab_ref = refs[3:6]
     wholes = refs[6:9]
-    sum_ref, ids_ref = refs[9:11]
-    far_x, from_low, from_high, total, rows_ref, shard, ids = refs[11:18]
-    local_sem, up_sem, down_sem, x_sem, y_sem, c_sem, block_sem = refs[18:25]
-    rx_send, rx_recv, ru_send, ru_recv, rd_send, rd_recv = refs[25:31]
-    id_send, id_recv, table_sem, copy_sem = refs[31:35]
+    sum_ref, ids_ref, near_ref, far_ref = refs[9:13]
+    far_x, from_low, from_high, total, rows_ref, shard, ids = refs[13:20]
+    local_sem, up_sem, down_sem, x_sem, y_sem, c_sem, block_sem = refs[20:27]
+    rx_send, rx_recv, ru_send, ru_recv, rd_send, rd_recv = refs[27:33]
+    id_send, id_recv, table_sem, copy_sem = refs[33:37]
+    su_send, sd_send, sx_send, sy_send, sc_send, s_recv, keep_sem = refs[37:44]
     z, x, y, c = coordinates(depth)
     mine = slot(z, x, y, c)
     dp, head = z * 2 + x, y * 2 + c
@@ -415,18 +313,18 @@
 
     for goal in goals:
         rows_x[goal].wait_recv()
-        part = rows_ref[goal * 2 + x] + far_x[goal]
+        both = rows_ref[goal * 2 + x] + far_x[goal]
 
         @pl.when(goal > z)
         def rising():
             @pl.when(z > 0)
             def more():
                 rows_up(goal).wait_recv()
-                total[goal] = part + from_low[goal]
+                total[goal] = both + from_low[goal]
 
             @pl.when(z == 0)
             def alone():
-                total[goal] = part
+                total[goal] = both
 
             rows_up(goal).start()
 
@@ -435,17 +333,17 @@
             @pl.when(z < depth - 1)
             def more():
                 rows_down(goal).wait_recv()
-                total[goal] = part + from_high[goal]
+                total[goal] = both + from_high[goal]
 
             @pl.when(z == depth - 1)
             def alone():
-                total[goal] = part
+                total[goal] = both
 
             rows_down(goal).start()
 
         @pl.when(goal == z)
         def here():
-            total[goal] = part
+            total[goal] = both
 
     for step in range(depth):
         for sign in (1, -1) if step else (1,):
@@ -472,6 +370,95 @@
 
             sum_ref[...] = total[goal]
 
+    def shared(source, ref, quarter, group, send_sem, target):
+        where = ref.at[quarter, group]
+        return pltpu.make_async_remote_copy(
+            where if source is None else source,
+            where,
+            send_sem,
+            s_recv.at[quarter if ref is near_ref else 2 + quarter, group],
+            device_id=target,
+            device_id_type=MESH,
+        )
+
+    own_shared = sum_ref.at[pl.ds(0, part)]
+    keep_shared = pltpu.make_async_copy(own_shared, near_ref.at[0, dp], keep_sem)
+    keep_shared.start()
+
+    def plane(group):
+        return near_ref.at[0, group]
+
+    def shared_y(source, group):
+        return pltpu.make_async_remote_copy(
+            source,
+            near_ref.at[1, group],
+            sy_send.at[group],
+            s_recv.at[1, group],
+            device_id=across_y,
+            device_id_type=MESH,
+        )
+
+    def shared_c(source, quarter, group):
+        return pltpu.make_async_remote_copy(
+            source,
+            far_ref.at[quarter, group],
+            sc_send.at[quarter, group],
+            s_recv.at[2 + quarter, group],
+            device_id=across_c,
+            device_id_type=MESH,
+        )
+
+    @pl.when(z < depth - 1)
+    def shared_up():
+        shared(own_shared, near_ref, 0, dp, su_send.at[0], device(z + 1, x, y, c)).start()
+
+    @pl.when(z > 0)
+    def shared_down():
+        shared(own_shared, near_ref, 0, dp, sd_send.at[0], device(z - 1, x, y, c)).start()
+
+    shared(own_shared, near_ref, 0, dp, sx_send.at[z], across_x).start()
+    shared_y(own_shared, dp).start()
+    shared_c(own_shared, 0, dp).start()
+    for step in range(1, depth):
+
+        @pl.when(z - step >= 0)
+        def shared_risen():
+            group = (z - step) * 2 + x
+            copy = shared(
+                None, near_ref, 0, group, su_send.at[step], device(z + 1, x, y, c)
+            )
+            copy.wait_recv()
+
+            @pl.when(z < depth - 1)
+            def further():
+                copy.start()
+
+            shared(None, near_ref, 0, group, sx_send.at[z - step], across_x).start()
+            shared_y(plane(group), group).start()
+            shared_c(plane(group), 0, group).start()
+
+        @pl.when(z + step < depth)
+        def shared_fallen():
+            group = (z + step) * 2 + x
+            copy = shared(
+                None, near_ref, 0, group, sd_send.at[step], device(z - 1, x, y, c)
+            )
+            copy.wait_recv()
+
+            @pl.when(z > 0)
+            def further():
+                copy.start()
+
+            shared(None, near_ref, 0, group, sx_send.at[z + step], across_x).start()
+            shared_y(plane(group), group).start()
+            shared_c(plane(group), 0, group).start()
+
+    for place in range(depth):
+        group = place * 2 + 1 - x
+        shared(None, near_ref, 0, group, sx_send.at[place], across_x).wait_recv()
+        shared_y(plane(group), group).start()
+        shared_c(plane(group), 0, group).start()
+
     for step in range(depth):
         for sign in (1, -1) if step else (1,):
 
@@ -482,11 +469,35 @@
                     arrive(block)
                     send(onward, block, across_c, c_sem.at[block // 2])
 
+    for group in range(groups):
+        shared_y(plane(group), group).wait_recv()
+        shared_c(near_ref.at[1, group], 1, group).start()
+
     for block in range(depth * 8):
 
         @pl.when(block % 2 != c)
         def from_core():
             arrive(block)
+
+    for group in range(groups):
+        for quarter in range(2):
+            shared_c(near_ref.at[quarter, group], quarter, group).wait_recv()
+
+    keep_shared.wait()
+    for group in range(groups):
+        shared_y(plane(group), group).wait_send()
+        for quarter in range(2):
+            shared_c(near_ref.at[quarter, group], quarter, group).wait_send()
+    for place in range(depth):
+        shared(None, near_ref, 0, dp, sx_send.at[place], across_x).wait_send()
+
+        @pl.when((z - place >= 0) & (z < depth - 1))
+        def shared_rose():
+            shared(None, near_ref, 0, dp, su_send.at[place], across_x).wait_send()
+
+        @pl.when((z + place < depth) & (z > 0))
+        def shared_fell():
+            shared(None, near_ref, 0, dp, sd_send.at[place], across_x).wait_send()
 
     for copy in local:
         copy.wait()
@@ -540,10 +551,11 @@
     return pl.pallas_call(
         functools.partial(start_kernel, depth),
         out_shape=[jax.ShapeDtypeStruct((blocks,) + piece.shape, low) for piece in pieces]
-        + [jax.ShapeDtypeStruct((height, width), low), jax.ShapeDtypeStruct(told, jnp.int32)],
+        + [jax.ShapeDtypeStruct((height, width), low), jax.ShapeDtypeStruct(told, jnp.int32)]
+        + [jax.ShapeDtypeStruct((2, groups, vocab_ids.shape[0] // blocks, width), low)] * 2,
         in_specs=[ANY] * 4
         + [pl.BlockSpec(memory_space=pltpu.VMEM), pl.BlockSpec(memory_space=pltpu.SMEM)],
-        out_specs=[ANY] * 3 + [pl.BlockSpec(memory_space=pltpu.VMEM)] * 2,
+        out_specs=[ANY] * 3 + [pl.BlockSpec(memory_space=pltpu.VMEM)] * 2 + [ANY] * 2,
         scratch_shapes=[buffer] * 4
         + [
             pltpu.VMEM((groups, height, width), low),
@@ -555,7 +567,9 @@
         + [dma((depth * 2, 3)), dma((depth * 4, 3)), dma((blocks, 3))]
         + [dma((depth,))] * 6
         + [dma((groups, 2))] * 2
-        + [dma(())] * 2,
+        + [dma(())] * 2
+        + [dma((depth,))] * 3
+        + [dma((groups,)), dma((2, groups)), dma((4, groups)), dma(())],
         compiler_params=pltpu.CompilerParams(
             collective_id=0, has_side_effects=True, vmem_limit_bytes=58 * 2**20
         ),
@@ -1140,6 +1154,337 @@
     )(*tables, table_grads, small, gain_sums, *gains, block_grads, *blocks, bases)
 
 
+NONE = pl.CostEstimate(flops=0, bytes_accessed=0, transcendentals=0)
+LARGE = 58 * 2**20
+CHUNK = 512
+
+
+def inverse_rms(value):
+    return lax.rsqrt(jnp.mean(value * value, axis=-1, keepdims=True) + eps_norm)
+
+
+def norm_back(value, r, gain, grad):
+    scaled = grad * gain
+    d_value = r * scaled - value * (r * r * r) * jnp.mean(value * scaled, axis=-1, keepdims=True)
+    return d_value, jnp.sum(grad * value * r, axis=0, keepdims=True)
+
+
+def local_call(kernel, name, outs, args, scratch=(), remain=()):
+    vmem = pl.BlockSpec(memory_space=pltpu.VMEM)
+    return pl.pallas_call(
+        kernel,
+        out_shape=[jax.ShapeDtypeStruct(shape, kind) for shape, kind in outs],
+        in_specs=[ANY if place in remain else vmem for place in range(len(args))],
+        out_specs=[vmem] * len(outs),
+        scratch_shapes=list(scratch),
+        compiler_params=pltpu.CompilerParams(vmem_limit_bytes=LARGE),
+        cost_estimate=NONE,
+        name=name,
+    )(*args)
+
+
+def project_kernel(hidden_ref, gain_ref, weight_ref, cosine_ref, sine_ref, *refs):
+    normed_ref, query_ref, own_ref = refs
+    hidden = hidden_ref[...]
+    normed = (hidden * inverse_rms(hidden) * gain_ref[...]).astype(low)
+    normed_ref[...] = normed
+    cosine, sine = cosine_ref[...], sine_ref[...]
+    first = lax.broadcasted_iota(jnp.int32, cosine.shape, 1) % HD < HD // 2
+    for index in range(3 * D // 128):
+        columns = pl.ds(index * 128, 128)
+        value = contract_cols(normed, weight_ref[columns])
+        if index < 2 * D // 128:
+            turned = jnp.where(
+                first, -pltpu.roll(value, 128 - HD // 2, 1), pltpu.roll(value, HD // 2, 1)
+            )
+            value = value * cosine + turned * sine
+        if index < D // 128:
+            query_ref[:, columns] = value.astype(low)
+        else:
+            own_ref[:, pl.ds(index * 128 - D, 128)] = value.astype(low)
+
+
+def project(hidden, gain, weight, cosine, sine):
+    rows = hidden.shape[0]
+    outs = [((rows, D), low), ((rows, D), low), ((rows, 2 * D), low)]
+    return local_call(project_kernel, "project", outs, [hidden, gain, weight, cosine, sine])
+
+
+def allowed(rows_ref, columns_ref):
+    return (rows_ref[:, 0:1] == columns_ref[0:1]) & (rows_ref[:, 1:2] >= columns_ref[1:2])
+
+
+def pair_of_heads(index):
+    return pl.ds(index * 128, 128)
+
+
+def attention_weight(query, keys, allow):
+    score = jnp.where(allow, contract_cols(query, keys) * scale, -1e30)
+    power = jnp.exp(score - jnp.max(score, axis=-1, keepdims=True))
+    return power * (1.0 / jnp.sum(power, axis=-1, keepdims=True))
+
+
+def forward_kernel(hidden_ref, query_ref, own_ref, far_ref, rows_ref, columns_ref, *refs):
+    out_weight, gain_ref, gate_hbm, down_hbm, output_ref, merged_ref, middle_ref = refs[:7]
+    gates, downs, sems = refs[7:]
+    copies = weight_copies(gate_hbm, down_hbm, gates, downs, sems)
+    for group in copies:
+        for copy in group:
+            copy.start()
+    allow = allowed(rows_ref, columns_ref)
+    rows = hidden_ref.shape[0]
+    first = lax.broadcasted_iota(jnp.int32, (rows, 128), 1) < HD
+
+    @pl.loop(0, D // 128)
+    def heads(index):
+        columns = pl.ds(pl.multiple_of(index * 128, 128), 128)
+        values_at = pl.ds(pl.multiple_of(index * 128 + D, 128), 128)
+        query = query_ref[:, columns]
+        keys = jnp.concatenate([own_ref[:, columns], far_ref[:, columns]], axis=0)
+        values = jnp.concatenate([own_ref[:, values_at], far_ref[:, values_at]], axis=0)
+        mixed = []
+        for side in range(2):
+            mine = jnp.where(first == (side == 0), query, jnp.zeros_like(query))
+            weight = attention_weight(mine, keys, allow).astype(low)
+            mixed.append(product(weight, values))
+        merged_ref[:, columns] = jnp.where(first, mixed[0], mixed[1]).astype(low)
+
+    middle = hidden_ref[...] + contract_cols(merged_ref[...], out_weight[...])
+    middle_ref[...] = middle
+    normed = (middle * inverse_rms(middle) * gain_ref[...]).astype(low)
+    output_ref[...] = middle
+    for index, group in enumerate(copies):
+        for copy in group:
+            copy.wait()
+        gate = contract_cols(normed, gates[pl.ds(index * CHUNK, CHUNK)])
+        up = contract_cols(normed, gates[pl.ds(FF + index * CHUNK, CHUNK)])
+        action = (gate * jax.nn.sigmoid(gate) * up).astype(low)
+        output_ref[...] += product(action, downs[pl.ds(index * CHUNK, CHUNK)])
+
+
+def weight_copies(gate_hbm, down_hbm, gates, downs, sems):
+    groups = []
+    for index in range(FF // CHUNK):
+        parts = [
+            (gate_hbm, gates, index * CHUNK),
+            (gate_hbm, gates, FF + index * CHUNK),
+            (down_hbm, downs, index * CHUNK),
+        ]
+        groups.append(
+            [
+                pltpu.make_async_copy(
+                    source.at[pl.ds(at, CHUNK)], goal.at[pl.ds(at, CHUNK)], sems.at[index, place]
+                )
+                for place, (source, goal, at) in enumerate(parts)
+            ]
+        )
+    return groups
+
+
+def weight_buffers():
+    return [
+        pltpu.VMEM((2 * FF, D), low),
+        pltpu.VMEM((FF, D), low),
+        pltpu.SemaphoreType.DMA((FF // CHUNK, 3)),
+    ]
+
+
+def forward(hidden, query, own, far, rows, columns, w_out, gain, w_gu, w_down):
+    count = hidden.shape[0]
+    outs = [((count, D), jnp.float32), ((count, D), low), ((count, D), jnp.float32)]
+    args = [hidden, query, own, far, rows, columns, w_out, gain, w_gu, w_down]
+    return local_call(forward_kernel, "forward", outs, args, weight_buffers(), (8, 9))
+
+
+def backward_kernel(gradient_ref, middle_ref, query_ref, own_ref, far_ref, *refs):
+    rows_ref, columns_ref, out_weight, gain_ref, gate_hbm, down_hbm = refs[:6]
+    d_query_ref, d_own_ref, d_far_ref, d_middle_ref, gain_out = refs[6:11]
+    low_ref, normed_ref, action_ref, d_gate_ref, middle_low_ref = refs[11:16]
+    gates, downs, sems, total = refs[16:]
+    copies = weight_copies(gate_hbm, down_hbm, gates, downs, sems)
+    for group in copies:
+        for copy in group:
+            copy.start()
+    gradient = gradient_ref[...]
+    grad_low = gradient.astype(low)
+    low_ref[...] = grad_low
+    middle = middle_ref[...]
+    r = inverse_rms(middle)
+    normed = (middle * r * gain_ref[...]).astype(low)
+    normed_ref[...] = normed
+    total[...] = jnp.zeros_like(total)
+    for index, group in enumerate(copies):
+        for copy in group:
+            copy.wait()
+        first = pl.ds(index * CHUNK, CHUNK)
+        second = pl.ds(FF + index * CHUNK, CHUNK)
+        gate = contract_cols(normed, gates[first])
+        up = contract_cols(normed, gates[second])
+        chance = jax.nn.sigmoid(gate)
+        action_ref[:, first] = (gate * chance * up).astype(low)
+        d_action = contract_cols(grad_low, downs[first])
+        d_gate = (d_action * up * (chance + gate * chance * (1.0 - chance))).astype(low)
+        d_up = (d_action * gate * chance).astype(low)
+        d_gate_ref[:, first] = d_gate
+        d_gate_ref[:, second] = d_up
+        total[...] += product(d_gate, gates[first]) + product(d_up, gates[second])
+    d_middle, gain_out[...] = norm_back(middle, r, gain_ref[...], total[...])
+    d_middle = gradient + d_middle
+    d_middle_ref[...] = d_middle
+    middle_low = d_middle.astype(low)
+    middle_low_ref[...] = middle_low
+    total[...] = product(middle_low, out_weight[...])
+    allow = allowed(rows_ref, columns_ref)
+    rows = gradient.shape[0]
+    first = lax.broadcasted_iota(jnp.int32, (rows, 128), 1) < HD
+    first_all = lax.broadcasted_iota(jnp.int32, (2 * rows, 128), 1) < HD
+
+    @pl.loop(0, D // 128)
+    def heads(index):
+        columns = pl.ds(pl.multiple_of(index * 128, 128), 128)
+        values_at = pl.ds(pl.multiple_of(index * 128 + D, 128), 128)
+        query = query_ref[:, columns]
+        upstream = total[:, columns].astype(low)
+        keys = jnp.concatenate([own_ref[:, columns], far_ref[:, columns]], axis=0)
+        values = jnp.concatenate([own_ref[:, values_at], far_ref[:, values_at]], axis=0)
+        d_queries, d_keys, d_values = [], [], []
+        for side in range(2):
+            mine = jnp.where(first == (side == 0), query, jnp.zeros_like(query))
+            grad = jnp.where(first == (side == 0), upstream, jnp.zeros_like(upstream))
+            weight = attention_weight(mine, keys, allow)
+            d_values.append(contract_rows(weight.astype(low), upstream))
+            d_weight = contract_cols(grad, values)
+            d_score = weight * (d_weight - jnp.sum(d_weight * weight, axis=-1, keepdims=True))
+            d_score = d_score.astype(low)
+            d_queries.append(product(d_score, keys) * scale)
+            d_keys.append(contract_rows(d_score, query) * scale)
+        d_query_ref[:, columns] = jnp.where(first, *d_queries).astype(low)
+        d_key = jnp.where(first_all, *d_keys)
+        d_value = jnp.where(first_all, *d_values)
+        d_own_ref[:, columns] = d_key[:rows]
+        d_own_ref[:, values_at] = d_value[:rows]
+        d_far_ref[:, columns] = d_key[rows:].astype(low)
+        d_far_ref[:, values_at] = d_value[rows:].astype(low)
+
+
+def backward(gradient, middle, query, own, far, rows, columns, w_out, gain, w_gu, w_down):
+    count = gradient.shape[0]
+    f32 = jnp.float32
+    outs = [
+        ((count, D), low),
+        ((count, 2 * D), f32),
+        ((count, 2 * D), low),
+        ((count, D), f32),
+        ((1, D), f32),
+        ((count, D), low),
+        ((count, D), low),
+        ((count, FF), low),
+        ((count, 2 * FF), low),
+        ((count, D), low),
+    ]
+    args = [gradient, middle, query, own, far, rows, columns, w_out, gain, w_gu, w_down]
+    scratch = weight_buffers() + [pltpu.VMEM((count, D), f32)]
+    return local_call(backward_kernel, "backward", outs, args, scratch, (9, 10))
+
+
+def unproject_kernel(d_query_ref, d_own_ref, d_far_ref, d_middle_ref, hidden_ref, *refs):
+    gain_ref, weight_ref, cosine_ref, sine_ref, gradient_ref, gain_out, d_qkv_ref = refs
+    cosine, sine = cosine_ref[...], sine_ref[...]
+    first = lax.broadcasted_iota(jnp.int32, cosine.shape, 1) % HD < HD // 2
+    for index in range(3 * D // 128):
+        columns = pl.ds(index * 128, 128)
+        if index < D // 128:
+            value = d_query_ref[:, columns].astype(jnp.float32)
+        else:
+            there = pl.ds(index * 128 - D, 128)
+            value = d_own_ref[:, there] + d_far_ref[:, there].astype(jnp.float32)
+            value = value.astype(low).astype(jnp.float32)
+        if index < 2 * D // 128:
+            part = value * sine
+            turned = jnp.where(
+                first, pltpu.roll(part, 128 - HD // 2, 1), -pltpu.roll(part, HD // 2, 1)
+            )
+            value = value * cosine + turned
+        d_qkv_ref[:, columns] = value.astype(low)
+    hidden = hidden_ref[...]
+    d_hidden, gain_out[...] = norm_back(
+        hidden, inverse_rms(hidden), gain_ref[...], product(d_qkv_ref[...], weight_ref[...])
+    )
+    gradient_ref[...] = d_middle_ref[...] + d_hidden
+
+
+def unproject(d_query, d_own, d_far, d_middle, hidden, gain, weight, cosine, sine):
+    rows = hidden.shape[0]
+    outs = [((rows, D), jnp.float32), ((1, D), jnp.float32), ((rows, 3 * D), low)]
+    args = [d_query, d_own, d_far, d_middle, hidden, gain, weight, cosine, sine]
+    return local_call(unproject_kernel, "unproject", outs, args)
+
+
+def weigh_kernel(*refs):
+    pairs = [refs[4 * index : 4 * index + 4] for index in range(4)]
+    outs = refs[16:20]
+    now = pl.program_id(0)
+
+    def gradient(index):
+        left_one, left_two, right_one, right_two = pairs[index]
+        total = contract_rows(left_one[...], right_one[...])
+        total = total + contract_rows(left_two[...], right_two[...])
+        outs[index][...] = total.astype(low).reshape(outs[index].shape)
+
+    gradient(0)
+    gradient(1)
+
+    @pl.when(now < 6)
+    def qkv():
+        gradient(2)
+
+    @pl.when(now >= 6)
+    def out():
+        gradient(3)
+
+
+def weigh(d_gates, normed_twos, actions, lows, d_qkvs, normeds, middles, merges, blocks):
+    rows = lows[0].shape[0]
+
+    def both(arrays, width, place):
+        return [(array, pl.BlockSpec((rows, width), place)) for array in arrays]
+
+    def whole(arrays):
+        return [(array, pl.BlockSpec((rows, D), lambda i: (0, 0))) for array in arrays]
+
+    def early(i):
+        return (0, jnp.minimum(i, 5))
+
+    def late(i):
+        return (0, jnp.maximum(i - 6, 0))
+
+    listed = both(d_gates, 768, lambda i: (0, i)) + whole(normed_twos)
+    listed += both(actions, 384, lambda i: (0, i)) + whole(lows)
+    listed += both(d_qkvs, 384, early) + whole(normeds)
+    listed += both(middles, 384, late) + whole(merges)
+    part = blocks // 8
+    return pl.pallas_call(
+        weigh_kernel,
+        grid=(8,),
+        out_shape=[
+            jax.ShapeDtypeStruct((blocks, 2 * FF // blocks, D), low),
+            jax.ShapeDtypeStruct((blocks, FF // blocks, D), low),
+            jax.ShapeDtypeStruct((3 * D, D), low),
+            jax.ShapeDtypeStruct((D, D), low),
+        ],
+        in_specs=[spec for unused, spec in listed],
+        out_specs=[
+            pl.BlockSpec((part, 2 * FF // blocks, D), lambda i: (i, 0, 0)),
+            pl.BlockSpec((part, FF // blocks, D), lambda i: (i, 0, 0)),
+            pl.BlockSpec((384, D), lambda i: (jnp.minimum(i, 5), 0)),
+            pl.BlockSpec((384, D), lambda i: (jnp.maximum(i - 6, 0), 0)),
+        ],
+        compiler_params=pltpu.CompilerParams(vmem_limit_bytes=LARGE),
+        cost_estimate=NONE,
+        name="weigh",
+    )(*[array for array, unused in listed])
+
+
 def loss_kernel(hidden_ref, gain_ref, near_ref, far_ref, own_ref, other_ref, weight_ref, *refs):
     gradient_ref, gain_out, loss_ref, near_out, far_out, logits, teach = refs
     head = lax.axis_index("head")
@@ -1147,7 +1492,7 @@
     half = rows // 2
     size = near_ref.shape[1]
     hidden = hidden_ref[...]
-    r = lax.rsqrt(jnp.mean(hidden * hidden, axis=-1, keepdims=True) + eps_norm)
+    r = inverse_rms(hidden)
     normed = (hidden * r * gain_ref[...]).astype(low)
     parts = [(near_ref, near_out, 0, 0), (near_ref, near_out, 1, 2)]
     parts += [(far_ref, far_out, 0, 1), (far_ref, far_out, 1, 3)]
@@ -1178,11 +1523,7 @@
     loss_ref[...] = jnp.broadcast_to(
         jnp.sum(loss * weighting, axis=0, keepdims=True), loss_ref.shape
     )
-    scaled = gradient * gain_ref[...]
-    gradient_ref[...] = r * scaled - hidden * (r * r * r) * jnp.mean(
-        hidden * scaled, axis=-1, keepdims=True
-    )
-    gain_out[...] = jnp.sum(gradient * hidden * r, axis=0, keepdims=True)
+    gradient_ref[...], gain_out[...] = norm_back(hidden, r, gain_ref[...], gradient)
 
 
 def distill(hidden, gain, near, far, own, other, weighting):
@@ -1236,7 +1577,7 @@
     widths = [3 * D // device_total, D // device_total, 2 * FF // device_total, FF // device_total]
     cuts = [sum(widths[:index]) for index in range(5)]
     block_low = block.T.astype(low)
-    attention, gate_up, down, rows_in, codes = start(
+    attention, gate_up, down, rows_in, codes, near, far = start(
         [block_low[: cuts[2]], block_low[cuts[2] : cuts[3]], block_low[cuts[3] :]],
         table,
         (token_ids * 2 + valid).reshape(-1, 1, tokens),
@@ -1256,9 +1597,8 @@
         gate_up.reshape(-1, D),
         down.reshape(-1, D),
     ]
-    quarter = lax.all_gather(rows_in[:part], "dp", axis=0, tiled=True)
-    near = jnp.stack([quarter, swap(quarter, head_count, 2)])
-    far = swap(near, head_count, 1)
+    near = near.reshape(2, -1, D)
+    far = far.reshape(2, -1, D)
     hidden = rows_in[part:].astype(jnp.float32)
 
     teacher_own = lax.dynamic_index_in_dim(teacher, batch, 0, keepdims=False)
@@ -1272,18 +1612,24 @@
     own_lengths = lax.dynamic_index_in_dim(lengths, batch, 0, keepdims=False)[0]
     segment, position = segments(own_lengths, places)
     segment_far, unused = segments(own_lengths, places_far)
-    places_all = jnp.concatenate([places, places_far])
-    segment_all = jnp.concatenate([segment, segment_far])
-    allow = (segment[:, None] == segment_all[None, :]) & (places[:, None] >= places_all[None, :])
+    queries_at = jnp.stack([segment, places], axis=1)
+    keys_at = jnp.stack(
+        [jnp.concatenate([segment, segment_far]), jnp.concatenate([places, places_far])]
+    )
     freqs = jnp.exp(jnp.arange(0, HD, 2, dtype=jnp.float32) * (-math.log(10000.0) / HD))
-    angle = position.astype(jnp.float32)[:, None] * freqs[None, :]
-    angle = jnp.concatenate([angle, angle], axis=1)
+    angle = position.astype(jnp.float32)[:, None] * jnp.tile(freqs, 4)[None, :]
     cosine, sine = jnp.cos(angle), jnp.sin(angle)
 
+    w_qkv, w_out, w_gu, w_down = weights
     saves = []
     for repeat in range(2):
-        hidden, saved = layer_forward(hidden, weights, gains, cosine, sine, allow, head_count)
-        saves.append(saved)
+        normed, query, own = project(hidden, gains[0:1], w_qkv, cosine, sine)
+        other = swap(own, head_count, 1)
+        output, merged, middle = forward(
+            hidden, query, own, other, queries_at, keys_at, w_out, gains[1:2], w_gu, w_down
+        )
+        saves.append((hidden, normed, query, own, other, merged, middle))
+        hidden = output
 
     gradient, d_gain_final, loss_sum, d_near, d_far = distill(
         hidden, gains[2:3], near, far, teacher_own, teacher_far, weighting[:, None]
@@ -1297,21 +1643,31 @@
         d_quarter.astype(low), "dp", scatter_dimension=0, tiled=True
     )
 
-    block_grads = None
     d_gains = [0.0, 0.0]
+    parts = []
     for repeat in range(2):
-        gradient, layer_grads, d_gain_one, d_gain_two = layer_backward(
-            gradient, weights, gains, saves[1 - repeat], cosine, sine, allow, head_count
-        )
-        d_gains = [d_gains[0] + d_gain_one, d_gains[1] + d_gain_two]
-        if block_grads is None:
-            block_grads = layer_grads
-        else:
-            block_grads = [total + extra for total, extra in zip(block_grads, layer_grads)]
-
-    d_qkv, d_out, d_gu, d_down = [
-        piece.astype(low).reshape(device_total, -1, D) for piece in block_grads
-    ]
+        hidden, normed, query, own, other, merged, middle = saves[1 - repeat]
+        back = backward(
+            gradient, middle, query, own, other, queries_at, keys_at, w_out, gains[1:2], w_gu, w_down
+        )
+        d_query, d_own, d_other, d_middle, d_gain_two = back[:5]
+        grad_low, normed_two, action, d_gate, middle_low = back[5:]
+        gradient, d_gain_one, d_qkv = unproject(
+            d_query,
+            d_own,
+            swap(d_other, head_count, 1),
+            d_middle,
+            hidden,
+            gains[0:1],
+            w_qkv,
+            cosine,
+            sine,
+        )
+        parts.append((d_gate, normed_two, action, grad_low, d_qkv, normed, middle_low, merged))
+        d_gains = [d_gains[0] + d_gain_one[0], d_gains[1] + d_gain_two[0]]
+
+    d_gu, d_down, d_qkv, d_out = weigh(*zip(*parts), device_total)
+    d_qkv, d_out = [piece.reshape(device_total, -1, D) for piece in (d_qkv, d_out)]
     rows_back = jnp.concatenate([chosen_grads, gradient.astype(low)], axis=0)
     step = 80 if shard_rows % 80 == 0 else 40
     quarter = -(-shard_rows // (step * head_count)) * step

time: 736 us -> 668 us (0.908)
  Pallas kernels: 373 us -> 547 us
  matrix products: 114 us -> 0 us
  waiting for transfers between devices: 121 us -> 45.1 us
  other arithmetic: 48.6 us -> 21.4 us
  local copies, waits for them, and re-layouts: 45.8 us -> 28.3 us
    pallas_call x0 -> x9, Pallas kernels: none -> 127 us  [the longest x8 108 us: local_call(): pl.pallas_call(kernel, out_shape=[jax.ShapeDtypeStruct(shape, kind) for s...]
    dot_general x36 -> x0, matrix products: 114 us -> none  [the longest x8 41.9 us: contract_rows(): lax.dot_general(left, right, (((0,), (0,)), ((), ())), preferred_element_...]
    reduce_scatter x1, waiting for transfers between devices: 57.6 us -> 0.01 us  [on_device(): lax.psum_scatter(d_quarter.astype(low), 'dp', scatter_dimension=0, tiled=...]
    pallas_call x1, Pallas kernels: 132 us -> 163 us  [start(): pl.pallas_call(functools.partial(start_kernel, depth), out_shape=[jax.Sha...]
    pallas_call x1, Pallas kernels: 178 us -> 194 us  [finish(): pl.pallas_call(functools.partial(finish_kernel, depth, heights, tile), ou...]
    ppermute x9 -> x7, waiting for transfers between devices: 55.9 us -> 45 us  [swap(): lax.ppermute(value, 'head', [(h, h ^ offset) for h in range(head_count)])]
    unnamed x259 -> x27, local copies, waits for them, and re-layouts: 16.4 us -> 6.06 us
    convert_element_type x10 -> x1, other arithmetic: 10.4 us -> 1.93 us  [on_device(): hidden = rows_in[part:].astype(jnp.float32)]
  transfers between devices with their start and end apart: 11 -> 8, of which waited for: 4 -> 4; matrix products, arithmetic and copies ran while one was open for 21% -> 3% of each run, Pallas kernels for 18% -> 18%
where the time goes in v7:
time: 668 us; the launch traced here: 661 us
  Pallas kernels  547 us (82%)
  waiting for transfers between devices  45.1 us (7%)
  local copies, waits for them, and re-layouts  28.3 us (4%)
  other arithmetic  21.4 us (3%)
  between operations  16.2 us (2%)
    pallas_call x1, Pallas kernels, finish(): pl.pallas_call(functools.partial(finish_kernel, depth, heights, tile), ou...  194 us
    pallas_call x1, Pallas kernels, start(): pl.pallas_call(functools.partial(start_kernel, depth), out_shape=[jax.Sha...  163 us
    pallas_call x8, Pallas kernels, local_call(): pl.pallas_call(kernel, out_shape=[jax.ShapeDtypeStruct(shape, kind) for s...  108 us
    pallas_call x1, Pallas kernels, update(): pl.pallas_call(functools.partial(update_kernel, steps, cuts), grid=(steps...  48.8 us
    ppermute x7, waiting for transfers between devices, swap(): lax.ppermute(value, 'head', [(h, h ^ offset) for h in range(head_count)])  45 us
    pallas_call x1, Pallas kernels, weigh(): pl.pallas_call(weigh_kernel, grid=(8,), out_shape=[jax.ShapeDtypeStruct((...  19.3 us
    pallas_call x1, Pallas kernels, distill(): pl.pallas_call(loss_kernel, out_shape=[jax.ShapeDtypeStruct(hidden.shape,...  13.7 us
  transfers between devices with their start and end apart: 8, of which 4 were waited for; matrix products, arithmetic and copies ran while one was open for 3% of the time, Pallas kernels for 18%

profile of v7, /device:TPU:0, one launch (start us, length us, event | category | flops | bytes accessed | tf_op | source)
XLA Modules:
  0.0 661.0 jit_solution(7032858641777557942)
XLA Ops:
  7.2 0.0 reduce-scatter.2.cloned.1.call-start
  7.3 1.5 copy.38
  8.8 0.7 slice.79.refs_1_
  9.5 0.7 fusion.10
  10.3 0.6 fusion.13
  10.9 0.1 mul.55
  11.0 1.4 fusion.11
  12.4 1.3 multiply_add_fusion
  13.7 163.3 %start.1 = (bf16[32,96,768]{2,1,0:T(8,128)(2,1)}, bf16[32,192,768]{2,1,0:T(8,128)(2,1)}, bf16[32,96,768]{2,1,0:T(8,128)(2,1)}, bf16[384,768]{1,0:T(8,128)(2,1)},...) custom-call(bf16[96,768]{1,0:T(8,128)(2,1)} %get-tuple-element.154.refs_0_, ...), custom_call_target="tpu_custom_call" | custom-call | tf_op jit(solution)/shard_map/start/pallas_call | solution.py:551
  177.0 1.9 slice_convert_fusion.hidden_ref
  178.9 4.0 slice.66
  184.4 0.7 convert_add_fusion.1
  185.1 1.2 multiply_sine_fusion
  186.3 5.4 project.2
  191.7 0.4 collective-permute-start
  192.1 1.5 dynamic-slice_bitcast_fusion
  193.6 1.4 collective-permute-start.2
  195.0 0.6 fusion.5
  195.7 2.4 slice.69
  198.1 0.8 copy.39.rows_ref.refs_0_
  198.9 0.6 pad_add_fusion.columns_ref.refs_1_
  199.5 0.9 copy-done.2
  200.4 15.5 %forward.2 = (f32[256,768]{1,0:T(8,128)}, bf16[256,768]{1,0:T(8,128)(2,1)}, f32[256,768]{1,0:T(8,128)}) custom-call(f32[256,768]{1,0:T(8,128)} %slice_convert_fusion.hidden_ref, bf16[256,768]{1,0:T(8,128)(2,1)} %get-tuple-element.84.query_ref, bf16[256,1536]{1,0:T(8,128)(2,1)} %get-tuple-element.85.own_ref, bf16[256,1536]{1,0:T(8,128)(2,1)} %copy-done.2, ...), custom_call_target="tpu_custom_call" | custom-call | tf_op jit(solution)/shard_map/forward/pallas_call | solution.py:1174
  215.9 5.3 project.3
  221.3 0.8 copy.41.weight_ref
  222.1 1.7 collective-permute-done.1.far_ref
  223.8 0.9 copy-done.3
  224.7 15.8 %forward.3 = (f32[256,768]{1,0:T(8,128)}, bf16[256,768]{1,0:T(8,128)(2,1)}, f32[256,768]{1,0:T(8,128)}) custom-call(f32[256,768]{1,0:T(8,128)} %get-tuple-element.88.hidden_ref, bf16[256,768]{1,0:T(8,128)(2,1)} %get-tuple-element.89.query_ref, bf16[256,1536]{1,0:T(8,128)(2,1)} %get-tuple-element.90.own_ref, bf16[256,1536]{1,0:T(8,128)(2,1)} %copy-done.3, ...), custom_call_target="tpu_custom_call" | custom-call | tf_op jit(solution)/shard_map/forward/pallas_call | solution.py:1174
  240.5 1.0 copy-done.5
  241.4 13.7 %distill.1 = (f32[256,768]{1,0:T(8,128)}, f32[1,768]{1,0:T(1,128)}, f32[8,128]{1,0:T(8,128)}, bf16[2,1024,768]{2,1,0:T(8,128)(2,1)}, bf16[2,1024,768]{2,1,0:T(8,128)(2,1)}) custom-call(f32[256,768]{1,0:T(8,128)} %get-tuple-element.91.hidden_ref, f32[1,768]{1,0:T(1,128)} %get-tuple-element.155.gain_ref, bf16[2,1024,768]{2,1,0:T(8,128)(2,1)} %bitcast.76, ...), custom_call_target="tpu_custom_call" | custom-call | tf_op jit(solution)/shard_map/distill/pallas_call | solution.py:1534
  255.1 0.5 collective-permute-start.5
  255.6 5.7 collective-permute-done.5
  261.4 2.7 add_convert_fusion
  264.0 0.1 slice_bitcast_fusion
  264.2 0.7 collective-permute-start.6
  264.8 35.8 %collective-permute-done.6 = bf16[1024,768]{1,0:T(8,128)(2,1)S(1)} collective-permute-done((bf16[1024,768]{1,0:T(8,128)(2,1)S(1)}, bf16[1024,768]{1,0:T(8,128)(2,1)S(1)}, u32[]{:S(2)}, u32[]{:S(2)}) %collective-permute-start.6) | collective-permute-done | bytes 1572896 | tf_op jit(solution)/shard_map/ppermute | solution.py:60
  300.7 1.6 fusion
  302.3 0.0 reduce-scatter.2.cloned.1.call-update
  302.3 26.3 %backward.2 = (bf16[256,768]{1,0:T(8,128)(2,1)}, f32[256,1536]{1,0:T(8,128)}, bf16[256,1536]{1,0:T(8,128)(2,1)}, f32[256,768]{1,0:T(8,128)}, f32[1,768]{1,0:T(1,...) custom-call(f32[256,768]{1,0:T(8,128)} %get-tuple-element.95.gradien, ...), custom_call_target="tpu_custom_call" | custom-call | tf_op jit(solution)/shard_map/backward/pallas_call | solution.py:1174
  328.6 0.1 collective-permute-start.3
  328.7 0.7 dynamic-slice_bitcast_fusion.2
  329.4 1.8 collective-permute-done.3.d_far_ref
  331.2 0.9 copy-done.7
  332.0 6.7 %unproject.2 = (f32[256,768]{1,0:T(8,128)}, f32[1,768]{1,0:T(1,128)}, bf16[256,2304]{1,0:T(8,128)(2,1)}) custom-call(bf16[256,768]{1,0:T(8,128)(2,1)} %get-tuple-element.98.d_query_ref, f32[256,1536]{1,0:T(8,128)} %get-tuple-element.99.d_own_ref, bf16[256,1536]{1,0:T(8,128)(2,1)} %copy-done.7, f32[256,768]{1,0:T(8,128)} %get-tuple-element.101.d_middle_ref, ...), custom_call_target="tpu_custom_call" | custom-call | tf_op jit(solution)/shard_map/unproject/pallas_call | solution.py:1174
  338.8 26.3 %backward.3 = (bf16[256,768]{1,0:T(8,128)(2,1)}, f32[256,1536]{1,0:T(8,128)}, bf16[256,1536]{1,0:T(8,128)(2,1)}, f32[256,768]{1,0:T(8,128)}, f32[1,768]{1,0:T(1,...) custom-call(f32[256,768]{1,0:T(8,128)} %get-tuple-element.102.gradie, ...), custom_call_target="tpu_custom_call" | custom-call | tf_op jit(solution)/shard_map/backward/pallas_call | solution.py:1174
  365.0 0.1 collective-permute-start.4
  365.2 0.6 fusion.6
  365.8 0.6 and_select_fusion.refs_4_
  366.4 1.2 slice.74
  367.6 0.7 add_reduce_fusion
  368.3 0.9 copy-done.6
  369.2 6.6 unproject.3
  375.8 1.2 convert_element_type.105
  377.0 0.7 add_reduce_fusion.1
  377.7 1.4 concatenate.62
  379.1 19.3 %weigh.1 = (bf16[32,192,768]{2,1,0:T(8,128)(2,1)}, bf16[32,96,768]{2,1,0:T(8,128)(2,1)}, bf16[2304,768]{1,0:T(8,128)(2,1)}, bf16[768,768]{1,0:T(8,128)(2,1)}) custom-call(bf16[256,6144]{1,0:T(8,128)(2,1)} %get-tuple-element.97.refs_0_, bf16[256,6144]{1,0:T(8,128)(2,1)} %get-tuple-element.104.refs_1_, bf16[256,768]{1,0:T(8,128)(2,1)} %get-tuple-element.105.refs_2_, ...), custom_call_target="tpu_custom_call" | custom-call | tf_op jit(solution)/shard_map/weigh/pallas_call | solution.py:1466
  398.3 0.6 pad_bitcast_fusion.refs_5_
  398.9 5.1 pad_maximum_fusion.refs_0_
  404.0 1.8 pad_maximum_fusion.1.refs_3_
  405.8 193.8 %finish.1 = (f32[384,768]{1,0:T(8,128)}, bf16[4,1040,768]{2,1,0:T(8,128)(2,1)}, f32[24,128]{1,0:T(8,128)}) custom-call(bf16[32,96,768]{2,1,0:T(8,128)(2,1)} %pad_maximum_fusion.refs_0_, bf16[32,192,768]{2,1,0:T(8,128)(2,1)} %get-tuple-element.125.refs_1_, bf16[32,96,768]{2,1,0:T(8,128)(2,1)} %get-tuple-element.126.refs_2_, ...), custom_call_target="tpu_custom_call" | custom-call | tf_op jit(solution)/shard_map/finish/pallas_call | solution.py:982
  599.6 1.3 reshape.213.refs_5_
  601.0 2.7 copy.44
  603.6 48.8 %update.1 = (f32[4000,768]{1,0:T(8,128)}, f32[4000,768]{1,0:T(8,128)}, f32[4000,768]{1,0:T(8,128)}, bf16[4000,768]{1,0:T(8,128)(2,1)}, f32[8,128]{1,0:T(8,128)},...) custom-call(f32[4000,768]{1,0:T(8,128)} %refs_0_.1, ...), custom_call_target="tpu_custom_call" | custom-call | tf_op jit(solution)/shard_map/update/pallas_call | solution.py:1136
  652.4 1.3 fusion.12
  (41 shorter events, 0.2 us)
Async XLA Ops:
  7.2 3.1 copy-start
  7.2 396.8 %reduce-scatter.2.cloned.1.call-start = ((), (), s32[]{:S(2)}) async-start(), calls=%async_computation.1 | async-start | bytes 1769472 | tf_op jit(solution)/shard_map/reduce_scatter | solution.py:1642
  182.9 9.2 %copy-start.4 = (bf16[2,128,4096]{2,1,0:T(8,128)(2,1)S(1)}, bf16[2,128,4096]{2,1,0:T(8,128)(2,1)}, u32[]{:S(2)}) copy-start(bf16[2,128,4096]{2,1,0:T(8,128)(2,1)} %param.19) | copy-start | bytes 6291460
  191.7 7.8 %collective-permute-start = (bf16[256,1536]{1,0:T(8,128)(2,1)}, bf16[256,1536]{1,0:T(8,128)(2,1)S(1)}, u32[]{:S(2)}, u32[]{:S(2)}) collective-permute-start(bf16[256,1536]{1,0:T(8,128)(2,1)} %get-tuple-element.85.own_ref), channel_id=1, source_target_pairs={{0,1},{1,0},{2,3},{3,2},{4,5},{5,4},{6,7},{7,6},{8,9},{9,8},{10,11... | collective-permute-start | bytes 2359304 | tf_op jit(solution)/shard_map/ppermute | solution.py:60
  193.6 46.9 %collective-permute-start.2 = (bf16[128,4096]{1,0:T(8,128)(2,1)}, bf16[128,4096]{1,0:T(8,128)(2,1)S(1)}, u32[]{:S(2)}, u32[]{:S(2)}) collective-permute-start(bf16[128,4096]{1,0:T(8,128)(2,1)} %get-tuple-element.151), channel_id=1, source_target_pairs={{0,2},{1,3},{2,0},{3,1},{4,6},{5,7},{6,4},{7,5},{8,10},{9,11},{10,... | collective-permute-start | bytes 3145736 | tf_op jit(solution)/shard_map/ppermute | solution.py:60
  199.5 0.9 copy-start.2
  215.9 5.3 copy-start.8
  221.3 2.5 collective-permute-start.1
  223.8 0.9 copy-start.3
  240.5 1.0 copy-start.5
  255.1 6.3 collective-permute-start.5
  264.2 36.5 %collective-permute-start.6 = (bf16[1024,768]{1,0:T(8,128)(2,1)S(1)}, bf16[1024,768]{1,0:T(8,128)(2,1)S(1)}, u32[]{:S(2)}, u32[]{:S(2)}) collective-permute-start(bf16[1024,768]{1,0:T(8,128)(2,1)S(1)} %slice_bitcast_fusion), channel_id=1, source_target_pairs={{0,2},{1,3},{2,0},{3,1},{4,6},{5,7},{6,4},{7,5},{8,10},{9,11},{10,... | collective-permute-start | bytes 4718600 | tf_op jit(solution)/shard_map/ppermute | solution.py:60
  328.6 2.6 collective-permute-start.3
  331.2 0.9 copy-start.7
  338.8 28.8 %copy-start.9 = (f32[1,768]{1,0:T(1,128)S(1)}, f32[1,768]{1,0:T(1,128)}, u32[]{:S(2)}) copy-start(f32[1,768]{1,0:T(1,128)} %get-tuple-element.134) | copy-start | bytes 9220
  338.8 28.9 %copy-start.10 = (f32[1,768]{1,0:T(1,128)S(1)}, f32[1,768]{1,0:T(1,128)}, u32[]{:S(2)}) copy-start(f32[1,768]{1,0:T(1,128)} %get-tuple-element.132) | copy-start | bytes 9220
  365.0 3.3 collective-permute-start.4
  368.3 0.9 copy-start.6
  369.2 7.8 %copy-start.11 = (f32[1,768]{1,0:T(1,128)S(1)}, f32[1,768]{1,0:T(1,128)}, u32[]{:S(2)}) copy-start(f32[1,768]{1,0:T(1,128)} %get-tuple-element.130) | copy-start | bytes 9220
  603.6 50.1 %copy-start.1 = (s32[2,1,3]{2,1,0:T(1,128)S(1)}, s32[2,1,3]{2,1,0:T(1,128)}, u32[]{:S(2)}) copy-start(s32[2,1,3]{2,1,0:T(1,128)} %param.16) | copy-start | bytes 76
Sparse Core Ops, SparseCore 0:
  302.4 75.2 reduce-scatter.1

commit v8 on v7

--- a/solution.py
+++ b/solution.py
@@ -155,7 +155,7 @@
             def telling():
                 tell(group, rank).start()
 
-    def gather(group):
+    def gather(stage, group):
         def load(first, read):
             @pl.loop(0, (tokens if first else part) // 16)
             def some(index):
@@ -169,8 +169,9 @@
                     lines, axis=0
                 ).astype(low)
 
-        load(0, lambda index: vocab_ref[(head * groups + group) * part + index])
-        for second in range(2):
+        if stage == 0:
+            load(0, lambda index: vocab_ref[(head * groups + group) * part + index])
+        for second in range(2 if stage else 0):
             load(part + second * tokens, lambda index: ids[group, second, 0, index] >> 1)
 
     def own(block, piece, target, sem):
@@ -206,34 +207,34 @@
         device(z, x, 1 - y, c),
         device(z, x, y, 1 - c),
     )
-    rows_x = [
-        pltpu.make_async_remote_copy(
-            rows_ref.at[goal * 2 + 1 - x],
-            far_x.at[goal],
-            rx_send.at[goal],
-            rx_recv.at[goal],
+    spans = (pl.ds(0, part), pl.ds(part, 2 * tokens))
+
+    def rows_x(stage, goal):
+        return pltpu.make_async_remote_copy(
+            rows_ref.at[goal * 2 + 1 - x, spans[stage]],
+            far_x.at[goal, spans[stage]],
+            rx_send.at[stage, goal],
+            rx_recv.at[stage, goal],
             device_id=across_x,
             device_id_type=MESH,
         )
-        for goal in range(depth)
-    ]
-
-    def rows_up(goal):
+
+    def rows_up(stage, goal):
         return pltpu.make_async_remote_copy(
-            total.at[goal],
-            from_low.at[goal],
-            ru_send.at[goal],
-            ru_recv.at[goal],
+            total.at[goal, spans[stage]],
+            from_low.at[goal, spans[stage]],
+            ru_send.at[stage, goal],
+            ru_recv.at[stage, goal],
             device_id=device(z + 1, x, y, c),
             device_id_type=MESH,
         )
 
-    def rows_down(goal):
+    def rows_down(stage, goal):
         return pltpu.make_async_remote_copy(
-            total.at[goal],
-            from_high.at[goal],
-            rd_send.at[goal],
-            rd_recv.at[goal],
+            total.at[goal, spans[stage]],
+            from_high.at[goal, spans[stage]],
+            rd_send.at[stage, goal],
+            rd_recv.at[stage, goal],
             device_id=device(z - 1, x, y, c),
             device_id_type=MESH,
         )
@@ -241,6 +242,62 @@
     goals = [
         goal for pair in zip(range(depth // 2), range(depth - 1, 0, -1)) for goal in pair
     ]
+    goals += [goal for goal in range(depth) if goal not in goals]
+
+    def reduce(stage):
+        span = spans[stage]
+        for goal in goals:
+            rows_x(stage, goal).wait_recv()
+            both = rows_ref[goal * 2 + x, span] + far_x[goal, span]
+
+            @pl.when(goal > z)
+            def rising():
+                @pl.when(z > 0)
+                def more():
+                    rows_up(stage, goal).wait_recv()
+                    total[goal, span] = both + from_low[goal, span]
+
+                @pl.when(z == 0)
+                def alone():
+                    total[goal, span] = both
+
+                rows_up(stage, goal).start()
+
+            @pl.when(goal < z)
+            def falling():
+                @pl.when(z < depth - 1)
+                def more():
+                    rows_down(stage, goal).wait_recv()
+                    total[goal, span] = both + from_high[goal, span]
+
+                @pl.when(z == depth - 1)
+                def alone():
+                    total[goal, span] = both
+
+                rows_down(stage, goal).start()
+
+            @pl.when(goal == z)
+            def here():
+                total[goal, span] = both
+
+    def land(stage):
+        span = spans[stage]
+        for goal in range(depth):
+
+            @pl.when(goal == z)
+            def landed():
+                @pl.when(z > 0)
+                def low_part():
+                    rows_up(stage, goal).wait_recv()
+                    total[goal, span] = total[goal, span] + from_low[goal, span]
+
+                @pl.when(z < depth - 1)
+                def high_part():
+                    rows_down(stage, goal).wait_recv()
+                    total[goal, span] = total[goal, span] + from_high[goal, span]
+
+                sum_ref[span] = total[goal, span]
+
     local = [
         pltpu.make_async_copy(pieces[piece], wholes[piece].at[mine], local_sem.at[piece])
         for piece in range(3)
@@ -260,6 +317,12 @@
     for copy in local:
         copy.start()
     shard[pl.ds(shard_rows, 8)] = jnp.zeros((8, shard.shape[1]), jnp.float32)
+    fetch.wait()
+    for goal in goals:
+        gather(0, goal * 2 + 1 - x)
+        rows_x(0, goal).start()
+    for goal in goals:
+        gather(0, goal * 2 + x)
     keep.wait()
     for group in range(groups):
         for second in range(2):
@@ -270,12 +333,6 @@
 
     to_scalars = pltpu.make_async_copy(ids_ref, ids, copy_sem)
     to_scalars.start()
-    fetch.wait()
-    to_scalars.wait()
-    for goal in goals:
-        gather(goal * 2 + 1 - x)
-        rows_x[goal].start()
-    nearer = list(goals)
 
     def spread(block, over_x):
         send(onward, block, across_y, y_sem.at[block // 4])
@@ -283,8 +340,7 @@
             send(onward, block, across_x, x_sem.at[block // 8])
         send(onward, block, across_c, c_sem.at[block // 2])
 
-    for step in range(1, depth):
-
+    def pass_on(step):
         @pl.when(z - step >= 0)
         def risen():
             block = slot(z - step, x, y, c)
@@ -307,68 +363,28 @@
 
             spread(block, True)
 
-        for goal in nearer[:2]:
-            gather(goal * 2 + x)
-        nearer = nearer[2:]
-
-    for goal in goals:
-        rows_x[goal].wait_recv()
-        both = rows_ref[goal * 2 + x] + far_x[goal]
-
-        @pl.when(goal > z)
-        def rising():
-            @pl.when(z > 0)
-            def more():
-                rows_up(goal).wait_recv()
-                total[goal] = both + from_low[goal]
-
-            @pl.when(z == 0)
-            def alone():
-                total[goal] = both
-
-            rows_up(goal).start()
-
-        @pl.when(goal < z)
-        def falling():
-            @pl.when(z < depth - 1)
-            def more():
-                rows_down(goal).wait_recv()
-                total[goal] = both + from_high[goal]
-
-            @pl.when(z == depth - 1)
-            def alone():
-                total[goal] = both
-
-            rows_down(goal).start()
-
-        @pl.when(goal == z)
-        def here():
-            total[goal] = both
-
-    for step in range(depth):
+    def crossed(step):
         for sign in (1, -1) if step else (1,):
 
             @pl.when((z + sign * step >= 0) & (z + sign * step < depth))
-            def crossed():
+            def there():
                 block = slot(z + sign * step, 1 - x, y, c)
                 arrive(block)
                 spread(block, False)
 
-    for goal in range(depth):
-
-        @pl.when(goal == z)
-        def landed():
-            @pl.when(z > 0)
-            def low_part():
-                rows_up(goal).wait_recv()
-                total[goal] = total[goal] + from_low[goal]
-
-            @pl.when(z < depth - 1)
-            def high_part():
-                rows_down(goal).wait_recv()
-                total[goal] = total[goal] + from_high[goal]
-
-            sum_ref[...] = total[goal]
+    pass_on(1)
+    to_scalars.wait()
+    for goal in goals:
+        gather(1, goal * 2 + 1 - x)
+        rows_x(1, goal).start()
+    for step in range(2, min(depth, 3)):
+        pass_on(step)
+    reduce(0)
+    for goal in goals:
+        gather(1, goal * 2 + x)
+    for step in range(3, depth):
+        pass_on(step)
+    land(0)
 
     def shared(source, ref, quarter, group, send_sem, target):
         where = ref.at[quarter, group]
@@ -453,17 +469,22 @@
             shared_y(plane(group), group).start()
             shared_c(plane(group), 0, group).start()
 
+    crossed(0)
+    reduce(1)
+    for step in range(1, depth):
+        crossed(step)
     for place in range(depth):
         group = place * 2 + 1 - x
         shared(None, near_ref, 0, group, sx_send.at[place], across_x).wait_recv()
         shared_y(plane(group), group).start()
         shared_c(plane(group), 0, group).start()
+    land(1)
 
     for step in range(depth):
         for sign in (1, -1) if step else (1,):
 
             @pl.when((z + sign * step >= 0) & (z + sign * step < depth))
-            def crossed():
+            def level():
                 for side in (x, 1 - x):
                     block = slot(z + sign * step, side, 1 - y, c)
                     arrive(block)
@@ -509,15 +530,16 @@
                 tell(group, rank).wait_send()
 
     for goal in range(depth):
-        rows_x[goal].wait_send()
-
-        @pl.when(goal > z)
-        def rose():
-            rows_up(goal).wait_send()
-
-        @pl.when(goal < z)
-        def fell():
-            rows_down(goal).wait_send()
+        for stage in range(2):
+            rows_x(stage, goal).wait_send()
+
+            @pl.when(goal > z)
+            def rose():
+                rows_up(stage, goal).wait_send()
+
+            @pl.when(goal < z)
+            def fell():
+                rows_down(stage, goal).wait_send()
 
     def sent(block, target, sem):
         for piece in range(3):
@@ -565,7 +587,7 @@
         + [dma((3,))]
         + [dma((depth, 3))] * 3
         + [dma((depth * 2, 3)), dma((depth * 4, 3)), dma((blocks, 3))]
-        + [dma((depth,))] * 6
+        + [dma((2, depth))] * 6
         + [dma((groups, 2))] * 2
         + [dma(())] * 2
         + [dma((depth,))] * 3
@@ -1020,11 +1042,9 @@
 def moments(gradient, first, second):
     first_new = beta_one * first + (1.0 - beta_one) * gradient
     second_new = beta_two * second + (1.0 - beta_two) * gradient * gradient
-    direction = (
-        first_new
-        / (1.0 - beta_one**STEP)
-        / (jnp.sqrt(second_new / (1.0 - beta_two**STEP)) + adam_eps)
-    )
+    second_hat = second_new * (1.0 / (1.0 - beta_two**STEP))
+    root = second_hat * lax.rsqrt(second_hat) + adam_eps
+    direction = first_new * (1.0 / (1.0 - beta_one**STEP)) / root
     return direction, first_new, second_new
 
 
@@ -1035,7 +1055,7 @@
     table_new, table_m_new, table_v_new, table_low = refs[14:18]
     values_ref, gains_new, gains_m_new, gains_v_new = refs[18:22]
     block_new, block_m_new, block_v_new, block_low = refs[22:26]
-    bases, turned, factor_ref, bases_sem = refs[26:30]
+    bases, turned, factor_ref, chosen, bases_sem = refs[26:31]
     now = pl.program_id(0)
 
     def base(index):
@@ -1049,8 +1069,8 @@
         lanes = lax.broadcasted_iota(jnp.int32, small_ref.shape, 1)
 
         def value_at(place):
-            chosen = (lines == place // 128) & (lanes == place % 128)
-            return jnp.sum(jnp.where(chosen, small_ref[...], 0.0), axis=(0, 1), keepdims=True)
+            there = (lines == place // 128) & (lanes == place % 128)
+            return jnp.sum(jnp.where(there, small_ref[...], 0.0), axis=(0, 1), keepdims=True)
 
         count = value_at(3 * D + 1)
         gain_grads = sums_ref[...] / count
@@ -1080,31 +1100,36 @@
         mine = (spots >= cuts[index]) & (spots < cuts[index + 1])
         return jnp.where(mine, value, 0.0).astype(low)
 
-    for index in range(4):
-
-        @pl.when(now == min(2 + index, steps - 1))
+    third = turned.shape[0] // 3
+    for turn in range(12):
+        index, lines = turn // 3, pl.ds(turn % 3 * third, third)
+
+        @pl.when(now == min(4 + turn, steps - 1))
         def rotate():
-            base(index).wait()
-            term = contract_rows(
-                bases[index].astype(low), columns(index, grad_ref[...] * factor_ref[0:1, 0:1])
-            )
-            turned[...] = term if index == 0 else turned[...] + term
-
-    @pl.when(now == min(6, steps - 1))
+            if turn % 3 == 0:
+                base(index).wait()
+                chosen[...] = columns(index, grad_ref[...] * factor_ref[0:1, 0:1])
+            term = contract_rows(bases[index, :, lines].astype(low), chosen[...])
+            turned[lines] = term if index == 0 else turned[lines] + term
+
+    @pl.when(now == min(16, steps - 1))
     def move():
         direction, block_m_new[...], block_v_new[...] = moments(
             turned[...], block_m_ref[...], block_v_ref[...]
         )
         turned[...] = direction
-        block_new[...] = jnp.zeros_like(block_new)
-
-    for index in range(4):
-
-        @pl.when(now == min(7 + index, steps - 1))
+
+    for turn in range(12):
+        index, lines = turn // 3, pl.ds(turn % 3 * third, third)
+
+        @pl.when(now == min(17 + turn, steps - 1))
         def rotate_back():
-            block_new[...] += product(bases[index].astype(low), columns(index, turned[...]))
-
-    @pl.when(now == min(11, steps - 1))
+            if turn % 3 == 0:
+                chosen[...] = columns(index, turned[...])
+            term = product(bases[index, lines].astype(low), chosen[...])
+            block_new[lines] = term if index == 0 else block_new[lines] + term
+
+    @pl.when(now == min(29, steps - 1))
     def store():
         block = block_ref[...]
         block = block - rate_block * (block_new[...] + decay_rate * block)
@@ -1116,7 +1141,7 @@
     rows, width = tables[0].shape
     tile = max(
         size
-        for size in range(8, 201, 8)
+        for size in range(8, 101, 8)
         if rows % size == 0 and (size % 16 == 0 or rows % 16)
     )
     steps = rows // tile
@@ -1147,6 +1172,7 @@
             pltpu.VMEM(bases.shape, f32),
             pltpu.VMEM(matrix.shape, f32),
             pltpu.VMEM((8, 128), f32),
+            pltpu.VMEM(matrix.shape, low),
             pltpu.SemaphoreType.DMA((4,)),
         ],
         compiler_params=pltpu.CompilerParams(vmem_limit_bytes=58 * 2**20),
@@ -1154,7 +1180,10 @@
     )(*tables, table_grads, small, gain_sums, *gains, block_grads, *blocks, bases)
 
 
-NONE = pl.CostEstimate(flops=0, bytes_accessed=0, transcendentals=0)
+def cost(flops):
+    return pl.CostEstimate(flops=flops, bytes_accessed=10**6, transcendentals=0)
+
+
 LARGE = 58 * 2**20
 CHUNK = 512
 
@@ -1169,7 +1198,7 @@
     return d_value, jnp.sum(grad * value * r, axis=0, keepdims=True)
 
 
-def local_call(kernel, name, outs, args, scratch=(), remain=()):
+def local_call(kernel, name, flops, outs, args, scratch=(), remain=()):
     vmem = pl.BlockSpec(memory_space=pltpu.VMEM)
     return pl.pallas_call(
         kernel,
@@ -1178,7 +1207,7 @@
         out_specs=[vmem] * len(outs),
         scratch_shapes=list(scratch),
         compiler_params=pltpu.CompilerParams(vmem_limit_bytes=LARGE),
-        cost_estimate=NONE,
+        cost_estimate=cost(flops),
         name=name,
     )(*args)
 
@@ -1207,7 +1236,7 @@
 def project(hidden, gain, weight, cosine, sine):
     rows = hidden.shape[0]
     outs = [((rows, D), low), ((rows, D), low), ((rows, 2 * D), low)]
-    return local_call(project_kernel, "project", outs, [hidden, gain, weight, cosine, sine])
+    return local_call(project_kernel, "project", 6 * 10**9, outs, [hidden, gain, weight, cosine, sine])
 
 
 def allowed(rows_ref, columns_ref):
@@ -1293,7 +1322,7 @@
     count = hidden.shape[0]
     outs = [((count, D), jnp.float32), ((count, D), low), ((count, D), jnp.float32)]
     args = [hidden, query, own, far, rows, columns, w_out, gain, w_gu, w_down]
-    return local_call(forward_kernel, "forward", outs, args, weight_buffers(), (8, 9))
+    return local_call(forward_kernel, "forward", 17 * 10**9, outs, args, weight_buffers(), (8, 9))
 
 
 def backward_kernel(gradient_ref, middle_ref, query_ref, own_ref, far_ref, *refs):
@@ -1384,7 +1413,7 @@
     ]
     args = [gradient, middle, query, own, far, rows, columns, w_out, gain, w_gu, w_down]
     scratch = weight_buffers() + [pltpu.VMEM((count, D), f32)]
-    return local_call(backward_kernel, "backward", outs, args, scratch, (9, 10))
+    return local_call(backward_kernel, "backward", 30 * 10**9, outs, args, scratch, (9, 10))
 
 
 def unproject_kernel(d_query_ref, d_own_ref, d_far_ref, d_middle_ref, hidden_ref, *refs):
@@ -1417,7 +1446,7 @@
     rows = hidden.shape[0]
     outs = [((rows, D), jnp.float32), ((1, D), jnp.float32), ((rows, 3 * D), low)]
     args = [d_query, d_own, d_far, d_middle, hidden, gain, weight, cosine, sine]
-    return local_call(unproject_kernel, "unproject", outs, args)
+    return local_call(unproject_kernel, "unproject", 10**6, outs, args)
 
 
 def weigh_kernel(*refs):
@@ -1480,7 +1509,7 @@
             pl.BlockSpec((384, D), lambda i: (jnp.maximum(i - 6, 0), 0)),
         ],
         compiler_params=pltpu.CompilerParams(vmem_limit_bytes=LARGE),
-        cost_estimate=NONE,
+        cost_estimate=cost(10**6),
         name="weigh",
     )(*[array for array, unused in listed])
 
@@ -1636,12 +1665,9 @@
     )
     d_gain_final, loss_sum = d_gain_final[0], loss_sum[0, 0]
     f32 = jnp.float32
-    d_near = d_near.astype(f32) + swap(d_far, head_count, 1).astype(f32)
-    d_near = d_near.astype(low)
-    d_quarter = d_near[0].astype(f32) + swap(d_near[1], head_count, 2).astype(f32)
-    chosen_grads = lax.psum_scatter(
-        d_quarter.astype(low), "dp", scatter_dimension=0, tiled=True
-    )
+    gradient, d_far = lax.optimization_barrier((gradient, swap(d_far, head_count, 1)))
+    d_near = (d_near.astype(f32) + d_far.astype(f32)).astype(low)
+    d_quarter = swap(d_near[1], head_count, 2)
 
     d_gains = [0.0, 0.0]
     parts = []
@@ -1663,6 +1689,10 @@
             cosine,
             sine,
         )
+        if repeat == 0:
+            gradient, d_quarter = lax.optimization_barrier((gradient, d_quarter))
+            d_quarter = (d_near[0].astype(f32) + d_quarter.astype(f32)).astype(low)
+            chosen_grads = lax.psum_scatter(d_quarter, "dp", scatter_dimension=0, tiled=True)
         parts.append((d_gate, normed_two, action, grad_low, d_qkv, normed, middle_low, merged))
         d_gains = [d_gains[0] + d_gain_one[0], d_gains[1] + d_gain_two[0]]
 

time: 668 us -> 640 us (0.958)
  waiting for transfers between devices: 45.1 us -> 20.6 us
  Pallas kernels: 547 us -> 539 us
    ppermute x7, waiting for transfers between devices: 45 us -> 15.3 us  [swap(): lax.ppermute(value, 'head', [(h, h ^ offset) for h in range(head_count)])]
    pallas_call x1, Pallas kernels: 48.8 us -> 61.5 us  [update(): pl.pallas_call(functools.partial(update_kernel, steps, cuts), grid=(steps...]
    pallas_call x1, Pallas kernels: 163 us -> 152 us  [start(): pl.pallas_call(functools.partial(start_kernel, depth), out_shape=[jax.Sha...]
    pallas_call x1, Pallas kernels: 194 us -> 185 us  [finish(): pl.pallas_call(functools.partial(finish_kernel, depth, heights, tile), ou...]
  transfers between devices with their start and end apart: 8 -> 8, of which waited for: 4 -> 4; matrix products, arithmetic and copies ran while one was open for 3% -> 3% of each run, Pallas kernels for 18% -> 16%
where the time goes in v8:
time: 640 us; the launch traced here: 630 us
  Pallas kernels  539 us (84%)
  local copies, waits for them, and re-layouts  27.4 us (4%)
  other arithmetic  22.8 us (4%)
  waiting for transfers between devices  20.6 us (3%)
  between operations  16 us (2%)
    pallas_call x1, Pallas kernels, finish(): pl.pallas_call(functools.partial(finish_kernel, depth, heights, tile), ou...  185 us
    pallas_call x1, Pallas kernels, start(): pl.pallas_call(functools.partial(start_kernel, depth), out_shape=[jax.Sha...  152 us
    pallas_call x8, Pallas kernels, local_call(): pl.pallas_call(kernel, out_shape=[jax.ShapeDtypeStruct(shape, kind) for s...  108 us
    pallas_call x1, Pallas kernels, update(): pl.pallas_call(functools.partial(update_kernel, steps, cuts), grid=(steps...  61.5 us
    pallas_call x1, Pallas kernels, weigh(): pl.pallas_call(weigh_kernel, grid=(8,), out_shape=[jax.ShapeDtypeStruct((...  19.3 us
    ppermute x7, waiting for transfers between devices, swap(): lax.ppermute(value, 'head', [(h, h ^ offset) for h in range(head_count)])  15.3 us
    pallas_call x1, Pallas kernels, distill(): pl.pallas_call(loss_kernel, out_shape=[jax.ShapeDtypeStruct(hidden.shape,...  13.7 us
  transfers between devices with their start and end apart: 8, of which 4 were waited for; matrix products, arithmetic and copies ran while one was open for 3% of the time, Pallas kernels for 16%

profile of v8, /device:TPU:0, one launch (start us, length us, event | category | flops | bytes accessed | tf_op | source)
XLA Modules:
  0.0 629.7 jit_solution(12807610129000552339)
XLA Ops:
  7.2 0.0 copy-start
  7.2 0.0 reduce-scatter.2.cloned.1.call-start
  7.3 1.5 copy.38
  8.8 0.7 slice.79.refs_1_
  9.5 0.7 fusion.10
  10.3 0.6 fusion.13
  10.9 0.1 mul.55
  11.0 1.4 fusion.11
  12.4 1.3 multiply_add_fusion
  13.7 151.7 %start.1 = (bf16[32,96,768]{2,1,0:T(8,128)(2,1)}, bf16[32,192,768]{2,1,0:T(8,128)(2,1)}, bf16[32,96,768]{2,1,0:T(8,128)(2,1)}, bf16[384,768]{1,0:T(8,128)(2,1)},...) custom-call(bf16[96,768]{1,0:T(8,128)(2,1)} %get-tuple-element.162.refs_0_, ...), custom_call_target="tpu_custom_call" | custom-call | tf_op jit(solution)/shard_map/start/pallas_call | solution.py:573
  165.4 1.9 slice_convert_fusion.hidden_ref
  167.3 4.0 slice.66
  172.7 0.7 convert_add_fusion.1
  173.3 1.2 multiply_sine_fusion
  174.6 5.3 project.2
  179.9 0.4 collective-permute-start
  180.3 2.4 slice.69
  182.7 0.6 fusion.5
  183.4 0.8 copy.39.rows_ref.refs_0_
  184.2 0.6 pad_add_fusion.columns_ref.refs_1_
  184.8 0.9 copy-done.9
  185.7 15.7 %forward.2 = (f32[256,768]{1,0:T(8,128)}, bf16[256,768]{1,0:T(8,128)(2,1)}, f32[256,768]{1,0:T(8,128)}) custom-call(f32[256,768]{1,0:T(8,128)} %slice_convert_fusion.hidden_ref, bf16[256,768]{1,0:T(8,128)(2,1)} %get-tuple-element.88.query_ref, bf16[256,1536]{1,0:T(8,128)(2,1)} %get-tuple-element.89.own_ref, bf16[256,1536]{1,0:T(8,128)(2,1)} %copy-done.9, ...), custom_call_target="tpu_custom_call" | custom-call | flops 16999999488 | bytes 1000000 | tf_op jit(solution)/shard_map/forward/pallas_call | solution.py:1203
  201.4 5.5 project.3
  206.9 0.1 collective-permute-start.1
  207.0 1.2 dynamic-slice_bitcast_fusion
  208.1 1.5 collective-permute-start.2
  209.6 0.8 copy.41.weight_ref
  210.4 15.7 %forward.3 = (f32[256,768]{1,0:T(8,128)}, bf16[256,768]{1,0:T(8,128)(2,1)}, f32[256,768]{1,0:T(8,128)}) custom-call(f32[256,768]{1,0:T(8,128)} %get-tuple-element.92.hidden_ref, bf16[256,768]{1,0:T(8,128)(2,1)} %get-tuple-element.93.query_ref, bf16[256,1536]{1,0:T(8,128)(2,1)} %get-tuple-element.94.own_ref, ...), custom_call_target="tpu_custom_call" | custom-call | flops 16999999488 | bytes 1000000 | tf_op jit(solution)/shard_map/forward/pallas_call | solution.py:1203
  226.2 7.5 %collective-permute-done.2.other_ref = bf16[128,4096]{1,0:T(8,128)(2,1)S(1)} collective-permute-done((bf16[128,4096]{1,0:T(8,128)(2,1)S(1)}, bf16[128,4096]{1,0:T(8,128)(2,1)S(1)}, u32[]{:S(2)}, u32[]{:S(2)}) %collective-permute-start.2) | collective-permute-done | bytes 1048608 | tf_op jit(solution)/shard_map/ppermute | solution.py:60
  233.6 1.0 copy-done.3
  234.6 13.7 %distill.1 = (f32[256,768]{1,0:T(8,128)}, f32[1,768]{1,0:T(1,128)}, f32[8,128]{1,0:T(8,128)}, bf16[2,1024,768]{2,1,0:T(8,128)(2,1)}, bf16[2,1024,768]{2,1,0:T(8,128)(2,1)}) custom-call(f32[256,768]{1,0:T(8,128)} %get-tuple-element.95.hidden_ref, f32[1,768]{1,0:T(1,128)} %get-tuple-element.163.gain_ref, bf16[2,1024,768]{2,1,0:T(8,128)(2,1)} %bitcast.64, ...), custom_call_target="tpu_custom_call" | custom-call | tf_op jit(solution)/shard_map/distill/pallas_call | solution.py:1563
  248.3 0.4 collective-permute-start.3
  248.7 5.9 collective-permute-done.3
  254.6 2.7 add_convert_fusion
  257.3 1.2 slice_bitcast_fusion.1
  258.5 1.5 collective-permute-start.5
  260.0 26.3 %backward.2 = (bf16[256,768]{1,0:T(8,128)(2,1)}, f32[256,1536]{1,0:T(8,128)}, bf16[256,1536]{1,0:T(8,128)(2,1)}, f32[256,768]{1,0:T(8,128)}, f32[1,768]{1,0:T(1,...) custom-call(f32[256,768]{1,0:T(8,128)} %get-tuple-element.101.gradie, ...), custom_call_target="tpu_custom_call" | custom-call | flops 30000001024 | bytes 1000000 | tf_op jit(solution)/shard_map/backward/pallas_call | solution.py:1203
  286.2 0.1 collective-permute-start.4
  286.3 0.7 dynamic-slice_bitcast_fusion.2
  287.0 1.9 collective-permute-done.4.d_far_ref
  288.9 6.6 %unproject.2 = (f32[256,768]{1,0:T(8,128)}, f32[1,768]{1,0:T(1,128)}, bf16[256,2304]{1,0:T(8,128)(2,1)}) custom-call(bf16[256,768]{1,0:T(8,128)(2,1)} %get-tuple-element.104.d_query_ref, f32[256,1536]{1,0:T(8,128)} %get-tuple-element.105.d_own_ref, bf16[256,1536]{1,0:T(8,128)(2,1)} %collective-permute-done.4.d_far_ref, ...), custom_call_target="tpu_custom_call" | custom-call | flops 1000000 | bytes 1000000 | tf_op jit(solution)/shard_map/unproject/pallas_call | solution.py:1203
  295.5 3.0 fusion
  298.5 0.0 reduce-scatter.2.cloned.1.call-update
  298.5 26.3 %backward.3 = (bf16[256,768]{1,0:T(8,128)(2,1)}, f32[256,1536]{1,0:T(8,128)}, bf16[256,1536]{1,0:T(8,128)(2,1)}, f32[256,768]{1,0:T(8,128)}, f32[1,768]{1,0:T(1,...) custom-call(f32[256,768]{1,0:T(8,128)} %get-tuple-element.111.gradie, ...), custom_call_target="tpu_custom_call" | custom-call | flops 30000001024 | bytes 1000000 | tf_op jit(solution)/shard_map/backward/pallas_call | solution.py:1203
  324.9 0.2 collective-permute-start.6
  325.1 0.6 fusion.6
  325.7 0.6 and_select_fusion.refs_4_
  326.3 1.2 slice.74
  327.6 0.7 add_reduce_fusion
  328.3 0.9 copy-done.4
  329.1 6.6 %unproject.3 = (f32[256,768]{1,0:T(8,128)}, f32[1,768]{1,0:T(1,128)}, bf16[256,2304]{1,0:T(8,128)(2,1)}) custom-call(bf16[256,768]{1,0:T(8,128)(2,1)} %get-tuple-element.121.d_query_ref, f32[256,1536]{1,0:T(8,128)} %get-tuple-element.122.d_own_ref, bf16[256,1536]{1,0:T(8,128)(2,1)} %copy-done.4, f32[256,768]{1,0:T(8,128)} %get-tuple-element.124.d_middle_ref, ...), custom_call_target="tpu_custom_call" | custom-call | flops 1000000 | bytes 1000000 | tf_op jit(solution)/shard_map/unproject/pallas_call | solution.py:1203
  335.7 1.2 convert_element_type.105
  336.9 0.7 add_reduce_fusion.1
  337.6 1.4 concatenate.62
  339.0 19.3 %weigh.1 = (bf16[32,192,768]{2,1,0:T(8,128)(2,1)}, bf16[32,96,768]{2,1,0:T(8,128)(2,1)}, bf16[2304,768]{1,0:T(8,128)(2,1)}, bf16[768,768]{1,0:T(8,128)(2,1)}) custom-call(bf16[256,6144]{1,0:T(8,128)(2,1)} %get-tuple-element.103.refs_0_, bf16[256,6144]{1,0:T(8,128)(2,1)} %get-tuple-element.113.refs_1_, bf16[256,768]{1,0:T(8,128)(2,1)} %get-tuple-element.114.refs_2_, ...), custom_call_target="tpu_custom_call" | custom-call | flops 1000000 | bytes 1000000 | tf_op jit(solution)/shard_map/weigh/pallas_call | solution.py:1495
  358.3 0.6 pad_bitcast_fusion.refs_5_
  358.9 5.1 pad_maximum_fusion.refs_0_
  364.0 5.3 reduce-scatter.2.cloned.1.call-done
  369.3 1.8 pad_maximum_fusion.1.refs_3_
  371.1 184.5 %finish.1 = (f32[384,768]{1,0:T(8,128)}, bf16[4,1040,768]{2,1,0:T(8,128)(2,1)}, f32[24,128]{1,0:T(8,128)}) custom-call(bf16[32,96,768]{2,1,0:T(8,128)(2,1)} %pad_maximum_fusion.refs_0_, bf16[32,192,768]{2,1,0:T(8,128)(2,1)} %get-tuple-element.134.refs_1_, bf16[32,96,768]{2,1,0:T(8,128)(2,1)} %get-tuple-element.135.refs_2_, ...), custom_call_target="tpu_custom_call" | custom-call | tf_op jit(solution)/shard_map/finish/pallas_call | solution.py:1004
  555.6 1.3 reshape.213.refs_5_
  556.9 2.7 copy.44
  559.6 61.5 %update.1 = (f32[4000,768]{1,0:T(8,128)}, f32[4000,768]{1,0:T(8,128)}, f32[4000,768]{1,0:T(8,128)}, bf16[4000,768]{1,0:T(8,128)(2,1)}, f32[8,128]{1,0:T(8,128)},...) custom-call(f32[4000,768]{1,0:T(8,128)} %refs_0_.1, ...), custom_call_target="tpu_custom_call" | custom-call | tf_op jit(solution)/shard_map/update/pallas_call | solution.py:1161
  621.0 1.3 fusion.12
  (37 shorter events, 0.2 us)
Async XLA Ops:
  7.2 3.1 copy-start
  7.2 362.1 %reduce-scatter.2.cloned.1.call-start = ((), (), s32[]{:S(2)}) async-start(), calls=%async_computation.1 | async-start | bytes 1769472 | tf_op jit(solution)/shard_map/reduce_scatter | solution.py:1695
  179.9 4.9 collective-permute-start
  184.8 0.9 copy-start.9
  201.4 5.5 copy-start.2
  206.9 2.7 copy-start.5
  206.9 3.5 collective-permute-start.1
  208.1 25.5 %collective-permute-start.2 = (bf16[128,4096]{1,0:T(8,128)(2,1)S(1)}, bf16[128,4096]{1,0:T(8,128)(2,1)S(1)}, u32[]{:S(2)}, u32[]{:S(2)}) collective-permute-start(bf16[128,4096]{1,0:T(8,128)(2,1)S(1)} %get-tuple-element.159), channel_id=1, source_target_pairs={{0,2},{1,3},{2,0},{3,1},{4,6},{5,7},{6,4},{7,5},{8,10},{9,11},{10,... | collective-permute-start | bytes 3145736 | tf_op jit(solution)/shard_map/ppermute | solution.py:60
  233.6 1.0 copy-start.3
  248.3 6.3 collective-permute-start.3
  258.5 37.0 %collective-permute-start.5 = (bf16[1024,768]{1,0:T(8,128)(2,1)}, bf16[1024,768]{1,0:T(8,128)(2,1)}, u32[]{:S(2)}, u32[]{:S(2)}) collective-permute-start(bf16[1024,768]{1,0:T(8,128)(2,1)} %slice_bitcast_fusion.1), channel_id=1, source_target_pairs={{0,2},{1,3},{2,0},{3,1},{4,6},{5,7},{6,4},{7,5},{8,10},{9,11},{10,... | collective-permute-start | bytes 4718600 | tf_op jit(solution)/shard_map/ppermute | solution.py:60
  286.2 2.7 collective-permute-start.4
  298.5 29.0 %copy-start.6 = (f32[1,768]{1,0:T(1,128)S(1)}, f32[1,768]{1,0:T(1,128)}, u32[]{:S(2)}) copy-start(f32[1,768]{1,0:T(1,128)} %get-tuple-element.142) | copy-start | bytes 9220
  298.5 29.0 %copy-start.7 = (f32[1,768]{1,0:T(1,128)S(1)}, f32[1,768]{1,0:T(1,128)}, u32[]{:S(2)}) copy-start(f32[1,768]{1,0:T(1,128)} %get-tuple-element.140) | copy-start | bytes 9220
  324.9 3.4 collective-permute-start.6
  328.3 0.9 copy-start.4
  329.1 7.8 %copy-start.8 = (f32[1,768]{1,0:T(1,128)S(1)}, f32[1,768]{1,0:T(1,128)}, u32[]{:S(2)}) copy-start(f32[1,768]{1,0:T(1,128)} %get-tuple-element.138) | copy-start | bytes 9220
  559.6 62.8 %copy-start.1 = (s32[2,1,3]{2,1,0:T(1,128)S(1)}, s32[2,1,3]{2,1,0:T(1,128)}, u32[]{:S(2)}) copy-start(s32[2,1,3]{2,1,0:T(1,128)} %param.16) | copy-start | bytes 76
Sparse Core Ops, SparseCore 0:
  298.6 70.6 reduce-scatter.1

commit v9 on v8

--- a/solution.py
+++ b/solution.py
@@ -94,15 +94,15 @@
 
 
 def start_kernel(depth, *refs):
-    pieces = refs[0:3]
-    table_ref, codes_ref, vocab_ref = refs[3:6]
-    wholes = refs[6:9]
-    sum_ref, ids_ref, near_ref, far_ref = refs[9:13]
-    far_x, from_low, from_high, total, rows_ref, shard, ids = refs[13:20]
-    local_sem, up_sem, down_sem, x_sem, y_sem, c_sem, block_sem = refs[20:27]
-    rx_send, rx_recv, ru_send, ru_recv, rd_send, rd_recv = refs[27:33]
-    id_send, id_recv, table_sem, copy_sem = refs[33:37]
-    su_send, sd_send, sx_send, sy_send, sc_send, s_recv, keep_sem = refs[37:44]
+    pieces = refs[0:4]
+    table_ref, codes_ref, vocab_ref = refs[4:7]
+    wholes = refs[7:11]
+    sum_ref, ids_ref, near_ref, far_ref = refs[11:15]
+    far_x, from_low, from_high, total, rows_ref, shard, ids = refs[15:22]
+    local_sem, up_sem, down_sem, x_sem, y_sem, c_sem, block_sem = refs[22:29]
+    rx_send, rx_recv, ru_send, ru_recv, rd_send, rd_recv = refs[29:35]
+    id_send, id_recv, table_sem, copy_sem = refs[35:39]
+    su_send, sd_send, sx_send, sy_send, sc_send, s_recv, keep_sem = refs[39:46]
     z, x, y, c = coordinates(depth)
     mine = slot(z, x, y, c)
     dp, head = z * 2 + x, y * 2 + c
@@ -195,11 +195,11 @@
         )
 
     def send(make, block, target, sem):
-        for piece in range(3):
+        for piece in range(4):
             make(block, piece, target, sem).start()
 
     def arrive(block):
-        for piece in range(3):
+        for piece in range(4):
             onward(block, piece, device(z, x, y, 1 - c), c_sem.at[0]).wait_recv()
 
     across_x, across_y, across_c = (
@@ -300,7 +300,7 @@
 
     local = [
         pltpu.make_async_copy(pieces[piece], wholes[piece].at[mine], local_sem.at[piece])
-        for piece in range(3)
+        for piece in range(4)
     ]
     send(own, mine, across_y, y_sem.at[mine // 4])
 
@@ -542,7 +542,7 @@
                 rows_down(stage, goal).wait_send()
 
     def sent(block, target, sem):
-        for piece in range(3):
+        for piece in range(4):
             onward(block, piece, target, sem).wait_send()
 
     for step in range(depth):
@@ -575,18 +575,18 @@
         out_shape=[jax.ShapeDtypeStruct((blocks,) + piece.shape, low) for piece in pieces]
         + [jax.ShapeDtypeStruct((height, width), low), jax.ShapeDtypeStruct(told, jnp.int32)]
         + [jax.ShapeDtypeStruct((2, groups, vocab_ids.shape[0] // blocks, width), low)] * 2,
-        in_specs=[ANY] * 4
+        in_specs=[ANY] * 5
         + [pl.BlockSpec(memory_space=pltpu.VMEM), pl.BlockSpec(memory_space=pltpu.SMEM)],
-        out_specs=[ANY] * 3 + [pl.BlockSpec(memory_space=pltpu.VMEM)] * 2 + [ANY] * 2,
+        out_specs=[ANY] * 4 + [pl.BlockSpec(memory_space=pltpu.VMEM)] * 2 + [ANY] * 2,
         scratch_shapes=[buffer] * 4
         + [
             pltpu.VMEM((groups, height, width), low),
             pltpu.VMEM((table.shape[0] + 8, width), jnp.float32),
             pltpu.SMEM(told, jnp.int32),
         ]
-        + [dma((3,))]
-        + [dma((depth, 3))] * 3
-        + [dma((depth * 2, 3)), dma((depth * 4, 3)), dma((blocks, 3))]
+        + [dma((4,))]
+        + [dma((depth, 4))] * 3
+        + [dma((depth * 2, 4)), dma((depth * 4, 4)), dma((blocks, 4))]
         + [dma((2, depth))] * 6
         + [dma((groups, 2))] * 2
         + [dma(())] * 2
@@ -1055,7 +1055,7 @@
     table_new, table_m_new, table_v_new, table_low = refs[14:18]
     values_ref, gains_new, gains_m_new, gains_v_new = refs[18:22]
     block_new, block_m_new, block_v_new, block_low = refs[22:26]
-    bases, turned, factor_ref, chosen, bases_sem = refs[26:31]
+    bases, turned, factor_ref, bases_sem = refs[26:30]
     now = pl.program_id(0)
 
     def base(index):
@@ -1100,36 +1100,31 @@
         mine = (spots >= cuts[index]) & (spots < cuts[index + 1])
         return jnp.where(mine, value, 0.0).astype(low)
 
-    third = turned.shape[0] // 3
-    for turn in range(12):
-        index, lines = turn // 3, pl.ds(turn % 3 * third, third)
-
-        @pl.when(now == min(4 + turn, steps - 1))
+    for index in range(4):
+
+        @pl.when(now == min(1 + index, steps - 1))
         def rotate():
-            if turn % 3 == 0:
-                base(index).wait()
-                chosen[...] = columns(index, grad_ref[...] * factor_ref[0:1, 0:1])
-            term = contract_rows(bases[index, :, lines].astype(low), chosen[...])
-            turned[lines] = term if index == 0 else turned[lines] + term
-
-    @pl.when(now == min(16, steps - 1))
+            base(index).wait()
+            term = contract_rows(
+                bases[index].astype(low), columns(index, grad_ref[...] * factor_ref[0:1, 0:1])
+            )
+            turned[...] = term if index == 0 else turned[...] + term
+
+    @pl.when(now == min(5, steps - 1))
     def move():
         direction, block_m_new[...], block_v_new[...] = moments(
             turned[...], block_m_ref[...], block_v_ref[...]
         )
         turned[...] = direction
 
-    for turn in range(12):
-        index, lines = turn // 3, pl.ds(turn % 3 * third, third)
-
-        @pl.when(now == min(17 + turn, steps - 1))
+    for index in range(4):
+
+        @pl.when(now == min(5 + index, steps - 1))
         def rotate_back():
-            if turn % 3 == 0:
-                chosen[...] = columns(index, turned[...])
-            term = product(bases[index, lines].astype(low), chosen[...])
-            block_new[lines] = term if index == 0 else block_new[lines] + term
-
-    @pl.when(now == min(29, steps - 1))
+            term = product(bases[index].astype(low), columns(index, turned[...]))
+            block_new[...] = term if index == 0 else block_new[...] + term
+
+    @pl.when(now == min(8, steps - 1))
     def store():
         block = block_ref[...]
         block = block - rate_block * (block_new[...] + decay_rate * block)
@@ -1141,7 +1136,7 @@
     rows, width = tables[0].shape
     tile = max(
         size
-        for size in range(8, 101, 8)
+        for size in range(8, 401, 8)
         if rows % size == 0 and (size % 16 == 0 or rows % 16)
     )
     steps = rows // tile
@@ -1172,7 +1167,6 @@
             pltpu.VMEM(bases.shape, f32),
             pltpu.VMEM(matrix.shape, f32),
             pltpu.VMEM((8, 128), f32),
-            pltpu.VMEM(matrix.shape, low),
             pltpu.SemaphoreType.DMA((4,)),
         ],
         compiler_params=pltpu.CompilerParams(vmem_limit_bytes=58 * 2**20),
@@ -1322,7 +1316,7 @@
     count = hidden.shape[0]
     outs = [((count, D), jnp.float32), ((count, D), low), ((count, D), jnp.float32)]
     args = [hidden, query, own, far, rows, columns, w_out, gain, w_gu, w_down]
-    return local_call(forward_kernel, "forward", 17 * 10**9, outs, args, weight_buffers(), (8, 9))
+    return local_call(forward_kernel, "forward", 5 * 10**9, outs, args, weight_buffers(), (8, 9))
 
 
 def backward_kernel(gradient_ref, middle_ref, query_ref, own_ref, far_ref, *refs):
@@ -1451,25 +1445,32 @@
 
 def weigh_kernel(*refs):
     pairs = [refs[4 * index : 4 * index + 4] for index in range(4)]
-    outs = refs[16:20]
+    gate_out, down_out, joined, qkv, out = refs[16:21]
     now = pl.program_id(0)
 
     def gradient(index):
         left_one, left_two, right_one, right_two = pairs[index]
         total = contract_rows(left_one[...], right_one[...])
-        total = total + contract_rows(left_two[...], right_two[...])
-        outs[index][...] = total.astype(low).reshape(outs[index].shape)
-
-    gradient(0)
-    gradient(1)
+        return total + contract_rows(left_two[...], right_two[...])
+
+    gate_out[...] = gradient(0).astype(low).reshape(gate_out.shape)
+    down_out[...] = gradient(1).astype(low).reshape(down_out.shape)
 
     @pl.when(now < 6)
-    def qkv():
-        gradient(2)
+    def first():
+        qkv[pl.ds(pl.multiple_of(now * 384, 384), 384)] = gradient(2)
 
     @pl.when(now >= 6)
-    def out():
-        gradient(3)
+    def second():
+        out[pl.ds(pl.multiple_of((now - 6) * 384, 384), 384)] = gradient(3)
+
+    @pl.when(now == 7)
+    def join():
+        blocks = joined.shape[0]
+        tall, flat = 3 * D // blocks, D // blocks
+        for block in range(blocks):
+            parts = [qkv[block * tall : (block + 1) * tall], out[block * flat : (block + 1) * flat]]
+            joined[block] = jnp.concatenate(parts, axis=0).astype(low)
 
 
 def weigh(d_gates, normed_twos, actions, lows, d_qkvs, normeds, middles, merges, blocks):
@@ -1498,16 +1499,15 @@
         out_shape=[
             jax.ShapeDtypeStruct((blocks, 2 * FF // blocks, D), low),
             jax.ShapeDtypeStruct((blocks, FF // blocks, D), low),
-            jax.ShapeDtypeStruct((3 * D, D), low),
-            jax.ShapeDtypeStruct((D, D), low),
+            jax.ShapeDtypeStruct((blocks, 4 * D // blocks, D), low),
         ],
         in_specs=[spec for unused, spec in listed],
         out_specs=[
             pl.BlockSpec((part, 2 * FF // blocks, D), lambda i: (i, 0, 0)),
             pl.BlockSpec((part, FF // blocks, D), lambda i: (i, 0, 0)),
-            pl.BlockSpec((384, D), lambda i: (jnp.minimum(i, 5), 0)),
-            pl.BlockSpec((384, D), lambda i: (jnp.maximum(i - 6, 0), 0)),
+            pl.BlockSpec((blocks, 4 * D // blocks, D), lambda i: (0, 0, 0)),
         ],
+        scratch_shapes=[pltpu.VMEM((3 * D, D), jnp.float32), pltpu.VMEM((D, D), jnp.float32)],
         compiler_params=pltpu.CompilerParams(vmem_limit_bytes=LARGE),
         cost_estimate=cost(10**6),
         name="weigh",
@@ -1606,8 +1606,9 @@
     widths = [3 * D // device_total, D // device_total, 2 * FF // device_total, FF // device_total]
     cuts = [sum(widths[:index]) for index in range(5)]
     block_low = block.T.astype(low)
-    attention, gate_up, down, rows_in, codes, near, far = start(
-        [block_low[: cuts[2]], block_low[cuts[2] : cuts[3]], block_low[cuts[3] :]],
+    pieces = [block_low[cuts[index] : cuts[index + 1]] for index in range(4)]
+    *weights, rows_in, codes, near, far = start(
+        pieces,
         table,
         (token_ids * 2 + valid).reshape(-1, 1, tokens),
         vocab_ids,
@@ -1620,12 +1621,7 @@
     )
     local = jnp.concatenate([vocab, codes >> 1], axis=1) - offset
     owned = (local >= 0) & (local < shard_rows)
-    weights = [
-        attention[:, : cuts[1]].reshape(-1, D),
-        attention[:, cuts[1] :].reshape(-1, D),
-        gate_up.reshape(-1, D),
-        down.reshape(-1, D),
-    ]
+    weights = [weight.reshape(-1, D) for weight in weights]
     near = near.reshape(2, -1, D)
     far = far.reshape(2, -1, D)
     hidden = rows_in[part:].astype(jnp.float32)
@@ -1659,6 +1655,8 @@
         )
         saves.append((hidden, normed, query, own, other, merged, middle))
         hidden = output
+        if repeat == 0:
+            hidden, teacher_far = lax.optimization_barrier((hidden, teacher_far))
 
     gradient, d_gain_final, loss_sum, d_near, d_far = distill(
         hidden, gains[2:3], near, far, teacher_own, teacher_far, weighting[:, None]
@@ -1696,8 +1694,7 @@
         parts.append((d_gate, normed_two, action, grad_low, d_qkv, normed, middle_low, merged))
         d_gains = [d_gains[0] + d_gain_one[0], d_gains[1] + d_gain_two[0]]
 
-    d_gu, d_down, d_qkv, d_out = weigh(*zip(*parts), device_total)
-    d_qkv, d_out = [piece.reshape(device_total, -1, D) for piece in (d_qkv, d_out)]
+    d_gu, d_down, d_attention = weigh(*zip(*parts), device_total)
     rows_back = jnp.concatenate([chosen_grads, gradient.astype(low)], axis=0)
     step = 80 if shard_rows % 80 == 0 else 40
     quarter = -(-shard_rows // (step * head_count)) * step
@@ -1705,7 +1702,7 @@
     small = [d_gains[0], d_gains[1], d_gain_final, loss_sum[None], jnp.sum(weighting)[None]]
     small = jnp.pad(jnp.concatenate(small), (0, 6 * 128 - 2)).reshape(-1, 128)
     block_grads, table_grads, small = finish(
-        [jnp.concatenate([d_qkv, d_out], axis=1), d_gu, d_down],
+        [d_attention, d_gu, d_down],
         rows_back,
         jnp.where(owned, local, -1).reshape(1, -1),
         small,

time: 640 us -> 604 us (0.944)
  Pallas kernels: 539 us -> 513 us
    pallas_call x1, Pallas kernels: 61.5 us -> 40.1 us  [update(): pl.pallas_call(functools.partial(update_kernel, steps, cuts), grid=(steps...]
  transfers between devices with their start and end apart: 8 -> 8, of which waited for: 4 -> 5; matrix products, arithmetic and copies ran while one was open for 3% -> 2% of each run, Pallas kernels for 16% -> 17%
where the time goes in v9:
time: 604 us; the launch traced here: 597 us
  Pallas kernels  513 us (85%)
  waiting for transfers between devices  24.6 us (4%)
  local copies, waits for them, and re-layouts  21.3 us (4%)
  other arithmetic  17.7 us (3%)
  between operations  16 us (3%)
    pallas_call x1, Pallas kernels, finish(): pl.pallas_call(functools.partial(finish_kernel, depth, heights, tile), ou...  178 us
    pallas_call x1, Pallas kernels, start(): pl.pallas_call(functools.partial(start_kernel, depth), out_shape=[jax.Sha...  152 us
    pallas_call x8, Pallas kernels, local_call(): pl.pallas_call(kernel, out_shape=[jax.ShapeDtypeStruct(shape, kind) for s...  108 us
    pallas_call x1, Pallas kernels, update(): pl.pallas_call(functools.partial(update_kernel, steps, cuts), grid=(steps...  40.1 us
    pallas_call x1, Pallas kernels, weigh(): pl.pallas_call(weigh_kernel, grid=(8,), out_shape=[jax.ShapeDtypeStruct((...  20.4 us
    ppermute x7, waiting for transfers between devices, swap(): lax.ppermute(value, 'head', [(h, h ^ offset) for h in range(head_count)])  15.3 us
    pallas_call x1, Pallas kernels, distill(): pl.pallas_call(loss_kernel, out_shape=[jax.ShapeDtypeStruct(hidden.shape,...  13.7 us
  transfers between devices with their start and end apart: 8, of which 5 were waited for; matrix products, arithmetic and copies ran while one was open for 2% of the time, Pallas kernels for 17%

profile of v9, /device:TPU:0, one launch (start us, length us, event | category | flops | bytes accessed | tf_op | source)
XLA Modules:
  0.0 596.8 jit_solution(3889651402728589895)
XLA Ops:
  7.2 0.0 copy-start
  7.2 0.0 reduce-scatter.2.cloned.1.call-start
  7.3 1.5 copy.38
  8.8 0.6 slice.75.refs_1_
  9.4 0.7 slice.74.refs_0_
  10.1 0.7 slice.77.refs_3_
  10.7 0.7 slice.76.refs_2_
  11.5 0.6 fusion.12
  12.1 0.1 mul.55
  12.2 1.4 fusion.10
  13.6 1.3 multiply_add_fusion
  14.9 152.4 %start.1 = (bf16[32,72,768]{2,1,0:T(8,128)(2,1)}, bf16[32,24,768]{2,1,0:T(8,128)(2,1)}, bf16[32,192,768]{2,1,0:T(8,128)(2,1)}, bf16[32,96,768]{2,1,0:T(8,128)(2,...) custom-call(bf16[72,768]{1,0:T(8,128)(2,1)} %slice.74.refs_0_, ...), custom_call_target="tpu_custom_call" | custom-call | tf_op jit(solution)/shard_map/start/pallas_call | solution.py:573
  167.3 1.9 slice_convert_fusion.hidden_ref
  170.5 0.7 convert_add_fusion.1
  171.2 1.2 multiply_sine_fusion
  172.4 5.4 project.2
  177.9 0.4 collective-permute-start
  178.3 1.2 dynamic-slice_bitcast_fusion
  179.5 1.5 collective-permute-start.1
  180.9 0.6 fusion.5
  181.6 0.8 copy.39.rows_ref.refs_0_
  182.4 0.6 pad_add_fusion.columns_ref.refs_1_
  183.0 15.6 %forward.2 = (f32[256,768]{1,0:T(8,128)}, bf16[256,768]{1,0:T(8,128)(2,1)}, f32[256,768]{1,0:T(8,128)}) custom-call(f32[256,768]{1,0:T(8,128)} %slice_convert_fusion.hidden_ref, bf16[256,768]{1,0:T(8,128)(2,1)} %get-tuple-element.90.query_ref, bf16[256,1536]{1,0:T(8,128)(2,1)} %get-tuple-element.91.own_ref, bf16[256,1536]{1,0:T(8,128)(2,1)} %collective-permute-done.far_ref, ...), custom_call_target="tpu_custom_call" | custom-call | flops 5000000000 | bytes 1000000 | tf_op jit(solution)/shard_map/forward/pallas_call | solution.py:1197
  198.6 6.0 %collective-permute-done.1.other_ref = bf16[128,4096]{1,0:T(8,128)(2,1)S(1)} collective-permute-done((bf16[128,4096]{1,0:T(8,128)(2,1)S(1)}, bf16[128,4096]{1,0:T(8,128)(2,1)S(1)}, u32[]{:S(2)}, u32[]{:S(2)}) %collective-permute-start.1) | collective-permute-done | bytes 1048608 | tf_op jit(solution)/shard_map/ppermute | solution.py:60
  204.6 5.7 project.3
  210.4 0.8 copy.41.weight_ref
  211.2 1.7 collective-permute-done.2.far_ref
  212.8 0.9 copy-done.9
  213.7 15.8 %forward.3 = (f32[256,768]{1,0:T(8,128)}, bf16[256,768]{1,0:T(8,128)(2,1)}, f32[256,768]{1,0:T(8,128)}) custom-call(f32[256,768]{1,0:T(8,128)} %get-tuple-element.96.hidden_ref, bf16[256,768]{1,0:T(8,128)(2,1)} %get-tuple-element.97.query_ref, bf16[256,1536]{1,0:T(8,128)(2,1)} %get-tuple-element.98.own_ref, bf16[256,1536]{1,0:T(8,128)(2,1)} %copy-done.9, ...), custom_call_target="tpu_custom_call" | custom-call | flops 5000000000 | bytes 1000000 | tf_op jit(solution)/shard_map/forward/pallas_call | solution.py:1197
  229.5 13.7 %distill.1 = (f32[256,768]{1,0:T(8,128)}, f32[1,768]{1,0:T(1,128)}, f32[8,128]{1,0:T(8,128)}, bf16[2,1024,768]{2,1,0:T(8,128)(2,1)}, bf16[2,1024,768]{2,1,0:T(8,128)(2,1)}) custom-call(f32[256,768]{1,0:T(8,128)} %get-tuple-element.99.hidden_ref, f32[1,768]{1,0:T(1,128)} %get-tuple-element.165.gain_ref, bf16[2,1024,768]{2,1,0:T(8,128)(2,1)} %bitcast.61, ...), custom_call_target="tpu_custom_call" | custom-call | tf_op jit(solution)/shard_map/distill/pallas_call | solution.py:1563
  243.2 0.5 collective-permute-start.3
  243.7 5.7 collective-permute-done.3
  249.4 2.7 add_convert_fusion
  252.1 1.2 slice_bitcast_fusion.1
  253.4 1.5 collective-permute-start.5
  254.8 26.3 %backward.2 = (bf16[256,768]{1,0:T(8,128)(2,1)}, f32[256,1536]{1,0:T(8,128)}, bf16[256,1536]{1,0:T(8,128)(2,1)}, f32[256,768]{1,0:T(8,128)}, f32[1,768]{1,0:T(1,...) custom-call(f32[256,768]{1,0:T(8,128)} %get-tuple-element.106.gradie, ...), custom_call_target="tpu_custom_call" | custom-call | flops 30000001024 | bytes 1000000 | tf_op jit(solution)/shard_map/backward/pallas_call | solution.py:1197
  281.1 0.1 collective-permute-start.4
  281.2 0.7 dynamic-slice_bitcast_fusion.2
  281.9 1.9 collective-permute-done.4.d_far_ref
  283.8 6.6 %unproject.2 = (f32[256,768]{1,0:T(8,128)}, f32[1,768]{1,0:T(1,128)}, bf16[256,2304]{1,0:T(8,128)(2,1)}) custom-call(bf16[256,768]{1,0:T(8,128)(2,1)} %get-tuple-element.109.d_query_ref, f32[256,1536]{1,0:T(8,128)} %get-tuple-element.110.d_own_ref, bf16[256,1536]{1,0:T(8,128)(2,1)} %collective-permute-done.4.d_far_ref, ...), custom_call_target="tpu_custom_call" | custom-call | flops 1000000 | bytes 1000000 | tf_op jit(solution)/shard_map/unproject/pallas_call | solution.py:1197
  290.3 3.0 fusion
  293.3 0.0 reduce-scatter.2.cloned.1.call-update
  293.4 0.0 copy-start.7
  293.4 26.3 %backward.3 = (bf16[256,768]{1,0:T(8,128)(2,1)}, f32[256,1536]{1,0:T(8,128)}, bf16[256,1536]{1,0:T(8,128)(2,1)}, f32[256,768]{1,0:T(8,128)}, f32[1,768]{1,0:T(1,...) custom-call(f32[256,768]{1,0:T(8,128)} %get-tuple-element.116.gradie, ...), custom_call_target="tpu_custom_call" | custom-call | flops 30000001024 | bytes 1000000 | tf_op jit(solution)/shard_map/backward/pallas_call | solution.py:1197
  319.7 0.2 collective-permute-start.6
  319.9 0.6 fusion.6
  320.5 0.6 and_select_fusion.refs_4_
  321.1 1.2 slice.70
  322.3 0.7 add_reduce_fusion
  323.0 0.0 copy-start.4
  323.0 0.9 copy-done.4
  323.9 6.6 %unproject.3 = (f32[256,768]{1,0:T(8,128)}, f32[1,768]{1,0:T(1,128)}, bf16[256,2304]{1,0:T(8,128)(2,1)}) custom-call(bf16[256,768]{1,0:T(8,128)(2,1)} %get-tuple-element.126.d_query_ref, f32[256,1536]{1,0:T(8,128)} %get-tuple-element.127.d_own_ref, bf16[256,1536]{1,0:T(8,128)(2,1)} %copy-done.4, f32[256,768]{1,0:T(8,128)} %get-tuple-element.129.d_middle_ref, ...), custom_call_target="tpu_custom_call" | custom-call | flops 1000000 | bytes 1000000 | tf_op jit(solution)/shard_map/unproject/pallas_call | solution.py:1197
  330.5 1.2 convert_element_type.105
  331.7 0.7 add_reduce_fusion.1
  332.4 1.4 concatenate.58
  333.8 20.4 %weigh.1 = (bf16[32,192,768]{2,1,0:T(8,128)(2,1)}, bf16[32,96,768]{2,1,0:T(8,128)(2,1)}, bf16[32,96,768]{2,1,0:T(8,128)(2,1)}) custom-call(bf16[256,6144]{1,0:T(8,128)(2,1)} %get-tuple-element.108.refs_0_, bf16[256,6144]{1,0:T(8,128)(2,1)} %get-tuple-element.118.refs_1_, bf16[256,768]{1,0:T(8,128)(2,1)} %get-tuple-element.119.refs_2_, ...), custom_call_target="tpu_custom_call" | custom-call | flops 1000000 | bytes 1000000 | tf_op jit(solution)/shard_map/weigh/pallas_call | solution.py:1496
  354.3 0.6 pad_bitcast_fusion.refs_5_
  354.9 9.2 %reduce-scatter.2.cloned.1.call-done = bf16[128,768]{1,0:T(8,128)(2,1)} async-done(((bf16[1024,768]{1,0:T(8,128)(2,1)}), bf16[128,768]{1,0:T(8,128)(2,1)}) %reduce-scatter.2.cloned.1.call-update) | async-done | bytes 196624 | tf_op jit(solution)/shard_map/reduce_scatter | solution.py:1693
  364.1 1.8 pad_maximum_fusion.refs_3_
  365.9 178.3 %finish.1 = (f32[384,768]{1,0:T(8,128)}, bf16[4,1040,768]{2,1,0:T(8,128)(2,1)}, f32[24,128]{1,0:T(8,128)}) custom-call(bf16[32,96,768]{2,1,0:T(8,128)(2,1)} %get-tuple-element.137.refs_0_, bf16[32,192,768]{2,1,0:T(8,128)(2,1)} %get-tuple-element.138.refs_1_, bf16[32,96,768]{2,1,0:T(8,128)(2,1)} %get-tuple-element.139.refs_2_, ...), custom_call_target="tpu_custom_call" | custom-call | tf_op jit(solution)/shard_map/finish/pallas_call | solution.py:1004
  544.1 1.3 reshape.205.refs_5_
  545.4 2.6 copy.44
  548.1 40.1 %update.1 = (f32[4000,768]{1,0:T(8,128)}, f32[4000,768]{1,0:T(8,128)}, f32[4000,768]{1,0:T(8,128)}, bf16[4000,768]{1,0:T(8,128)(2,1)}, f32[8,128]{1,0:T(8,128)},...) custom-call(f32[4000,768]{1,0:T(8,128)} %refs_0_.1, ...), custom_call_target="tpu_custom_call" | custom-call | tf_op jit(solution)/shard_map/update/pallas_call | solution.py:1156
  588.2 1.3 fusion.11
  (36 shorter events, 0.2 us)
Async XLA Ops:
  7.2 4.3 copy-start
  7.2 356.9 %reduce-scatter.2.cloned.1.call-start = ((), (), s32[]{:S(2)}) async-start(), calls=%async_computation.1 | async-start | bytes 1769472 | tf_op jit(solution)/shard_map/reduce_scatter | solution.py:1693
  172.4 5.9 copy-start.2
  177.9 5.1 collective-permute-start
  179.5 25.1 %collective-permute-start.1 = (bf16[128,4096]{1,0:T(8,128)(2,1)S(1)}, bf16[128,4096]{1,0:T(8,128)(2,1)S(1)}, u32[]{:S(2)}, u32[]{:S(2)}) collective-permute-start(bf16[128,4096]{1,0:T(8,128)(2,1)S(1)} %get-tuple-element.164), channel_id=1, source_target_pairs={{0,2},{1,3},{2,0},{3,1},{4,6},{5,7},{6,4},{7,5},{8,10},{9,11},{10,... | collective-permute-start | bytes 3145736 | tf_op jit(solution)/shard_map/ppermute | solution.py:60
  204.6 5.7 copy-start.3
  204.6 5.7 copy-start.5
  210.3 2.5 collective-permute-start.2
  212.8 0.9 copy-start.9
  243.2 6.3 %collective-permute-start.3 = (bf16[2,1024,768]{2,1,0:T(8,128)(2,1)}, bf16[2,1024,768]{2,1,0:T(8,128)(2,1)S(1)}, u32[]{:S(2)}, u32[]{:S(2)}) collective-permute-start(bf16[2,1024,768]{2,1,0:T(8,128)(2,1)} %get-tuple-element.105), channel_id=1, source_target_pairs={{0,1},{1,0},{2,3},{3,2},{4,5},{5,4},{6,7},{7,6},{8,9},{9,8},{10,11... | collective-permute-start | bytes 9437192 | tf_op jit(solution)/shard_map/ppermute | solution.py:60
  253.4 37.0 %collective-permute-start.5 = (bf16[1024,768]{1,0:T(8,128)(2,1)}, bf16[1024,768]{1,0:T(8,128)(2,1)}, u32[]{:S(2)}, u32[]{:S(2)}) collective-permute-start(bf16[1024,768]{1,0:T(8,128)(2,1)} %slice_bitcast_fusion.1), channel_id=1, source_target_pairs={{0,2},{1,3},{2,0},{3,1},{4,6},{5,7},{6,4},{7,5},{8,10},{9,11},{10,... | collective-permute-start | bytes 4718600 | tf_op jit(solution)/shard_map/ppermute | solution.py:60
  281.1 2.7 collective-permute-start.4
  293.4 28.9 %copy-start.6 = (f32[1,768]{1,0:T(1,128)S(1)}, f32[1,768]{1,0:T(1,128)}, u32[]{:S(2)}) copy-start(f32[1,768]{1,0:T(1,128)} %get-tuple-element.146) | copy-start | bytes 9220
  293.4 29.0 %copy-start.7 = (f32[1,768]{1,0:T(1,128)S(1)}, f32[1,768]{1,0:T(1,128)}, u32[]{:S(2)}) copy-start(f32[1,768]{1,0:T(1,128)} %get-tuple-element.144) | copy-start | bytes 9220
  319.7 3.4 collective-permute-start.6
  323.0 0.9 copy-start.4
  323.9 7.8 %copy-start.8 = (f32[1,768]{1,0:T(1,128)S(1)}, f32[1,768]{1,0:T(1,128)}, u32[]{:S(2)}) copy-start(f32[1,768]{1,0:T(1,128)} %get-tuple-element.142) | copy-start | bytes 9220
  548.1 41.4 %copy-start.1 = (s32[2,1,3]{2,1,0:T(1,128)S(1)}, s32[2,1,3]{2,1,0:T(1,128)}, u32[]{:S(2)}) copy-start(s32[2,1,3]{2,1,0:T(1,128)} %param.16) | copy-start | bytes 76
Sparse Core Ops, SparseCore 0:
  293.5 70.5 reduce-scatter.1

commit v10 on v9

--- a/solution.py
+++ b/solution.py
@@ -630,7 +630,8 @@
     local_sem, c_send, c_recv, p_send, p_recv, s_send, s_recv = refs[23:30]
     u_send, u_recv, d_send, d_recv = refs[30:34]
     own_sem, ru_send, rd_send, rx_send, r_recv = refs[34:39]
-    t_send, t_recv, ty_send, ty_recv, o_send, o_recv, e_send, e_recv = refs[39:47]
+    t_send, t_recv, ty_send, ty_recv, o_send, o_recv = refs[39:45]
+    e_send, e_recv, f_send, f_recv = refs[45:49]
     z, x, y, c = coordinates(depth)
     dp = z * 2 + x
     firsts = [sum(heights[:index]) for index in range(3)]
@@ -640,39 +641,50 @@
         device(z, x, 1 - y, c),
         device(z, x, y, 1 - c),
     )
-    even = c == 0
-    across_p = tuple(jnp.where(even, a, b) for a, b in zip(across_y, across_x))
-    across_s = tuple(jnp.where(even, b, a) for a, b in zip(across_y, across_x))
-    own_p, own_s = jnp.where(even, y, x), jnp.where(even, x, y)
-    partners = [across_c, across_y, across_x]
-    reach = 1
-    while reach < depth:
-        partners.append(device(z ^ reach, x, y, c))
-        reach = reach * 2
+
+    def y_first(place, core):
+        return (core == 0) & (place >= 0)
+
+    def across_p(place):
+        first = y_first(place, c)
+        return tuple(jnp.where(first, one, two) for one, two in zip(across_y, across_x))
+
+    def across_s(place):
+        first = y_first(place, c)
+        return tuple(jnp.where(first, two, one) for one, two in zip(across_y, across_x))
+
+    def own_p(place, core=c):
+        return jnp.where(y_first(place, core), y, x)
+
+    def own_s(place, core=c):
+        return jnp.where(y_first(place, core), x, y)
+
+    def own_block(place):
+        return (place * 2 + x) * 2 + y
+
+    def mate(offset):
+        return device(z, (x + offset // 4) % 2, (y + offset // 2) % 2, (c + offset) % 2)
 
     barrier = pltpu.get_barrier_semaphore()
-    for target in partners[:3] + partners[4:]:
-        pl.semaphore_signal(barrier, 1, device_id=target, device_id_type=MESH)
-
-    @pl.when(z > 0)
-    def below():
-        pl.semaphore_signal(barrier, 1, device_id=down, device_id_type=MESH)
-
-    @pl.when(z < depth - 1)
-    def above():
-        pl.semaphore_signal(barrier, 1, device_id=up, device_id_type=MESH)
-
-    pl.semaphore_wait(
-        barrier, len(partners) - 1 + jnp.where(z > 0, 1, 0) + jnp.where(z < depth - 1, 1, 0)
-    )
+    for offset in range(1, 8):
+        pl.semaphore_signal(barrier, 1, device_id=mate(offset), device_id_type=MESH)
+    for other in range(depth):
+
+        @pl.when(other != z)
+        def hello():
+            pl.semaphore_signal(
+                barrier, 1, device_id=device(other, x, y, c), device_id_type=MESH
+            )
+
+    pl.semaphore_wait(barrier, 7 + depth - 1)
 
     def remote(source, goal, send_sem, recv_sem, target):
         return pltpu.make_async_remote_copy(
             source, goal, send_sem, recv_sem, device_id=target, device_id_type=MESH
         )
 
-    def block_of(place, s, p):
-        return place * 4 + jnp.where(even, s * 2 + p, p * 2 + s)
+    def block_of(place, s, p, core=c):
+        return place * 4 + jnp.where(y_first(place, core), s * 2 + p, p * 2 + s)
 
     def local(block, piece):
         return pltpu.make_async_copy(
@@ -693,65 +705,83 @@
     def over_p(place, s):
         pair = place * 2 + s
         return remote(
-            total.at[block_of(place, s, 1 - own_p)],
+            total.at[block_of(place, s, 1 - own_p(place))],
             far_p.at[pair],
             p_send.at[pair],
             p_recv.at[pair],
-            across_p,
+            across_p(place),
         )
 
     def over_s(place):
         return remote(
-            total.at[block_of(place, 1 - own_s, own_p)],
+            total.at[block_of(place, 1 - own_s(place), own_p(place))],
             far_s.at[place],
             s_send.at[place],
             s_recv.at[place],
-            across_s,
-        )
-
-    def rise(place):
-        block = block_of(place, own_s, own_p)
+            across_s(place),
+        )
+
+    half = total.shape[1] // 2
+
+    def rise(place, side):
+        lines = pl.ds(side * half, half)
         return remote(
-            total.at[block], from_low.at[place], u_send.at[place], u_recv.at[place], up
-        )
-
-    def fall(place):
-        block = block_of(place, own_s, own_p)
+            total.at[own_block(place), lines],
+            from_low.at[place, lines],
+            u_send.at[place, side],
+            u_recv.at[place, side],
+            up,
+        )
+
+    def fall(place, side):
+        lines = pl.ds(side * half, half)
         return remote(
-            total.at[block], from_high.at[place], d_send.at[place], d_recv.at[place], down
-        )
-
-    def own_rows(send_sem, target):
-        return remote(rows_ref, rows.at[dp], send_sem, r_recv.at[dp], target)
-
-    def rows_on(place, send_sem, target):
-        there = place * 2 + x
-        return remote(rows.at[there], rows.at[there], send_sem, r_recv.at[there], target)
-
-    own = pltpu.make_async_copy(rows_ref, rows.at[dp], own_sem)
+            total.at[own_block(place), lines],
+            from_high.at[place, lines],
+            d_send.at[place, side],
+            d_recv.at[place, side],
+            down,
+        )
+
+    def add_half(block, side, buffer, place):
+        lines = pl.ds(side * half, half)
+        value = total[block, lines].astype(jnp.float32) + buffer[place, lines].astype(jnp.float32)
+        total[block, lines] = value.astype(low)
+
+    def own_rows(send_sem, target, side):
+        return remote(rows_ref, rows.at[side, z], send_sem, r_recv.at[side, z], target)
+
+    def rows_on(place, send_sem, target, side):
+        return remote(
+            rows.at[0, place], rows.at[side, place], send_sem, r_recv.at[side, place], target
+        )
+
+    own = pltpu.make_async_copy(rows_ref, rows.at[0, z], own_sem)
     own.start()
 
     @pl.when(z < depth - 1)
     def first_up():
-        own_rows(ru_send.at[0], up).start()
+        own_rows(ru_send.at[0], up, 0).start()
 
     @pl.when(z > 0)
     def first_down():
-        own_rows(rd_send.at[0], down).start()
-
-    own_rows(rx_send.at[z], across_x).start()
+        own_rows(rd_send.at[0], down, 0).start()
+
+    own_rows(rx_send.at[z], across_x, 1).start()
 
     for turn in range(2):
-        for s, s_there in ((1 - own_s, 1 - own_p), (own_s, own_p)):
-            p, p_there = (1 - own_p, 1 - own_s) if turn == 0 else (own_p, own_s)
+        for side in range(2):
 
             def launch(place):
+                s, p = own_s(place, 1 - c), own_p(place, 1 - c)
+                s, p = (s if side else 1 - s), (p if turn else 1 - p)
+                there = block_of(place, s, p, 1 - c)
+                s, p = own_s(place), own_p(place)
+                s, p = (s if side else 1 - s), (p if turn else 1 - p)
+                here = block_of(place, s, p)
                 for piece in range(3):
-                    over_c(
-                        place * 4 + jnp.where(even, p_there * 2 + s_there, s_there * 2 + p_there),
-                        piece,
-                    ).start()
-                    local(block_of(place, s, p), piece).start()
+                    over_c(there, piece).start()
+                    local(here, piece).start()
 
             by_distance(depth, z, launch)
 
@@ -760,70 +790,66 @@
             local(block, piece).wait()
             over_c(block, piece).wait_recv()
 
-    def give_p():
-        for s in (1 - own_s, own_s):
+    def give_p(along_y):
+        for side in range(2):
 
             def give(place):
-                block = block_of(place, s, 1 - own_p)
-                ready(block)
-                add_into(total, block, (far_c, block))
-                over_p(place, s).start()
+                @pl.when(y_first(place, c) == along_y)
+                def now():
+                    s = own_s(place)
+                    s = s if side else 1 - s
+                    block = block_of(place, s, 1 - own_p(place))
+                    ready(block)
+                    add_into(total, block, (far_c, block))
+                    over_p(place, s).start()
 
             by_distance(depth, z, give)
 
-    @pl.when(even)
-    def early():
-        give_p()
+    give_p(True)
 
     for step in range(1, depth):
 
         @pl.when(z - step >= 0)
         def risen():
-            rows_on(z - step, ru_send.at[step], up).wait_recv()
+            rows_on(z - step, ru_send.at[step], up, 0).wait_recv()
 
             @pl.when(z < depth - 1)
             def further():
-                rows_on(z - step, ru_send.at[step], up).start()
-
-            rows_on(z - step, rx_send.at[z - step], across_x).start()
+                rows_on(z - step, ru_send.at[step], up, 0).start()
+
+            rows_on(z - step, rx_send.at[z - step], across_x, 1).start()
 
         @pl.when(z + step < depth)
         def fallen():
-            rows_on(z + step, rd_send.at[step], down).wait_recv()
+            rows_on(z + step, rd_send.at[step], down, 0).wait_recv()
 
             @pl.when(z > 0)
             def further():
-                rows_on(z + step, rd_send.at[step], down).start()
-
-            rows_on(z + step, rx_send.at[z + step], across_x).start()
-
-    @pl.when(c == 1)
-    def late():
-        give_p()
-
+                rows_on(z + step, rd_send.at[step], down, 0).start()
+
+            rows_on(z + step, rx_send.at[z + step], across_x, 1).start()
+
+    give_p(False)
     own.wait()
-    for place in range(depth):
-        there = place * 2 + 1 - x
-        remote(
-            rows.at[there], rows.at[there], rx_send.at[place], r_recv.at[there], across_x
-        ).wait_recv()
 
     height = part.shape[0]
-    count = places_ref.shape[1]
-
-    def collect(rank, core, goal):
+    count = places_ref.shape[2]
+
+    def collect(rank, core, goal, side):
         @pl.loop(0, height // tile)
         def tiles(index):
             first = index * tile
+            lines = pl.ds(pl.multiple_of(first, tile), tile)
             at = (
                 (rank * 2 + core) * height
                 + first
                 + lax.broadcasted_iota(jnp.int32, (tile, count), 0)
             )
-            picked = jnp.where(at == places_ref[...], 1.0, 0.0).astype(low)
-            goal[pl.ds(pl.multiple_of(first, tile), tile)] = product(
-                picked, rows[...].reshape(count, rows.shape[2])
-            ).astype(low)
+            picked = jnp.where(at == places_ref[side], 1.0, 0.0).astype(low)
+            value = product(picked, rows[side].reshape(count, rows.shape[3]))
+            if side:
+                value = value + goal[lines].astype(jnp.float32)
+            goal[lines] = value.astype(low)
 
     def over_t(rank):
         index = jnp.where(rank == y, 1, 0)
@@ -838,11 +864,15 @@
         def step(index):
             act(pl.ds(pl.multiple_of(index * chunk, chunk), chunk))
 
-    collect(1 - y, 1 - c, given.at[0])
+    collect(1 - y, 1 - c, given.at[0], 0)
+    collect(1 - y, c, part, 0)
+    collect(y, 1 - c, given.at[1], 0)
+    collect(y, c, mine, 0)
+    for place in range(depth):
+        rows_on(place, rx_send.at[place], across_x, 1).wait_recv()
+    collect(1 - y, 1 - c, given.at[0], 1)
     over_t(1 - y).start()
-    collect(y, 1 - c, given.at[1])
-    over_t(y).start()
-    collect(1 - y, c, part)
+    collect(1 - y, c, part, 1)
     over_t(1 - y).wait_recv()
 
     def first_sum(lines):
@@ -853,13 +883,16 @@
     pieces_of(first_sum)
     over_part = remote(part, far_part, ty_send, ty_recv, across_y)
     over_part.start()
-    collect(y, c, mine)
+    collect(y, 1 - c, given.at[1], 1)
+    over_t(y).start()
+    collect(y, c, mine, 1)
 
     def give_s(place):
-        block = block_of(place, 1 - own_s, own_p)
+        s = 1 - own_s(place)
+        block = block_of(place, s, own_p(place))
         ready(block)
-        over_p(place, 1 - own_s).wait_recv()
-        add_into(total, block, (far_c, block), (far_p, place * 2 + 1 - own_s))
+        over_p(place, s).wait_recv()
+        add_into(total, block, (far_c, block), (far_p, place * 2 + s))
         over_s(place).start()
 
     by_distance(depth, z, give_s)
@@ -896,42 +929,46 @@
     keep.start()
 
     def give_z(place):
-        block = block_of(place, own_s, own_p)
+        block = own_block(place)
+        s = own_s(place)
         ready(block)
-        over_p(place, own_s).wait_recv()
+        over_p(place, s).wait_recv()
         over_s(place).wait_recv()
-        add_into(total, block, (far_c, block), (far_p, place * 2 + own_s), (far_s, place))
-
-        @pl.when(place > z)
-        def rising():
-            @pl.when(z > 0)
-            def more():
-                rise(place).wait_recv()
-                add_into(total, block, (from_low, place))
-
-            rise(place).start()
-
-        @pl.when(place < z)
-        def falling():
-            @pl.when(z < depth - 1)
-            def more():
-                fall(place).wait_recv()
-                add_into(total, block, (from_high, place))
-
-            fall(place).start()
+        add_into(total, block, (far_c, block), (far_p, place * 2 + s), (far_s, place))
+        for side in range(2):
+
+            @pl.when(place > z)
+            def rising():
+                @pl.when(z > 0)
+                def more():
+                    rise(place, side).wait_recv()
+                    add_half(block, side, from_low, place)
+
+                rise(place, side).start()
+
+            @pl.when(place < z)
+            def falling():
+                @pl.when(z < depth - 1)
+                def more():
+                    fall(place, side).wait_recv()
+                    add_half(block, side, from_high, place)
+
+                fall(place, side).start()
 
     by_distance(depth, z, give_z)
-    grad_ref[...] = total[block_of(z, own_s, own_p)].astype(jnp.float32)
-
-    @pl.when(z > 0)
-    def low_part():
-        rise(z).wait_recv()
-        grad_ref[...] = grad_ref[...] + from_low[z].astype(jnp.float32)
-
-    @pl.when(z < depth - 1)
-    def high_part():
-        fall(z).wait_recv()
-        grad_ref[...] = grad_ref[...] + from_high[z].astype(jnp.float32)
+    grad_ref[...] = total[own_block(z)].astype(jnp.float32)
+    for side in range(2):
+        there = pl.ds(side * half, half)
+
+        @pl.when(z > 0)
+        def low_part():
+            rise(z, side).wait_recv()
+            grad_ref[there] = grad_ref[there] + from_low[z, there].astype(jnp.float32)
+
+        @pl.when(z < depth - 1)
+        def high_part():
+            fall(z, side).wait_recv()
+            grad_ref[there] = grad_ref[there] + from_high[z, there].astype(jnp.float32)
 
     lines = lax.broadcasted_iota(jnp.int32, small.shape[1:], 0)
     lanes = lax.broadcasted_iota(jnp.int32, small.shape[1:], 1)
@@ -939,16 +976,41 @@
     grad_squares = jnp.sum(grad_ref[...] * grad_ref[...])
     small[0] = small_ref[...] + jnp.where(last, jnp.sum(squares) + grad_squares, 0.0)
 
-    def exchange(turn):
+    def exchange(offset):
         return remote(
-            small.at[turn], far_small.at[turn], e_send.at[turn], e_recv.at[turn], partners[turn]
-        )
-
-    for turn in range(len(partners)):
-        exchange(turn).start()
-        exchange(turn).wait_recv()
-        small[turn + 1] = small[turn] + far_small[turn]
-    small_out[...] = small[len(partners)]
+            small.at[0], small.at[offset], e_send.at[offset], e_recv.at[offset], mate(offset)
+        )
+
+    def announce(other, source):
+        where = far_small.at[source]
+        return remote(where, where, f_send.at[other], f_recv.at[source], device(other, x, y, c))
+
+    for offset in range(1, 8):
+        exchange(offset).start()
+    for offset in range(1, 8):
+        exchange(offset).wait_recv()
+    gathered = jnp.zeros(small.shape[1:], jnp.float32)
+    for rank in range(8):
+        gathered = gathered + small[
+            (x + rank // 4) % 2 * 4 + (y + rank // 2) % 2 * 2 + (c + rank) % 2
+        ]
+    far_small[z] = gathered
+    for other in range(depth):
+
+        @pl.when(other != z)
+        def telling():
+            announce(other, z).start()
+
+    for other in range(depth):
+
+        @pl.when(other != z)
+        def hearing():
+            announce(other, other).wait_recv()
+
+    gathered = far_small[0]
+    for other in range(1, depth):
+        gathered = gathered + far_small[other]
+    small_out[...] = gathered
     out(1 - y, c).wait_recv()
     out(1 - y, c).start()
     out(y, 1 - c).wait_recv()
@@ -959,12 +1021,18 @@
     out_mine(1, across_c).wait_send()
     out(1 - y, c).wait_send()
     over_part.wait_send()
-    for turn in range(len(partners)):
-        exchange(turn).wait_send()
+    for offset in range(1, 8):
+        exchange(offset).wait_send()
+    for other in range(depth):
+
+        @pl.when(other != z)
+        def told():
+            announce(other, z).wait_send()
+
     for rank in range(2):
         over_t(rank).wait_send()
     for place in range(depth):
-        rows_on(place, rx_send.at[place], across_x).wait_send()
+        rows_on(place, rx_send.at[place], across_x, 1).wait_send()
         over_s(place).wait_send()
         for side in range(2):
             over_p(place, side).wait_send()
@@ -972,21 +1040,23 @@
                 for piece in range(3):
                     over_c((place * 2 + side) * 2 + rank, piece).wait_send()
 
-        @pl.when(place > z)
-        def rose():
-            rise(place).wait_send()
-
-        @pl.when(place < z)
-        def fell():
-            fall(place).wait_send()
+        for side in range(2):
+
+            @pl.when(place > z)
+            def rose():
+                rise(place, side).wait_send()
+
+            @pl.when(place < z)
+            def fell():
+                fall(place, side).wait_send()
 
         @pl.when((z - place >= 0) & (z < depth - 1))
         def rows_rose():
-            rows_on(z, ru_send.at[place], up).wait_send()
+            rows_on(z, ru_send.at[place], up, 0).wait_send()
 
         @pl.when((z + place < depth) & (z > 0))
         def rows_fell():
-            rows_on(z, rd_send.at[place], down).wait_send()
+            rows_on(z, rd_send.at[place], down, 0).wait_send()
 
 
 def finish(pieces, rows, places, small, quarter, tile):
@@ -994,7 +1064,6 @@
     heights = [piece.shape[1] for piece in pieces]
     height, width = sum(heights), pieces[0].shape[2]
     depth = blocks // 8
-    turns = 3 + (depth - 1).bit_length()
     dma = pltpu.SemaphoreType.DMA
     vmem = pl.BlockSpec(memory_space=pltpu.VMEM)
 
@@ -1013,30 +1082,39 @@
         scratch_shapes=[buffer(depth * 4), buffer(depth * 4), buffer(depth * 2)]
         + [buffer(depth)] * 3
         + [
-            pltpu.VMEM((depth * 2,) + rows.shape, low),
+            pltpu.VMEM((2, depth) + rows.shape, low),
             pltpu.VMEM((2, quarter, width), low),
             pltpu.VMEM((2, quarter, width), low),
             pltpu.VMEM((quarter, width), low),
             pltpu.VMEM((quarter, width), low),
             pltpu.VMEM((quarter, width), low),
-            pltpu.VMEM((turns + 1,) + small.shape, jnp.float32),
-            pltpu.VMEM((turns,) + small.shape, jnp.float32),
+            pltpu.VMEM((8,) + small.shape, jnp.float32),
+            pltpu.VMEM((depth,) + small.shape, jnp.float32),
         ]
         + [dma((depth * 4, 3))] * 3
         + [dma((depth * 2,))] * 2
-        + [dma((depth,))] * 6
+        + [dma((depth,))] * 2
+        + [dma((depth, 2))] * 4
         + [dma(())]
         + [dma((depth,))] * 3
-        + [dma((depth * 2,))]
+        + [dma((2, depth))]
         + [dma((2,))] * 2
         + [dma(())] * 2
         + [dma((3,)), dma((4,))]
-        + [dma((turns,))] * 2,
+        + [dma((8,))] * 2
+        + [dma((depth,))] * 2,
         compiler_params=pltpu.CompilerParams(
             collective_id=1, has_side_effects=True, vmem_limit_bytes=62 * 2**20
         ),
         name="finish",
     )(*pieces, rows, places, small)
+
+
+def by_side(places, depth):
+    places = places.reshape(depth, 2, -1)
+    x = lax.axis_index("dp") % 2
+    sides = [lax.dynamic_index_in_dim(places, side, 1, keepdims=False) for side in (x, 1 - x)]
+    return jnp.stack(sides).reshape(2, 1, -1)
 
 
 def moments(gradient, first, second):
@@ -1649,15 +1727,14 @@
     saves = []
     for repeat in range(2):
         normed, query, own = project(hidden, gains[0:1], w_qkv, cosine, sine)
+        if repeat == 1:
+            own, teacher_far = lax.optimization_barrier((own, teacher_far))
         other = swap(own, head_count, 1)
         output, merged, middle = forward(
             hidden, query, own, other, queries_at, keys_at, w_out, gains[1:2], w_gu, w_down
         )
         saves.append((hidden, normed, query, own, other, merged, middle))
         hidden = output
-        if repeat == 0:
-            hidden, teacher_far = lax.optimization_barrier((hidden, teacher_far))
-
     gradient, d_gain_final, loss_sum, d_near, d_far = distill(
         hidden, gains[2:3], near, far, teacher_own, teacher_far, weighting[:, None]
     )
@@ -1704,7 +1781,7 @@
     block_grads, table_grads, small = finish(
         [d_attention, d_gu, d_down],
         rows_back,
-        jnp.where(owned, local, -1).reshape(1, -1),
+        by_side(jnp.where(owned, local, -1), dp_count // 2),
         small,
         quarter,
         tile,

time: 604 us -> 593 us (0.982)
  transfers between devices with their start and end apart: 8 -> 8, of which waited for: 5 -> 5; matrix products, arithmetic and copies ran while one was open for 2% -> 2% of each run, Pallas kernels for 17% -> 18%
where the time goes in v10:
time: 593 us; the launch traced here: 586 us
  Pallas kernels  508 us (86%)
  local copies, waits for them, and re-layouts  21.5 us (4%)
  waiting for transfers between devices  18.8 us (3%)
  other arithmetic  17.7 us (3%)
  between operations  15.9 us (3%)
    pallas_call x1, Pallas kernels, finish(): pl.pallas_call(functools.partial(finish_kernel, depth, heights, tile), ou...  173 us
    pallas_call x1, Pallas kernels, start(): pl.pallas_call(functools.partial(start_kernel, depth), out_shape=[jax.Sha...  152 us
    pallas_call x8, Pallas kernels, local_call(): pl.pallas_call(kernel, out_shape=[jax.ShapeDtypeStruct(shape, kind) for s...  108 us
    pallas_call x1, Pallas kernels, update(): pl.pallas_call(functools.partial(update_kernel, steps, cuts), grid=(steps...  40.1 us
    pallas_call x1, Pallas kernels, weigh(): pl.pallas_call(weigh_kernel, grid=(8,), out_shape=[jax.ShapeDtypeStruct((...  20.5 us
    pallas_call x1, Pallas kernels, distill(): pl.pallas_call(loss_kernel, out_shape=[jax.ShapeDtypeStruct(hidden.shape,...  13.7 us
  transfers between devices with their start and end apart: 8, of which 5 were waited for; matrix products, arithmetic and copies ran while one was open for 2% of the time, Pallas kernels for 18%

profile of v10, /device:TPU:0, one launch (start us, length us, event | category | flops | bytes accessed | tf_op | source)
XLA Modules:
  0.0 585.7 jit_solution(1206063219187195784)
XLA Ops:
  7.2 0.0 copy-start
  7.2 0.0 reduce-scatter.2.cloned.1.call-start
  7.3 1.5 copy.41
  8.8 0.6 slice.75.refs_1_
  9.4 0.7 slice.74.refs_0_
  10.1 0.7 slice.77.refs_3_
  10.7 0.7 slice.76.refs_2_
  11.5 0.6 fusion.11
  12.1 0.1 mul.55
  12.2 1.4 fusion.9
  13.6 1.3 multiply_add_fusion
  14.9 152.4 %start.1 = (bf16[32,72,768]{2,1,0:T(8,128)(2,1)}, bf16[32,24,768]{2,1,0:T(8,128)(2,1)}, bf16[32,192,768]{2,1,0:T(8,128)(2,1)}, bf16[32,96,768]{2,1,0:T(8,128)(2,...) custom-call(bf16[72,768]{1,0:T(8,128)(2,1)} %slice.74.refs_0_, ...), custom_call_target="tpu_custom_call" | custom-call | tf_op jit(solution)/shard_map/start/pallas_call | solution.py:573
  167.3 1.9 slice_convert_fusion.hidden_ref
  170.5 0.7 convert_add_fusion.1
  171.2 1.2 multiply_sine_fusion
  172.4 5.4 project.2
  177.9 0.4 collective-permute-start
  178.3 1.2 dynamic-slice_bitcast_fusion
  179.5 1.5 collective-permute-start.1
  180.9 0.6 fusion.4
  181.6 0.6 pad_add_fusion.1.columns_ref.refs_1_
  182.2 0.8 copy.42.rows_ref.refs_0_
  183.0 15.5 %forward.2 = (f32[256,768]{1,0:T(8,128)}, bf16[256,768]{1,0:T(8,128)(2,1)}, f32[256,768]{1,0:T(8,128)}) custom-call(f32[256,768]{1,0:T(8,128)} %slice_convert_fusion.hidden_ref, bf16[256,768]{1,0:T(8,128)(2,1)} %get-tuple-element.90.query_ref, bf16[256,1536]{1,0:T(8,128)(2,1)} %get-tuple-element.91.own_ref, bf16[256,1536]{1,0:T(8,128)(2,1)} %collective-permute-done.far_ref, ...), custom_call_target="tpu_custom_call" | custom-call | flops 5000000000 | bytes 1000000 | tf_op jit(solution)/shard_map/forward/pallas_call | solution.py:1275
  198.6 5.4 project.3
  203.9 0.6 collective-permute-done.1.other_ref
  204.6 1.0 copy.44.weight_ref
  205.6 1.5 collective-permute-done.2.far_ref
  207.1 0.9 copy-done.9
  208.0 15.7 %forward.3 = (f32[256,768]{1,0:T(8,128)}, bf16[256,768]{1,0:T(8,128)(2,1)}, f32[256,768]{1,0:T(8,128)}) custom-call(f32[256,768]{1,0:T(8,128)} %get-tuple-element.95.hidden_ref, bf16[256,768]{1,0:T(8,128)(2,1)} %get-tuple-element.96.query_ref, bf16[256,1536]{1,0:T(8,128)(2,1)} %get-tuple-element.98.own_ref, bf16[256,1536]{1,0:T(8,128)(2,1)} %copy-done.9, ...), custom_call_target="tpu_custom_call" | custom-call | flops 5000000000 | bytes 1000000 | tf_op jit(solution)/shard_map/forward/pallas_call | solution.py:1275
  223.7 13.7 %distill.1 = (f32[256,768]{1,0:T(8,128)}, f32[1,768]{1,0:T(1,128)}, f32[8,128]{1,0:T(8,128)}, bf16[2,1024,768]{2,1,0:T(8,128)(2,1)}, bf16[2,1024,768]{2,1,0:T(8,128)(2,1)}) custom-call(f32[256,768]{1,0:T(8,128)} %get-tuple-element.99.hidden_ref, f32[1,768]{1,0:T(1,128)} %get-tuple-element.167.gain_ref, bf16[2,1024,768]{2,1,0:T(8,128)(2,1)} %bitcast.58, ...), custom_call_target="tpu_custom_call" | custom-call | tf_op jit(solution)/shard_map/distill/pallas_call | solution.py:1641
  237.4 0.3 collective-permute-start.3
  237.7 5.7 collective-permute-done.3
  243.5 2.7 add_convert_fusion
  246.1 1.2 slice_bitcast_fusion.1
  247.4 1.5 collective-permute-start.5
  248.8 26.3 %backward.2 = (bf16[256,768]{1,0:T(8,128)(2,1)}, f32[256,1536]{1,0:T(8,128)}, bf16[256,1536]{1,0:T(8,128)(2,1)}, f32[256,768]{1,0:T(8,128)}, f32[1,768]{1,0:T(1,...) custom-call(f32[256,768]{1,0:T(8,128)} %get-tuple-element.106.gradie, ...), custom_call_target="tpu_custom_call" | custom-call | flops 30000001024 | bytes 1000000 | tf_op jit(solution)/shard_map/backward/pallas_call | solution.py:1275
  275.1 0.1 collective-permute-start.4
  275.2 2.6 collective-permute-done.4.d_far_ref
  277.8 6.6 %unproject.2 = (f32[256,768]{1,0:T(8,128)}, f32[1,768]{1,0:T(1,128)}, bf16[256,2304]{1,0:T(8,128)(2,1)}) custom-call(bf16[256,768]{1,0:T(8,128)(2,1)} %get-tuple-element.109.d_query_ref, f32[256,1536]{1,0:T(8,128)} %get-tuple-element.110.d_own_ref, bf16[256,1536]{1,0:T(8,128)(2,1)} %collective-permute-done.4.d_far_ref, ...), custom_call_target="tpu_custom_call" | custom-call | flops 1000000 | bytes 1000000 | tf_op jit(solution)/shard_map/unproject/pallas_call | solution.py:1275
  284.4 3.0 fusion
  287.4 0.0 reduce-scatter.2.cloned.1.call-update
  287.4 0.0 copy-start.7
  287.4 26.3 %backward.3 = (bf16[256,768]{1,0:T(8,128)(2,1)}, f32[256,1536]{1,0:T(8,128)}, bf16[256,1536]{1,0:T(8,128)(2,1)}, f32[256,768]{1,0:T(8,128)}, f32[1,768]{1,0:T(1,...) custom-call(f32[256,768]{1,0:T(8,128)} %get-tuple-element.116.gradie, ...), custom_call_target="tpu_custom_call" | custom-call | flops 30000001024 | bytes 1000000 | tf_op jit(solution)/shard_map/backward/pallas_call | solution.py:1275
  313.7 0.2 collective-permute-start.6
  313.9 0.7 constant_dynamic-slice_fusion.2
  314.7 0.6 fusion.5
  315.3 0.6 pad_add_fusion.refs_4_
  315.9 1.2 slice.70
  317.1 0.7 add_reduce_fusion
  317.9 0.0 copy-start.4
  317.9 0.9 copy-done.4
  318.7 6.6 %unproject.3 = (f32[256,768]{1,0:T(8,128)}, f32[1,768]{1,0:T(1,128)}, bf16[256,2304]{1,0:T(8,128)(2,1)}) custom-call(bf16[256,768]{1,0:T(8,128)(2,1)} %get-tuple-element.126.d_query_ref, f32[256,1536]{1,0:T(8,128)} %get-tuple-element.127.d_own_ref, bf16[256,1536]{1,0:T(8,128)(2,1)} %copy-done.4, f32[256,768]{1,0:T(8,128)} %get-tuple-element.129.d_middle_ref, ...), custom_call_target="tpu_custom_call" | custom-call | flops 1000000 | bytes 1000000 | tf_op jit(solution)/shard_map/unproject/pallas_call | solution.py:1275
  325.4 1.2 convert_element_type.105
  326.5 0.7 add_reduce_fusion.1
  327.3 1.4 concatenate.63
  328.6 20.5 %weigh.1 = (bf16[32,192,768]{2,1,0:T(8,128)(2,1)}, bf16[32,96,768]{2,1,0:T(8,128)(2,1)}, bf16[32,96,768]{2,1,0:T(8,128)(2,1)}) custom-call(bf16[256,6144]{1,0:T(8,128)(2,1)} %get-tuple-element.108.refs_0_, bf16[256,6144]{1,0:T(8,128)(2,1)} %get-tuple-element.118.refs_1_, bf16[256,768]{1,0:T(8,128)(2,1)} %get-tuple-element.119.refs_2_, ...), custom_call_target="tpu_custom_call" | custom-call | flops 1000000 | bytes 1000000 | tf_op jit(solution)/shard_map/weigh/pallas_call | solution.py:1574
  349.1 0.6 pad_bitcast_fusion.refs_5_
  349.7 8.3 %reduce-scatter.2.cloned.1.call-done = bf16[128,768]{1,0:T(8,128)(2,1)} async-done(((bf16[1024,768]{1,0:T(8,128)(2,1)}), bf16[128,768]{1,0:T(8,128)(2,1)}) %reduce-scatter.2.cloned.1.call-update) | async-done | bytes 196624 | tf_op jit(solution)/shard_map/reduce_scatter | solution.py:1770
  358.0 1.8 pad_maximum_fusion.refs_3_
  359.8 173.4 %finish.1 = (f32[384,768]{1,0:T(8,128)}, bf16[4,1040,768]{2,1,0:T(8,128)(2,1)}, f32[24,128]{1,0:T(8,128)}) custom-call(bf16[32,96,768]{2,1,0:T(8,128)(2,1)} %get-tuple-element.137.refs_0_, bf16[32,192,768]{2,1,0:T(8,128)(2,1)} %get-tuple-element.138.refs_1_, bf16[32,96,768]{2,1,0:T(8,128)(2,1)} %get-tuple-element.139.refs_2_, ...), custom_call_target="tpu_custom_call" | custom-call | tf_op jit(solution)/shard_map/finish/pallas_call | solution.py:1073
  533.2 1.3 reshape.194.refs_5_
  534.5 2.6 copy.49
  537.2 40.1 %update.1 = (f32[4000,768]{1,0:T(8,128)}, f32[4000,768]{1,0:T(8,128)}, f32[4000,768]{1,0:T(8,128)}, bf16[4000,768]{1,0:T(8,128)(2,1)}, f32[8,128]{1,0:T(8,128)},...) custom-call(f32[4000,768]{1,0:T(8,128)} %refs_0_.1, ...), custom_call_target="tpu_custom_call" | custom-call | tf_op jit(solution)/shard_map/update/pallas_call | solution.py:1234
  577.3 1.3 fusion.10
  (41 shorter events, 0.3 us)
Async XLA Ops:
  7.2 4.3 copy-start
  7.2 350.8 %reduce-scatter.2.cloned.1.call-start = ((), (), s32[]{:S(2)}) async-start(), calls=%async_computation.1 | async-start | bytes 1769472 | tf_op jit(solution)/shard_map/reduce_scatter | solution.py:1770
  172.4 5.9 %copy-start.2 = (bf16[2,128,4096]{2,1,0:T(8,128)(2,1)S(1)}, bf16[2,128,4096]{2,1,0:T(8,128)(2,1)}, u32[]{:S(2)}) copy-start(bf16[2,128,4096]{2,1,0:T(8,128)(2,1)} %param.19) | copy-start | bytes 6291460
  177.9 5.1 collective-permute-start
  179.5 25.1 %collective-permute-start.1 = (bf16[128,4096]{1,0:T(8,128)(2,1)S(1)}, bf16[128,4096]{1,0:T(8,128)(2,1)S(1)}, u32[]{:S(2)}, u32[]{:S(2)}) collective-permute-start(bf16[128,4096]{1,0:T(8,128)(2,1)S(1)} %get-tuple-element.164), channel_id=1, source_target_pairs={{0,2},{1,3},{2,0},{3,1},{4,6},{5,7},{6,4},{7,5},{8,10},{9,11},{10,... | collective-permute-start | bytes 3145736 | tf_op jit(solution)/shard_map/ppermute | solution.py:60
  198.6 6.0 %copy-start.5 = (s32[8,2,1,128]{3,2,1,0:T(1,128)S(1)}, s32[8,2,1,128]{3,2,1,0:T(1,128)}, u32[]{:S(2)}) copy-start(s32[8,2,1,128]{3,2,1,0:T(1,128)} %get-tuple-element.103) | copy-start | bytes 24580
  204.6 19.1 %copy-start.3 = (bf16[128,4096]{1,0:T(8,128)(2,1)}, bf16[128,4096]{1,0:T(8,128)(2,1)S(1)}, u32[]{:S(2)}) copy-start(bf16[128,4096]{1,0:T(8,128)(2,1)S(1)} %collective-permute-done.1.other_ref) | copy-start | bytes 3145732
  204.6 2.5 collective-permute-start.2
  207.1 0.9 copy-start.9
  237.4 6.1 %collective-permute-start.3 = (bf16[2,1024,768]{2,1,0:T(8,128)(2,1)}, bf16[2,1024,768]{2,1,0:T(8,128)(2,1)S(1)}, u32[]{:S(2)}, u32[]{:S(2)}) collective-permute-start(bf16[2,1024,768]{2,1,0:T(8,128)(2,1)} %get-tuple-element.105), channel_id=1, source_target_pairs={{0,1},{1,0},{2,3},{3,2},{4,5},{5,4},{6,7},{7,6},{8,9},{9,8},{10,11... | collective-permute-start | bytes 9437192 | tf_op jit(solution)/shard_map/ppermute | solution.py:60
  247.4 37.0 %collective-permute-start.5 = (bf16[1024,768]{1,0:T(8,128)(2,1)}, bf16[1024,768]{1,0:T(8,128)(2,1)}, u32[]{:S(2)}, u32[]{:S(2)}) collective-permute-start(bf16[1024,768]{1,0:T(8,128)(2,1)} %slice_bitcast_fusion.1), channel_id=1, source_target_pairs={{0,2},{1,3},{2,0},{3,1},{4,6},{5,7},{6,4},{7,5},{8,10},{9,11},{10,... | collective-permute-start | bytes 4718600 | tf_op jit(solution)/shard_map/ppermute | solution.py:60
  275.1 2.7 collective-permute-start.4
  287.4 29.7 %copy-start.6 = (f32[1,768]{1,0:T(1,128)S(1)}, f32[1,768]{1,0:T(1,128)}, u32[]{:S(2)}) copy-start(f32[1,768]{1,0:T(1,128)} %get-tuple-element.146) | copy-start | bytes 9220
  287.4 29.8 %copy-start.7 = (f32[1,768]{1,0:T(1,128)S(1)}, f32[1,768]{1,0:T(1,128)}, u32[]{:S(2)}) copy-start(f32[1,768]{1,0:T(1,128)} %get-tuple-element.144) | copy-start | bytes 9220
  313.7 4.2 collective-permute-start.6
  317.9 0.9 copy-start.4
  318.7 7.8 %copy-start.8 = (f32[1,768]{1,0:T(1,128)S(1)}, f32[1,768]{1,0:T(1,128)}, u32[]{:S(2)}) copy-start(f32[1,768]{1,0:T(1,128)} %get-tuple-element.142) | copy-start | bytes 9220
  537.2 41.4 %copy-start.1 = (s32[2,1,3]{2,1,0:T(1,128)S(1)}, s32[2,1,3]{2,1,0:T(1,128)}, u32[]{:S(2)}) copy-start(s32[2,1,3]{2,1,0:T(1,128)} %param.16) | copy-start | bytes 76
Sparse Core Ops, SparseCore 0:
  287.5 70.4 reduce-scatter.1

commit v11 on v10

--- a/solution.py
+++ b/solution.py
@@ -1336,7 +1336,7 @@
     rows = hidden_ref.shape[0]
     first = lax.broadcasted_iota(jnp.int32, (rows, 128), 1) < HD
 
-    @pl.loop(0, D // 128)
+    @pl.loop(0, D // 128, unroll=2)
     def heads(index):
         columns = pl.ds(pl.multiple_of(index * 128, 128), 128)
         values_at = pl.ds(pl.multiple_of(index * 128 + D, 128), 128)
@@ -1440,7 +1440,7 @@
     first = lax.broadcasted_iota(jnp.int32, (rows, 128), 1) < HD
     first_all = lax.broadcasted_iota(jnp.int32, (2 * rows, 128), 1) < HD
 
-    @pl.loop(0, D // 128)
+    @pl.loop(0, D // 128, unroll=2)
     def heads(index):
         columns = pl.ds(pl.multiple_of(index * 128, 128), 128)
         values_at = pl.ds(pl.multiple_of(index * 128 + D, 128), 128)

time: 593 us -> 592 us (level)
  transfers between devices with their start and end apart: 8 -> 8, of which waited for: 5 -> 6; matrix products, arithmetic and copies ran while one was open for 2% -> 2% of each run, Pallas kernels for 18% -> 18%
where the time goes in v11:
time: 592 us; the launch traced here: 585 us
  Pallas kernels  504 us (85%)
  waiting for transfers between devices  21.8 us (4%)
  local copies, waits for them, and re-layouts  21.5 us (4%)
  other arithmetic  17.7 us (3%)
  between operations  15.9 us (3%)
    pallas_call x1, Pallas kernels, finish(): pl.pallas_call(functools.partial(finish_kernel, depth, heights, tile), ou...  173 us
    pallas_call x1, Pallas kernels, start(): pl.pallas_call(functools.partial(start_kernel, depth), out_shape=[jax.Sha...  152 us
    pallas_call x8, Pallas kernels, local_call(): pl.pallas_call(kernel, out_shape=[jax.ShapeDtypeStruct(shape, kind) for s...  104 us
    pallas_call x1, Pallas kernels, update(): pl.pallas_call(functools.partial(update_kernel, steps, cuts), grid=(steps...  40.1 us
    pallas_call x1, Pallas kernels, weigh(): pl.pallas_call(weigh_kernel, grid=(8,), out_shape=[jax.ShapeDtypeStruct((...  20.4 us
    pallas_call x1, Pallas kernels, distill(): pl.pallas_call(loss_kernel, out_shape=[jax.ShapeDtypeStruct(hidden.shape,...  13.7 us
    ppermute x7, waiting for transfers between devices, swap(): lax.ppermute(value, 'head', [(h, h ^ offset) for h in range(head_count)])  11.9 us
  transfers between devices with their start and end apart: 8, of which 6 were waited for; matrix products, arithmetic and copies ran while one was open for 2% of the time, Pallas kernels for 18%

profile of v11, /device:TPU:0, one launch (start us, length us, event | category | flops | bytes accessed | tf_op | source)
XLA Modules:
  0.0 585.2 jit_solution(8319142057139256346)
XLA Ops:
  7.2 0.0 copy-start
  7.2 0.0 reduce-scatter.2.cloned.1.call-start
  7.3 1.5 copy.41
  8.8 0.6 slice.75.refs_1_
  9.4 0.7 slice.74.refs_0_
  10.1 0.7 slice.77.refs_3_
  10.7 0.7 slice.76.refs_2_
  11.5 0.6 fusion.11
  12.1 0.1 mul.55
  12.2 1.4 fusion.9
  13.6 1.3 multiply_add_fusion
  14.9 152.4 %start.1 = (bf16[32,72,768]{2,1,0:T(8,128)(2,1)}, bf16[32,24,768]{2,1,0:T(8,128)(2,1)}, bf16[32,192,768]{2,1,0:T(8,128)(2,1)}, bf16[32,96,768]{2,1,0:T(8,128)(2,...) custom-call(bf16[72,768]{1,0:T(8,128)(2,1)} %slice.74.refs_0_, ...), custom_call_target="tpu_custom_call" | custom-call | tf_op jit(solution)/shard_map/start/pallas_call | solution.py:573
  167.3 1.9 slice_convert_fusion.hidden_ref
  170.5 0.7 convert_add_fusion.1
  171.2 1.2 multiply_sine_fusion
  172.4 5.4 project.2
  177.9 0.4 collective-permute-start
  178.3 1.2 dynamic-slice_bitcast_fusion
  179.5 1.5 collective-permute-start.1
  180.9 0.6 fusion.4
  181.6 0.6 pad_add_fusion.1.columns_ref.refs_1_
  182.2 0.8 copy.42.rows_ref.refs_0_
  183.0 15.1 %forward.2 = (f32[256,768]{1,0:T(8,128)}, bf16[256,768]{1,0:T(8,128)(2,1)}, f32[256,768]{1,0:T(8,128)}) custom-call(f32[256,768]{1,0:T(8,128)} %slice_convert_fusion.hidden_ref, bf16[256,768]{1,0:T(8,128)(2,1)} %get-tuple-element.90.query_ref, bf16[256,1536]{1,0:T(8,128)(2,1)} %get-tuple-element.91.own_ref, bf16[256,1536]{1,0:T(8,128)(2,1)} %collective-permute-done.far_ref, ...), custom_call_target="tpu_custom_call" | custom-call | flops 5000000000 | bytes 1000000 | tf_op jit(solution)/shard_map/forward/pallas_call | solution.py:1275
  198.1 5.4 project.3
  203.5 1.1 collective-permute-done.1.other_ref
  204.6 1.0 copy.44.weight_ref
  205.6 1.5 collective-permute-done.2.far_ref
  207.1 0.9 copy-done.9
  208.0 15.2 %forward.3 = (f32[256,768]{1,0:T(8,128)}, bf16[256,768]{1,0:T(8,128)(2,1)}, f32[256,768]{1,0:T(8,128)}) custom-call(f32[256,768]{1,0:T(8,128)} %get-tuple-element.95.hidden_ref, bf16[256,768]{1,0:T(8,128)(2,1)} %get-tuple-element.96.query_ref, bf16[256,1536]{1,0:T(8,128)(2,1)} %get-tuple-element.98.own_ref, bf16[256,1536]{1,0:T(8,128)(2,1)} %copy-done.9, ...), custom_call_target="tpu_custom_call" | custom-call | flops 5000000000 | bytes 1000000 | tf_op jit(solution)/shard_map/forward/pallas_call | solution.py:1275
  223.2 13.7 %distill.1 = (f32[256,768]{1,0:T(8,128)}, f32[1,768]{1,0:T(1,128)}, f32[8,128]{1,0:T(8,128)}, bf16[2,1024,768]{2,1,0:T(8,128)(2,1)}, bf16[2,1024,768]{2,1,0:T(8,128)(2,1)}) custom-call(f32[256,768]{1,0:T(8,128)} %get-tuple-element.99.hidden_ref, f32[1,768]{1,0:T(1,128)} %get-tuple-element.167.gain_ref, bf16[2,1024,768]{2,1,0:T(8,128)(2,1)} %bitcast.58, ...), custom_call_target="tpu_custom_call" | custom-call | tf_op jit(solution)/shard_map/distill/pallas_call | solution.py:1641
  236.9 0.4 collective-permute-start.3
  237.3 5.7 collective-permute-done.3
  243.0 2.7 add_convert_fusion
  245.7 1.2 slice_bitcast_fusion.1
  246.9 1.5 collective-permute-start.5
  248.4 25.1 %backward.2 = (bf16[256,768]{1,0:T(8,128)(2,1)}, f32[256,1536]{1,0:T(8,128)}, bf16[256,1536]{1,0:T(8,128)(2,1)}, f32[256,768]{1,0:T(8,128)}, f32[1,768]{1,0:T(1,...) custom-call(f32[256,768]{1,0:T(8,128)} %get-tuple-element.106.gradie, ...), custom_call_target="tpu_custom_call" | custom-call | flops 30000001024 | bytes 1000000 | tf_op jit(solution)/shard_map/backward/pallas_call | solution.py:1275
  273.5 0.1 collective-permute-start.4
  273.6 2.6 collective-permute-done.4.d_far_ref
  276.2 6.6 %unproject.2 = (f32[256,768]{1,0:T(8,128)}, f32[1,768]{1,0:T(1,128)}, bf16[256,2304]{1,0:T(8,128)(2,1)}) custom-call(bf16[256,768]{1,0:T(8,128)(2,1)} %get-tuple-element.109.d_query_ref, f32[256,1536]{1,0:T(8,128)} %get-tuple-element.110.d_own_ref, bf16[256,1536]{1,0:T(8,128)(2,1)} %collective-permute-done.4.d_far_ref, ...), custom_call_target="tpu_custom_call" | custom-call | flops 1000000 | bytes 1000000 | tf_op jit(solution)/shard_map/unproject/pallas_call | solution.py:1275
  282.7 1.0 collective-permute-done.5
  283.7 3.0 fusion
  286.7 0.0 reduce-scatter.2.cloned.1.call-update
  286.7 0.0 copy-start.7
  286.7 25.1 %backward.3 = (bf16[256,768]{1,0:T(8,128)(2,1)}, f32[256,1536]{1,0:T(8,128)}, bf16[256,1536]{1,0:T(8,128)(2,1)}, f32[256,768]{1,0:T(8,128)}, f32[1,768]{1,0:T(1,...) custom-call(f32[256,768]{1,0:T(8,128)} %get-tuple-element.116.gradie, ...), custom_call_target="tpu_custom_call" | custom-call | flops 30000001024 | bytes 1000000 | tf_op jit(solution)/shard_map/backward/pallas_call | solution.py:1275
  311.8 0.1 collective-permute-start.6
  311.9 0.7 constant_dynamic-slice_fusion.2
  312.7 0.6 fusion.5
  313.3 0.6 pad_add_fusion.refs_4_
  313.9 1.2 slice.70
  315.1 0.7 add_reduce_fusion
  315.9 0.9 copy-done.4
  316.7 6.6 %unproject.3 = (f32[256,768]{1,0:T(8,128)}, f32[1,768]{1,0:T(1,128)}, bf16[256,2304]{1,0:T(8,128)(2,1)}) custom-call(bf16[256,768]{1,0:T(8,128)(2,1)} %get-tuple-element.126.d_query_ref, f32[256,1536]{1,0:T(8,128)} %get-tuple-element.127.d_own_ref, bf16[256,1536]{1,0:T(8,128)(2,1)} %copy-done.4, f32[256,768]{1,0:T(8,128)} %get-tuple-element.129.d_middle_ref, ...), custom_call_target="tpu_custom_call" | custom-call | flops 1000000 | bytes 1000000 | tf_op jit(solution)/shard_map/unproject/pallas_call | solution.py:1275
  323.3 1.2 convert_element_type.105
  324.5 0.7 add_reduce_fusion.1
  325.2 1.4 concatenate.63
  326.6 20.4 %weigh.1 = (bf16[32,192,768]{2,1,0:T(8,128)(2,1)}, bf16[32,96,768]{2,1,0:T(8,128)(2,1)}, bf16[32,96,768]{2,1,0:T(8,128)(2,1)}) custom-call(bf16[256,6144]{1,0:T(8,128)(2,1)} %get-tuple-element.108.refs_0_, bf16[256,6144]{1,0:T(8,128)(2,1)} %get-tuple-element.118.refs_1_, bf16[256,768]{1,0:T(8,128)(2,1)} %get-tuple-element.119.refs_2_, ...), custom_call_target="tpu_custom_call" | custom-call | flops 1000000 | bytes 1000000 | tf_op jit(solution)/shard_map/weigh/pallas_call | solution.py:1574
  347.1 0.6 pad_bitcast_fusion.refs_5_
  347.7 9.9 %reduce-scatter.2.cloned.1.call-done = bf16[128,768]{1,0:T(8,128)(2,1)} async-done(((bf16[1024,768]{1,0:T(8,128)(2,1)}), bf16[128,768]{1,0:T(8,128)(2,1)}) %reduce-scatter.2.cloned.1.call-update) | async-done | bytes 196624 | tf_op jit(solution)/shard_map/reduce_scatter | solution.py:1770
  357.6 1.8 pad_maximum_fusion.refs_3_
  359.3 173.4 %finish.1 = (f32[384,768]{1,0:T(8,128)}, bf16[4,1040,768]{2,1,0:T(8,128)(2,1)}, f32[24,128]{1,0:T(8,128)}) custom-call(bf16[32,96,768]{2,1,0:T(8,128)(2,1)} %get-tuple-element.137.refs_0_, bf16[32,192,768]{2,1,0:T(8,128)(2,1)} %get-tuple-element.138.refs_1_, bf16[32,96,768]{2,1,0:T(8,128)(2,1)} %get-tuple-element.139.refs_2_, ...), custom_call_target="tpu_custom_call" | custom-call | tf_op jit(solution)/shard_map/finish/pallas_call | solution.py:1073
  532.8 1.3 reshape.194.refs_5_
  534.1 2.6 copy.49
  536.7 40.1 %update.1 = (f32[4000,768]{1,0:T(8,128)}, f32[4000,768]{1,0:T(8,128)}, f32[4000,768]{1,0:T(8,128)}, bf16[4000,768]{1,0:T(8,128)(2,1)}, f32[8,128]{1,0:T(8,128)},...) custom-call(f32[4000,768]{1,0:T(8,128)} %refs_0_.1, ...), custom_call_target="tpu_custom_call" | custom-call | tf_op jit(solution)/shard_map/update/pallas_call | solution.py:1234
  576.8 1.3 fusion.10
  (41 shorter events, 0.3 us)
Async XLA Ops:
  7.2 4.3 copy-start
  7.2 350.4 %reduce-scatter.2.cloned.1.call-start = ((), (), s32[]{:S(2)}) async-start(), calls=%async_computation.1 | async-start | bytes 1769472 | tf_op jit(solution)/shard_map/reduce_scatter | solution.py:1770
  172.4 5.9 %copy-start.2 = (bf16[2,128,4096]{2,1,0:T(8,128)(2,1)S(1)}, bf16[2,128,4096]{2,1,0:T(8,128)(2,1)}, u32[]{:S(2)}) copy-start(bf16[2,128,4096]{2,1,0:T(8,128)(2,1)} %param.19) | copy-start | bytes 6291460
  177.9 5.1 collective-permute-start
  179.5 25.1 %collective-permute-start.1 = (bf16[128,4096]{1,0:T(8,128)(2,1)S(1)}, bf16[128,4096]{1,0:T(8,128)(2,1)S(1)}, u32[]{:S(2)}, u32[]{:S(2)}) collective-permute-start(bf16[128,4096]{1,0:T(8,128)(2,1)S(1)} %get-tuple-element.164), channel_id=1, source_target_pairs={{0,2},{1,3},{2,0},{3,1},{4,6},{5,7},{6,4},{7,5},{8,10},{9,11},{10,... | collective-permute-start | bytes 3145736 | tf_op jit(solution)/shard_map/ppermute | solution.py:60
  198.1 6.5 %copy-start.5 = (s32[8,2,1,128]{3,2,1,0:T(1,128)S(1)}, s32[8,2,1,128]{3,2,1,0:T(1,128)}, u32[]{:S(2)}) copy-start(s32[8,2,1,128]{3,2,1,0:T(1,128)} %get-tuple-element.103) | copy-start | bytes 24580
  204.6 18.6 %copy-start.3 = (bf16[128,4096]{1,0:T(8,128)(2,1)}, bf16[128,4096]{1,0:T(8,128)(2,1)S(1)}, u32[]{:S(2)}) copy-start(bf16[128,4096]{1,0:T(8,128)(2,1)S(1)} %collective-permute-done.1.other_ref) | copy-start | bytes 3145732
  204.6 2.5 collective-permute-start.2
  207.1 0.9 copy-start.9
  236.9 6.1 %collective-permute-start.3 = (bf16[2,1024,768]{2,1,0:T(8,128)(2,1)}, bf16[2,1024,768]{2,1,0:T(8,128)(2,1)S(1)}, u32[]{:S(2)}, u32[]{:S(2)}) collective-permute-start(bf16[2,1024,768]{2,1,0:T(8,128)(2,1)} %get-tuple-element.105), channel_id=1, source_target_pairs={{0,1},{1,0},{2,3},{3,2},{4,5},{5,4},{6,7},{7,6},{8,9},{9,8},{10,11... | collective-permute-start | bytes 9437192 | tf_op jit(solution)/shard_map/ppermute | solution.py:60
  246.9 36.8 %collective-permute-start.5 = (bf16[1024,768]{1,0:T(8,128)(2,1)}, bf16[1024,768]{1,0:T(8,128)(2,1)}, u32[]{:S(2)}, u32[]{:S(2)}) collective-permute-start(bf16[1024,768]{1,0:T(8,128)(2,1)} %slice_bitcast_fusion.1), channel_id=1, source_target_pairs={{0,2},{1,3},{2,0},{3,1},{4,6},{5,7},{6,4},{7,5},{8,10},{9,11},{10,... | collective-permute-start | bytes 4718600 | tf_op jit(solution)/shard_map/ppermute | solution.py:60
  273.5 2.7 collective-permute-start.4
  286.7 28.4 %copy-start.6 = (f32[1,768]{1,0:T(1,128)S(1)}, f32[1,768]{1,0:T(1,128)}, u32[]{:S(2)}) copy-start(f32[1,768]{1,0:T(1,128)} %get-tuple-element.146) | copy-start | bytes 9220
  286.7 28.5 %copy-start.7 = (f32[1,768]{1,0:T(1,128)S(1)}, f32[1,768]{1,0:T(1,128)}, u32[]{:S(2)}) copy-start(f32[1,768]{1,0:T(1,128)} %get-tuple-element.144) | copy-start | bytes 9220
  311.8 4.1 collective-permute-start.6
  315.9 0.9 copy-start.4
  316.7 7.8 %copy-start.8 = (f32[1,768]{1,0:T(1,128)S(1)}, f32[1,768]{1,0:T(1,128)}, u32[]{:S(2)}) copy-start(f32[1,768]{1,0:T(1,128)} %get-tuple-element.142) | copy-start | bytes 9220
  536.7 41.4 %copy-start.1 = (s32[2,1,3]{2,1,0:T(1,128)S(1)}, s32[2,1,3]{2,1,0:T(1,128)}, u32[]{:S(2)}) copy-start(s32[2,1,3]{2,1,0:T(1,128)} %param.16) | copy-start | bytes 76
Sparse Core Ops, SparseCore 0:
  286.8 70.7 reduce-scatter.1
